TPU v7x, 128 devices: a whole 4x4x4 slice. The times are simulated.
128 devices in a mesh: tm: 16 (over y, x), block: 8 (over z, core).
Axes of the slice: x: 4, y: 4, z: 4, core: 2. Of those that a mesh axis runs over, the one named last changes fastest.
Arguments:
- noise: float32 [4096, 64], P('tm'), may hold values from -6 to 6
- retain: float32 [4096, 16], P('tm', 'block'), may hold values from 0.25 to 1
- control_weight: bfloat16 [64, 16, 128, 128], P(None, 'block'), may hold values from -0.0625 to 0.0625
- input_weight: float32 [64, 2048], P(None, 'block'), may hold values from -0.75 to 0.75
- initial_state: float32 [2048], P('block'), may hold values from -6 to 6
- norm_gain: float32 [2048], P('block'), may hold values from 0.5 to 1.5
- gate_weight: bfloat16 [2048, 8192], P(None, 'block'), may hold values from -0.125 to 0.125
- up_weight: bfloat16 [2048, 8192], P(None, 'block'), may hold values from -0.125 to 0.125
- down_weight: bfloat16 [8192, 2048], P('block'), may hold values from -0.09375 to 0.09375
Outputs:
- layer_out: bfloat16 [4096, 2048], P('tm', 'block')
All inputs are finite; a program needn't handle non-finite values.
Results may differ from a plain program's by a relative error of at most 0.013.
Values may be sent and summed in bfloat16 or wider, within the bound.
No kernel may reach another device: no remote copies, remote signals or barrier semaphores. Data moves between devices by JAX's collectives and lax.ppermute only.
A program may use at most 192 MiB of HBM per device.

v0:
```python
import math

import jax
import jax.numpy as jnp
from jax import lax
from jax.sharding import PartitionSpec as P


def matmul_maps(left, right):
    return jnp.einsum("...jk,...kl->...jl", left, right, precision=lax.Precision.HIGHEST)


def matvec_maps(matrix, vector):
    return jnp.einsum("...jk,...k->...j", matrix, vector, precision=lax.Precision.HIGHEST)


def compose(earlier, later):
    return (matmul_maps(later[0], earlier[0]), matvec_maps(later[0], earlier[1]) + later[1])


def body(
    noise,
    retain,
    control_weight,
    input_weight,
    initial_state,
    norm_gain,
    gate_weight,
    up_weight,
    down_weight,
):
    steps_dev, controls = noise.shape
    blocks_here = retain.shape[1]
    width = control_weight.shape[2]
    span_steps = min(16, steps_dev)
    group_count = steps_dev // span_steps
    factor = 1.0 / math.sqrt(steps_dev * lax.axis_size("tm"))
    raw = control_weight.astype(jnp.float32)
    skew = ((raw - jnp.swapaxes(raw, 2, 3)) / math.sqrt(2.0)).astype(jnp.bfloat16)
    noise_low = noise.astype(jnp.bfloat16)
    identity = jnp.eye(width, dtype=jnp.float32)
    drive = jnp.dot(noise, input_weight, precision=lax.Precision.HIGHEST).reshape(
        steps_dev, blocks_here, width
    )
    drive = drive * jnp.sqrt(1.0 - retain * retain)[:, :, None]
    noise_turns = noise_low.reshape(group_count, span_steps, controls).transpose(1, 0, 2)
    retain_turns = retain.reshape(group_count, span_steps, blocks_here).transpose(1, 0, 2)
    drive_turns = drive.reshape(group_count, span_steps, blocks_here, width).transpose(1, 0, 2, 3)

    def build(weights, kept):
        summed = (
            jnp.einsum("gi,ibjk->gbjk", weights, skew, preferred_element_type=jnp.float32) * factor
        )
        return kept[:, :, None, None] * (identity + summed)

    start_prod = jnp.broadcast_to(identity, (group_count, blocks_here, width, width))
    start_off = jnp.zeros((group_count, blocks_here, width), jnp.float32)
    turn_items = (noise_turns, retain_turns, drive_turns)

    def advance(carry, item):
        trans = build(item[0], item[1])
        return (compose(carry, (trans, item[2])), trans)

    group_maps, stored = lax.scan(advance, (start_prod, start_off), turn_items)
    group_prod, group_off = group_maps
    level_prod, level_off = (group_prod, group_off)
    while level_prod.shape[0] > 1:
        members = level_prod.shape[0]
        paired = members // 2 * 2
        merged = compose(
            (level_prod[0:paired:2], level_off[0:paired:2]),
            (level_prod[1:paired:2], level_off[1:paired:2]),
        )
        level_prod, level_off = merged
    device_prod, device_off = (level_prod[0], level_off[0])
    own_start = initial_state.reshape(blocks_here, width)
    every_prod, every_off = (
        lax.all_gather(device_prod[None], "tm", axis=0, tiled=True),
        lax.all_gather(device_off[None], "tm", axis=0, tiled=True),
    )
    position = lax.axis_index("tm")

    def absorb_map(member, state):
        moved = matvec_maps(every_prod[member], state) + every_off[member]
        return jnp.where(member < position, moved, state)

    entry = lax.fori_loop(0, lax.axis_size("tm"), absorb_map, own_start)

    def forward(state, item):
        return (matvec_maps(item[0], state) + item[1], state)

    starts = lax.scan(forward, entry, (group_prod, group_off))[1]

    def replay(state, item):
        fresh = matvec_maps(item[0], state) + item[1]
        return (fresh, fresh)

    history = lax.scan(replay, starts, (stored, drive_turns))[1]
    states = history.transpose(1, 0, 2, 3).reshape(steps_dev, blocks_here, width)
    scaled = states * lax.rsqrt(jnp.mean(states * states, axis=-1, keepdims=True) + 1e-05)
    normed = (
        (scaled * norm_gain.reshape(blocks_here, width))
        .reshape(steps_dev, blocks_here * width)
        .astype(jnp.bfloat16)
    )
    piece = lax.all_gather(normed, "block", axis=1, tiled=True)
    gate = jnp.dot(piece, gate_weight, preferred_element_type=jnp.float32)
    upward = jnp.dot(piece, up_weight, preferred_element_type=jnp.float32)
    hidden = (jax.nn.silu(gate) * upward).astype(jnp.bfloat16)
    partial_out = jnp.dot(hidden, down_weight, preferred_element_type=jnp.float32)
    mixed = lax.psum_scatter(
        partial_out.astype(jnp.bfloat16), "block", scatter_dimension=1, tiled=True
    ).astype(jnp.float32)
    return (states.reshape(steps_dev, blocks_here * width) + mixed).astype(jnp.bfloat16)


def solution(mesh):
    placed = (
        P("tm", None),
        P("tm", "block"),
        P(None, "block", None, None),
        P(None, "block"),
        P("block"),
        P("block"),
        P(None, "block"),
        P(None, "block"),
        P("block", None),
    )
    return jax.shard_map(
        body, mesh=mesh, in_specs=placed, out_specs=P("tm", "block"), check_vma=False
    )
```

profile of v0, /device:TPU:0, one launch (start us, length us, event | category | flops | bytes accessed | tf_op | source)
XLA Modules:
  0.0 493.8 jit_solution(4617019198739204739)
XLA Ops:
  8.0 6.5 %copy.51 = bf16[64,2,128,128]{2,0,3,1:T(8,128)(2,1)} copy(bf16[64,2,128,128]{3,2,1,0:T(8,128)(2,1)} %param.19) | data formatting | bytes 8388608 | tf_op args[2]
  14.6 7.9 %copy.52 = f32[64,2,128,128]{3,0,2,1:T(8,128)} copy(bf16[64,2,128,128]{2,0,3,1:T(8,128)(2,1)} %copy.51) | data formatting | bytes 12582912 | tf_op jit(solution)/shard_map/convert_element_type | solution.py:38
  22.5 8.2 %fusion.21 = bf16[64,2,128,128]{3,0,2,1:T(8,128)(2,1)} fusion(f32[64,2,128,128]{3,0,2,1:T(8,128)} %copy.52, bf16[64,2,128,128]{2,0,3,1:T(8,128)(2,1)} %copy.51), kind=kLoop, calls=%fused_computation.34 | loop fusion | flops 8388608 | bytes 16777216 | tf_op jit(solution)/shard_map/convert_element_type | solution.py:39
  33.7 202.1 %while.55 = (s32[]{:T(128)}, f32[16,2,128,128]{3,2,1,0:T(8,128)}, f32[16,2,128]{2,1,0:T(2,128)S(1)}, f32[16,16,2,128,128]{4,1,3,2,0:T(8,128)}, f32[16,16,2]{1,2,...) while((s32[]{:T(128)}, f32[16,2,128,128]{3,2,1,0:T(8,128)}, ...), condition=%wide.region_1.2_spmd.clone, body=%wide.region_0.1_spmd.clone.sunk | while | flops 880320512 | bytes 29612432 | solution.py:64
  42.1 4.2 fusion.98
  54.7 4.2 fusion.98
  67.3 4.2 fusion.98
  71.6 4.2 bitcast_dynamic-update-slice_fusion.8
  80.0 4.2 fusion.98
  84.3 4.3 bitcast_dynamic-update-slice_fusion.8
  92.7 4.2 fusion.98
  105.3 4.2 fusion.98
  117.9 4.2 fusion.98
  130.5 4.2 fusion.98
  143.2 4.2 fusion.98
  155.8 4.2 fusion.98
  168.4 4.2 fusion.98
  172.7 4.2 bitcast_dynamic-update-slice_fusion.8
  181.1 4.2 fusion.98
  185.3 4.3 bitcast_dynamic-update-slice_fusion.8
  193.7 4.2 fusion.98
  206.4 4.2 fusion.98
  219.0 4.2 fusion.98
  231.6 4.2 fusion.98
  246.7 23.7 %all_gather.10 = f32[16,2,128]{2,1,0:T(2,128)S(1)} all-gather(f32[1,2,128]{2,1,0:T(2,128)S(1)} %slice_add_fusion.3), channel_id=1, replica_groups=mesh['tm'=16,'block'=8] {'tm'}, dimensions={0}, use_global_device_ids=true | all-gather | bytes 17408 | tf_op jit(solution)/shard_map/all_gather | solution.py:79
  270.4 19.1 %all-gather.6.cloned.1.call-done = f32[32,128,128]{2,1,0:T(8,128)} async-done(((f32[2,128,128]{2,1,0:T(8,128)}), f32[32,128,128]{2,1,0:T(8,128)}) %all-gather.6.cloned.1.call-update) | async-done | bytes 2097168 | tf_op jit(solution)/shard_map/all_gather | solution.py:78
  289.5 19.9 %while.52 = (s32[]{:T(128)}, f32[2,128]{1,0:T(2,128)S(1)}, s32[]{:T(128)}, f32[16,2,128,128]{3,2,1,0:T(8,128)}, f32[16,2,128]{2,1,0:T(2,128)S(1)}, /*index=5*/s32[]{:T(128)}) while((s32[]{:T(128)}, f32[2,128]{1,0:T(2,128)S(1)}, s32[]{:T(128)}, f32[16,2,128,128]{3,2,1,0:T(8,128)}, f32[16,2,128]{2,1,0:T(2,128)S(1)}, /*index=5*/s32[]{:T(128)}) %tuple.108), condition=%wide.region_3.4_spmd, body=%wide.region_2.3_spmd.sunk | while | flops 393731 | bytes 137811 | solution.py:87
  309.4 5.4 %while.53 = (s32[]{:T(128)}, f32[2,128]{1,0:T(2,128)S(1)}, f32[16,2,128]{2,1,0:T(2,128)S(1)}, f32[16,2,128,128]{3,2,1,0:T(8,128)S(1)}, f32[16,2,128]{2,1,0:T(2,128)S(1)}, /*index=5*/s32[]{:T(128)}) while((s32[]{:T(128)}, f32[2,128]{1,0:T(2,128)S(1)}, f32[16,2,128]{2,1,0:T(2,128)S(1)}, f32[16,2,128,128]{3,2,1,0:T(8,128)S(1)}, ...), condition=%wide.region_5.6_spmd, body=%wide.region_4.5_spmd.sunk | while | flops 393474 | bytes 138321 | solution.py:92
  314.8 101.9 %while.54 = (s32[]{:T(128)}, f32[16,2,128]{2,1,0:T(2,128)S(1)}, f32[16,16,2,128]{3,2,1,0:T(2,128)S(1)}, f32[16,16,2,128,128]{4,1,3,2,0:T(8,128)}, f32[16,16,2,128]{3,2,1,0:T(2,128)}, /*index=5*/s32[]{:T(128)}) while((s32[]{:T(128)}, f32[16,2,128]{2,1,0:T(2,128)S(1)}, f32[16,16,2,128]{3,2,1,0:T(2,128)S(1)}, f32[16,16,2,128,128]{4,1,3,2,0:T(8,128)}, ...), condition=%wide.region_7.8_spmd, body=%wide.region_6.7_spmd.sunk | while | flops 6295554 | bytes 6389837 | solution.py:98
  418.7 23.1 %all-gather.4.cloned.1.call-done = bf16[256,2048]{1,0:T(8,128)(2,1)} async-done(((bf16[256,256]{1,0:T(8,128)(2,1)}), bf16[256,2048]{1,0:T(8,128)(2,1)}) %all-gather.4.cloned.1.call-update) | async-done | bytes 1048592 | tf_op jit(solution)/shard_map/all_gather | solution.py:106
  445.6 6.9 %convolution_convert_fusion = bf16[256,2048]{1,0:T(8,128)(2,1)} fusion(bf16[1024,2048]{1,0:T(8,128)(2,1)} %param.25, bf16[256,2048]{1,0:T(8,128)(2,1)S(1)} %copy-done.10, bf16[2048,1024]{1,0:T(8,128)(2,1)} %param.24, f32[256,1024]{1,0:T(8,128)S(1)} %fusion.48), kind=kOutput, calls=%fused_computation.35 | convolution fusion | flops 2149580800 | bytes 11534336 | tf_op jit(solution)/shard_map/dot_general | solution.py:110
  452.6 33.1 %reduce-scatter.2.cloned.1.call-done = bf16[256,256]{1,0:T(8,128)(2,1)} async-done(((bf16[256,2048]{1,0:T(8,128)(2,1)}), bf16[256,256]{1,0:T(8,128)(2,1)}) %reduce-scatter.2.cloned.1.call-update) | async-done | bytes 131088 | tf_op jit(solution)/shard_map/reduce_scatter | solution.py:111
  (335 shorter events, 265.8 us)
Async XLA Ops:
  6.5 24.3 %copy-start = (f32[64,256]{1,0:T(8,128)S(1)}, f32[64,256]{1,0:T(8,128)}, u32[]{:S(2)}) copy-start(f32[64,256]{1,0:T(8,128)} %param.20) | copy-start | bytes 196612
  6.5 282.9 %all-gather.6.cloned.1.call-start = ((), (), s32[]{:S(2)}) async-start(), calls=%async_computation.3 | async-start | bytes 2228224 | tf_op jit(solution)/shard_map/all_gather | solution.py:78
  22.5 8.2 %copy-start.8 = (f32[256,64]{0,1:T(8,128)S(1)}, f32[256,64]{0,1:T(8,128)}, u32[]{:S(2)}) copy-start(f32[256,64]{0,1:T(8,128)} %param.17) | copy-start | bytes 196612
  37.9 3.9 copy-start.2
  50.5 3.9 copy-start.2
  63.2 3.9 copy-start.2
  75.8 3.9 copy-start.2
  88.5 3.9 copy-start.2
  101.1 3.9 copy-start.2
  113.8 3.9 copy-start.2
  126.4 3.9 copy-start.2
  139.0 3.9 copy-start.2
  151.6 3.9 copy-start.2
  164.3 3.9 copy-start.2
  176.9 3.9 copy-start.2
  189.6 3.9 copy-start.2
  202.2 3.9 copy-start.2
  214.8 3.9 copy-start.2
  227.4 3.9 copy-start.2
  235.9 0.7 copy-start.6
  239.2 2.9 copy-start.3
  239.9 0.8 copy-start.4
  240.7 48.8 %copy-start.7 = (f32[256]{0:T(256)S(1)}, f32[256]{0:T(256)}, u32[]{:S(2)}) copy-start(f32[256]{0:T(256)} %param.21) | copy-start | bytes 3076
  242.1 199.7 %all-gather.4.cloned.1.call-start = ((), (), s32[]{:S(2)}) async-start(), calls=%async_computation.1 | async-start | bytes 1179648 | tf_op jit(solution)/shard_map/all_gather | solution.py:106
  244.8 69.9 %copy-start.5 = (f32[16,16,2,128]{3,2,1,0:T(2,128)S(1)}, f32[16,16,2,128]{3,2,1,0:T(2,128)}, u32[]{:S(2)}) copy-start(f32[16,16,2,128]{3,2,1,0:T(2,128)} %custom-call.2) | copy-start | bytes 786436
  314.8 103.1 %copy-start.9 = (f32[256]{0:T(256)S(1)}, f32[256]{0:T(256)}, u32[]{:S(2)}) copy-start(f32[256]{0:T(256)} %param.22) | copy-start | bytes 3076
  418.6 67.0 %reduce-scatter.2.cloned.1.call-start = ((), (), s32[]{:S(2)}) async-start(), calls=%async_computation.2 | async-start | bytes 1179648 | tf_op jit(solution)/shard_map/reduce_scatter | solution.py:111
  441.7 3.8 copy-start.10
  445.6 41.6 %copy-start.1 = (f32[64,256]{1,0:T(8,128)S(1)}, f32[64,256]{1,0:T(8,128)}, u32[]{:S(2)}) copy-start(f32[64,256]{1,0:T(8,128)} %param.20) | copy-start | bytes 196612
Sparse Core Ops, SparseCore 0:
  242.2 47.2 all-gather.5
  418.7 22.9 all-gather.3
  452.7 32.9 reduce-scatter.1
where the time goes:
time: 497 us; the launch traced here: 494 us
  matrix products  304 us (61%)
  waiting for transfers between devices  75.3 us (15%)
  local copies, waits for them, and re-layouts  51 us (10%)
  other arithmetic  25 us (5%)
  blocking collectives  23.7 us (5%)
  between operations  13.3 us (3%)
    dot_general x68, matrix products, matvec_maps(): jnp.einsum('...jk,...k->...j', matrix, vector, precision=lax.Precision.HI...  153 us
    dot_general x20, matrix products, matmul_maps(): jnp.einsum('...jk,...kl->...jl', left, right, precision=lax.Precision.HIG...  72.6 us
    dot_general x16, matrix products, build(): jnp.einsum('gi,ibjk->gbjk', weights, skew, preferred_element_type=jnp.flo...  67.4 us
    reduce_scatter x1, waiting for transfers between devices, body(): lax.psum_scatter(partial_out.astype(jnp.bfloat16), 'block', scatter_dimen...  33.1 us
    dynamic_slice x16, local copies, waits for them, and re-layouts, body(): history = lax.scan(replay, starts, (stored, drive_turns))[1]  27.7 us
    all_gather x1, blocking collectives, body(): lax.all_gather(device_off[None], 'tm', axis=0, tiled=True)  23.7 us
    all_gather x1, waiting for transfers between devices, body(): piece = lax.all_gather(normed, 'block', axis=1, tiled=True)  23.1 us
    all_gather x1, waiting for transfers between devices, body(): lax.all_gather(device_prod[None], 'tm', axis=0, tiled=True)  19.1 us
  transfers between devices with their start and end apart: 3, of which 3 were waited for; matrix products, arithmetic and copies ran while one was open for 1% of the time, Pallas kernels for 0%

commit v1 on v0

v1 whole, which is shorter than its diff:
```python
import functools
import math

import jax
import jax.numpy as jnp
from jax import lax
from jax.experimental import pallas as pl
from jax.experimental.pallas import tpu as pltpu
from jax.sharding import PartitionSpec as P

F32 = jnp.float32
BF16 = jnp.bfloat16
GROUPS = 16
SPAN = 16
WIDTH = 128
ROWS = 144
PITCH = 129
MAP_ROWS = 144
VMEM = pl.BlockSpec(memory_space=pltpu.VMEM)
SMEM = pl.BlockSpec(memory_space=pltpu.SMEM)
ANY = pl.BlockSpec(memory_space=pl.ANY)


def split3(v):
    hi = v.astype(BF16)
    rest = v - hi.astype(F32)
    mid = rest.astype(BF16)
    return hi, mid, (rest - mid.astype(F32)).astype(BF16)


def pack_map(ref, b, matrix, offset, kept):
    ref[b, :WIDTH, :] = matrix.astype(BF16)
    row = lax.broadcasted_iota(jnp.int32, (16, WIDTH), 0)
    tail = jnp.zeros((16, WIDTH), F32)
    kept_row = jnp.full((1, WIDTH), 1.0, F32) * kept
    for k, part in enumerate((*split3(offset), *split3(kept_row))):
        tail = jnp.where(row == k, jnp.broadcast_to(part.astype(F32), (16, WIDTH)), tail)
    ref[b, WIDTH:, :] = tail.astype(BF16)


def unpack_map(ref, b):
    matrix = ref[b, :WIDTH, :]
    tail = ref[b, WIDTH:, :].astype(F32)
    offset = tail[0:1] + tail[1:2] + tail[2:3]
    kept = tail[3:4] + tail[4:5] + tail[5:6]
    return matrix, offset, kept


def row_times(h, matrix):
    row = lax.broadcasted_iota(jnp.int32, (16, WIDTH), 0)
    hi = h.astype(BF16).astype(F32)
    lo = h - hi
    both = jnp.where(row == 0, jnp.broadcast_to(hi, (16, WIDTH)), jnp.broadcast_to(lo, (16, WIDTH)))
    out = jnp.dot(both.astype(BF16), matrix, preferred_element_type=F32)
    return out[0:1] + out[1:2]


def compose_kernel(
    noise_ref, retain_s, retain_ref, cw_ref, iw_ref, q_ref, off_ref, send_ref, grp_ref, kept_ref, skw, am, tx, qs, sem
):
    steps = noise_ref.shape[0]
    rows = lax.broadcasted_iota(jnp.int32, (WIDTH, WIDTH), 0)
    cols = lax.broadcasted_iota(jnp.int32, (WIDTH, WIDTH), 1)
    eye = (rows == cols).astype(F32)
    eye_low = eye.astype(BF16)
    noise = noise_ref[...]
    drive = jnp.dot(noise, iw_ref[...], precision=lax.Precision.HIGHEST, preferred_element_type=F32)
    kept = retain_ref[...]
    scale = jnp.sqrt(1.0 - kept * kept)
    for b in range(2):
        off_ref[b * steps : (b + 1) * steps, :] = drive[:, b * WIDTH : (b + 1) * WIDTH] * scale[:, b : b + 1]

    def skew_body(i, carry):
        for b in range(2):
            raw = cw_ref[i, b]
            turned = lax.dot_general(eye_low, raw, (((1,), (1,)), ((), ())), preferred_element_type=F32)
            diff = ((turned - raw.astype(F32)) * (1.0 / math.sqrt(2.0))).astype(BF16).astype(F32)
            skw[pl.ds((b * 64 + i) * PITCH, WIDTH), :] = diff
        return carry

    lax.fori_loop(0, 64, skew_body, 0, unroll=2)
    low = (noise.astype(BF16).astype(F32) * (1.0 / 64.0)).astype(BF16)

    def build_body(j, carry):
        w = jnp.concatenate(
            [skw[pl.ds(b * 64 * PITCH + j, 64, stride=PITCH), :] for b in range(2)], axis=1
        ).astype(BF16)
        out = jnp.dot(low, w, preferred_element_type=F32)
        for b in range(2):
            am[pl.ds(b * steps * PITCH + j, steps, stride=PITCH), :] = out[:, b * WIDTH : (b + 1) * WIDTH]
        return carry

    lax.fori_loop(0, WIDTH, build_body, 0, unroll=2)
    tail_row = lax.broadcasted_iota(jnp.int32, (ROWS - WIDTH, WIDTH), 0)

    def init(c, carry):
        tx[c, :WIDTH, :] = eye
        tx[c, WIDTH:, :] = jnp.zeros((ROWS - WIDTH, WIDTH), F32)
        return carry

    lax.fori_loop(0, 2 * GROUPS, init, 0)

    def step(s, carry):
        slot = lax.rem(s, 2)

        @pl.when(s >= 2)
        def _():
            pltpu.make_async_copy(qs.at[slot], q_ref.at[s], sem.at[slot]).wait()

        def group(g, inner):
            t = g * SPAN + s
            for b in range(2):
                c = g * 2 + b
                x = tx[c]
                w = am[pl.ds((b * steps + t) * PITCH, WIDTH), :].astype(BF16)
                y = (x + jnp.dot(x.astype(BF16), w, preferred_element_type=F32)) * retain_s[t, b]
                push = off_ref[pl.ds(b * steps + t, 1), :]
                tail = y[WIDTH:, :] + jnp.where(
                    tail_row == 0, jnp.broadcast_to(push, (ROWS - WIDTH, WIDTH)), 0.0
                )
                tx[c, :WIDTH, :] = y[:WIDTH]
                tx[c, WIDTH:, :] = tail
                qs[slot, c] = y[:WIDTH].astype(BF16)
                off_ref[pl.ds(b * steps + t, 1), :] = tail[:1]
            return inner

        lax.fori_loop(0, GROUPS, group, 0, unroll=4)
        pltpu.make_async_copy(qs.at[slot], q_ref.at[s], sem.at[slot]).start()
        return carry

    lax.fori_loop(0, SPAN, step, 0)
    for s in (SPAN - 2, SPAN - 1):
        pltpu.make_async_copy(qs.at[s % 2], q_ref.at[s], sem.at[s % 2]).wait()

    keeps = [
        [
            lax.fori_loop(0, SPAN, lambda i, a, g=g, b=b: a * retain_s[g * SPAN + i, b], jnp.float32(1.0))
            for b in range(2)
        ]
        for g in range(GROUPS)
    ]
    for g in range(GROUPS):
        for b in range(2):
            c = g * 2 + b
            kept_ref[g, b] = keeps[g][b]
            m = tx[c, :WIDTH, :] - eye * keeps[g][b]
            tx[c, :WIDTH, :] = m
            grp_ref[c] = m.astype(BF16)
    stride = 1
    while stride < GROUPS:
        for g1 in range(0, GROUPS, 2 * stride):
            g2 = g1 + stride
            for b in range(2):
                first, second = tx[g1 * 2 + b], tx[g2 * 2 + b]
                prod = jnp.dot(first.astype(BF16), second[:WIDTH].astype(BF16), preferred_element_type=F32)
                k1, k2 = keeps[g1][b], keeps[g2][b]
                tx[g1 * 2 + b, :WIDTH, :] = prod[:WIDTH] + first[:WIDTH] * k2 + second[:WIDTH] * k1
                tx[g1 * 2 + b, WIDTH:, :] = prod[WIDTH:] + first[WIDTH:] * k2 + second[WIDTH:]
                keeps[g1][b] = k1 * k2
        stride *= 2
    for b in range(2):
        pack_map(send_ref, b, tx[b, :WIDTH, :], tx[b, WIDTH : WIDTH + 1, :], keeps[0][b])


def compose(noise, retain, control_weight, input_weight):
    steps = noise.shape[0]
    return pl.pallas_call(
        compose_kernel,
        out_shape=(
            jax.ShapeDtypeStruct((SPAN, 2 * GROUPS, WIDTH, WIDTH), BF16),
            jax.ShapeDtypeStruct((2 * steps, WIDTH), F32),
            jax.ShapeDtypeStruct((2, MAP_ROWS, WIDTH), BF16),
            jax.ShapeDtypeStruct((2 * GROUPS, WIDTH, WIDTH), BF16),
            jax.ShapeDtypeStruct((GROUPS, 2), F32),
        ),
        in_specs=[VMEM, SMEM, VMEM, VMEM, VMEM],
        out_specs=(ANY, VMEM, VMEM, VMEM, SMEM),
        scratch_shapes=[
            pltpu.VMEM((128 * PITCH + 8, WIDTH), F32),
            pltpu.VMEM((2 * steps * PITCH + 8, WIDTH), F32),
            pltpu.VMEM((2 * GROUPS, ROWS, WIDTH), F32),
            pltpu.VMEM((2, 2 * GROUPS, WIDTH, WIDTH), BF16),
            pltpu.SemaphoreType.DMA((2,)),
        ],
        compiler_params=pltpu.CompilerParams(vmem_limit_bytes=60 * 1024 * 1024),
        name="compose",
    )(noise, retain, retain, control_weight, input_weight)


def row_kernel(place_s, m0, m1, m2, m3, out_ref, held):
    x = place_s[1]
    for k, ref in enumerate((m0, m1, m2, m3)):
        held[lax.rem(x + 4 - k, 4)] = ref[...]
    for b in range(2):
        parts = []
        for k in range(4):
            matrix, offset, kept = unpack_map(held.at[k], b)
            parts.append((matrix.astype(F32), offset, kept))
        while len(parts) > 1:
            merged = []
            for (m1_, o1, k1), (m2_, o2, k2) in zip(parts[::2], parts[1::2]):
                low = m2_.astype(BF16)
                prod = jnp.dot(m1_.astype(BF16), low, preferred_element_type=F32)
                merged.append((prod + m1_ * k2 + m2_ * k1, row_times(o1, low) + o1 * k2 + o2, k1 * k2))
            parts = merged
        pack_map(out_ref, b, *parts[0])


def row_map(place, maps):
    return pl.pallas_call(
        row_kernel,
        out_shape=jax.ShapeDtypeStruct((2, MAP_ROWS, WIDTH), BF16),
        in_specs=[SMEM] + [VMEM] * 4,
        out_specs=VMEM,
        scratch_shapes=[pltpu.VMEM((4, 2, MAP_ROWS, WIDTH), BF16)],
        name="row_map",
    )(place, *maps)


def replay_kernel(place_s, kept_s, init_ref, y1, y2, y3, x1, x2, x3, off_ref, grp_ref, gain_ref, q_ref,
                  states_ref, normed_ref, start):
    g = pl.program_id(0)
    steps = SPAN * GROUPS

    @pl.when(g == 0)
    def _():
        for b in range(2):
            h = init_ref[b : b + 1, :]
            for place, refs in ((place_s[0], (y1, y2, y3)), (place_s[1], (x1, x2, x3))):
                for k in (3, 2, 1):
                    matrix, offset, kept = unpack_map(refs[k - 1], b)
                    h = jnp.where(k <= place, h * kept + row_times(h, matrix) + offset, h)
            start[b : b + 1, :] = h

    for b in range(2):
        h = start[b : b + 1, :]
        spread = jnp.broadcast_to(h, (WIDTH, WIDTH)).T
        last = off_ref[pl.ds(b * steps + g * SPAN + SPAN - 1, 1), :]
        start[b : b + 1, :] = h * kept_s[g, b] + row_times(h, grp_ref[g * 2 + b]) + last
        rows = []
        for s in range(SPAN):
            rows.append(jnp.sum(q_ref[s, b].astype(F32) * spread, axis=0, keepdims=True))
        base = pl.multiple_of(b * steps + g * SPAN, SPAN)
        states = jnp.concatenate(rows, axis=0) + off_ref[pl.ds(base, SPAN), :]
        states_ref[:, b * WIDTH : (b + 1) * WIDTH] = states
        mean = jnp.mean(states * states, axis=-1, keepdims=True)
        normed = states * lax.rsqrt(mean + 1e-05) * gain_ref[b : b + 1, :]
        normed_ref[:, b * WIDTH : (b + 1) * WIDTH] = normed.astype(BF16)


def replay(place, kept, init, y_maps, x_maps, off, grp, gain, q):
    steps = SPAN * GROUPS
    return pl.pallas_call(
        replay_kernel,
        grid=(GROUPS,),
        out_shape=(
            jax.ShapeDtypeStruct((steps, 2 * WIDTH), F32),
            jax.ShapeDtypeStruct((steps, 2 * WIDTH), BF16),
        ),
        in_specs=[SMEM, SMEM]
        + [VMEM] * 10
        + [pl.BlockSpec((SPAN, 2, WIDTH, WIDTH), lambda g: (0, g, 0, 0))],
        out_specs=(
            pl.BlockSpec((SPAN, 2 * WIDTH), lambda g: (g, 0)),
            pl.BlockSpec((SPAN, 2 * WIDTH), lambda g: (g, 0)),
        ),
        scratch_shapes=[pltpu.VMEM((8, WIDTH), F32)],
        name="replay",
    )(place, kept, init, *y_maps, *x_maps, off, grp, gain, q)


def x_back(v, k):
    return lax.ppermute(v, "tm", [(y * 4 + x, y * 4 + (x + k) % 4) for y in range(4) for x in range(4)])


def y_back(v, k):
    return lax.ppermute(v, "tm", [(y * 4 + x, (y + k) % 4 * 4 + x) for y in range(4) for x in range(4)])


def z_back(v, k):
    return lax.ppermute(v, "block", [(z * 2 + c, (z + k) % 4 * 2 + c) for z in range(4) for c in range(2)])


def other_core(v):
    return lax.ppermute(v, "block", [(s, s ^ 1) for s in range(8)])


def body(
    noise,
    retain,
    control_weight,
    input_weight,
    initial_state,
    norm_gain,
    gate_weight,
    up_weight,
    down_weight,
):
    tm = lax.axis_index("tm")
    block = lax.axis_index("block")
    z, core = block // 2, block % 2
    place = jnp.stack([tm // 4, tm % 4]).astype(jnp.int32)
    q, off, own, grp, kept = compose(noise, retain, control_weight, input_weight)
    x_maps = [x_back(own, k) for k in (1, 2, 3)]
    total = row_map(place, [own, *x_maps])
    y_maps = [y_back(total, k) for k in (1, 2, 3)]
    states, normed = replay(
        place, kept, initial_state.reshape(2, WIDTH), y_maps, x_maps, off, grp, norm_gain.reshape(2, WIDTH), q
    )
    mine = jnp.stack([normed] + [z_back(normed, k) for k in (1, 2, 3)])
    theirs = other_core(mine)
    both = jnp.where(core == 0, jnp.stack([mine, theirs], 1), jnp.stack([theirs, mine], 1))
    both = both[(z - jnp.arange(4)) % 4]
    piece = both.transpose(2, 0, 1, 3).reshape(256, 2048)
    gate = jnp.dot(piece, gate_weight, preferred_element_type=F32)
    upward = jnp.dot(piece, up_weight, preferred_element_type=F32)
    hidden = (jax.nn.silu(gate) * upward).astype(BF16)
    part = jnp.dot(hidden, down_weight, preferred_element_type=F32).astype(BF16)
    part = part.reshape(256, 4, 2, 256).transpose(2, 1, 0, 3)
    kept_half = lax.dynamic_index_in_dim(part, core, 0, keepdims=False)
    sent_half = lax.dynamic_index_in_dim(part, 1 - core, 0, keepdims=False)
    chip = kept_half.astype(F32) + other_core(sent_half).astype(F32)
    mixed = lax.dynamic_index_in_dim(chip, z, 0, keepdims=False)
    chip = chip.astype(BF16)
    for k in (1, 2, 3):
        mixed = mixed + z_back(lax.dynamic_index_in_dim(chip, (z + k) % 4, 0, keepdims=False), k).astype(F32)
    return (states + mixed).astype(BF16)


def solution(mesh):
    placed = (
        P("tm", None),
        P("tm", "block"),
        P(None, "block", None, None),
        P(None, "block"),
        P("block"),
        P("block"),
        P(None, "block"),
        P(None, "block"),
        P("block", None),
    )
    return jax.shard_map(body, mesh=mesh, in_specs=placed, out_specs=P("tm", "block"), check_vma=False)
```

time: 497 us -> 132 us (0.27)
  matrix products: 304 us -> 9.41 us
  Pallas kernels: 0 us -> 68 us
  waiting for transfers between devices: 75.3 us -> 19.1 us
  local copies, waits for them, and re-layouts: 51 us -> 8.63 us
  blocking collectives: 23.7 us -> 0 us
  starting transfers between devices: 0.09 us -> 23.2 us
  other arithmetic: 25 us -> 2.74 us
  between operations: 13.3 us -> 0.16 us
    dot_general x107 -> x2, matrix products: 304 us -> 9.41 us  [the longest x1 5.95 us: body(): part = jnp.dot(hidden, down_weight, preferred_element_type=F32).astype(BF16)]
    pallas_call x0 -> x3, Pallas kernels: none -> 68 us  [the longest x1 49.1 us: compose(): pl.pallas_call(compose_kernel, out_shape=(jax.ShapeDtypeStruct((SPAN, 2 *...]
    all_gather x2 -> x0, waiting for transfers between devices: 42.1 us -> none  [the longest x1 23.1 us: body(): piece = lax.all_gather(normed, 'block', axis=1, tiled=True)]
    reduce_scatter x1 -> x0, waiting for transfers between devices: 33.1 us -> none  [body(): lax.psum_scatter(partial_out.astype(jnp.bfloat16), 'block', scatter_dimen...]
    dynamic_slice x16 -> x1, local copies, waits for them, and re-layouts: 27.7 us -> 2.17 us  [body(): kept_half = lax.dynamic_index_in_dim(part, core, 0, keepdims=False)]
    all_gather x1 -> x0, blocking collectives: 23.7 us -> none  [body(): lax.all_gather(device_off[None], 'tm', axis=0, tiled=True)]
    ppermute x0 -> x14, starting transfers between devices: none -> 23.2 us  [the longest x6 11.1 us: z_back(): lax.ppermute(v, 'block', [(z * 2 + c, (z + k) % 4 * 2 + c) for z in range...]
    ppermute x0 -> x14, waiting for transfers between devices: none -> 19.1 us  [the longest x6 9.8 us: z_back(): lax.ppermute(v, 'block', [(z * 2 + c, (z + k) % 4 * 2 + c) for z in range...]
  transfers between devices with their start and end apart: 3 -> 14, of which waited for: 3 -> 13; matrix products, arithmetic and copies ran while one was open for 1% -> 0% of each run, Pallas kernels for 0% -> 0%
where the time goes in v1:
time: 132 us; the launch traced here: 131 us
  Pallas kernels  68 us (52%)
  starting transfers between devices  23.2 us (18%)
  waiting for transfers between devices  19.1 us (14%)
  matrix products  9.41 us (7%)
  local copies, waits for them, and re-layouts  8.63 us (7%)
  other arithmetic  2.74 us (2%)
    pallas_call x1, Pallas kernels, compose(): pl.pallas_call(compose_kernel, out_shape=(jax.ShapeDtypeStruct((SPAN, 2 *...  49.1 us
    pallas_call x1, Pallas kernels, replay(): pl.pallas_call(replay_kernel, grid=(GROUPS,), out_shape=(jax.ShapeDtypeSt...  16.7 us
    ppermute x6, starting transfers between devices, z_back(): lax.ppermute(v, 'block', [(z * 2 + c, (z + k) % 4 * 2 + c) for z in range...  11.1 us
    ppermute x6, waiting for transfers between devices, z_back(): lax.ppermute(v, 'block', [(z * 2 + c, (z + k) % 4 * 2 + c) for z in range...  9.8 us
    dot_general x1, matrix products, body(): part = jnp.dot(hidden, down_weight, preferred_element_type=F32).astype(BF16)  5.95 us
    ppermute x3, starting transfers between devices, y_back(): lax.ppermute(v, 'tm', [(y * 4 + x, (y + k) % 4 * 4 + x) for y in range(4)...  5.83 us
    ppermute x3, starting transfers between devices, x_back(): lax.ppermute(v, 'tm', [(y * 4 + x, y * 4 + (x + k) % 4) for y in range(4)...  5.8 us
    unnamed x17, local copies, waits for them, and re-layouts  4.49 us
  transfers between devices with their start and end apart: 14, of which 13 were waited for; matrix products, arithmetic and copies ran while one was open for 0% of the time, Pallas kernels for 0%

profile of v1, /device:TPU:0, one launch (start us, length us, event | category | flops | bytes accessed | tf_op | source)
XLA Modules:
  0.0 131.3 jit_solution(1865977647788998714)
XLA Ops:
  0.0 1.6 %copy.15.noise_ref = f32[256,64]{1,0:T(8,128)} copy(f32[256,64]{0,1:T(8,128)} %param.9) | data formatting | bytes 131072 | tf_op args[0]
  1.6 1.5 %copy.16.retain_s.retain_ref = f32[256,2]{1,0:T(8,128)} copy(f32[256,2]{0,1:T(2,128)} %param.10) | data formatting | bytes 4096 | tf_op args[1]
  3.1 49.1 %compose.1 = (bf16[16,32,128,128]{3,2,1,0:T(8,128)(2,1)}, f32[512,128]{1,0:T(8,128)}, bf16[2,144,128]{2,1,0:T(8,128)(2,1)}, bf16[32,128,128]{2,1,0:T(8,128)(2,1)}, f32[16,2]{1,0:T(8,128)}) custom-call(f32[256,64]{1,0:T(8,128)} %copy.15.noise_ref, f32[256,2]{1,0:T(8,128)} %copy.16.retain_s.retain_ref, f32[256,2]{1,0:T(8,128)} %copy.16.retain_s.retain_ref, ...), custom_call_target="tpu_custom_call" | custom-call | tf_op jit(solution)/shard_map/compose/pallas_call | solution.py:167
  52.2 1.6 %collective-permute-start = (bf16[2,144,128]{2,1,0:T(8,128)(2,1)}, bf16[2,144,128]{2,1,0:T(8,128)(2,1)S(1)}, u32[]{:S(2)}, u32[]{:S(2)}) collective-permute-start(bf16[2,144,128]{2,1,0:T(8,128)(2,1)} %get-tuple-element.13.m0), channel_id=1, source_target_pairs={{0,8},{8,16},{16,24},{24,0},{32,40},{40,48},{48,56},{56,32},{64,72... | collective-permute-start | bytes 221192 | tf_op jit(solution)/shard_map/ppermute | solution.py:273
  53.9 2.7 %collective-permute-start.1 = (bf16[2,144,128]{2,1,0:T(8,128)(2,1)}, bf16[2,144,128]{2,1,0:T(8,128)(2,1)S(1)}, u32[]{:S(2)}, u32[]{:S(2)}) collective-permute-start(bf16[2,144,128]{2,1,0:T(8,128)(2,1)} %get-tuple-element.13.m0), channel_id=1, source_target_pairs={{0,16},{8,24},{16,0},{24,8},{32,48},{40,56},{48,32},{56,40},{64,80... | collective-permute-start | bytes 221192 | tf_op jit(solution)/shard_map/ppermute | solution.py:273
  56.6 1.4 %collective-permute-start.2 = (bf16[2,144,128]{2,1,0:T(8,128)(2,1)}, bf16[2,144,128]{2,1,0:T(8,128)(2,1)S(1)}, u32[]{:S(2)}, u32[]{:S(2)}) collective-permute-start(bf16[2,144,128]{2,1,0:T(8,128)(2,1)} %get-tuple-element.13.m0), channel_id=1, source_target_pairs={{0,24},{8,0},{16,8},{24,16},{32,56},{40,32},{48,40},{56,48},{64,88... | collective-permute-start | bytes 221192 | tf_op jit(solution)/shard_map/ppermute | solution.py:273
  58.6 1.7 %collective-permute-done.1.m2.x2 = bf16[2,144,128]{2,1,0:T(8,128)(2,1)S(1)} collective-permute-done((bf16[2,144,128]{2,1,0:T(8,128)(2,1)}, bf16[2,144,128]{2,1,0:T(8,128)(2,1)S(1)}, u32[]{:S(2)}, u32[]{:S(2)}) %collective-permute-start.1) | collective-permute-done | bytes 73760 | tf_op jit(solution)/shard_map/ppermute | solution.py:273
  60.4 0.8 collective-permute-done.2.m3.x3
  61.8 2.1 %row_map.1 = bf16[2,144,128]{2,1,0:T(8,128)(2,1)} custom-call(s32[2]{0:T(128)} %pad_add_fusion.place_s, bf16[2,144,128]{2,1,0:T(8,128)(2,1)} %get-tuple-element.13.m0, bf16[2,144,128]{2,1,0:T(8,128)(2,1)} %copy-done, bf16[2,144,128]{2,1,0:T(8,128)(2,1)} %copy-done.1, bf16[2,144,128]{2,1,0:T(8,128)(2,1)} %copy-done.2), custom_call_target="tpu_custom_call" | custom-call | tf_op jit(solution)/shard_map/row_map/pallas_call | solution.py:210
  63.9 1.6 %collective-permute-start.3 = (bf16[2,144,128]{2,1,0:T(8,128)(2,1)}, bf16[2,144,128]{2,1,0:T(8,128)(2,1)S(1)}, u32[]{:S(2)}, u32[]{:S(2)}) collective-permute-start(bf16[2,144,128]{2,1,0:T(8,128)(2,1)} %row_map.1), channel_id=1, source_target_pairs={{0,32},{8,40},{16,48},{24,56},{32,64},{40,72},{48,80},{56,88},{64,... | collective-permute-start | bytes 221192 | tf_op jit(solution)/shard_map/ppermute | solution.py:277
  65.5 2.9 %collective-permute-start.4 = (bf16[2,144,128]{2,1,0:T(8,128)(2,1)}, bf16[2,144,128]{2,1,0:T(8,128)(2,1)S(1)}, u32[]{:S(2)}, u32[]{:S(2)}) collective-permute-start(bf16[2,144,128]{2,1,0:T(8,128)(2,1)} %row_map.1), channel_id=1, source_target_pairs={{0,64},{8,72},{16,80},{24,88},{32,96},{40,104},{48,112},{56,120},{... | collective-permute-start | bytes 221192 | tf_op jit(solution)/shard_map/ppermute | solution.py:277
  68.4 1.3 %collective-permute-start.5 = (bf16[2,144,128]{2,1,0:T(8,128)(2,1)}, bf16[2,144,128]{2,1,0:T(8,128)(2,1)S(1)}, u32[]{:S(2)}, u32[]{:S(2)}) collective-permute-start(bf16[2,144,128]{2,1,0:T(8,128)(2,1)} %row_map.1), channel_id=1, source_target_pairs={{0,96},{8,104},{16,112},{24,120},{32,0},{40,8},{48,16},{56,24},{64... | collective-permute-start | bytes 221192 | tf_op jit(solution)/shard_map/ppermute | solution.py:277
  70.3 1.4 %collective-permute-done.4.y2 = bf16[2,144,128]{2,1,0:T(8,128)(2,1)S(1)} collective-permute-done((bf16[2,144,128]{2,1,0:T(8,128)(2,1)}, bf16[2,144,128]{2,1,0:T(8,128)(2,1)S(1)}, u32[]{:S(2)}, u32[]{:S(2)}) %collective-permute-start.4) | collective-permute-done | bytes 73760 | tf_op jit(solution)/shard_map/ppermute | solution.py:277
  71.7 1.2 collective-permute-done.5.y3
  73.6 16.7 %replay.1 = (f32[256,256]{1,0:T(8,128)}, bf16[256,256]{1,0:T(8,128)(2,1)}) custom-call(s32[2]{0:T(128)} %pad_add_fusion.place_s, f32[16,2]{1,0:T(8,128)} %get-tuple-element.12.kept_s, f32[2,128]{1,0:T(2,128)} %bitcast.55, bf16[2,144,128]{2,1,0:T(8,128)(2,1)} %copy-done.4, bf16[2,144,128]{2,1,0:T(8,128)(2,1)} %copy-done.5, bf16[2,144,128]{2,1,0:T(8,128)(2,1)} %copy-done.6, ...), custom_call_target="tpu_custom_call" | custom-call | tf_op jit(solution)/shard_map/replay/pallas_call | solution.py:253
  90.3 1.9 %collective-permute-start.6 = (bf16[256,256]{1,0:T(8,128)(2,1)}, bf16[256,256]{1,0:T(8,128)(2,1)S(1)}, u32[]{:S(2)}, u32[]{:S(2)}) collective-permute-start(bf16[256,256]{1,0:T(8,128)(2,1)} %get-tuple-element.18), channel_id=1, source_target_pairs={{0,2},{1,3},{2,4},{3,5},{4,6},{5,7},{6,0},{7,1},{8,10},{9,11},{10,... | collective-permute-start | bytes 393224 | tf_op jit(solution)/shard_map/ppermute | solution.py:281
  92.2 3.6 %collective-permute-start.7 = (bf16[256,256]{1,0:T(8,128)(2,1)}, bf16[256,256]{1,0:T(8,128)(2,1)S(1)}, u32[]{:S(2)}, u32[]{:S(2)}) collective-permute-start(bf16[256,256]{1,0:T(8,128)(2,1)} %get-tuple-element.18), channel_id=1, source_target_pairs={{0,4},{1,5},{2,6},{3,7},{4,0},{5,1},{6,2},{7,3},{8,12},{9,13},{10,... | collective-permute-start | bytes 393224 | tf_op jit(solution)/shard_map/ppermute | solution.py:281
  95.8 1.0 collective-permute-start.8
  96.8 1.8 %collective-permute-done.6 = bf16[256,256]{1,0:T(8,128)(2,1)S(1)} collective-permute-done((bf16[256,256]{1,0:T(8,128)(2,1)}, bf16[256,256]{1,0:T(8,128)(2,1)S(1)}, u32[]{:S(2)}, u32[]{:S(2)}) %collective-permute-start.6) | collective-permute-done | bytes 131104 | tf_op jit(solution)/shard_map/ppermute | solution.py:281
  98.6 1.7 %collective-permute-done.7 = bf16[256,256]{1,0:T(8,128)(2,1)S(1)} collective-permute-done((bf16[256,256]{1,0:T(8,128)(2,1)}, bf16[256,256]{1,0:T(8,128)(2,1)S(1)}, u32[]{:S(2)}, u32[]{:S(2)}) %collective-permute-start.7) | collective-permute-done | bytes 131104 | tf_op jit(solution)/shard_map/ppermute | solution.py:281
  101.0 1.0 fusion.9
  102.3 1.8 %collective-permute-done.9 = bf16[4,256,256]{2,1,0:T(8,128)(2,1)S(1)} collective-permute-done((bf16[4,256,256]{2,1,0:T(8,128)(2,1)S(1)}, bf16[4,256,256]{2,1,0:T(8,128)(2,1)S(1)}, u32[]{:S(2)}, u32[]{:S(2)}) %collective-permute-start.9) | collective-permute-done | bytes 524320 | tf_op jit(solution)/shard_map/ppermute | solution.py:285
  105.5 3.5 %fusion.11 = f32[256,1024]{1,0:T(8,128)S(1)} fusion(bf16[256,2048]{0,1:T(8,128)(2,1)S(1)} %bitcast.47, bf16[2048,1024]{1,0:T(8,128)(2,1)} %param.15), kind=kOutput, calls=%fused_computation.30 | convolution fusion | flops 1073741824 | bytes 6291456 | tf_op jit(solution)/shard_map/dot_general | solution.py:315
  108.9 5.9 %convolution_convert_fusion = bf16[256,2048]{1,0:T(8,128)(2,1)S(1)} fusion(bf16[1024,2048]{1,0:T(8,128)(2,1)} %param.17, bf16[256,2048]{0,1:T(8,128)(2,1)S(1)} %bitcast.48, bf16[2048,1024]{1,0:T(8,128)(2,1)} %param.16, f32[256,1024]{1,0:T(8,128)S(1)} %fusion.11), kind=kOutput, calls=%fused_computation.1 | convolution fusion | flops 2149580800 | bytes 11534336 | tf_op jit(solution)/shard_map/dot_general | solution.py:318
  114.9 0.8 reshape.66
  115.7 2.2 %constant_dynamic-slice_fusion.1 = (bf16[256,4,1,256]{3,2,1,0:T(2,128)(2,1)S(1)}, bf16[256,4,1,256]{3,2,1,0:T(2,128)(2,1)S(1)}) fusion(bf16[256,4,2,256]{3,2,1,0:T(2,128)(2,1)S(1)} %reshape.66, s32[]{:T(128)S(6)} %select_n.90, s32[]{:T(128)S(6)} %select_n.91), kind=kLoop, calls=%fused_computation.23 | loop fusion | bytes 2097160 | tf_op jit(solution)/shard_map/jit(dynamic_index_in_dim)/dynamic_slice | solution.py:320
  118.3 1.8 %collective-permute-done.10 = bf16[4,256,256]{2,1,0:T(8,128)(2,1)S(1)} collective-permute-done((bf16[4,256,256]{2,1,0:T(8,128)(2,1)S(1)}, bf16[4,256,256]{2,1,0:T(8,128)(2,1)S(1)}, u32[]{:S(2)}, u32[]{:S(2)}) %collective-permute-start.10) | collective-permute-done | bytes 524320 | tf_op jit(solution)/shard_map/ppermute | solution.py:285
  120.3 1.0 collective-permute-start.11
  121.3 2.8 %collective-permute-start.12 = (bf16[256,256]{1,0:T(8,128)(2,1)S(1)}, bf16[256,256]{1,0:T(8,128)(2,1)S(1)}, u32[]{:S(2)}, u32[]{:S(2)}) collective-permute-start(bf16[256,256]{1,0:T(8,128)(2,1)S(1)} %get-tuple-element.25), channel_id=1, source_target_pairs={{0,4},{1,5},{2,6},{3,7},{4,0},{5,1},{6,2},{7,3},{8,12},{9,13},{10,... | collective-permute-start | bytes 393224 | tf_op jit(solution)/shard_map/ppermute | solution.py:281
  124.1 0.8 collective-permute-start.13
  124.9 2.6 %collective-permute-done.11 = bf16[256,256]{1,0:T(8,128)(2,1)S(1)} collective-permute-done((bf16[256,256]{1,0:T(8,128)(2,1)S(1)}, bf16[256,256]{1,0:T(8,128)(2,1)S(1)}, u32[]{:S(2)}, u32[]{:S(2)}) %collective-permute-start.11) | collective-permute-done | bytes 131104 | tf_op jit(solution)/shard_map/ppermute | solution.py:281
  127.5 2.9 %collective-permute-done.12 = bf16[256,256]{1,0:T(8,128)(2,1)S(1)} collective-permute-done((bf16[256,256]{1,0:T(8,128)(2,1)S(1)}, bf16[256,256]{1,0:T(8,128)(2,1)S(1)}, u32[]{:S(2)}, u32[]{:S(2)}) %collective-permute-start.12) | collective-permute-done | bytes 131104 | tf_op jit(solution)/shard_map/ppermute | solution.py:281
  (30 shorter events, 6.2 us)
Async XLA Ops:
  52.2 6.4 %collective-permute-start = (bf16[2,144,128]{2,1,0:T(8,128)(2,1)}, bf16[2,144,128]{2,1,0:T(8,128)(2,1)S(1)}, u32[]{:S(2)}, u32[]{:S(2)}) collective-permute-start(bf16[2,144,128]{2,1,0:T(8,128)(2,1)} %get-tuple-element.13.m0), channel_id=1, source_target_pairs={{0,8},{8,16},{16,24},{24,0},{32,40},{40,48},{48,56},{56,32},{64,72... | collective-permute-start | bytes 221192 | tf_op jit(solution)/shard_map/ppermute | solution.py:273
  53.9 6.5 %collective-permute-start.1 = (bf16[2,144,128]{2,1,0:T(8,128)(2,1)}, bf16[2,144,128]{2,1,0:T(8,128)(2,1)S(1)}, u32[]{:S(2)}, u32[]{:S(2)}) collective-permute-start(bf16[2,144,128]{2,1,0:T(8,128)(2,1)} %get-tuple-element.13.m0), channel_id=1, source_target_pairs={{0,16},{8,24},{16,0},{24,8},{32,48},{40,56},{48,32},{56,40},{64,80... | collective-permute-start | bytes 221192 | tf_op jit(solution)/shard_map/ppermute | solution.py:273
  56.6 4.6 %collective-permute-start.2 = (bf16[2,144,128]{2,1,0:T(8,128)(2,1)}, bf16[2,144,128]{2,1,0:T(8,128)(2,1)S(1)}, u32[]{:S(2)}, u32[]{:S(2)}) collective-permute-start(bf16[2,144,128]{2,1,0:T(8,128)(2,1)} %get-tuple-element.13.m0), channel_id=1, source_target_pairs={{0,24},{8,0},{16,8},{24,16},{32,56},{40,32},{48,40},{56,48},{64,88... | collective-permute-start | bytes 221192 | tf_op jit(solution)/shard_map/ppermute | solution.py:273
  58.6 2.5 %copy-start = (bf16[2,144,128]{2,1,0:T(8,128)(2,1)}, bf16[2,144,128]{2,1,0:T(8,128)(2,1)S(1)}, u32[]{:S(2)}) copy-start(bf16[2,144,128]{2,1,0:T(8,128)(2,1)S(1)} %collective-permute-done.m1.x1) | copy-start | bytes 221188
  60.4 0.8 copy-start.1
  61.2 0.6 copy-start.2
  63.9 6.4 %collective-permute-start.3 = (bf16[2,144,128]{2,1,0:T(8,128)(2,1)}, bf16[2,144,128]{2,1,0:T(8,128)(2,1)S(1)}, u32[]{:S(2)}, u32[]{:S(2)}) collective-permute-start(bf16[2,144,128]{2,1,0:T(8,128)(2,1)} %row_map.1), channel_id=1, source_target_pairs={{0,32},{8,40},{16,48},{24,56},{32,64},{40,72},{48,80},{56,88},{64,... | collective-permute-start | bytes 221192 | tf_op jit(solution)/shard_map/ppermute | solution.py:277
  65.5 6.2 %collective-permute-start.4 = (bf16[2,144,128]{2,1,0:T(8,128)(2,1)}, bf16[2,144,128]{2,1,0:T(8,128)(2,1)S(1)}, u32[]{:S(2)}, u32[]{:S(2)}) collective-permute-start(bf16[2,144,128]{2,1,0:T(8,128)(2,1)} %row_map.1), channel_id=1, source_target_pairs={{0,64},{8,72},{16,80},{24,88},{32,96},{40,104},{48,112},{56,120},{... | collective-permute-start | bytes 221192 | tf_op jit(solution)/shard_map/ppermute | solution.py:277
  68.4 4.6 %collective-permute-start.5 = (bf16[2,144,128]{2,1,0:T(8,128)(2,1)}, bf16[2,144,128]{2,1,0:T(8,128)(2,1)S(1)}, u32[]{:S(2)}, u32[]{:S(2)}) collective-permute-start(bf16[2,144,128]{2,1,0:T(8,128)(2,1)} %row_map.1), channel_id=1, source_target_pairs={{0,96},{8,104},{16,112},{24,120},{32,0},{40,8},{48,16},{56,24},{64... | collective-permute-start | bytes 221192 | tf_op jit(solution)/shard_map/ppermute | solution.py:277
  70.3 2.7 %copy-start.4 = (bf16[2,144,128]{2,1,0:T(8,128)(2,1)}, bf16[2,144,128]{2,1,0:T(8,128)(2,1)S(1)}, u32[]{:S(2)}) copy-start(bf16[2,144,128]{2,1,0:T(8,128)(2,1)S(1)} %collective-permute-done.3.y1) | copy-start | bytes 221188
  71.7 1.2 copy-start.5
  73.0 0.6 copy-start.6
  90.3 8.4 %collective-permute-start.6 = (bf16[256,256]{1,0:T(8,128)(2,1)}, bf16[256,256]{1,0:T(8,128)(2,1)S(1)}, u32[]{:S(2)}, u32[]{:S(2)}) collective-permute-start(bf16[256,256]{1,0:T(8,128)(2,1)} %get-tuple-element.18), channel_id=1, source_target_pairs={{0,2},{1,3},{2,4},{3,5},{4,6},{5,7},{6,0},{7,1},{8,10},{9,11},{10,... | collective-permute-start | bytes 393224 | tf_op jit(solution)/shard_map/ppermute | solution.py:281
  92.2 8.1 %collective-permute-start.7 = (bf16[256,256]{1,0:T(8,128)(2,1)}, bf16[256,256]{1,0:T(8,128)(2,1)S(1)}, u32[]{:S(2)}, u32[]{:S(2)}) collective-permute-start(bf16[256,256]{1,0:T(8,128)(2,1)} %get-tuple-element.18), channel_id=1, source_target_pairs={{0,4},{1,5},{2,6},{3,7},{4,0},{5,1},{6,2},{7,3},{8,12},{9,13},{10,... | collective-permute-start | bytes 393224 | tf_op jit(solution)/shard_map/ppermute | solution.py:281
  95.8 5.2 %collective-permute-start.8 = (bf16[256,256]{1,0:T(8,128)(2,1)}, bf16[256,256]{1,0:T(8,128)(2,1)S(1)}, u32[]{:S(2)}, u32[]{:S(2)}) collective-permute-start(bf16[256,256]{1,0:T(8,128)(2,1)} %get-tuple-element.18), channel_id=1, source_target_pairs={{0,6},{1,7},{2,0},{3,1},{4,2},{5,3},{6,4},{7,5},{8,14},{9,15},{10,... | collective-permute-start | bytes 393224 | tf_op jit(solution)/shard_map/ppermute | solution.py:281
  102.0 2.2 %collective-permute-start.9 = (bf16[4,256,256]{2,1,0:T(8,128)(2,1)S(1)}, bf16[4,256,256]{2,1,0:T(8,128)(2,1)S(1)}, u32[]{:S(2)}, u32[]{:S(2)}) collective-permute-start(bf16[4,256,256]{2,1,0:T(8,128)(2,1)S(1)} %get-tuple-element.27), channel_id=1, source_target_pairs={{0,1},{1,0},{2,3},{3,2},{4,5},{5,4},{6,7},{7,6},{8,9},{9,8},{10,11... | collective-permute-start | bytes 1572872 | tf_op jit(solution)/shard_map/ppermute | solution.py:285
  115.7 14.8 %copy-start.3 = (f32[256,256]{1,0:T(8,128)S(1)}, f32[256,256]{1,0:T(8,128)}, u32[]{:S(2)}) copy-start(f32[256,256]{1,0:T(8,128)} %get-tuple-element.17) | copy-start | bytes 786436
  118.0 2.0 %collective-permute-start.10 = (bf16[4,256,256]{2,1,0:T(8,128)(2,1)S(1)}, bf16[4,256,256]{2,1,0:T(8,128)(2,1)S(1)}, u32[]{:S(2)}, u32[]{:S(2)}) collective-permute-start(bf16[4,256,256]{2,1,0:T(8,128)(2,1)S(1)} %bitcast.49), channel_id=1, source_target_pairs={{0,1},{1,0},{2,3},{3,2},{4,5},{5,4},{6,7},{7,6},{8,9},{9,8},{10,11... | collective-permute-start | bytes 1572872 | tf_op jit(solution)/shard_map/ppermute | solution.py:285
  120.3 7.2 %collective-permute-start.11 = (bf16[256,256]{1,0:T(8,128)(2,1)S(1)}, bf16[256,256]{1,0:T(8,128)(2,1)S(1)}, u32[]{:S(2)}, u32[]{:S(2)}) collective-permute-start(bf16[256,256]{1,0:T(8,128)(2,1)S(1)} %get-tuple-element.23), channel_id=1, source_target_pairs={{0,2},{1,3},{2,4},{3,5},{4,6},{5,7},{6,0},{7,1},{8,10},{9,11},{10,... | collective-permute-start | bytes 393224 | tf_op jit(solution)/shard_map/ppermute | solution.py:281
  121.3 9.1 %collective-permute-start.12 = (bf16[256,256]{1,0:T(8,128)(2,1)S(1)}, bf16[256,256]{1,0:T(8,128)(2,1)S(1)}, u32[]{:S(2)}, u32[]{:S(2)}) collective-permute-start(bf16[256,256]{1,0:T(8,128)(2,1)S(1)} %get-tuple-element.25), channel_id=1, source_target_pairs={{0,4},{1,5},{2,6},{3,7},{4,0},{5,1},{6,2},{7,3},{8,12},{9,13},{10,... | collective-permute-start | bytes 393224 | tf_op jit(solution)/shard_map/ppermute | solution.py:281
  124.1 6.5 %collective-permute-start.13 = (bf16[256,256]{1,0:T(8,128)(2,1)S(1)}, bf16[256,256]{1,0:T(8,128)(2,1)S(1)}, u32[]{:S(2)}, u32[]{:S(2)}) collective-permute-start(bf16[256,256]{1,0:T(8,128)(2,1)S(1)} %get-tuple-element.24), channel_id=1, source_target_pairs={{0,6},{1,7},{2,0},{3,1},{4,2},{5,3},{6,4},{7,5},{8,14},{9,15},{10,... | collective-permute-start | bytes 393224 | tf_op jit(solution)/shard_map/ppermute | solution.py:281

commit v2 on v1

v2 whole, which is shorter than its diff:
```python
import functools
import math

import jax
import jax.numpy as jnp
from jax import lax
from jax.experimental import pallas as pl
from jax.experimental.pallas import tpu as pltpu
from jax.sharding import PartitionSpec as P

F32 = jnp.float32
BF16 = jnp.bfloat16
GROUPS = 16
SPAN = 16
WIDTH = 128
ROWS = 144
PITCH = 129
MAP_ROWS = 144
VMEM = pl.BlockSpec(memory_space=pltpu.VMEM)
SMEM = pl.BlockSpec(memory_space=pltpu.SMEM)
ANY = pl.BlockSpec(memory_space=pl.ANY)


def split3(v):
    hi = v.astype(BF16)
    rest = v - hi.astype(F32)
    mid = rest.astype(BF16)
    return hi, mid, (rest - mid.astype(F32)).astype(BF16)


def pack_map(ref, b, matrix, offset, kept):
    ref[b, :WIDTH, :] = matrix.astype(BF16)
    row = lax.broadcasted_iota(jnp.int32, (16, WIDTH), 0)
    tail = jnp.zeros((16, WIDTH), F32)
    kept_row = jnp.full((1, WIDTH), 1.0, F32) * kept
    for k, part in enumerate((*split3(offset), *split3(kept_row))):
        tail = jnp.where(row == k, jnp.broadcast_to(part.astype(F32), (16, WIDTH)), tail)
    ref[b, WIDTH:, :] = tail.astype(BF16)


def unpack_map(ref, b):
    matrix = ref[b, :WIDTH, :]
    tail = ref[b, WIDTH:, :].astype(F32)
    offset = tail[0:1] + tail[1:2] + tail[2:3]
    kept = tail[3:4] + tail[4:5] + tail[5:6]
    return matrix, offset, kept


def row_times(h, matrix):
    row = lax.broadcasted_iota(jnp.int32, (16, WIDTH), 0)
    hi = h.astype(BF16).astype(F32)
    lo = h - hi
    both = jnp.where(row == 0, jnp.broadcast_to(hi, (16, WIDTH)), jnp.broadcast_to(lo, (16, WIDTH)))
    out = jnp.dot(both.astype(BF16), matrix, preferred_element_type=F32)
    return out[0:1] + out[1:2]


def compose_kernel(
    place_s, noise_ref, retain_s, retain_ref, cw_ref, iw_ref, q_ref, off_ref, send_ref, grp_ref, kept_ref, skw, am, sem
):
    steps = noise_ref.shape[1]
    loads = [
        pltpu.make_async_copy(cw_ref.at[pl.ds(32 * k, 32)], q_ref.at[k], sem.at[k]) for k in range(4)
    ]
    for load in loads:
        load.start()
    rows = lax.broadcasted_iota(jnp.int32, (WIDTH, WIDTH), 0)
    cols = lax.broadcasted_iota(jnp.int32, (WIDTH, WIDTH), 1)
    eye = (rows == cols).astype(F32)
    noise = noise_ref[...].T
    drive = jnp.dot(noise, iw_ref[...], precision=lax.Precision.HIGHEST, preferred_element_type=F32)
    kept = retain_ref[...]
    scale = jnp.sqrt(1.0 - kept * kept)
    for b in range(2):
        spread = jnp.broadcast_to(scale[b : b + 1, :], (WIDTH, steps)).T
        off_ref[b * steps : (b + 1) * steps, :] = drive[:, b * WIDTH : (b + 1) * WIDTH] * spread

    def skew_body(base, i, carry):
        for b in range(2):
            raw = q_ref[base // 16, i * 2 + b]
            diff = (raw.T.astype(F32) - raw.astype(F32)) * (1.0 / math.sqrt(2.0))
            skw[pl.ds((b * 64 + base + i) * PITCH, WIDTH), :] = diff.astype(BF16).astype(F32)
        return carry

    for k in range(4):
        loads[k].wait()
        lax.fori_loop(0, 16, functools.partial(skew_body, 16 * k), 0, unroll=8)
    low = (noise.astype(BF16).astype(F32) * (1.0 / 64.0)).astype(BF16)

    def build_body(j, carry):
        w = jnp.concatenate(
            [skw[pl.ds(b * 64 * PITCH + j, 64, stride=PITCH), :] for b in range(2)], axis=1
        ).astype(BF16)
        out = jnp.dot(low, w, preferred_element_type=F32)
        for b in range(2):
            am[pl.ds(b * steps * PITCH + j, steps, stride=PITCH), :] = out[:, b * WIDTH : (b + 1) * WIDTH]
        return carry

    lax.fori_loop(0, WIDTH, build_body, 0, unroll=16)
    tail_rows = ROWS - WIDTH
    tail_row = lax.broadcasted_iota(jnp.int32, (tail_rows, WIDTH), 0)
    zero = jnp.zeros((WIDTH, WIDTH), BF16)

    def run(c):
        return skw.at[pl.ds(pl.multiple_of(c * ROWS, 16), ROWS), :]

    def step_matrix(t, b):
        return am[pl.ds((b * steps + t) * PITCH, WIDTH), :]

    def finish(s, g, b, matrix, tail):
        t = g * SPAN + s
        c = g * 2 + b
        rate = retain_s[b, t]
        push = off_ref[pl.ds(b * steps + t, 1), :]
        matrix = matrix * rate
        placed = jnp.where(tail_row == 0, jnp.broadcast_to(push, (tail_rows, WIDTH)), 0.0)
        tail = placed if tail is None else tail * rate + placed
        run(c)[:WIDTH, :] = matrix
        run(c)[WIDTH:, :] = tail
        q_ref[s, c] = matrix.astype(BF16)
        off_ref[pl.ds(b * steps + t, 1), :] = tail[:1]
        return rate

    def first(g, carry):
        for b in range(2):
            kept_ref[g, b] = finish(0, g, b, eye + step_matrix(g * SPAN, b), None)
        return carry

    lax.fori_loop(0, GROUPS, first, 0, unroll=4)

    def step(s, carry):
        def group(g, inner):
            t = g * SPAN + s
            now = [run(g * 2 + b)[...] for b in range(2)]
            low0, low1 = [step_matrix(t, b).astype(BF16) for b in range(2)]
            w = jnp.concatenate(
                [jnp.concatenate([low0, zero], axis=1), jnp.concatenate([zero, low1], axis=1)], axis=0
            )
            both = jnp.concatenate([x.astype(BF16) for x in now], axis=1)
            turned = jnp.dot(both, w, preferred_element_type=F32)
            for b in range(2):
                y = now[b] + turned[:, b * WIDTH : (b + 1) * WIDTH]
                rate = finish(s, g, b, y[:WIDTH], y[WIDTH:])
                kept_ref[g, b] = kept_ref[g, b] * rate
            return inner

        lax.fori_loop(0, GROUPS, group, 0, unroll=16)
        return carry

    lax.fori_loop(1, SPAN, step, 0)

    keeps = [[kept_ref[g, b] for b in range(2)] for g in range(GROUPS)]
    for g in range(GROUPS):
        for b in range(2):
            c = g * 2 + b
            m = run(c)[:WIDTH, :] - eye * keeps[g][b]
            run(c)[:WIDTH, :] = m
            grp_ref[c] = m.astype(BF16)
    stride = 1
    while stride < GROUPS:
        for g1 in range(0, GROUPS, 2 * stride):
            g2 = g1 + stride
            for b in range(2):
                one, two = run(g1 * 2 + b)[...], run(g2 * 2 + b)[...]
                prod = jnp.dot(one.astype(BF16), two[:WIDTH].astype(BF16), preferred_element_type=F32)
                k1, k2 = keeps[g1][b], keeps[g2][b]
                run(g1 * 2 + b)[:WIDTH, :] = prod[:WIDTH] + one[:WIDTH] * k2 + two[:WIDTH] * k1
                run(g1 * 2 + b)[WIDTH:, :] = prod[WIDTH:] + one[WIDTH:] * k2 + two[WIDTH:]
                keeps[g1][b] = k1 * k2
        stride *= 2
    for b in range(2):
        pack_map(send_ref, b, run(b)[:WIDTH, :], run(b)[WIDTH : WIDTH + 1, :], keeps[0][b])


def compose(place, noise, retain, control_weight, input_weight):
    steps = noise.shape[1]
    return pl.pallas_call(
        compose_kernel,
        out_shape=(
            pltpu.VMEM((SPAN, 2 * GROUPS, WIDTH, WIDTH), BF16),
            pltpu.VMEM((2 * steps, WIDTH), F32),
            pltpu.VMEM((2, MAP_ROWS, WIDTH), BF16),
            pltpu.VMEM((2 * GROUPS, WIDTH, WIDTH), BF16),
            jax.ShapeDtypeStruct((GROUPS, 2), F32),
        ),
        in_specs=[SMEM, VMEM, SMEM, VMEM, ANY, VMEM],
        out_specs=(VMEM, VMEM, VMEM, VMEM, SMEM),
        scratch_shapes=[
            pltpu.VMEM((128 * PITCH + 8, WIDTH), F32),
            pltpu.VMEM((2 * steps * PITCH + 8, WIDTH), F32),
            pltpu.SemaphoreType.DMA((4,)),
        ],
        compiler_params=pltpu.CompilerParams(vmem_limit_bytes=44_500_000),
        name="compose",
    )(place, noise, retain, retain, control_weight.reshape(-1, WIDTH, WIDTH), input_weight)


def row_kernel(place_s, m0, m1, m2, m3, out_ref, held):
    x = place_s[1]
    for k, ref in enumerate((m0, m1, m2, m3)):
        held[lax.rem(x + 4 - k, 4)] = ref[...]
    for b in range(2):
        parts = []
        for k in range(4):
            matrix, offset, kept = unpack_map(held.at[k], b)
            parts.append((matrix.astype(F32), offset, kept))
        while len(parts) > 1:
            merged = []
            for (m1_, o1, k1), (m2_, o2, k2) in zip(parts[::2], parts[1::2]):
                low = m2_.astype(BF16)
                prod = jnp.dot(m1_.astype(BF16), low, preferred_element_type=F32)
                merged.append((prod + m1_ * k2 + m2_ * k1, row_times(o1, low) + o1 * k2 + o2, k1 * k2))
            parts = merged
        pack_map(out_ref, b, *parts[0])


def row_map(place, maps):
    return pl.pallas_call(
        row_kernel,
        out_shape=jax.ShapeDtypeStruct((2, MAP_ROWS, WIDTH), BF16),
        in_specs=[SMEM] + [VMEM] * 4,
        out_specs=VMEM,
        scratch_shapes=[pltpu.VMEM((4, 2, MAP_ROWS, WIDTH), BF16)],
        compiler_params=pltpu.CompilerParams(vmem_limit_bytes=8_000_000),
        name="row_map",
    )(place, *maps)


def replay_kernel(place_s, kept_s, init_ref, y1, y2, y3, x1, x2, x3, off_ref, grp_ref, gain_ref, q_ref,
                  states_ref, normed_ref):
    steps = SPAN * GROUPS
    entry = []
    for b in range(2):
        h = init_ref[b : b + 1, :]
        for place, refs in ((place_s[0], (y1, y2, y3)), (place_s[1], (x1, x2, x3))):
            for k in (3, 2, 1):
                matrix, offset, kept = unpack_map(refs[k - 1], b)
                h = jnp.where(k <= place, h * kept + row_times(h, matrix) + offset, h)
        entry.append(h)

    def group(g, starts):
        after = []
        for b in range(2):
            c = g * 2 + b
            h = starts[b]
            spread = jnp.broadcast_to(h, (WIDTH, WIDTH)).T
            last = off_ref[pl.ds(b * steps + g * SPAN + SPAN - 1, 1), :]
            after.append(h * kept_s[g, b] + row_times(h, grp_ref[c]) + last)
            rows = [jnp.sum(q_ref[s, c].astype(F32) * spread, axis=0, keepdims=True) for s in range(SPAN)]
            base = pl.multiple_of(g * SPAN, SPAN)
            states = jnp.concatenate(rows, axis=0) + off_ref[pl.ds(b * steps + base, SPAN), :]
            states_ref[pl.ds(base, SPAN), b * WIDTH : (b + 1) * WIDTH] = states
            mean = jnp.mean(states * states, axis=-1, keepdims=True)
            normed = states * lax.rsqrt(mean + 1e-05) * gain_ref[b : b + 1, :]
            normed_ref[pl.ds(base, SPAN), b * WIDTH : (b + 1) * WIDTH] = normed.astype(BF16)
        return tuple(after)

    lax.fori_loop(0, GROUPS, group, tuple(entry), unroll=2)


def replay(place, kept, init, y_maps, x_maps, off, grp, gain, q):
    steps = SPAN * GROUPS
    return pl.pallas_call(
        replay_kernel,
        out_shape=(
            jax.ShapeDtypeStruct((steps, 2 * WIDTH), F32),
            jax.ShapeDtypeStruct((steps, 2 * WIDTH), BF16),
        ),
        in_specs=[SMEM, SMEM] + [VMEM] * 11,
        out_specs=(VMEM, VMEM),
        compiler_params=pltpu.CompilerParams(vmem_limit_bytes=16_000_000),
        name="replay",
    )(place, kept, init, *y_maps, *x_maps, off, grp, gain, pltpu.with_memory_space_constraint(q, pltpu.VMEM))


def forward_kernel(place_s, m0, m1, m2, m3, theirs_ref, gate_ref, up_ref, down_ref, keep_ref, send_ref, hidden):
    z, core = place_s[2], place_s[3]
    wide = 2 * WIDTH

    def at(k, c):
        return pl.multiple_of((lax.rem(z + k, 4) * 2 + c) * wide, wide)

    parts = [(m0, 0, 0), (m1, 3, 0), (m2, 2, 0), (m3, 1, 0)]
    parts += [(theirs_ref.at[k], (4 - k) % 4, 1) for k in range(4)]
    for n in range(0, gate_ref.shape[1], wide):
        gate = up = None
        for ref, k, other in parts:
            chunk = ref[...]
            row = at(k, 1 - core if other else core)
            g = jnp.dot(chunk, gate_ref[pl.ds(row, wide), n : n + wide], preferred_element_type=F32)
            u = jnp.dot(chunk, up_ref[pl.ds(row, wide), n : n + wide], preferred_element_type=F32)
            gate = g if gate is None else gate + g
            up = u if up is None else up + u
        hidden[:, n : n + wide] = (gate / (1.0 + jnp.exp(-gate)) * up).astype(BF16)
    low = hidden[...]
    for ref, c in ((send_ref, 1 - core), (keep_ref, core)):
        for k in range(4):
            out = jnp.dot(low, down_ref[:, pl.ds(at(k, c), wide)], preferred_element_type=F32)
            ref[k] = out.astype(BF16)


def forward(place, mine, theirs, gate_weight, up_weight, down_weight):
    steps = mine[0].shape[0]
    weights = [pltpu.with_memory_space_constraint(w, pltpu.VMEM) for w in (gate_weight, up_weight, down_weight)]
    half = jax.ShapeDtypeStruct((4, steps, 2 * WIDTH), BF16)
    return pl.pallas_call(
        forward_kernel,
        out_shape=(half, half),
        in_specs=[SMEM] + [VMEM] * 8,
        out_specs=(VMEM, VMEM),
        scratch_shapes=[pltpu.VMEM((steps, gate_weight.shape[1]), BF16)],
        compiler_params=pltpu.CompilerParams(vmem_limit_bytes=16_000_000),
        name="forward",
    )(place, *mine, theirs, *weights)


def x_back(v, k):
    return lax.ppermute(v, "tm", [(y * 4 + x, y * 4 + (x + k) % 4) for y in range(4) for x in range(4)])


def y_back(v, k):
    return lax.ppermute(v, "tm", [(y * 4 + x, (y + k) % 4 * 4 + x) for y in range(4) for x in range(4)])


def z_back(v, k):
    return lax.ppermute(v, "block", [(z * 2 + c, (z + k) % 4 * 2 + c) for z in range(4) for c in range(2)])


def other_core(v):
    return lax.ppermute(v, "block", [(s, s ^ 1) for s in range(8)])


def body(
    noise,
    retain,
    control_weight,
    input_weight,
    initial_state,
    norm_gain,
    gate_weight,
    up_weight,
    down_weight,
):
    tm = lax.axis_index("tm")
    block = lax.axis_index("block")
    z, core = block // 2, block % 2
    place = jnp.stack([tm // 4, tm % 4, z, core]).astype(jnp.int32)
    q, off, own, grp, kept = compose(place, noise.T, retain.T, control_weight, input_weight)
    x_maps = [x_back(own, k) for k in (1, 2, 3)]
    total = row_map(place, [own, *x_maps])
    y_maps = [y_back(total, k) for k in (1, 2, 3)]
    states, normed = replay(
        place, kept, initial_state.reshape(2, WIDTH), y_maps, x_maps, off, grp, norm_gain.reshape(2, WIDTH), q
    )
    mine = [normed] + [z_back(normed, k) for k in (1, 2, 3)]
    theirs = other_core(jnp.stack(mine))
    keep, sent = forward(place, mine, theirs, gate_weight, up_weight, down_weight)
    chip = keep.astype(F32) + other_core(sent).astype(F32)
    low = chip.astype(BF16)
    mixed = chip[0]
    for k in (1, 2, 3):
        mixed = mixed + z_back(low[k], k).astype(F32)
    return (states + mixed).astype(BF16)


def solution(mesh):
    placed = (
        P("tm", None),
        P("tm", "block"),
        P(None, "block", None, None),
        P(None, "block"),
        P("block"),
        P("block"),
        P(None, "block"),
        P(None, "block"),
        P("block", None),
    )
    return jax.shard_map(body, mesh=mesh, in_specs=placed, out_specs=P("tm", "block"), check_vma=False)
```

time: 132 us -> 80 us (0.61)
  Pallas kernels: 68 us -> 32.6 us
  matrix products: 9.41 us -> 0 us
  local copies, waits for them, and re-layouts: 8.63 us -> 0.75 us
  waiting for transfers between devices: 19.1 us -> 26.6 us
  starting transfers between devices: 23.2 us -> 18.2 us
    pallas_call x2 -> x3, Pallas kernels: 65.8 us -> 31.5 us  [the longest x1 20.3 us: compose(): pl.pallas_call(compose_kernel, out_shape=(pltpu.VMEM((SPAN, 2 * GROUPS, W...]
    dot_general x2 -> x0, matrix products: 9.41 us -> none  [the longest x1 5.95 us: body(): part = jnp.dot(hidden, down_weight, preferred_element_type=F32).astype(BF16)]
    unnamed x17 -> x14, local copies, waits for them, and re-layouts: 4.49 us -> 0.72 us
    ppermute x6, waiting for transfers between devices: 9.8 us -> 12.8 us  [z_back(): lax.ppermute(v, 'block', [(z * 2 + c, (z + k) % 4 * 2 + c) for z in range...]
    ppermute x3, waiting for transfers between devices: 2.53 us -> 5.12 us  [x_back(): lax.ppermute(v, 'tm', [(y * 4 + x, y * 4 + (x + k) % 4) for y in range(4)...]
    ppermute x6, starting transfers between devices: 11.1 us -> 8.63 us  [z_back(): lax.ppermute(v, 'block', [(z * 2 + c, (z + k) % 4 * 2 + c) for z in range...]
    dynamic_slice x1 -> x0, local copies, waits for them, and re-layouts: 2.17 us -> none  [body(): kept_half = lax.dynamic_index_in_dim(part, core, 0, keepdims=False)]
    ppermute x3, waiting for transfers between devices: 3.21 us -> 5.04 us  [y_back(): lax.ppermute(v, 'tm', [(y * 4 + x, (y + k) % 4 * 4 + x) for y in range(4)...]
  transfers between devices with their start and end apart: 14 -> 14, of which waited for: 13 -> 14; matrix products, arithmetic and copies ran while one was open for 0% -> 0% of each run, Pallas kernels for 0% -> 0%
where the time goes in v2:
time: 80 us; the launch traced here: 79.9 us
  Pallas kernels  32.6 us (41%)
  waiting for transfers between devices  26.6 us (33%)
  starting transfers between devices  18.2 us (23%)
  other arithmetic  1.61 us (2%)
    pallas_call x1, Pallas kernels, compose(): pl.pallas_call(compose_kernel, out_shape=(pltpu.VMEM((SPAN, 2 * GROUPS, W...  20.3 us
    ppermute x6, waiting for transfers between devices, z_back(): lax.ppermute(v, 'block', [(z * 2 + c, (z + k) % 4 * 2 + c) for z in range...  12.8 us
    ppermute x6, starting transfers between devices, z_back(): lax.ppermute(v, 'block', [(z * 2 + c, (z + k) % 4 * 2 + c) for z in range...  8.63 us
    pallas_call x1, Pallas kernels, replay(): pl.pallas_call(replay_kernel, out_shape=(jax.ShapeDtypeStruct((steps, 2 *...  7.19 us
    ppermute x3, waiting for transfers between devices, x_back(): lax.ppermute(v, 'tm', [(y * 4 + x, y * 4 + (x + k) % 4) for y in range(4)...  5.12 us
    ppermute x3, waiting for transfers between devices, y_back(): lax.ppermute(v, 'tm', [(y * 4 + x, (y + k) % 4 * 4 + x) for y in range(4)...  5.04 us
    ppermute x3, starting transfers between devices, y_back(): lax.ppermute(v, 'tm', [(y * 4 + x, (y + k) % 4 * 4 + x) for y in range(4)...  4.69 us
    ppermute x3, starting transfers between devices, x_back(): lax.ppermute(v, 'tm', [(y * 4 + x, y * 4 + (x + k) % 4) for y in range(4)...  4.6 us
  transfers between devices with their start and end apart: 14, of which 14 were waited for; matrix products, arithmetic and copies ran while one was open for 0% of the time, Pallas kernels for 0%

profile of v2, /device:TPU:0, one launch (start us, length us, event | category | flops | bytes accessed | tf_op | source)
XLA Modules:
  0.0 79.9 jit_solution(7299146322418507132)
XLA Ops:
  0.0 0.7 pad_add_fusion.place_s
  0.7 20.3 %compose.1 = (bf16[16,32,128,128]{3,2,1,0:T(8,128)(2,1)S(1)}, f32[512,128]{1,0:T(8,128)S(1)}, bf16[2,144,128]{2,1,0:T(8,128)(2,1)S(1)}, bf16[32,128,128]{2,1,0:T(8,128)(2,1)S(1)}, f32[16,2]{1,0:T(8,128)}) custom-call(s32[4]{0:T(128)} %pad_add_fusion.place_s, f32[64,256]{1,0:T(8,128)} %bitcast.38, f32[2,256]{1,0:T(2,128)} %bitcast.39, f32[2,256]{1,0:T(2,128)} %bitcast.40, ...), custom_call_target="tpu_custom_call" | custom-call | tf_op jit(solution)/shard_map/compose/pallas_call | solution.py:177
  21.0 2.9 %collective-permute-start.2 = (bf16[2,144,128]{2,1,0:T(8,128)(2,1)S(1)}, bf16[2,144,128]{2,1,0:T(8,128)(2,1)S(1)}, u32[]{:S(2)}, u32[]{:S(2)}) collective-permute-start(bf16[2,144,128]{2,1,0:T(8,128)(2,1)S(1)} %get-tuple-element.15.m0), channel_id=1, source_target_pairs={{0,24},{8,0},{16,8},{24,16},{32,56},{40,32},{48,40},{56,48},{64,88... | collective-permute-start | bytes 221192 | tf_op jit(solution)/shard_map/ppermute | solution.py:318
  23.9 0.8 %collective-permute-start.1 = (bf16[2,144,128]{2,1,0:T(8,128)(2,1)S(1)}, bf16[2,144,128]{2,1,0:T(8,128)(2,1)S(1)}, u32[]{:S(2)}, u32[]{:S(2)}) collective-permute-start(bf16[2,144,128]{2,1,0:T(8,128)(2,1)S(1)} %get-tuple-element.15.m0), channel_id=1, source_target_pairs={{0,16},{8,24},{16,0},{24,8},{32,48},{40,56},{48,32},{56,40},{64,80... | collective-permute-start | bytes 221192 | tf_op jit(solution)/shard_map/ppermute | solution.py:318
  24.7 0.9 %collective-permute-start = (bf16[2,144,128]{2,1,0:T(8,128)(2,1)S(1)}, bf16[2,144,128]{2,1,0:T(8,128)(2,1)S(1)}, u32[]{:S(2)}, u32[]{:S(2)}) collective-permute-start(bf16[2,144,128]{2,1,0:T(8,128)(2,1)S(1)} %get-tuple-element.15.m0), channel_id=1, source_target_pairs={{0,8},{8,16},{16,24},{24,0},{32,40},{40,48},{48,56},{56,32},{64,72... | collective-permute-start | bytes 221192 | tf_op jit(solution)/shard_map/ppermute | solution.py:318
  25.6 0.7 collective-permute-done.2.m3.x3
  26.3 3.7 %collective-permute-done.1.m2.x2 = bf16[2,144,128]{2,1,0:T(8,128)(2,1)S(1)} collective-permute-done((bf16[2,144,128]{2,1,0:T(8,128)(2,1)S(1)}, bf16[2,144,128]{2,1,0:T(8,128)(2,1)S(1)}, u32[]{:S(2)}, u32[]{:S(2)}) %collective-permute-start.1) | collective-permute-done | bytes 73760 | tf_op jit(solution)/shard_map/ppermute | solution.py:318
  30.0 0.7 collective-permute-done.m1.x1
  30.7 1.0 %row_map.1 = bf16[2,144,128]{2,1,0:T(8,128)(2,1)S(1)} custom-call(s32[4]{0:T(128)S(1)} %copy-done.3, bf16[2,144,128]{2,1,0:T(8,128)(2,1)S(1)} %get-tuple-element.15.m0, bf16[2,144,128]{2,1,0:T(8,128)(2,1)S(1)} %collective-permute-done.m1.x1, bf16[2,144,128]{2,1,0:T(8,128)(2,1)S(1)} %collective-permute-done.1.m2.x2, ...), custom_call_target="tpu_custom_call" | custom-call | tf_op jit(solution)/shard_map/row_map/pallas_call | solution.py:218
  31.8 3.1 %collective-permute-start.5 = (bf16[2,144,128]{2,1,0:T(8,128)(2,1)S(1)}, bf16[2,144,128]{2,1,0:T(8,128)(2,1)S(1)}, u32[]{:S(2)}, u32[]{:S(2)}) collective-permute-start(bf16[2,144,128]{2,1,0:T(8,128)(2,1)S(1)} %row_map.1), channel_id=1, source_target_pairs={{0,96},{8,104},{16,112},{24,120},{32,0},{40,8},{48,16},{56,24},{64... | collective-permute-start | bytes 221192 | tf_op jit(solution)/shard_map/ppermute | solution.py:322
  34.9 0.6 collective-permute-start.4
  35.5 1.0 %collective-permute-start.3 = (bf16[2,144,128]{2,1,0:T(8,128)(2,1)S(1)}, bf16[2,144,128]{2,1,0:T(8,128)(2,1)S(1)}, u32[]{:S(2)}, u32[]{:S(2)}) collective-permute-start(bf16[2,144,128]{2,1,0:T(8,128)(2,1)S(1)} %row_map.1), channel_id=1, source_target_pairs={{0,32},{8,40},{16,48},{24,56},{32,64},{40,72},{48,80},{56,88},{64,... | collective-permute-start | bytes 221192 | tf_op jit(solution)/shard_map/ppermute | solution.py:322
  36.5 0.5 collective-permute-done.5.y3
  37.0 3.8 %collective-permute-done.4.y2 = bf16[2,144,128]{2,1,0:T(8,128)(2,1)S(1)} collective-permute-done((bf16[2,144,128]{2,1,0:T(8,128)(2,1)S(1)}, bf16[2,144,128]{2,1,0:T(8,128)(2,1)S(1)}, u32[]{:S(2)}, u32[]{:S(2)}) %collective-permute-start.4) | collective-permute-done | bytes 73760 | tf_op jit(solution)/shard_map/ppermute | solution.py:322
  40.8 0.7 collective-permute-done.3.y1
  41.5 0.7 copy-done.4
  42.2 7.2 %replay.1 = (f32[256,256]{1,0:T(8,128)S(1)}, bf16[256,256]{1,0:T(8,128)(2,1)S(1)}) custom-call(s32[4]{0:T(128)S(1)} %copy-done.3, f32[16,2]{1,0:T(8,128)S(1)} %copy-done.4, f32[2,128]{1,0:T(2,128)S(1)} %bitcast.35, bf16[2,144,128]{2,1,0:T(8,128)(2,1)S(1)} %collective-permute-done.3.y1, bf16[2,144,128]{2,1,0:T(8,128)(2,1)S(1)} %collective-permute-done.4.y2, ...), custom_call_target="tpu_custom_call" | custom-call | tf_op jit(solution)/shard_map/replay/pallas_call | solution.py:263
  49.4 4.1 %collective-permute-start.8 = (bf16[256,256]{1,0:T(8,128)(2,1)S(1)}, bf16[256,256]{1,0:T(8,128)(2,1)S(1)}, u32[]{:S(2)}, u32[]{:S(2)}) collective-permute-start(bf16[256,256]{1,0:T(8,128)(2,1)S(1)} %get-tuple-element.20.m0), channel_id=1, source_target_pairs={{0,6},{1,7},{2,0},{3,1},{4,2},{5,3},{6,4},{7,5},{8,14},{9,15},{10,... | collective-permute-start | bytes 393224 | tf_op jit(solution)/shard_map/ppermute | solution.py:326
  53.5 1.3 %collective-permute-start.6 = (bf16[256,256]{1,0:T(8,128)(2,1)S(1)}, bf16[256,256]{1,0:T(8,128)(2,1)S(1)}, u32[]{:S(2)}, u32[]{:S(2)}) collective-permute-start(bf16[256,256]{1,0:T(8,128)(2,1)S(1)} %get-tuple-element.20.m0), channel_id=1, source_target_pairs={{0,2},{1,3},{2,4},{3,5},{4,6},{5,7},{6,0},{7,1},{8,10},{9,11},{10,... | collective-permute-start | bytes 393224 | tf_op jit(solution)/shard_map/ppermute | solution.py:326
  54.7 2.7 %collective-permute-done.8.m3 = bf16[256,256]{1,0:T(8,128)(2,1)S(1)} collective-permute-done((bf16[256,256]{1,0:T(8,128)(2,1)S(1)}, bf16[256,256]{1,0:T(8,128)(2,1)S(1)}, u32[]{:S(2)}, u32[]{:S(2)}) %collective-permute-start.8) | collective-permute-done | bytes 131104 | tf_op jit(solution)/shard_map/ppermute | solution.py:326
  57.4 2.7 %collective-permute-done.7.m2 = bf16[256,256]{1,0:T(8,128)(2,1)S(1)} collective-permute-done((bf16[256,256]{1,0:T(8,128)(2,1)S(1)}, bf16[256,256]{1,0:T(8,128)(2,1)S(1)}, u32[]{:S(2)}, u32[]{:S(2)}) %collective-permute-start.7) | collective-permute-done | bytes 131104 | tf_op jit(solution)/shard_map/ppermute | solution.py:326
  60.0 1.0 %collective-permute-done.6.m1 = bf16[256,256]{1,0:T(8,128)(2,1)S(1)} collective-permute-done((bf16[256,256]{1,0:T(8,128)(2,1)S(1)}, bf16[256,256]{1,0:T(8,128)(2,1)S(1)}, u32[]{:S(2)}, u32[]{:S(2)}) %collective-permute-start.6) | collective-permute-done | bytes 131104 | tf_op jit(solution)/shard_map/ppermute | solution.py:326
  61.2 1.9 %collective-permute-done.9.theirs_ref = bf16[4,256,256]{2,1,0:T(8,128)(2,1)S(1)} collective-permute-done((bf16[4,256,256]{2,1,0:T(8,128)(2,1)S(1)}, bf16[4,256,256]{2,1,0:T(8,128)(2,1)S(1)}, u32[]{:S(2)}, u32[]{:S(2)}) %collective-permute-start.9) | collective-permute-done | bytes 524320 | tf_op jit(solution)/shard_map/ppermute | solution.py:330
  63.1 4.0 %forward.1 = (bf16[4,256,256]{2,1,0:T(8,128)(2,1)S(1)}, bf16[4,256,256]{2,1,0:T(8,128)(2,1)S(1)}) custom-call(s32[4]{0:T(128)S(1)} %copy-done.3, bf16[256,256]{1,0:T(8,128)(2,1)S(1)} %get-tuple-element.20.m0, bf16[256,256]{1,0:T(8,128)(2,1)S(1)} %collective-permute-done.6.m1, bf16[256,256]{1,0:T(8,128)(2,1)S(1)} %collective-permute-done.7.m2, ...), custom_call_target="tpu_custom_call" | custom-call | tf_op jit(solution)/shard_map/forward/pallas_call | solution.py:306
  67.2 0.2 collective-permute-start.10
  67.4 1.8 %collective-permute-done.10 = bf16[4,256,256]{2,1,0:T(8,128)(2,1)S(1)} collective-permute-done((bf16[4,256,256]{2,1,0:T(8,128)(2,1)S(1)}, bf16[4,256,256]{2,1,0:T(8,128)(2,1)S(1)}, u32[]{:S(2)}, u32[]{:S(2)}) %collective-permute-start.10) | collective-permute-done | bytes 524320 | tf_op jit(solution)/shard_map/ppermute | solution.py:330
  69.1 0.1 fusion.5
  69.4 3.2 %collective-permute-start.13 = (bf16[256,256]{1,0:T(8,128)(2,1)S(1)}, bf16[256,256]{1,0:T(8,128)(2,1)S(1)}, u32[]{:S(2)}, u32[]{:S(2)}) collective-permute-start(bf16[256,256]{1,0:T(8,128)(2,1)S(1)} %get-tuple-element.26), channel_id=1, source_target_pairs={{0,6},{1,7},{2,0},{3,1},{4,2},{5,3},{6,4},{7,5},{8,14},{9,15},{10,... | collective-permute-start | bytes 393224 | tf_op jit(solution)/shard_map/ppermute | solution.py:326
  72.6 3.5 %collective-permute-done.11 = bf16[256,256]{1,0:T(8,128)(2,1)S(1)} collective-permute-done((bf16[256,256]{1,0:T(8,128)(2,1)S(1)}, bf16[256,256]{1,0:T(8,128)(2,1)S(1)}, u32[]{:S(2)}, u32[]{:S(2)}) %collective-permute-start.11) | collective-permute-done | bytes 131104 | tf_op jit(solution)/shard_map/ppermute | solution.py:326
  76.1 2.1 %collective-permute-done.13 = bf16[256,256]{1,0:T(8,128)(2,1)S(1)} collective-permute-done((bf16[256,256]{1,0:T(8,128)(2,1)S(1)}, bf16[256,256]{1,0:T(8,128)(2,1)S(1)}, u32[]{:S(2)}, u32[]{:S(2)}) %collective-permute-start.13) | collective-permute-done | bytes 131104 | tf_op jit(solution)/shard_map/ppermute | solution.py:326
  78.2 0.9 %collective-permute-done.12 = bf16[256,256]{1,0:T(8,128)(2,1)S(1)} collective-permute-done((bf16[256,256]{1,0:T(8,128)(2,1)S(1)}, bf16[256,256]{1,0:T(8,128)(2,1)S(1)}, u32[]{:S(2)}, u32[]{:S(2)}) %collective-permute-start.12) | collective-permute-done | bytes 131104 | tf_op jit(solution)/shard_map/ppermute | solution.py:326
  79.1 0.7 fusion.4
  (19 shorter events, 0.3 us)
Async XLA Ops:
  0.0 41.5 %copy-start.6 = (f32[256]{0:T(256)S(1)}, f32[256]{0:T(256)}, u32[]{:S(2)}) copy-start(f32[256]{0:T(256)} %param.14) | copy-start | bytes 3076
  0.0 41.5 %copy-start.5 = (f32[256]{0:T(256)S(1)}, f32[256]{0:T(256)}, u32[]{:S(2)}) copy-start(f32[256]{0:T(256)} %param.13) | copy-start | bytes 3076
  0.7 30.0 %copy-start.3 = (s32[4]{0:T(128)S(1)}, s32[4]{0:T(128)}, u32[]{:S(2)}) copy-start(s32[4]{0:T(128)} %pad_add_fusion.place_s) | copy-start | bytes 52
  21.0 5.3 %collective-permute-start.2 = (bf16[2,144,128]{2,1,0:T(8,128)(2,1)S(1)}, bf16[2,144,128]{2,1,0:T(8,128)(2,1)S(1)}, u32[]{:S(2)}, u32[]{:S(2)}) collective-permute-start(bf16[2,144,128]{2,1,0:T(8,128)(2,1)S(1)} %get-tuple-element.15.m0), channel_id=1, source_target_pairs={{0,24},{8,0},{16,8},{24,16},{32,56},{40,32},{48,40},{56,48},{64,88... | collective-permute-start | bytes 221192 | tf_op jit(solution)/shard_map/ppermute | solution.py:318
  23.9 6.1 %collective-permute-start.1 = (bf16[2,144,128]{2,1,0:T(8,128)(2,1)S(1)}, bf16[2,144,128]{2,1,0:T(8,128)(2,1)S(1)}, u32[]{:S(2)}, u32[]{:S(2)}) collective-permute-start(bf16[2,144,128]{2,1,0:T(8,128)(2,1)S(1)} %get-tuple-element.15.m0), channel_id=1, source_target_pairs={{0,16},{8,24},{16,0},{24,8},{32,48},{40,56},{48,32},{56,40},{64,80... | collective-permute-start | bytes 221192 | tf_op jit(solution)/shard_map/ppermute | solution.py:318
  24.7 6.0 %collective-permute-start = (bf16[2,144,128]{2,1,0:T(8,128)(2,1)S(1)}, bf16[2,144,128]{2,1,0:T(8,128)(2,1)S(1)}, u32[]{:S(2)}, u32[]{:S(2)}) collective-permute-start(bf16[2,144,128]{2,1,0:T(8,128)(2,1)S(1)} %get-tuple-element.15.m0), channel_id=1, source_target_pairs={{0,8},{8,16},{16,24},{24,0},{32,40},{40,48},{48,56},{56,32},{64,72... | collective-permute-start | bytes 221192 | tf_op jit(solution)/shard_map/ppermute | solution.py:318
  31.8 5.2 %collective-permute-start.5 = (bf16[2,144,128]{2,1,0:T(8,128)(2,1)S(1)}, bf16[2,144,128]{2,1,0:T(8,128)(2,1)S(1)}, u32[]{:S(2)}, u32[]{:S(2)}) collective-permute-start(bf16[2,144,128]{2,1,0:T(8,128)(2,1)S(1)} %row_map.1), channel_id=1, source_target_pairs={{0,96},{8,104},{16,112},{24,120},{32,0},{40,8},{48,16},{56,24},{64... | collective-permute-start | bytes 221192 | tf_op jit(solution)/shard_map/ppermute | solution.py:322
  34.9 5.9 %collective-permute-start.4 = (bf16[2,144,128]{2,1,0:T(8,128)(2,1)S(1)}, bf16[2,144,128]{2,1,0:T(8,128)(2,1)S(1)}, u32[]{:S(2)}, u32[]{:S(2)}) collective-permute-start(bf16[2,144,128]{2,1,0:T(8,128)(2,1)S(1)} %row_map.1), channel_id=1, source_target_pairs={{0,64},{8,72},{16,80},{24,88},{32,96},{40,104},{48,112},{56,120},{... | collective-permute-start | bytes 221192 | tf_op jit(solution)/shard_map/ppermute | solution.py:322
  35.5 6.0 %collective-permute-start.3 = (bf16[2,144,128]{2,1,0:T(8,128)(2,1)S(1)}, bf16[2,144,128]{2,1,0:T(8,128)(2,1)S(1)}, u32[]{:S(2)}, u32[]{:S(2)}) collective-permute-start(bf16[2,144,128]{2,1,0:T(8,128)(2,1)S(1)} %row_map.1), channel_id=1, source_target_pairs={{0,32},{8,40},{16,48},{24,56},{32,64},{40,72},{48,80},{56,88},{64,... | collective-permute-start | bytes 221192 | tf_op jit(solution)/shard_map/ppermute | solution.py:322
  41.5 0.7 copy-start.4
  42.2 20.9 %copy-start = (bf16[2048,1024]{1,0:T(8,128)(2,1)S(1)}, bf16[2048,1024]{1,0:T(8,128)(2,1)}, u32[]{:S(2)}) copy-start(bf16[2048,1024]{1,0:T(8,128)(2,1)} %gate_ref.1) | copy-start | bytes 12582916
  42.2 20.9 %copy-start.1 = (bf16[2048,1024]{1,0:T(8,128)(2,1)S(1)}, bf16[2048,1024]{1,0:T(8,128)(2,1)}, u32[]{:S(2)}) copy-start(bf16[2048,1024]{1,0:T(8,128)(2,1)} %up_ref.1) | copy-start | bytes 12582916
  42.2 20.9 %copy-start.2 = (bf16[1024,2048]{1,0:T(8,128)(2,1)S(1)}, bf16[1024,2048]{1,0:T(8,128)(2,1)}, u32[]{:S(2)}) copy-start(bf16[1024,2048]{1,0:T(8,128)(2,1)} %down_ref.1) | copy-start | bytes 12582916
  49.4 8.0 %collective-permute-start.8 = (bf16[256,256]{1,0:T(8,128)(2,1)S(1)}, bf16[256,256]{1,0:T(8,128)(2,1)S(1)}, u32[]{:S(2)}, u32[]{:S(2)}) collective-permute-start(bf16[256,256]{1,0:T(8,128)(2,1)S(1)} %get-tuple-element.20.m0), channel_id=1, source_target_pairs={{0,6},{1,7},{2,0},{3,1},{4,2},{5,3},{6,4},{7,5},{8,14},{9,15},{10,... | collective-permute-start | bytes 393224 | tf_op jit(solution)/shard_map/ppermute | solution.py:326
  53.5 6.6 %collective-permute-start.7 = (bf16[256,256]{1,0:T(8,128)(2,1)S(1)}, bf16[256,256]{1,0:T(8,128)(2,1)S(1)}, u32[]{:S(2)}, u32[]{:S(2)}) collective-permute-start(bf16[256,256]{1,0:T(8,128)(2,1)S(1)} %get-tuple-element.20.m0), channel_id=1, source_target_pairs={{0,4},{1,5},{2,6},{3,7},{4,0},{5,1},{6,2},{7,3},{8,12},{9,13},{10,... | collective-permute-start | bytes 393224 | tf_op jit(solution)/shard_map/ppermute | solution.py:326
  53.5 7.6 %collective-permute-start.6 = (bf16[256,256]{1,0:T(8,128)(2,1)S(1)}, bf16[256,256]{1,0:T(8,128)(2,1)S(1)}, u32[]{:S(2)}, u32[]{:S(2)}) collective-permute-start(bf16[256,256]{1,0:T(8,128)(2,1)S(1)} %get-tuple-element.20.m0), channel_id=1, source_target_pairs={{0,2},{1,3},{2,4},{3,5},{4,6},{5,7},{6,0},{7,1},{8,10},{9,11},{10,... | collective-permute-start | bytes 393224 | tf_op jit(solution)/shard_map/ppermute | solution.py:326
  61.1 2.0 %collective-permute-start.9 = (bf16[4,256,256]{2,1,0:T(8,128)(2,1)S(1)}, bf16[4,256,256]{2,1,0:T(8,128)(2,1)S(1)}, u32[]{:S(2)}, u32[]{:S(2)}) collective-permute-start(bf16[4,256,256]{2,1,0:T(8,128)(2,1)S(1)} %pad_maximum_fusion), channel_id=1, source_target_pairs={{0,1},{1,0},{2,3},{3,2},{4,5},{5,4},{6,7},{7,6},{8,9},{9,8},{10,11... | collective-permute-start | bytes 1572872 | tf_op jit(solution)/shard_map/ppermute | solution.py:330
  67.2 2.0 %collective-permute-start.10 = (bf16[4,256,256]{2,1,0:T(8,128)(2,1)S(1)}, bf16[4,256,256]{2,1,0:T(8,128)(2,1)S(1)}, u32[]{:S(2)}, u32[]{:S(2)}) collective-permute-start(bf16[4,256,256]{2,1,0:T(8,128)(2,1)S(1)} %get-tuple-element.22), channel_id=1, source_target_pairs={{0,1},{1,0},{2,3},{3,2},{4,5},{5,4},{6,7},{7,6},{8,9},{9,8},{10,11... | collective-permute-start | bytes 1572872 | tf_op jit(solution)/shard_map/ppermute | solution.py:330
  69.3 6.8 %collective-permute-start.11 = (bf16[256,256]{1,0:T(8,128)(2,1)S(1)}, bf16[256,256]{1,0:T(8,128)(2,1)S(1)}, u32[]{:S(2)}, u32[]{:S(2)}) collective-permute-start(bf16[256,256]{1,0:T(8,128)(2,1)S(1)} %get-tuple-element.25), channel_id=1, source_target_pairs={{0,2},{1,3},{2,4},{3,5},{4,6},{5,7},{6,0},{7,1},{8,10},{9,11},{10,... | collective-permute-start | bytes 393224 | tf_op jit(solution)/shard_map/ppermute | solution.py:326
  69.4 8.8 %collective-permute-start.13 = (bf16[256,256]{1,0:T(8,128)(2,1)S(1)}, bf16[256,256]{1,0:T(8,128)(2,1)S(1)}, u32[]{:S(2)}, u32[]{:S(2)}) collective-permute-start(bf16[256,256]{1,0:T(8,128)(2,1)S(1)} %get-tuple-element.26), channel_id=1, source_target_pairs={{0,6},{1,7},{2,0},{3,1},{4,2},{5,3},{6,4},{7,5},{8,14},{9,15},{10,... | collective-permute-start | bytes 393224 | tf_op jit(solution)/shard_map/ppermute | solution.py:326
  72.6 6.5 %collective-permute-start.12 = (bf16[256,256]{1,0:T(8,128)(2,1)S(1)}, bf16[256,256]{1,0:T(8,128)(2,1)S(1)}, u32[]{:S(2)}, u32[]{:S(2)}) collective-permute-start(bf16[256,256]{1,0:T(8,128)(2,1)S(1)} %get-tuple-element.27), channel_id=1, source_target_pairs={{0,4},{1,5},{2,6},{3,7},{4,0},{5,1},{6,2},{7,3},{8,12},{9,13},{10,... | collective-permute-start | bytes 393224 | tf_op jit(solution)/shard_map/ppermute | solution.py:326

commit v3 on v2

--- a/solution.py
+++ b/solution.py
@@ -195,10 +195,13 @@
     )(place, noise, retain, retain, control_weight.reshape(-1, WIDTH, WIDTH), input_weight)
 
 
+def order(held, refs, place, sign):
+    for k, ref in enumerate(refs):
+        held[lax.rem(place + 4 - k * sign, 4)] = ref[...]
+
+
 def row_kernel(place_s, m0, m1, m2, m3, out_ref, held):
-    x = place_s[1]
-    for k, ref in enumerate((m0, m1, m2, m3)):
-        held[lax.rem(x + 4 - k, 4)] = ref[...]
+    order(held, (m0, m1, m2, m3), place_s[1], 1 - 2 * place_s[3])
     for b in range(2):
         parts = []
         for k in range(4):
@@ -217,25 +220,28 @@
 def row_map(place, maps):
     return pl.pallas_call(
         row_kernel,
-        out_shape=jax.ShapeDtypeStruct((2, MAP_ROWS, WIDTH), BF16),
+        out_shape=(
+            jax.ShapeDtypeStruct((2, MAP_ROWS, WIDTH), BF16),
+            jax.ShapeDtypeStruct((4, 2, MAP_ROWS, WIDTH), BF16),
+        ),
         in_specs=[SMEM] + [VMEM] * 4,
-        out_specs=VMEM,
-        scratch_shapes=[pltpu.VMEM((4, 2, MAP_ROWS, WIDTH), BF16)],
+        out_specs=(VMEM, VMEM),
         compiler_params=pltpu.CompilerParams(vmem_limit_bytes=8_000_000),
         name="row_map",
     )(place, *maps)
 
 
-def replay_kernel(place_s, kept_s, init_ref, y1, y2, y3, x1, x2, x3, off_ref, grp_ref, gain_ref, q_ref,
-                  states_ref, normed_ref):
+def replay_kernel(place_s, kept_s, init_ref, y0, y1, y2, y3, row_ref, off_ref, grp_ref, gain_ref, q_ref,
+                  states_ref, normed_ref, held):
     steps = SPAN * GROUPS
+    order(held, (y0, y1, y2, y3), place_s[0], 1 - 2 * place_s[3])
     entry = []
     for b in range(2):
         h = init_ref[b : b + 1, :]
-        for place, refs in ((place_s[0], (y1, y2, y3)), (place_s[1], (x1, x2, x3))):
-            for k in (3, 2, 1):
-                matrix, offset, kept = unpack_map(refs[k - 1], b)
-                h = jnp.where(k <= place, h * kept + row_times(h, matrix) + offset, h)
+        for place, maps in ((place_s[0], held), (place_s[1], row_ref)):
+            for k in range(3):
+                matrix, offset, kept = unpack_map(maps.at[k], b)
+                h = jnp.where(k < place, h * kept + row_times(h, matrix) + offset, h)
         entry.append(h)
 
     def group(g, starts):
@@ -258,7 +264,7 @@
     lax.fori_loop(0, GROUPS, group, tuple(entry), unroll=2)
 
 
-def replay(place, kept, init, y_maps, x_maps, off, grp, gain, q):
+def replay(place, kept, init, y_maps, row, off, grp, gain, q):
     steps = SPAN * GROUPS
     return pl.pallas_call(
         replay_kernel,
@@ -266,36 +272,37 @@
             jax.ShapeDtypeStruct((steps, 2 * WIDTH), F32),
             jax.ShapeDtypeStruct((steps, 2 * WIDTH), BF16),
         ),
-        in_specs=[SMEM, SMEM] + [VMEM] * 11,
+        in_specs=[SMEM, SMEM] + [VMEM] * 10,
         out_specs=(VMEM, VMEM),
+        scratch_shapes=[pltpu.VMEM((4, 2, MAP_ROWS, WIDTH), BF16)],
         compiler_params=pltpu.CompilerParams(vmem_limit_bytes=16_000_000),
         name="replay",
-    )(place, kept, init, *y_maps, *x_maps, off, grp, gain, pltpu.with_memory_space_constraint(q, pltpu.VMEM))
+    )(place, kept, init, *y_maps, row, off, grp, gain, pltpu.with_memory_space_constraint(q, pltpu.VMEM))
 
 
 def forward_kernel(place_s, m0, m1, m2, m3, theirs_ref, gate_ref, up_ref, down_ref, keep_ref, send_ref, hidden):
     z, core = place_s[2], place_s[3]
+    sign = 1 - 2 * core
     wide = 2 * WIDTH
 
     def at(k, c):
-        return pl.multiple_of((lax.rem(z + k, 4) * 2 + c) * wide, wide)
-
-    parts = [(m0, 0, 0), (m1, 3, 0), (m2, 2, 0), (m3, 1, 0)]
-    parts += [(theirs_ref.at[k], (4 - k) % 4, 1) for k in range(4)]
+        return pl.multiple_of((lax.rem(z + 4 + k, 4) * 2 + c) * wide, wide)
+
+    parts = [(ref, at(-k * sign, core)) for k, ref in enumerate((m0, m1, m2, m3))]
+    parts += [(theirs_ref.at[k], at(k * sign, 1 - core)) for k in range(4)]
     for n in range(0, gate_ref.shape[1], wide):
         gate = up = None
-        for ref, k, other in parts:
+        for ref, row in parts:
             chunk = ref[...]
-            row = at(k, 1 - core if other else core)
             g = jnp.dot(chunk, gate_ref[pl.ds(row, wide), n : n + wide], preferred_element_type=F32)
             u = jnp.dot(chunk, up_ref[pl.ds(row, wide), n : n + wide], preferred_element_type=F32)
             gate = g if gate is None else gate + g
             up = u if up is None else up + u
         hidden[:, n : n + wide] = (gate / (1.0 + jnp.exp(-gate)) * up).astype(BF16)
     low = hidden[...]
-    for ref, c in ((send_ref, 1 - core), (keep_ref, core)):
+    for ref, c, ahead in ((send_ref, 1 - core, -sign), (keep_ref, core, sign)):
         for k in range(4):
-            out = jnp.dot(low, down_ref[:, pl.ds(at(k, c), wide)], preferred_element_type=F32)
+            out = jnp.dot(low, down_ref[:, pl.ds(at(k * ahead, c), wide)], preferred_element_type=F32)
             ref[k] = out.astype(BF16)
 
 
@@ -314,16 +321,19 @@
     )(place, *mine, theirs, *weights)
 
 
-def x_back(v, k):
-    return lax.ppermute(v, "tm", [(y * 4 + x, y * 4 + (x + k) % 4) for y in range(4) for x in range(4)])
-
-
-def y_back(v, k):
-    return lax.ppermute(v, "tm", [(y * 4 + x, (y + k) % 4 * 4 + x) for y in range(4) for x in range(4)])
-
-
-def z_back(v, k):
-    return lax.ppermute(v, "block", [(z * 2 + c, (z + k) % 4 * 2 + c) for z in range(4) for c in range(2)])
+def along(v, axis, way):
+    pairs = []
+    for source in range(128):
+        at = [source // 32, source // 8 % 4, source // 2 % 4, source % 2]
+        at[axis] = (at[axis] + way * (1 - 2 * at[3])) % 4
+        pairs.append((source, at[0] * 32 + at[1] * 8 + at[2] * 2 + at[3]))
+    return lax.ppermute(v, ("tm", "block"), pairs)
+
+
+def gather(v, axis):
+    one = along(v, axis, 1)
+    three = along(v, axis, -1)
+    return [v, one, along(one, axis, 1), three]
 
 
 def other_core(v):
@@ -346,21 +356,18 @@
     z, core = block // 2, block % 2
     place = jnp.stack([tm // 4, tm % 4, z, core]).astype(jnp.int32)
     q, off, own, grp, kept = compose(place, noise.T, retain.T, control_weight, input_weight)
-    x_maps = [x_back(own, k) for k in (1, 2, 3)]
-    total = row_map(place, [own, *x_maps])
-    y_maps = [y_back(total, k) for k in (1, 2, 3)]
+    total, row = row_map(place, gather(own, 1))
     states, normed = replay(
-        place, kept, initial_state.reshape(2, WIDTH), y_maps, x_maps, off, grp, norm_gain.reshape(2, WIDTH), q
+        place, kept, initial_state.reshape(2, WIDTH), gather(total, 0), row, off, grp, norm_gain.reshape(2, WIDTH), q
     )
-    mine = [normed] + [z_back(normed, k) for k in (1, 2, 3)]
+    mine = gather(normed, 2)
     theirs = other_core(jnp.stack(mine))
     keep, sent = forward(place, mine, theirs, gate_weight, up_weight, down_weight)
     chip = keep.astype(F32) + other_core(sent).astype(F32)
-    low = chip.astype(BF16)
-    mixed = chip[0]
-    for k in (1, 2, 3):
-        mixed = mixed + z_back(low[k], k).astype(F32)
-    return (states + mixed).astype(BF16)
+    two = along(chip[2].astype(BF16), 2, 1)
+    three = along(chip[3].astype(BF16), 2, -1)
+    one = along((chip[1] + two.astype(F32)).astype(BF16), 2, 1)
+    return (states + (chip[0] + three.astype(F32) + one.astype(F32))).astype(BF16)
 
 
 def solution(mesh):

time: 80 us -> 88.4 us (1.10)
  waiting for transfers between devices: 26.6 us -> 37.2 us
  starting transfers between devices: 18.2 us -> 16 us
    ppermute x12, waiting for transfers between devices: 23 us -> 33.5 us  [along(): return lax.ppermute(v, ('tm', 'block'), pairs)]
    ppermute x12, starting transfers between devices: 17.9 us -> 15.7 us  [along(): return lax.ppermute(v, ('tm', 'block'), pairs)]
  transfers between devices with their start and end apart: 14 -> 14, of which waited for: 14 -> 10; matrix products, arithmetic and copies ran while one was open for 0% -> 0% of each run, Pallas kernels for 0% -> 0%
where the time goes in v3:
time: 88.4 us; the launch traced here: 88.2 us
  waiting for transfers between devices  37.2 us (42%)
  Pallas kernels  32.6 us (37%)
  starting transfers between devices  16 us (18%)
  other arithmetic  1.56 us (2%)
    ppermute x12, waiting for transfers between devices, along(): return lax.ppermute(v, ('tm', 'block'), pairs)  33.5 us
    pallas_call x1, Pallas kernels, compose(): pl.pallas_call(compose_kernel, out_shape=(pltpu.VMEM((SPAN, 2 * GROUPS, W...  20.3 us
    ppermute x12, starting transfers between devices, along(): return lax.ppermute(v, ('tm', 'block'), pairs)  15.7 us
    pallas_call x1, Pallas kernels, replay(): pl.pallas_call(replay_kernel, out_shape=(jax.ShapeDtypeStruct((steps, 2 *...  7.22 us
    pallas_call x1, Pallas kernels, forward(): pl.pallas_call(forward_kernel, out_shape=(half, half), in_specs=[SMEM] +...  4.02 us
    ppermute x2, waiting for transfers between devices, other_core(): return lax.ppermute(v, 'block', [(s, s ^ 1) for s in range(8)])  3.69 us
  transfers between devices with their start and end apart: 14, of which 10 were waited for; matrix products, arithmetic and copies ran while one was open for 0% of the time, Pallas kernels for 0%

profile of v3, /device:TPU:0, one launch (start us, length us, event | category | flops | bytes accessed | tf_op | source)
XLA Modules:
  0.0 88.2 jit_solution(12095445587570396160)
XLA Ops:
  0.0 0.6 pad_add_fusion.place_s
  0.6 20.3 %compose.1 = (bf16[16,32,128,128]{3,2,1,0:T(8,128)(2,1)S(1)}, f32[512,128]{1,0:T(8,128)S(1)}, bf16[2,144,128]{2,1,0:T(8,128)(2,1)S(1)}, bf16[32,128,128]{2,1,0:T(8,128)(2,1)S(1)}, f32[16,2]{1,0:T(8,128)}) custom-call(s32[4]{0:T(128)} %pad_add_fusion.place_s, f32[64,256]{1,0:T(8,128)} %bitcast.40, f32[2,256]{1,0:T(2,128)} %bitcast.41, f32[2,256]{1,0:T(2,128)} %bitcast.42, ...), custom_call_target="tpu_custom_call" | custom-call | tf_op jit(solution)/shard_map/compose/pallas_call | solution.py:177
  20.9 1.6 %collective-permute-start = (bf16[2,144,128]{2,1,0:T(8,128)(2,1)S(1)}, bf16[2,144,128]{2,1,0:T(8,128)(2,1)S(1)}, u32[]{:S(2)}, u32[]{:S(2)}) collective-permute-start(bf16[2,144,128]{2,1,0:T(8,128)(2,1)S(1)} %get-tuple-element.17.m0), channel_id=1, source_target_pairs={{0,8},{1,25},{2,10},{3,27},{4,12},{5,29},{6,14},{7,31},{8,16},{9,1... | collective-permute-start | bytes 221192 | tf_op jit(solution)/shard_map/ppermute | solution.py:330
  22.6 1.7 %collective-permute-start.2 = (bf16[2,144,128]{2,1,0:T(8,128)(2,1)S(1)}, bf16[2,144,128]{2,1,0:T(8,128)(2,1)S(1)}, u32[]{:S(2)}, u32[]{:S(2)}) collective-permute-start(bf16[2,144,128]{2,1,0:T(8,128)(2,1)S(1)} %get-tuple-element.17.m0), channel_id=1, source_target_pairs={{0,24},{1,9},{2,26},{3,11},{4,28},{5,13},{6,30},{7,15},{8,0},{9,17... | collective-permute-start | bytes 221192 | tf_op jit(solution)/shard_map/ppermute | solution.py:330
  24.2 2.3 %collective-permute-done.m1 = bf16[2,144,128]{2,1,0:T(8,128)(2,1)S(1)} collective-permute-done((bf16[2,144,128]{2,1,0:T(8,128)(2,1)S(1)}, bf16[2,144,128]{2,1,0:T(8,128)(2,1)S(1)}, u32[]{:S(2)}, u32[]{:S(2)}) %collective-permute-start) | collective-permute-done | bytes 73760 | tf_op jit(solution)/shard_map/ppermute | solution.py:330
  26.6 1.0 %collective-permute-start.1 = (bf16[2,144,128]{2,1,0:T(8,128)(2,1)S(1)}, bf16[2,144,128]{2,1,0:T(8,128)(2,1)S(1)}, u32[]{:S(2)}, u32[]{:S(2)}) collective-permute-start(bf16[2,144,128]{2,1,0:T(8,128)(2,1)S(1)} %collective-permute-done.m1), channel_id=1, source_target_pairs={{0,8},{1,25},{2,10},{3,27},{4,12},{5,29},{6,14},{7,31},{8,16},{9,1... | collective-permute-start | bytes 221192 | tf_op jit(solution)/shard_map/ppermute | solution.py:330
  27.6 4.5 %collective-permute-done.1.m2 = bf16[2,144,128]{2,1,0:T(8,128)(2,1)S(1)} collective-permute-done((bf16[2,144,128]{2,1,0:T(8,128)(2,1)S(1)}, bf16[2,144,128]{2,1,0:T(8,128)(2,1)S(1)}, u32[]{:S(2)}, u32[]{:S(2)}) %collective-permute-start.1) | collective-permute-done | bytes 73760 | tf_op jit(solution)/shard_map/ppermute | solution.py:330
  32.1 1.0 %row_map.1 = (bf16[2,144,128]{2,1,0:T(8,128)(2,1)S(1)}, bf16[4,2,144,128]{3,2,1,0:T(8,128)(2,1)S(1)}) custom-call(s32[4]{0:T(128)S(1)} %copy-done.3, bf16[2,144,128]{2,1,0:T(8,128)(2,1)S(1)} %get-tuple-element.17.m0, bf16[2,144,128]{2,1,0:T(8,128)(2,1)S(1)} %collective-permute-done.m1, bf16[2,144,128]{2,1,0:T(8,128)(2,1)S(1)} %collective-permute-done.1.m2, ...), custom_call_target="tpu_custom_call" | custom-call | tf_op jit(solution)/shard_map/row_map/pallas_call | solution.py:221
  33.2 1.7 %collective-permute-start.3 = (bf16[2,144,128]{2,1,0:T(8,128)(2,1)S(1)}, bf16[2,144,128]{2,1,0:T(8,128)(2,1)S(1)}, u32[]{:S(2)}, u32[]{:S(2)}) collective-permute-start(bf16[2,144,128]{2,1,0:T(8,128)(2,1)S(1)} %get-tuple-element.18.y0), channel_id=1, source_target_pairs={{0,32},{1,97},{2,34},{3,99},{4,36},{5,101},{6,38},{7,103},{8,40},{... | collective-permute-start | bytes 221192 | tf_op jit(solution)/shard_map/ppermute | solution.py:330
  34.9 1.6 %collective-permute-start.5 = (bf16[2,144,128]{2,1,0:T(8,128)(2,1)S(1)}, bf16[2,144,128]{2,1,0:T(8,128)(2,1)S(1)}, u32[]{:S(2)}, u32[]{:S(2)}) collective-permute-start(bf16[2,144,128]{2,1,0:T(8,128)(2,1)S(1)} %get-tuple-element.18.y0), channel_id=1, source_target_pairs={{0,96},{1,33},{2,98},{3,35},{4,100},{5,37},{6,102},{7,39},{8,104},... | collective-permute-start | bytes 221192 | tf_op jit(solution)/shard_map/ppermute | solution.py:330
  36.5 2.3 %collective-permute-done.3.y1 = bf16[2,144,128]{2,1,0:T(8,128)(2,1)S(1)} collective-permute-done((bf16[2,144,128]{2,1,0:T(8,128)(2,1)S(1)}, bf16[2,144,128]{2,1,0:T(8,128)(2,1)S(1)}, u32[]{:S(2)}, u32[]{:S(2)}) %collective-permute-start.3) | collective-permute-done | bytes 73760 | tf_op jit(solution)/shard_map/ppermute | solution.py:330
  38.8 0.4 collective-permute-start.4
  39.3 5.1 %collective-permute-done.4.y2 = bf16[2,144,128]{2,1,0:T(8,128)(2,1)S(1)} collective-permute-done((bf16[2,144,128]{2,1,0:T(8,128)(2,1)S(1)}, bf16[2,144,128]{2,1,0:T(8,128)(2,1)S(1)}, u32[]{:S(2)}, u32[]{:S(2)}) %collective-permute-start.4) | collective-permute-done | bytes 73760 | tf_op jit(solution)/shard_map/ppermute | solution.py:330
  44.4 0.7 copy-done.4
  45.1 7.2 %replay.1 = (f32[256,256]{1,0:T(8,128)S(1)}, bf16[256,256]{1,0:T(8,128)(2,1)S(1)}) custom-call(s32[4]{0:T(128)S(1)} %copy-done.3, f32[16,2]{1,0:T(8,128)S(1)} %copy-done.4, f32[2,128]{1,0:T(2,128)S(1)} %bitcast.37, bf16[2,144,128]{2,1,0:T(8,128)(2,1)S(1)} %get-tuple-element.18.y0, bf16[2,144,128]{2,1,0:T(8,128)(2,1)S(1)} %collective-permute-done.3.y1, ...), custom_call_target="tpu_custom_call" | custom-call | tf_op jit(solution)/shard_map/replay/pallas_call | solution.py:269
  52.3 2.0 %collective-permute-start.6 = (bf16[256,256]{1,0:T(8,128)(2,1)S(1)}, bf16[256,256]{1,0:T(8,128)(2,1)S(1)}, u32[]{:S(2)}, u32[]{:S(2)}) collective-permute-start(bf16[256,256]{1,0:T(8,128)(2,1)S(1)} %get-tuple-element.24.m0), channel_id=1, source_target_pairs={{0,2},{1,7},{2,4},{3,1},{4,6},{5,3},{6,0},{7,5},{8,10},{9,15},{10,... | collective-permute-start | bytes 393224 | tf_op jit(solution)/shard_map/ppermute | solution.py:330
  54.3 2.2 %collective-permute-start.8 = (bf16[256,256]{1,0:T(8,128)(2,1)S(1)}, bf16[256,256]{1,0:T(8,128)(2,1)S(1)}, u32[]{:S(2)}, u32[]{:S(2)}) collective-permute-start(bf16[256,256]{1,0:T(8,128)(2,1)S(1)} %get-tuple-element.24.m0), channel_id=1, source_target_pairs={{0,6},{1,3},{2,0},{3,5},{4,2},{5,7},{6,4},{7,1},{8,14},{9,11},{10,... | collective-permute-start | bytes 393224 | tf_op jit(solution)/shard_map/ppermute | solution.py:330
  56.5 2.9 %collective-permute-done.6.m1 = bf16[256,256]{1,0:T(8,128)(2,1)S(1)} collective-permute-done((bf16[256,256]{1,0:T(8,128)(2,1)S(1)}, bf16[256,256]{1,0:T(8,128)(2,1)S(1)}, u32[]{:S(2)}, u32[]{:S(2)}) %collective-permute-start.6) | collective-permute-done | bytes 131104 | tf_op jit(solution)/shard_map/ppermute | solution.py:330
  59.4 6.2 %collective-permute-done.7.m2 = bf16[256,256]{1,0:T(8,128)(2,1)S(1)} collective-permute-done((bf16[256,256]{1,0:T(8,128)(2,1)S(1)}, bf16[256,256]{1,0:T(8,128)(2,1)S(1)}, u32[]{:S(2)}, u32[]{:S(2)}) %collective-permute-start.7) | collective-permute-done | bytes 131104 | tf_op jit(solution)/shard_map/ppermute | solution.py:330
  65.6 0.1 pad_maximum_fusion
  65.7 0.1 collective-permute-start.9
  65.7 1.9 %collective-permute-done.9.theirs_ref = bf16[4,256,256]{2,1,0:T(8,128)(2,1)S(1)} collective-permute-done((bf16[4,256,256]{2,1,0:T(8,128)(2,1)S(1)}, bf16[4,256,256]{2,1,0:T(8,128)(2,1)S(1)}, u32[]{:S(2)}, u32[]{:S(2)}) %collective-permute-start.9) | collective-permute-done | bytes 524320 | tf_op jit(solution)/shard_map/ppermute | solution.py:340
  67.7 4.0 %forward.1 = (bf16[4,256,256]{2,1,0:T(8,128)(2,1)S(1)}, bf16[4,256,256]{2,1,0:T(8,128)(2,1)S(1)}) custom-call(s32[4]{0:T(128)S(1)} %copy-done.3, bf16[256,256]{1,0:T(8,128)(2,1)S(1)} %get-tuple-element.24.m0, bf16[256,256]{1,0:T(8,128)(2,1)S(1)} %collective-permute-done.6.m1, bf16[256,256]{1,0:T(8,128)(2,1)S(1)} %collective-permute-done.7.m2, ...), custom_call_target="tpu_custom_call" | custom-call | tf_op jit(solution)/shard_map/forward/pallas_call | solution.py:313
  71.7 0.2 collective-permute-start.10
  71.9 1.8 %collective-permute-done.10 = bf16[4,256,256]{2,1,0:T(8,128)(2,1)S(1)} collective-permute-done((bf16[4,256,256]{2,1,0:T(8,128)(2,1)S(1)}, bf16[4,256,256]{2,1,0:T(8,128)(2,1)S(1)}, u32[]{:S(2)}, u32[]{:S(2)}) %collective-permute-start.10) | collective-permute-done | bytes 524320 | tf_op jit(solution)/shard_map/ppermute | solution.py:340
  73.7 0.1 fusion.6
  73.8 0.1 collective-permute-start.12
  73.9 3.2 %collective-permute-start.11 = (bf16[256,256]{1,0:T(8,128)(2,1)S(1)}, bf16[256,256]{1,0:T(8,128)(2,1)S(1)}, u32[]{:S(2)}, u32[]{:S(2)}) collective-permute-start(bf16[256,256]{1,0:T(8,128)(2,1)S(1)} %get-tuple-element.29), channel_id=1, source_target_pairs={{0,6},{1,3},{2,0},{3,5},{4,2},{5,7},{6,4},{7,1},{8,14},{9,11},{10,... | collective-permute-start | bytes 393224 | tf_op jit(solution)/shard_map/ppermute | solution.py:330
  77.2 4.0 %collective-permute-done.12 = bf16[256,256]{1,0:T(8,128)(2,1)S(1)} collective-permute-done((bf16[256,256]{1,0:T(8,128)(2,1)S(1)}, bf16[256,256]{1,0:T(8,128)(2,1)S(1)}, u32[]{:S(2)}, u32[]{:S(2)}) %collective-permute-start.12) | collective-permute-done | bytes 131104 | tf_op jit(solution)/shard_map/ppermute | solution.py:330
  81.2 0.1 collective-permute-start.13
  81.3 6.2 %collective-permute-done.13 = bf16[256,256]{1,0:T(8,128)(2,1)S(1)} collective-permute-done((bf16[256,256]{1,0:T(8,128)(2,1)S(1)}, bf16[256,256]{1,0:T(8,128)(2,1)S(1)}, u32[]{:S(2)}, u32[]{:S(2)}) %collective-permute-start.13) | collective-permute-done | bytes 131104 | tf_op jit(solution)/shard_map/ppermute | solution.py:330
  87.5 0.7 fusion.5
  (20 shorter events, 0.1 us)
Async XLA Ops:
  0.0 44.4 %copy-start.6 = (f32[256]{0:T(256)S(1)}, f32[256]{0:T(256)}, u32[]{:S(2)}) copy-start(f32[256]{0:T(256)} %param.14) | copy-start | bytes 3076
  0.0 44.4 %copy-start.5 = (f32[256]{0:T(256)S(1)}, f32[256]{0:T(256)}, u32[]{:S(2)}) copy-start(f32[256]{0:T(256)} %param.13) | copy-start | bytes 3076
  0.6 31.5 %copy-start.3 = (s32[4]{0:T(128)S(1)}, s32[4]{0:T(128)}, u32[]{:S(2)}) copy-start(s32[4]{0:T(128)} %pad_add_fusion.place_s) | copy-start | bytes 52
  20.9 5.6 %collective-permute-start = (bf16[2,144,128]{2,1,0:T(8,128)(2,1)S(1)}, bf16[2,144,128]{2,1,0:T(8,128)(2,1)S(1)}, u32[]{:S(2)}, u32[]{:S(2)}) collective-permute-start(bf16[2,144,128]{2,1,0:T(8,128)(2,1)S(1)} %get-tuple-element.17.m0), channel_id=1, source_target_pairs={{0,8},{1,25},{2,10},{3,27},{4,12},{5,29},{6,14},{7,31},{8,16},{9,1... | collective-permute-start | bytes 221192 | tf_op jit(solution)/shard_map/ppermute | solution.py:330
  22.6 5.0 %collective-permute-start.2 = (bf16[2,144,128]{2,1,0:T(8,128)(2,1)S(1)}, bf16[2,144,128]{2,1,0:T(8,128)(2,1)S(1)}, u32[]{:S(2)}, u32[]{:S(2)}) collective-permute-start(bf16[2,144,128]{2,1,0:T(8,128)(2,1)S(1)} %get-tuple-element.17.m0), channel_id=1, source_target_pairs={{0,24},{1,9},{2,26},{3,11},{4,28},{5,13},{6,30},{7,15},{8,0},{9,17... | collective-permute-start | bytes 221192 | tf_op jit(solution)/shard_map/ppermute | solution.py:330
  26.6 5.6 %collective-permute-start.1 = (bf16[2,144,128]{2,1,0:T(8,128)(2,1)S(1)}, bf16[2,144,128]{2,1,0:T(8,128)(2,1)S(1)}, u32[]{:S(2)}, u32[]{:S(2)}) collective-permute-start(bf16[2,144,128]{2,1,0:T(8,128)(2,1)S(1)} %collective-permute-done.m1), channel_id=1, source_target_pairs={{0,8},{1,25},{2,10},{3,27},{4,12},{5,29},{6,14},{7,31},{8,16},{9,1... | collective-permute-start | bytes 221192 | tf_op jit(solution)/shard_map/ppermute | solution.py:330
  33.2 5.6 %collective-permute-start.3 = (bf16[2,144,128]{2,1,0:T(8,128)(2,1)S(1)}, bf16[2,144,128]{2,1,0:T(8,128)(2,1)S(1)}, u32[]{:S(2)}, u32[]{:S(2)}) collective-permute-start(bf16[2,144,128]{2,1,0:T(8,128)(2,1)S(1)} %get-tuple-element.18.y0), channel_id=1, source_target_pairs={{0,32},{1,97},{2,34},{3,99},{4,36},{5,101},{6,38},{7,103},{8,40},{... | collective-permute-start | bytes 221192 | tf_op jit(solution)/shard_map/ppermute | solution.py:330
  34.9 4.4 %collective-permute-start.5 = (bf16[2,144,128]{2,1,0:T(8,128)(2,1)S(1)}, bf16[2,144,128]{2,1,0:T(8,128)(2,1)S(1)}, u32[]{:S(2)}, u32[]{:S(2)}) collective-permute-start(bf16[2,144,128]{2,1,0:T(8,128)(2,1)S(1)} %get-tuple-element.18.y0), channel_id=1, source_target_pairs={{0,96},{1,33},{2,98},{3,35},{4,100},{5,37},{6,102},{7,39},{8,104},... | collective-permute-start | bytes 221192 | tf_op jit(solution)/shard_map/ppermute | solution.py:330
  38.8 5.6 %collective-permute-start.4 = (bf16[2,144,128]{2,1,0:T(8,128)(2,1)S(1)}, bf16[2,144,128]{2,1,0:T(8,128)(2,1)S(1)}, u32[]{:S(2)}, u32[]{:S(2)}) collective-permute-start(bf16[2,144,128]{2,1,0:T(8,128)(2,1)S(1)} %collective-permute-done.3.y1), channel_id=1, source_target_pairs={{0,32},{1,97},{2,34},{3,99},{4,36},{5,101},{6,38},{7,103},{8,40},{... | collective-permute-start | bytes 221192 | tf_op jit(solution)/shard_map/ppermute | solution.py:330
  44.4 0.7 copy-start.4
  45.1 22.6 %copy-start = (bf16[2048,1024]{1,0:T(8,128)(2,1)S(1)}, bf16[2048,1024]{1,0:T(8,128)(2,1)}, u32[]{:S(2)}) copy-start(bf16[2048,1024]{1,0:T(8,128)(2,1)} %gate_ref.1) | copy-start | bytes 12582916
  45.1 22.6 %copy-start.1 = (bf16[2048,1024]{1,0:T(8,128)(2,1)S(1)}, bf16[2048,1024]{1,0:T(8,128)(2,1)}, u32[]{:S(2)}) copy-start(bf16[2048,1024]{1,0:T(8,128)(2,1)} %up_ref.1) | copy-start | bytes 12582916
  45.1 22.6 %copy-start.2 = (bf16[1024,2048]{1,0:T(8,128)(2,1)S(1)}, bf16[1024,2048]{1,0:T(8,128)(2,1)}, u32[]{:S(2)}) copy-start(bf16[1024,2048]{1,0:T(8,128)(2,1)} %down_ref.1) | copy-start | bytes 12582916
  52.3 7.1 %collective-permute-start.6 = (bf16[256,256]{1,0:T(8,128)(2,1)S(1)}, bf16[256,256]{1,0:T(8,128)(2,1)S(1)}, u32[]{:S(2)}, u32[]{:S(2)}) collective-permute-start(bf16[256,256]{1,0:T(8,128)(2,1)S(1)} %get-tuple-element.24.m0), channel_id=1, source_target_pairs={{0,2},{1,7},{2,4},{3,1},{4,6},{5,3},{6,0},{7,5},{8,10},{9,15},{10,... | collective-permute-start | bytes 393224 | tf_op jit(solution)/shard_map/ppermute | solution.py:330
  54.3 5.1 %collective-permute-start.8 = (bf16[256,256]{1,0:T(8,128)(2,1)S(1)}, bf16[256,256]{1,0:T(8,128)(2,1)S(1)}, u32[]{:S(2)}, u32[]{:S(2)}) collective-permute-start(bf16[256,256]{1,0:T(8,128)(2,1)S(1)} %get-tuple-element.24.m0), channel_id=1, source_target_pairs={{0,6},{1,3},{2,0},{3,5},{4,2},{5,7},{6,4},{7,1},{8,14},{9,11},{10,... | collective-permute-start | bytes 393224 | tf_op jit(solution)/shard_map/ppermute | solution.py:330
  59.4 6.2 %collective-permute-start.7 = (bf16[256,256]{1,0:T(8,128)(2,1)S(1)}, bf16[256,256]{1,0:T(8,128)(2,1)S(1)}, u32[]{:S(2)}, u32[]{:S(2)}) collective-permute-start(bf16[256,256]{1,0:T(8,128)(2,1)S(1)} %collective-permute-done.6.m1), channel_id=1, source_target_pairs={{0,2},{1,7},{2,4},{3,1},{4,6},{5,3},{6,0},{7,5},{8,10},{9,15},{10,... | collective-permute-start | bytes 393224 | tf_op jit(solution)/shard_map/ppermute | solution.py:330
  65.7 2.0 %collective-permute-start.9 = (bf16[4,256,256]{2,1,0:T(8,128)(2,1)S(1)}, bf16[4,256,256]{2,1,0:T(8,128)(2,1)S(1)}, u32[]{:S(2)}, u32[]{:S(2)}) collective-permute-start(bf16[4,256,256]{2,1,0:T(8,128)(2,1)S(1)} %pad_maximum_fusion), channel_id=1, source_target_pairs={{0,1},{1,0},{2,3},{3,2},{4,5},{5,4},{6,7},{7,6},{8,9},{9,8},{10,11... | collective-permute-start | bytes 1572872 | tf_op jit(solution)/shard_map/ppermute | solution.py:340
  71.7 2.0 %collective-permute-start.10 = (bf16[4,256,256]{2,1,0:T(8,128)(2,1)S(1)}, bf16[4,256,256]{2,1,0:T(8,128)(2,1)S(1)}, u32[]{:S(2)}, u32[]{:S(2)}) collective-permute-start(bf16[4,256,256]{2,1,0:T(8,128)(2,1)S(1)} %get-tuple-element.26), channel_id=1, source_target_pairs={{0,1},{1,0},{2,3},{3,2},{4,5},{5,4},{6,7},{7,6},{8,9},{9,8},{10,11... | collective-permute-start | bytes 1572872 | tf_op jit(solution)/shard_map/ppermute | solution.py:340
  73.8 7.3 %collective-permute-start.12 = (bf16[256,256]{1,0:T(8,128)(2,1)S(1)}, bf16[256,256]{1,0:T(8,128)(2,1)S(1)}, u32[]{:S(2)}, u32[]{:S(2)}) collective-permute-start(bf16[256,256]{1,0:T(8,128)(2,1)S(1)} %get-tuple-element.30), channel_id=1, source_target_pairs={{0,2},{1,7},{2,4},{3,1},{4,6},{5,3},{6,0},{7,5},{8,10},{9,15},{10,... | collective-permute-start | bytes 393224 | tf_op jit(solution)/shard_map/ppermute | solution.py:330
  73.9 7.4 %collective-permute-start.11 = (bf16[256,256]{1,0:T(8,128)(2,1)S(1)}, bf16[256,256]{1,0:T(8,128)(2,1)S(1)}, u32[]{:S(2)}, u32[]{:S(2)}) collective-permute-start(bf16[256,256]{1,0:T(8,128)(2,1)S(1)} %get-tuple-element.29), channel_id=1, source_target_pairs={{0,6},{1,3},{2,0},{3,5},{4,2},{5,7},{6,4},{7,1},{8,14},{9,11},{10,... | collective-permute-start | bytes 393224 | tf_op jit(solution)/shard_map/ppermute | solution.py:330
  81.2 6.2 %collective-permute-start.13 = (bf16[256,256]{1,0:T(8,128)(2,1)S(1)}, bf16[256,256]{1,0:T(8,128)(2,1)S(1)}, u32[]{:S(2)}, u32[]{:S(2)}) collective-permute-start(bf16[256,256]{1,0:T(8,128)(2,1)S(1)} %fusion.1), channel_id=1, source_target_pairs={{0,2},{1,7},{2,4},{3,1},{4,6},{5,3},{6,0},{7,5},{8,10},{9,15},{10,... | collective-permute-start | bytes 393224 | tf_op jit(solution)/shard_map/ppermute | solution.py:330

commit v4 on v2

--- a/solution.py
+++ b/solution.py
@@ -46,17 +46,31 @@
     return matrix, offset, kept
 
 
-def row_times(h, matrix):
+def two_parts(h):
     row = lax.broadcasted_iota(jnp.int32, (16, WIDTH), 0)
     hi = h.astype(BF16).astype(F32)
     lo = h - hi
-    both = jnp.where(row == 0, jnp.broadcast_to(hi, (16, WIDTH)), jnp.broadcast_to(lo, (16, WIDTH)))
-    out = jnp.dot(both.astype(BF16), matrix, preferred_element_type=F32)
+    return jnp.where(
+        row == 0, jnp.broadcast_to(hi, (16, WIDTH)), jnp.broadcast_to(lo, (16, WIDTH))
+    ).astype(BF16)
+
+
+def parts_times(parts, matrix):
+    out = jnp.dot(parts, matrix, preferred_element_type=F32)
     return out[0:1] + out[1:2]
 
 
+def row_times(h, matrix):
+    return parts_times(two_parts(h), matrix)
+
+
+def places():
+    tm, block = lax.axis_index("tm"), lax.axis_index("block")
+    return lax.div(tm, 4), lax.rem(tm, 4), lax.div(block, 2), lax.rem(block, 2)
+
+
 def compose_kernel(
-    place_s, noise_ref, retain_s, retain_ref, cw_ref, iw_ref, q_ref, off_ref, send_ref, grp_ref, kept_ref, skw, am, sem
+    noise_ref, retain_s, retain_ref, cw_ref, iw_ref, q_ref, off_ref, send_ref, grp_ref, kept_ref, skw, am, kept_s, sem
 ):
     steps = noise_ref.shape[1]
     loads = [
@@ -79,7 +93,7 @@
         for b in range(2):
             raw = q_ref[base // 16, i * 2 + b]
             diff = (raw.T.astype(F32) - raw.astype(F32)) * (1.0 / math.sqrt(2.0))
-            skw[pl.ds((b * 64 + base + i) * PITCH, WIDTH), :] = diff.astype(BF16).astype(F32)
+            skw[pl.ds((b * 64 + base + i) * PITCH, WIDTH), :] = diff
         return carry
 
     for k in range(4):
@@ -123,7 +137,7 @@
 
     def first(g, carry):
         for b in range(2):
-            kept_ref[g, b] = finish(0, g, b, eye + step_matrix(g * SPAN, b), None)
+            kept_s[g, b] = finish(0, g, b, eye + step_matrix(g * SPAN, b), None)
         return carry
 
     lax.fori_loop(0, GROUPS, first, 0, unroll=4)
@@ -141,7 +155,7 @@
             for b in range(2):
                 y = now[b] + turned[:, b * WIDTH : (b + 1) * WIDTH]
                 rate = finish(s, g, b, y[:WIDTH], y[WIDTH:])
-                kept_ref[g, b] = kept_ref[g, b] * rate
+                kept_s[g, b] = kept_s[g, b] * rate
             return inner
 
         lax.fori_loop(0, GROUPS, group, 0, unroll=16)
@@ -149,13 +163,14 @@
 
     lax.fori_loop(1, SPAN, step, 0)
 
-    keeps = [[kept_ref[g, b] for b in range(2)] for g in range(GROUPS)]
+    keeps = [[kept_s[g, b] for b in range(2)] for g in range(GROUPS)]
     for g in range(GROUPS):
         for b in range(2):
             c = g * 2 + b
             m = run(c)[:WIDTH, :] - eye * keeps[g][b]
             run(c)[:WIDTH, :] = m
             grp_ref[c] = m.astype(BF16)
+            kept_ref[c : c + 1, :] = jnp.full((1, WIDTH), 1.0, F32) * keeps[g][b]
     stride = 1
     while stride < GROUPS:
         for g1 in range(0, GROUPS, 2 * stride):
@@ -172,7 +187,7 @@
         pack_map(send_ref, b, run(b)[:WIDTH, :], run(b)[WIDTH : WIDTH + 1, :], keeps[0][b])
 
 
-def compose(place, noise, retain, control_weight, input_weight):
+def compose(noise, retain, control_weight, input_weight):
     steps = noise.shape[1]
     return pl.pallas_call(
         compose_kernel,
@@ -181,22 +196,23 @@
             pltpu.VMEM((2 * steps, WIDTH), F32),
             pltpu.VMEM((2, MAP_ROWS, WIDTH), BF16),
             pltpu.VMEM((2 * GROUPS, WIDTH, WIDTH), BF16),
-            jax.ShapeDtypeStruct((GROUPS, 2), F32),
+            pltpu.VMEM((2 * GROUPS, WIDTH), F32),
         ),
-        in_specs=[SMEM, VMEM, SMEM, VMEM, ANY, VMEM],
-        out_specs=(VMEM, VMEM, VMEM, VMEM, SMEM),
+        in_specs=[VMEM, SMEM, VMEM, ANY, VMEM],
+        out_specs=(VMEM, VMEM, VMEM, VMEM, VMEM),
         scratch_shapes=[
             pltpu.VMEM((128 * PITCH + 8, WIDTH), F32),
             pltpu.VMEM((2 * steps * PITCH + 8, WIDTH), F32),
+            pltpu.SMEM((GROUPS, 2), F32),
             pltpu.SemaphoreType.DMA((4,)),
         ],
         compiler_params=pltpu.CompilerParams(vmem_limit_bytes=44_500_000),
         name="compose",
-    )(place, noise, retain, retain, control_weight.reshape(-1, WIDTH, WIDTH), input_weight)
-
-
-def row_kernel(place_s, m0, m1, m2, m3, out_ref, held):
-    x = place_s[1]
+    )(noise, retain, retain, control_weight.reshape(-1, WIDTH, WIDTH), input_weight)
+
+
+def row_kernel(m0, m1, m2, m3, out_ref, held):
+    x = places()[1]
     for k, ref in enumerate((m0, m1, m2, m3)):
         held[lax.rem(x + 4 - k, 4)] = ref[...]
     for b in range(2):
@@ -214,25 +230,26 @@
         pack_map(out_ref, b, *parts[0])
 
 
-def row_map(place, maps):
+def row_map(maps):
     return pl.pallas_call(
         row_kernel,
         out_shape=jax.ShapeDtypeStruct((2, MAP_ROWS, WIDTH), BF16),
-        in_specs=[SMEM] + [VMEM] * 4,
+        in_specs=[VMEM] * 4,
         out_specs=VMEM,
         scratch_shapes=[pltpu.VMEM((4, 2, MAP_ROWS, WIDTH), BF16)],
         compiler_params=pltpu.CompilerParams(vmem_limit_bytes=8_000_000),
         name="row_map",
-    )(place, *maps)
-
-
-def replay_kernel(place_s, kept_s, init_ref, y1, y2, y3, x1, x2, x3, off_ref, grp_ref, gain_ref, q_ref,
+    )(*maps)
+
+
+def replay_kernel(kept_ref, init_ref, y1, y2, y3, x1, x2, x3, off_ref, grp_ref, gain_ref, q_ref,
                   states_ref, normed_ref):
     steps = SPAN * GROUPS
+    y, x = places()[:2]
     entry = []
     for b in range(2):
         h = init_ref[b : b + 1, :]
-        for place, refs in ((place_s[0], (y1, y2, y3)), (place_s[1], (x1, x2, x3))):
+        for place, refs in ((y, (y1, y2, y3)), (x, (x1, x2, x3))):
             for k in (3, 2, 1):
                 matrix, offset, kept = unpack_map(refs[k - 1], b)
                 h = jnp.where(k <= place, h * kept + row_times(h, matrix) + offset, h)
@@ -245,8 +262,12 @@
             h = starts[b]
             spread = jnp.broadcast_to(h, (WIDTH, WIDTH)).T
             last = off_ref[pl.ds(b * steps + g * SPAN + SPAN - 1, 1), :]
-            after.append(h * kept_s[g, b] + row_times(h, grp_ref[c]) + last)
-            rows = [jnp.sum(q_ref[s, c].astype(F32) * spread, axis=0, keepdims=True) for s in range(SPAN)]
+            parts = two_parts(h)
+            after.append(h * kept_ref[pl.ds(c, 1), :] + parts_times(parts, grp_ref[c]) + last)
+            rows = [jnp.sum(q_ref[s, c].astype(F32) * spread, axis=0, keepdims=True) for s in range(4)]
+            for s in range(4, SPAN, 2):
+                pair = parts_times(parts, jnp.concatenate([q_ref[s, c], q_ref[s + 1, c]], axis=1))
+                rows += [pair[:, :WIDTH], pair[:, WIDTH:]]
             base = pl.multiple_of(g * SPAN, SPAN)
             states = jnp.concatenate(rows, axis=0) + off_ref[pl.ds(b * steps + base, SPAN), :]
             states_ref[pl.ds(base, SPAN), b * WIDTH : (b + 1) * WIDTH] = states
@@ -255,10 +276,10 @@
             normed_ref[pl.ds(base, SPAN), b * WIDTH : (b + 1) * WIDTH] = normed.astype(BF16)
         return tuple(after)
 
-    lax.fori_loop(0, GROUPS, group, tuple(entry), unroll=2)
-
-
-def replay(place, kept, init, y_maps, x_maps, off, grp, gain, q):
+    lax.fori_loop(0, GROUPS, group, tuple(entry), unroll=8)
+
+
+def replay(kept, init, y_maps, x_maps, off, grp, gain, q):
     steps = SPAN * GROUPS
     return pl.pallas_call(
         replay_kernel,
@@ -266,15 +287,15 @@
             jax.ShapeDtypeStruct((steps, 2 * WIDTH), F32),
             jax.ShapeDtypeStruct((steps, 2 * WIDTH), BF16),
         ),
-        in_specs=[SMEM, SMEM] + [VMEM] * 11,
+        in_specs=[VMEM] * 12,
         out_specs=(VMEM, VMEM),
         compiler_params=pltpu.CompilerParams(vmem_limit_bytes=16_000_000),
         name="replay",
-    )(place, kept, init, *y_maps, *x_maps, off, grp, gain, pltpu.with_memory_space_constraint(q, pltpu.VMEM))
-
-
-def forward_kernel(place_s, m0, m1, m2, m3, theirs_ref, gate_ref, up_ref, down_ref, keep_ref, send_ref, hidden):
-    z, core = place_s[2], place_s[3]
+    )(kept, init, *y_maps, *x_maps, off, grp, gain, pltpu.with_memory_space_constraint(q, pltpu.VMEM))
+
+
+def forward_kernel(m0, m1, m2, m3, theirs_ref, gate_ref, up_ref, down_ref, keep_ref, send_ref, hidden):
+    z, core = places()[2:]
     wide = 2 * WIDTH
 
     def at(k, c):
@@ -299,19 +320,19 @@
             ref[k] = out.astype(BF16)
 
 
-def forward(place, mine, theirs, gate_weight, up_weight, down_weight):
+def forward(mine, theirs, gate_weight, up_weight, down_weight):
     steps = mine[0].shape[0]
     weights = [pltpu.with_memory_space_constraint(w, pltpu.VMEM) for w in (gate_weight, up_weight, down_weight)]
     half = jax.ShapeDtypeStruct((4, steps, 2 * WIDTH), BF16)
     return pl.pallas_call(
         forward_kernel,
         out_shape=(half, half),
-        in_specs=[SMEM] + [VMEM] * 8,
+        in_specs=[VMEM] * 8,
         out_specs=(VMEM, VMEM),
         scratch_shapes=[pltpu.VMEM((steps, gate_weight.shape[1]), BF16)],
         compiler_params=pltpu.CompilerParams(vmem_limit_bytes=16_000_000),
         name="forward",
-    )(place, *mine, theirs, *weights)
+    )(*mine, theirs, *weights)
 
 
 def x_back(v, k):
@@ -341,20 +362,16 @@
     up_weight,
     down_weight,
 ):
-    tm = lax.axis_index("tm")
-    block = lax.axis_index("block")
-    z, core = block // 2, block % 2
-    place = jnp.stack([tm // 4, tm % 4, z, core]).astype(jnp.int32)
-    q, off, own, grp, kept = compose(place, noise.T, retain.T, control_weight, input_weight)
+    q, off, own, grp, kept = compose(noise.T, retain.T, control_weight, input_weight)
     x_maps = [x_back(own, k) for k in (1, 2, 3)]
-    total = row_map(place, [own, *x_maps])
+    total = row_map([own, *x_maps])
     y_maps = [y_back(total, k) for k in (1, 2, 3)]
     states, normed = replay(
-        place, kept, initial_state.reshape(2, WIDTH), y_maps, x_maps, off, grp, norm_gain.reshape(2, WIDTH), q
+        kept, initial_state.reshape(2, WIDTH), y_maps, x_maps, off, grp, norm_gain.reshape(2, WIDTH), q
     )
     mine = [normed] + [z_back(normed, k) for k in (1, 2, 3)]
     theirs = other_core(jnp.stack(mine))
-    keep, sent = forward(place, mine, theirs, gate_weight, up_weight, down_weight)
+    keep, sent = forward(mine, theirs, gate_weight, up_weight, down_weight)
     chip = keep.astype(F32) + other_core(sent).astype(F32)
     low = chip.astype(BF16)
     mixed = chip[0]

time: 80 us -> 73.5 us (0.919)
  Pallas kernels: 32.6 us -> 27.4 us
    pallas_call x1, Pallas kernels: 7.19 us -> 3.67 us  [replay(): pl.pallas_call(replay_kernel, out_shape=(jax.ShapeDtypeStruct((steps, 2 *...]
where the time goes in v4:
time: 73.5 us; the launch traced here: 73.4 us
  Pallas kernels  27.4 us (37%)
  waiting for transfers between devices  26.6 us (36%)
  starting transfers between devices  18.2 us (25%)
  other arithmetic  0.95 us (1%)
    pallas_call x1, Pallas kernels, compose(): pl.pallas_call(compose_kernel, out_shape=(pltpu.VMEM((SPAN, 2 * GROUPS, W...  19.8 us
    ppermute x6, waiting for transfers between devices, z_back(): lax.ppermute(v, 'block', [(z * 2 + c, (z + k) % 4 * 2 + c) for z in range...  12.8 us
    ppermute x6, starting transfers between devices, z_back(): lax.ppermute(v, 'block', [(z * 2 + c, (z + k) % 4 * 2 + c) for z in range...  8.65 us
    ppermute x3, waiting for transfers between devices, x_back(): lax.ppermute(v, 'tm', [(y * 4 + x, y * 4 + (x + k) % 4) for y in range(4)...  5.12 us
    ppermute x3, waiting for transfers between devices, y_back(): lax.ppermute(v, 'tm', [(y * 4 + x, (y + k) % 4 * 4 + x) for y in range(4)...  5.04 us
    ppermute x3, starting transfers between devices, y_back(): lax.ppermute(v, 'tm', [(y * 4 + x, (y + k) % 4 * 4 + x) for y in range(4)...  4.69 us
    ppermute x3, starting transfers between devices, x_back(): lax.ppermute(v, 'tm', [(y * 4 + x, y * 4 + (x + k) % 4) for y in range(4)...  4.6 us
    ppermute x2, waiting for transfers between devices, other_core(): return lax.ppermute(v, 'block', [(s, s ^ 1) for s in range(8)])  3.69 us
  transfers between devices with their start and end apart: 14, of which 14 were waited for; matrix products, arithmetic and copies ran while one was open for 0% of the time, Pallas kernels for 0%

profile of v4, /device:TPU:0, one launch (start us, length us, event | category | flops | bytes accessed | tf_op | source)
XLA Modules:
  0.0 73.4 jit_solution(1721899480025061940)
XLA Ops:
  0.0 19.8 %compose.1 = (bf16[16,32,128,128]{3,2,1,0:T(8,128)(2,1)S(1)}, f32[512,128]{1,0:T(8,128)S(1)}, bf16[2,144,128]{2,1,0:T(8,128)(2,1)S(1)}, bf16[32,128,128]{2,1,0:T(8,128)(2,1)S(1)}, f32[32,128]{1,0:T(8,128)S(1)}) custom-call(f32[64,256]{1,0:T(8,128)} %bitcast.34, f32[2,256]{1,0:T(2,128)} %bitcast.35, f32[2,256]{1,0:T(2,128)} %bitcast.36, ...), custom_call_target="tpu_custom_call" | custom-call | tf_op jit(solution)/shard_map/compose/pallas_call | solution.py:192
  19.8 2.9 %collective-permute-start.2 = (bf16[2,144,128]{2,1,0:T(8,128)(2,1)S(1)}, bf16[2,144,128]{2,1,0:T(8,128)(2,1)S(1)}, u32[]{:S(2)}, u32[]{:S(2)}) collective-permute-start(bf16[2,144,128]{2,1,0:T(8,128)(2,1)S(1)} %get-tuple-element.15.m0), channel_id=1, source_target_pairs={{0,24},{8,0},{16,8},{24,16},{32,56},{40,32},{48,40},{56,48},{64,88... | collective-permute-start | bytes 221192 | tf_op jit(solution)/shard_map/ppermute | solution.py:339
  22.7 0.8 %collective-permute-start.1 = (bf16[2,144,128]{2,1,0:T(8,128)(2,1)S(1)}, bf16[2,144,128]{2,1,0:T(8,128)(2,1)S(1)}, u32[]{:S(2)}, u32[]{:S(2)}) collective-permute-start(bf16[2,144,128]{2,1,0:T(8,128)(2,1)S(1)} %get-tuple-element.15.m0), channel_id=1, source_target_pairs={{0,16},{8,24},{16,0},{24,8},{32,48},{40,56},{48,32},{56,40},{64,80... | collective-permute-start | bytes 221192 | tf_op jit(solution)/shard_map/ppermute | solution.py:339
  23.5 0.9 %collective-permute-start = (bf16[2,144,128]{2,1,0:T(8,128)(2,1)S(1)}, bf16[2,144,128]{2,1,0:T(8,128)(2,1)S(1)}, u32[]{:S(2)}, u32[]{:S(2)}) collective-permute-start(bf16[2,144,128]{2,1,0:T(8,128)(2,1)S(1)} %get-tuple-element.15.m0), channel_id=1, source_target_pairs={{0,8},{8,16},{16,24},{24,0},{32,40},{40,48},{48,56},{56,32},{64,72... | collective-permute-start | bytes 221192 | tf_op jit(solution)/shard_map/ppermute | solution.py:339
  24.4 0.7 collective-permute-done.2.m3.x3
  25.1 3.7 %collective-permute-done.1.m2.x2 = bf16[2,144,128]{2,1,0:T(8,128)(2,1)S(1)} collective-permute-done((bf16[2,144,128]{2,1,0:T(8,128)(2,1)S(1)}, bf16[2,144,128]{2,1,0:T(8,128)(2,1)S(1)}, u32[]{:S(2)}, u32[]{:S(2)}) %collective-permute-start.1) | collective-permute-done | bytes 73760 | tf_op jit(solution)/shard_map/ppermute | solution.py:339
  28.8 0.7 %collective-permute-done.m1.x1 = bf16[2,144,128]{2,1,0:T(8,128)(2,1)S(1)} collective-permute-done((bf16[2,144,128]{2,1,0:T(8,128)(2,1)S(1)}, bf16[2,144,128]{2,1,0:T(8,128)(2,1)S(1)}, u32[]{:S(2)}, u32[]{:S(2)}) %collective-permute-start) | collective-permute-done | bytes 73760 | tf_op jit(solution)/shard_map/ppermute | solution.py:339
  29.5 0.5 row_map.1
  30.0 3.1 %collective-permute-start.5 = (bf16[2,144,128]{2,1,0:T(8,128)(2,1)S(1)}, bf16[2,144,128]{2,1,0:T(8,128)(2,1)S(1)}, u32[]{:S(2)}, u32[]{:S(2)}) collective-permute-start(bf16[2,144,128]{2,1,0:T(8,128)(2,1)S(1)} %row_map.1), channel_id=1, source_target_pairs={{0,96},{8,104},{16,112},{24,120},{32,0},{40,8},{48,16},{56,24},{64... | collective-permute-start | bytes 221192 | tf_op jit(solution)/shard_map/ppermute | solution.py:343
  33.1 0.6 collective-permute-start.4
  33.7 1.0 %collective-permute-start.3 = (bf16[2,144,128]{2,1,0:T(8,128)(2,1)S(1)}, bf16[2,144,128]{2,1,0:T(8,128)(2,1)S(1)}, u32[]{:S(2)}, u32[]{:S(2)}) collective-permute-start(bf16[2,144,128]{2,1,0:T(8,128)(2,1)S(1)} %row_map.1), channel_id=1, source_target_pairs={{0,32},{8,40},{16,48},{24,56},{32,64},{40,72},{48,80},{56,88},{64,... | collective-permute-start | bytes 221192 | tf_op jit(solution)/shard_map/ppermute | solution.py:343
  34.7 0.5 collective-permute-done.5.y3
  35.2 3.8 %collective-permute-done.4.y2 = bf16[2,144,128]{2,1,0:T(8,128)(2,1)S(1)} collective-permute-done((bf16[2,144,128]{2,1,0:T(8,128)(2,1)S(1)}, bf16[2,144,128]{2,1,0:T(8,128)(2,1)S(1)}, u32[]{:S(2)}, u32[]{:S(2)}) %collective-permute-start.4) | collective-permute-done | bytes 73760 | tf_op jit(solution)/shard_map/ppermute | solution.py:343
  39.0 0.7 %collective-permute-done.3.y1 = bf16[2,144,128]{2,1,0:T(8,128)(2,1)S(1)} collective-permute-done((bf16[2,144,128]{2,1,0:T(8,128)(2,1)S(1)}, bf16[2,144,128]{2,1,0:T(8,128)(2,1)S(1)}, u32[]{:S(2)}, u32[]{:S(2)}) %collective-permute-start.3) | collective-permute-done | bytes 73760 | tf_op jit(solution)/shard_map/ppermute | solution.py:343
  39.8 3.7 %replay.1 = (f32[256,256]{1,0:T(8,128)S(1)}, bf16[256,256]{1,0:T(8,128)(2,1)S(1)}) custom-call(f32[32,128]{1,0:T(8,128)S(1)} %get-tuple-element.14.kept_ref, f32[2,128]{1,0:T(2,128)S(1)} %bitcast.31, bf16[2,144,128]{2,1,0:T(8,128)(2,1)S(1)} %collective-permute-done.3.y1, bf16[2,144,128]{2,1,0:T(8,128)(2,1)S(1)} %collective-permute-done.4.y2, ...), custom_call_target="tpu_custom_call" | custom-call | tf_op jit(solution)/shard_map/replay/pallas_call | solution.py:284
  43.5 4.1 %collective-permute-start.8 = (bf16[256,256]{1,0:T(8,128)(2,1)S(1)}, bf16[256,256]{1,0:T(8,128)(2,1)S(1)}, u32[]{:S(2)}, u32[]{:S(2)}) collective-permute-start(bf16[256,256]{1,0:T(8,128)(2,1)S(1)} %get-tuple-element.20.m0), channel_id=1, source_target_pairs={{0,6},{1,7},{2,0},{3,1},{4,2},{5,3},{6,4},{7,5},{8,14},{9,15},{10,... | collective-permute-start | bytes 393224 | tf_op jit(solution)/shard_map/ppermute | solution.py:347
  47.5 1.3 %collective-permute-start.6 = (bf16[256,256]{1,0:T(8,128)(2,1)S(1)}, bf16[256,256]{1,0:T(8,128)(2,1)S(1)}, u32[]{:S(2)}, u32[]{:S(2)}) collective-permute-start(bf16[256,256]{1,0:T(8,128)(2,1)S(1)} %get-tuple-element.20.m0), channel_id=1, source_target_pairs={{0,2},{1,3},{2,4},{3,5},{4,6},{5,7},{6,0},{7,1},{8,10},{9,11},{10,... | collective-permute-start | bytes 393224 | tf_op jit(solution)/shard_map/ppermute | solution.py:347
  48.8 2.7 %collective-permute-done.8.m3 = bf16[256,256]{1,0:T(8,128)(2,1)S(1)} collective-permute-done((bf16[256,256]{1,0:T(8,128)(2,1)S(1)}, bf16[256,256]{1,0:T(8,128)(2,1)S(1)}, u32[]{:S(2)}, u32[]{:S(2)}) %collective-permute-start.8) | collective-permute-done | bytes 131104 | tf_op jit(solution)/shard_map/ppermute | solution.py:347
  51.5 2.7 %collective-permute-done.7.m2 = bf16[256,256]{1,0:T(8,128)(2,1)S(1)} collective-permute-done((bf16[256,256]{1,0:T(8,128)(2,1)S(1)}, bf16[256,256]{1,0:T(8,128)(2,1)S(1)}, u32[]{:S(2)}, u32[]{:S(2)}) %collective-permute-start.7) | collective-permute-done | bytes 131104 | tf_op jit(solution)/shard_map/ppermute | solution.py:347
  54.1 1.0 %collective-permute-done.6.m1 = bf16[256,256]{1,0:T(8,128)(2,1)S(1)} collective-permute-done((bf16[256,256]{1,0:T(8,128)(2,1)S(1)}, bf16[256,256]{1,0:T(8,128)(2,1)S(1)}, u32[]{:S(2)}, u32[]{:S(2)}) %collective-permute-start.6) | collective-permute-done | bytes 131104 | tf_op jit(solution)/shard_map/ppermute | solution.py:347
  55.2 0.1 collective-permute-start.9
  55.3 1.9 %collective-permute-done.9.theirs_ref = bf16[4,256,256]{2,1,0:T(8,128)(2,1)S(1)} collective-permute-done((bf16[4,256,256]{2,1,0:T(8,128)(2,1)S(1)}, bf16[4,256,256]{2,1,0:T(8,128)(2,1)S(1)}, u32[]{:S(2)}, u32[]{:S(2)}) %collective-permute-start.9) | collective-permute-done | bytes 524320 | tf_op jit(solution)/shard_map/ppermute | solution.py:351
  57.2 3.5 %forward.1 = (bf16[4,256,256]{2,1,0:T(8,128)(2,1)S(1)}, bf16[4,256,256]{2,1,0:T(8,128)(2,1)S(1)}) custom-call(bf16[256,256]{1,0:T(8,128)(2,1)S(1)} %get-tuple-element.20.m0, bf16[256,256]{1,0:T(8,128)(2,1)S(1)} %collective-permute-done.6.m1, bf16[256,256]{1,0:T(8,128)(2,1)S(1)} %collective-permute-done.7.m2, bf16[256,256]{1,0:T(8,128)(2,1)S(1)} %collective-permute-done.8.m3, ...), custom_call_target="tpu_custom_call" | custom-call | tf_op jit(solution)/shard_map/forward/pallas_call | solution.py:327
  60.7 0.2 collective-permute-start.10
  60.9 1.8 %collective-permute-done.10 = bf16[4,256,256]{2,1,0:T(8,128)(2,1)S(1)} collective-permute-done((bf16[4,256,256]{2,1,0:T(8,128)(2,1)S(1)}, bf16[4,256,256]{2,1,0:T(8,128)(2,1)S(1)}, u32[]{:S(2)}, u32[]{:S(2)}) %collective-permute-start.10) | collective-permute-done | bytes 524320 | tf_op jit(solution)/shard_map/ppermute | solution.py:351
  62.7 0.1 fusion.5
  62.9 0.1 collective-permute-start.11
  62.9 3.2 %collective-permute-start.13 = (bf16[256,256]{1,0:T(8,128)(2,1)S(1)}, bf16[256,256]{1,0:T(8,128)(2,1)S(1)}, u32[]{:S(2)}, u32[]{:S(2)}) collective-permute-start(bf16[256,256]{1,0:T(8,128)(2,1)S(1)} %get-tuple-element.26), channel_id=1, source_target_pairs={{0,6},{1,7},{2,0},{3,1},{4,2},{5,3},{6,4},{7,5},{8,14},{9,15},{10,... | collective-permute-start | bytes 393224 | tf_op jit(solution)/shard_map/ppermute | solution.py:347
  66.2 3.5 %collective-permute-done.11 = bf16[256,256]{1,0:T(8,128)(2,1)S(1)} collective-permute-done((bf16[256,256]{1,0:T(8,128)(2,1)S(1)}, bf16[256,256]{1,0:T(8,128)(2,1)S(1)}, u32[]{:S(2)}, u32[]{:S(2)}) %collective-permute-start.11) | collective-permute-done | bytes 131104 | tf_op jit(solution)/shard_map/ppermute | solution.py:347
  69.7 2.1 %collective-permute-done.13 = bf16[256,256]{1,0:T(8,128)(2,1)S(1)} collective-permute-done((bf16[256,256]{1,0:T(8,128)(2,1)S(1)}, bf16[256,256]{1,0:T(8,128)(2,1)S(1)}, u32[]{:S(2)}, u32[]{:S(2)}) %collective-permute-start.13) | collective-permute-done | bytes 131104 | tf_op jit(solution)/shard_map/ppermute | solution.py:347
  71.8 0.9 %collective-permute-done.12 = bf16[256,256]{1,0:T(8,128)(2,1)S(1)} collective-permute-done((bf16[256,256]{1,0:T(8,128)(2,1)S(1)}, bf16[256,256]{1,0:T(8,128)(2,1)S(1)}, u32[]{:S(2)}, u32[]{:S(2)}) %collective-permute-start.12) | collective-permute-done | bytes 131104 | tf_op jit(solution)/shard_map/ppermute | solution.py:347
  72.6 0.7 %fusion.4 = bf16[256,256]{1,0:T(8,128)(2,1)} fusion(f32[256,256]{1,0:T(8,128)S(1)} %get-tuple-element.19, f32[4,256,256]{2,1,0:T(8,128)S(1)} %get-tuple-element.24, bf16[256,256]{1,0:T(8,128)(2,1)S(1)} %collective-permute-done.13, bf16[256,256]{1,0:T(8,128)(2,1)S(1)} %collective-permute-done.12, bf16[256,256]{1,0:T(8,128)(2,1)S(1)} %collective-permute-done.11), kind=kLoop, calls=%fused_computation.7 | loop fusion | flops 524288 | bytes 1048576 | tf_op jit(solution)/shard_map/convert_element_type | solution.py:380
  (14 shorter events, 0.1 us)
Async XLA Ops:
  0.0 39.8 %copy-start.4 = (f32[256]{0:T(256)S(1)}, f32[256]{0:T(256)}, u32[]{:S(2)}) copy-start(f32[256]{0:T(256)} %param.14) | copy-start | bytes 3076
  0.0 39.8 %copy-start.3 = (f32[256]{0:T(256)S(1)}, f32[256]{0:T(256)}, u32[]{:S(2)}) copy-start(f32[256]{0:T(256)} %param.13) | copy-start | bytes 3076
  19.8 5.3 %collective-permute-start.2 = (bf16[2,144,128]{2,1,0:T(8,128)(2,1)S(1)}, bf16[2,144,128]{2,1,0:T(8,128)(2,1)S(1)}, u32[]{:S(2)}, u32[]{:S(2)}) collective-permute-start(bf16[2,144,128]{2,1,0:T(8,128)(2,1)S(1)} %get-tuple-element.15.m0), channel_id=1, source_target_pairs={{0,24},{8,0},{16,8},{24,16},{32,56},{40,32},{48,40},{56,48},{64,88... | collective-permute-start | bytes 221192 | tf_op jit(solution)/shard_map/ppermute | solution.py:339
  22.7 6.1 %collective-permute-start.1 = (bf16[2,144,128]{2,1,0:T(8,128)(2,1)S(1)}, bf16[2,144,128]{2,1,0:T(8,128)(2,1)S(1)}, u32[]{:S(2)}, u32[]{:S(2)}) collective-permute-start(bf16[2,144,128]{2,1,0:T(8,128)(2,1)S(1)} %get-tuple-element.15.m0), channel_id=1, source_target_pairs={{0,16},{8,24},{16,0},{24,8},{32,48},{40,56},{48,32},{56,40},{64,80... | collective-permute-start | bytes 221192 | tf_op jit(solution)/shard_map/ppermute | solution.py:339
  23.5 6.0 %collective-permute-start = (bf16[2,144,128]{2,1,0:T(8,128)(2,1)S(1)}, bf16[2,144,128]{2,1,0:T(8,128)(2,1)S(1)}, u32[]{:S(2)}, u32[]{:S(2)}) collective-permute-start(bf16[2,144,128]{2,1,0:T(8,128)(2,1)S(1)} %get-tuple-element.15.m0), channel_id=1, source_target_pairs={{0,8},{8,16},{16,24},{24,0},{32,40},{40,48},{48,56},{56,32},{64,72... | collective-permute-start | bytes 221192 | tf_op jit(solution)/shard_map/ppermute | solution.py:339
  30.0 5.2 %collective-permute-start.5 = (bf16[2,144,128]{2,1,0:T(8,128)(2,1)S(1)}, bf16[2,144,128]{2,1,0:T(8,128)(2,1)S(1)}, u32[]{:S(2)}, u32[]{:S(2)}) collective-permute-start(bf16[2,144,128]{2,1,0:T(8,128)(2,1)S(1)} %row_map.1), channel_id=1, source_target_pairs={{0,96},{8,104},{16,112},{24,120},{32,0},{40,8},{48,16},{56,24},{64... | collective-permute-start | bytes 221192 | tf_op jit(solution)/shard_map/ppermute | solution.py:343
  33.1 5.9 %collective-permute-start.4 = (bf16[2,144,128]{2,1,0:T(8,128)(2,1)S(1)}, bf16[2,144,128]{2,1,0:T(8,128)(2,1)S(1)}, u32[]{:S(2)}, u32[]{:S(2)}) collective-permute-start(bf16[2,144,128]{2,1,0:T(8,128)(2,1)S(1)} %row_map.1), channel_id=1, source_target_pairs={{0,64},{8,72},{16,80},{24,88},{32,96},{40,104},{48,112},{56,120},{... | collective-permute-start | bytes 221192 | tf_op jit(solution)/shard_map/ppermute | solution.py:343
  33.7 6.0 %collective-permute-start.3 = (bf16[2,144,128]{2,1,0:T(8,128)(2,1)S(1)}, bf16[2,144,128]{2,1,0:T(8,128)(2,1)S(1)}, u32[]{:S(2)}, u32[]{:S(2)}) collective-permute-start(bf16[2,144,128]{2,1,0:T(8,128)(2,1)S(1)} %row_map.1), channel_id=1, source_target_pairs={{0,32},{8,40},{16,48},{24,56},{32,64},{40,72},{48,80},{56,88},{64,... | collective-permute-start | bytes 221192 | tf_op jit(solution)/shard_map/ppermute | solution.py:343
  39.8 17.4 %copy-start = (bf16[2048,1024]{1,0:T(8,128)(2,1)S(1)}, bf16[2048,1024]{1,0:T(8,128)(2,1)}, u32[]{:S(2)}) copy-start(bf16[2048,1024]{1,0:T(8,128)(2,1)} %gate_ref.1) | copy-start | bytes 12582916
  39.8 17.4 %copy-start.1 = (bf16[2048,1024]{1,0:T(8,128)(2,1)S(1)}, bf16[2048,1024]{1,0:T(8,128)(2,1)}, u32[]{:S(2)}) copy-start(bf16[2048,1024]{1,0:T(8,128)(2,1)} %up_ref.1) | copy-start | bytes 12582916
  39.8 17.4 %copy-start.2 = (bf16[1024,2048]{1,0:T(8,128)(2,1)S(1)}, bf16[1024,2048]{1,0:T(8,128)(2,1)}, u32[]{:S(2)}) copy-start(bf16[1024,2048]{1,0:T(8,128)(2,1)} %down_ref.1) | copy-start | bytes 12582916
  43.5 8.0 %collective-permute-start.8 = (bf16[256,256]{1,0:T(8,128)(2,1)S(1)}, bf16[256,256]{1,0:T(8,128)(2,1)S(1)}, u32[]{:S(2)}, u32[]{:S(2)}) collective-permute-start(bf16[256,256]{1,0:T(8,128)(2,1)S(1)} %get-tuple-element.20.m0), channel_id=1, source_target_pairs={{0,6},{1,7},{2,0},{3,1},{4,2},{5,3},{6,4},{7,5},{8,14},{9,15},{10,... | collective-permute-start | bytes 393224 | tf_op jit(solution)/shard_map/ppermute | solution.py:347
  47.5 6.6 %collective-permute-start.7 = (bf16[256,256]{1,0:T(8,128)(2,1)S(1)}, bf16[256,256]{1,0:T(8,128)(2,1)S(1)}, u32[]{:S(2)}, u32[]{:S(2)}) collective-permute-start(bf16[256,256]{1,0:T(8,128)(2,1)S(1)} %get-tuple-element.20.m0), channel_id=1, source_target_pairs={{0,4},{1,5},{2,6},{3,7},{4,0},{5,1},{6,2},{7,3},{8,12},{9,13},{10,... | collective-permute-start | bytes 393224 | tf_op jit(solution)/shard_map/ppermute | solution.py:347
  47.5 7.6 %collective-permute-start.6 = (bf16[256,256]{1,0:T(8,128)(2,1)S(1)}, bf16[256,256]{1,0:T(8,128)(2,1)S(1)}, u32[]{:S(2)}, u32[]{:S(2)}) collective-permute-start(bf16[256,256]{1,0:T(8,128)(2,1)S(1)} %get-tuple-element.20.m0), channel_id=1, source_target_pairs={{0,2},{1,3},{2,4},{3,5},{4,6},{5,7},{6,0},{7,1},{8,10},{9,11},{10,... | collective-permute-start | bytes 393224 | tf_op jit(solution)/shard_map/ppermute | solution.py:347
  55.2 2.0 %collective-permute-start.9 = (bf16[4,256,256]{2,1,0:T(8,128)(2,1)S(1)}, bf16[4,256,256]{2,1,0:T(8,128)(2,1)S(1)}, u32[]{:S(2)}, u32[]{:S(2)}) collective-permute-start(bf16[4,256,256]{2,1,0:T(8,128)(2,1)S(1)} %pad_maximum_fusion), channel_id=1, source_target_pairs={{0,1},{1,0},{2,3},{3,2},{4,5},{5,4},{6,7},{7,6},{8,9},{9,8},{10,11... | collective-permute-start | bytes 1572872 | tf_op jit(solution)/shard_map/ppermute | solution.py:351
  60.7 2.0 %collective-permute-start.10 = (bf16[4,256,256]{2,1,0:T(8,128)(2,1)S(1)}, bf16[4,256,256]{2,1,0:T(8,128)(2,1)S(1)}, u32[]{:S(2)}, u32[]{:S(2)}) collective-permute-start(bf16[4,256,256]{2,1,0:T(8,128)(2,1)S(1)} %get-tuple-element.22), channel_id=1, source_target_pairs={{0,1},{1,0},{2,3},{3,2},{4,5},{5,4},{6,7},{7,6},{8,9},{9,8},{10,11... | collective-permute-start | bytes 1572872 | tf_op jit(solution)/shard_map/ppermute | solution.py:351
  62.9 6.8 %collective-permute-start.11 = (bf16[256,256]{1,0:T(8,128)(2,1)S(1)}, bf16[256,256]{1,0:T(8,128)(2,1)S(1)}, u32[]{:S(2)}, u32[]{:S(2)}) collective-permute-start(bf16[256,256]{1,0:T(8,128)(2,1)S(1)} %get-tuple-element.25), channel_id=1, source_target_pairs={{0,2},{1,3},{2,4},{3,5},{4,6},{5,7},{6,0},{7,1},{8,10},{9,11},{10,... | collective-permute-start | bytes 393224 | tf_op jit(solution)/shard_map/ppermute | solution.py:347
  62.9 8.8 %collective-permute-start.13 = (bf16[256,256]{1,0:T(8,128)(2,1)S(1)}, bf16[256,256]{1,0:T(8,128)(2,1)S(1)}, u32[]{:S(2)}, u32[]{:S(2)}) collective-permute-start(bf16[256,256]{1,0:T(8,128)(2,1)S(1)} %get-tuple-element.26), channel_id=1, source_target_pairs={{0,6},{1,7},{2,0},{3,1},{4,2},{5,3},{6,4},{7,5},{8,14},{9,15},{10,... | collective-permute-start | bytes 393224 | tf_op jit(solution)/shard_map/ppermute | solution.py:347
  66.2 6.5 %collective-permute-start.12 = (bf16[256,256]{1,0:T(8,128)(2,1)S(1)}, bf16[256,256]{1,0:T(8,128)(2,1)S(1)}, u32[]{:S(2)}, u32[]{:S(2)}) collective-permute-start(bf16[256,256]{1,0:T(8,128)(2,1)S(1)} %get-tuple-element.27), channel_id=1, source_target_pairs={{0,4},{1,5},{2,6},{3,7},{4,0},{5,1},{6,2},{7,3},{8,12},{9,13},{10,... | collective-permute-start | bytes 393224 | tf_op jit(solution)/shard_map/ppermute | solution.py:347

commit v5 on v4

--- a/solution.py
+++ b/solution.py
@@ -211,7 +211,7 @@
     )(noise, retain, retain, control_weight.reshape(-1, WIDTH, WIDTH), input_weight)
 
 
-def row_kernel(m0, m1, m2, m3, out_ref, held):
+def row_kernel(m0, m1, m3, m2, out_ref, held):
     x = places()[1]
     for k, ref in enumerate((m0, m1, m2, m3)):
         held[lax.rem(x + 4 - k, 4)] = ref[...]
@@ -242,7 +242,7 @@
     )(*maps)
 
 
-def replay_kernel(kept_ref, init_ref, y1, y2, y3, x1, x2, x3, off_ref, grp_ref, gain_ref, q_ref,
+def replay_kernel(kept_ref, init_ref, y1, y3, y2, x1, x3, x2, off_ref, grp_ref, gain_ref, q_ref,
                   states_ref, normed_ref):
     steps = SPAN * GROUPS
     y, x = places()[:2]
@@ -294,7 +294,7 @@
     )(kept, init, *y_maps, *x_maps, off, grp, gain, pltpu.with_memory_space_constraint(q, pltpu.VMEM))
 
 
-def forward_kernel(m0, m1, m2, m3, theirs_ref, gate_ref, up_ref, down_ref, keep_ref, send_ref, hidden):
+def forward_kernel(m0, m1, m3, m2, theirs_ref, gate_ref, up_ref, down_ref, keep_ref, send_ref, hidden):
     z, core = places()[2:]
     wide = 2 * WIDTH
 
@@ -302,7 +302,7 @@
         return pl.multiple_of((lax.rem(z + k, 4) * 2 + c) * wide, wide)
 
     parts = [(m0, 0, 0), (m1, 3, 0), (m2, 2, 0), (m3, 1, 0)]
-    parts += [(theirs_ref.at[k], (4 - k) % 4, 1) for k in range(4)]
+    parts += [(theirs_ref.at[i], (4 - k) % 4, 1) for i, k in enumerate((0, 1, 3, 2))]
     for n in range(0, gate_ref.shape[1], wide):
         gate = up = None
         for ref, k, other in parts:
@@ -340,11 +340,15 @@
 
 
 def y_back(v, k):
-    return lax.ppermute(v, "tm", [(y * 4 + x, (y + k) % 4 * 4 + x) for y in range(4) for x in range(4)])
+    return lax.ppermute(v, "tm", [(y * 4 + x, (y + k) * 4 + x) for y in range(4 - k) for x in range(4)])
 
 
 def z_back(v, k):
     return lax.ppermute(v, "block", [(z * 2 + c, (z + k) % 4 * 2 + c) for z in range(4) for c in range(2)])
+
+
+def three(back, v):
+    return [back(v, k) for k in (1, 3, 2)]
 
 
 def other_core(v):
@@ -363,19 +367,19 @@
     down_weight,
 ):
     q, off, own, grp, kept = compose(noise.T, retain.T, control_weight, input_weight)
-    x_maps = [x_back(own, k) for k in (1, 2, 3)]
+    x_maps = three(x_back, own)
     total = row_map([own, *x_maps])
-    y_maps = [y_back(total, k) for k in (1, 2, 3)]
+    y_maps = three(y_back, total)
     states, normed = replay(
         kept, initial_state.reshape(2, WIDTH), y_maps, x_maps, off, grp, norm_gain.reshape(2, WIDTH), q
     )
-    mine = [normed] + [z_back(normed, k) for k in (1, 2, 3)]
+    mine = [normed] + three(z_back, normed)
     theirs = other_core(jnp.stack(mine))
     keep, sent = forward(mine, theirs, gate_weight, up_weight, down_weight)
     chip = keep.astype(F32) + other_core(sent).astype(F32)
     low = chip.astype(BF16)
     mixed = chip[0]
-    for k in (1, 2, 3):
+    for k in (2, 1, 3):
         mixed = mixed + z_back(low[k], k).astype(F32)
     return (states + mixed).astype(BF16)
 

time: 73.5 us -> 74.4 us (1.012); the launches traced: 73.4 us -> 73.5 us
  starting transfers between devices: 18.2 us -> 23.1 us
  waiting for transfers between devices: 26.6 us -> 21.8 us
    ppermute x3, starting transfers between devices: 4.69 us -> 8.35 us  [y_back(): lax.ppermute(v, 'tm', [(y * 4 + x, (y + k) * 4 + x) for y in range(4 - k)...]
    ppermute x3, waiting for transfers between devices: 5.04 us -> 1.95 us  [y_back(): lax.ppermute(v, 'tm', [(y * 4 + x, (y + k) * 4 + x) for y in range(4 - k)...]
    ppermute x6, waiting for transfers between devices: 12.8 us -> 11.5 us  [z_back(): lax.ppermute(v, 'block', [(z * 2 + c, (z + k) % 4 * 2 + c) for z in range...]
  transfers between devices with their start and end apart: 14 -> 14, of which waited for: 14 -> 12; matrix products, arithmetic and copies ran while one was open for 0% -> 0% of each run, Pallas kernels for 0% -> 0%
where the time goes in v5:
time: 74.4 us; the launch traced here: 73.5 us
  Pallas kernels  27.4 us (37%)
  starting transfers between devices  23.1 us (31%)
  waiting for transfers between devices  21.8 us (29%)
  other arithmetic  0.95 us (1%)
    pallas_call x1, Pallas kernels, compose(): pl.pallas_call(compose_kernel, out_shape=(pltpu.VMEM((SPAN, 2 * GROUPS, W...  19.8 us
    ppermute x6, waiting for transfers between devices, z_back(): lax.ppermute(v, 'block', [(z * 2 + c, (z + k) % 4 * 2 + c) for z in range...  11.5 us
    ppermute x6, starting transfers between devices, z_back(): lax.ppermute(v, 'block', [(z * 2 + c, (z + k) % 4 * 2 + c) for z in range...  9.24 us
    ppermute x3, starting transfers between devices, y_back(): lax.ppermute(v, 'tm', [(y * 4 + x, (y + k) * 4 + x) for y in range(4 - k)...  8.35 us
    ppermute x3, starting transfers between devices, x_back(): lax.ppermute(v, 'tm', [(y * 4 + x, y * 4 + (x + k) % 4) for y in range(4)...  5.21 us
    ppermute x3, waiting for transfers between devices, x_back(): lax.ppermute(v, 'tm', [(y * 4 + x, y * 4 + (x + k) % 4) for y in range(4)...  4.68 us
    ppermute x2, waiting for transfers between devices, other_core(): return lax.ppermute(v, 'block', [(s, s ^ 1) for s in range(8)])  3.68 us
    pallas_call x1, Pallas kernels, replay(): pl.pallas_call(replay_kernel, out_shape=(jax.ShapeDtypeStruct((steps, 2 *...  3.67 us
  transfers between devices with their start and end apart: 14, of which 12 were waited for; matrix products, arithmetic and copies ran while one was open for 0% of the time, Pallas kernels for 0%

profile of v5, /device:TPU:0, one launch (start us, length us, event | category | flops | bytes accessed | tf_op | source)
XLA Modules:
  0.0 73.5 jit_solution(2692064418280252526)
XLA Ops:
  0.0 19.8 %compose.1 = (bf16[16,32,128,128]{3,2,1,0:T(8,128)(2,1)S(1)}, f32[512,128]{1,0:T(8,128)S(1)}, bf16[2,144,128]{2,1,0:T(8,128)(2,1)S(1)}, bf16[32,128,128]{2,1,0:T(8,128)(2,1)S(1)}, f32[32,128]{1,0:T(8,128)S(1)}) custom-call(f32[64,256]{1,0:T(8,128)} %bitcast.34, f32[2,256]{1,0:T(2,128)} %bitcast.35, f32[2,256]{1,0:T(2,128)} %bitcast.36, ...), custom_call_target="tpu_custom_call" | custom-call | tf_op jit(solution)/shard_map/compose/pallas_call | solution.py:192
  19.8 3.2 %collective-permute-start.2 = (bf16[2,144,128]{2,1,0:T(8,128)(2,1)S(1)}, bf16[2,144,128]{2,1,0:T(8,128)(2,1)S(1)}, u32[]{:S(2)}, u32[]{:S(2)}) collective-permute-start(bf16[2,144,128]{2,1,0:T(8,128)(2,1)S(1)} %get-tuple-element.15.m0), channel_id=1, source_target_pairs={{0,16},{8,24},{16,0},{24,8},{32,48},{40,56},{48,32},{56,40},{64,80... | collective-permute-start | bytes 221192 | tf_op jit(solution)/shard_map/ppermute | solution.py:339
  23.0 1.1 %collective-permute-start.1 = (bf16[2,144,128]{2,1,0:T(8,128)(2,1)S(1)}, bf16[2,144,128]{2,1,0:T(8,128)(2,1)S(1)}, u32[]{:S(2)}, u32[]{:S(2)}) collective-permute-start(bf16[2,144,128]{2,1,0:T(8,128)(2,1)S(1)} %get-tuple-element.15.m0), channel_id=1, source_target_pairs={{0,24},{8,0},{16,8},{24,16},{32,56},{40,32},{48,40},{56,48},{64,88... | collective-permute-start | bytes 221192 | tf_op jit(solution)/shard_map/ppermute | solution.py:339
  24.1 0.9 %collective-permute-start = (bf16[2,144,128]{2,1,0:T(8,128)(2,1)S(1)}, bf16[2,144,128]{2,1,0:T(8,128)(2,1)S(1)}, u32[]{:S(2)}, u32[]{:S(2)}) collective-permute-start(bf16[2,144,128]{2,1,0:T(8,128)(2,1)S(1)} %get-tuple-element.15.m0), channel_id=1, source_target_pairs={{0,8},{8,16},{16,24},{24,0},{32,40},{40,48},{48,56},{56,32},{64,72... | collective-permute-start | bytes 221192 | tf_op jit(solution)/shard_map/ppermute | solution.py:339
  25.0 0.7 collective-permute-done.2.m2.x2
  25.7 1.7 %collective-permute-done.1.m3.x3 = bf16[2,144,128]{2,1,0:T(8,128)(2,1)S(1)} collective-permute-done((bf16[2,144,128]{2,1,0:T(8,128)(2,1)S(1)}, bf16[2,144,128]{2,1,0:T(8,128)(2,1)S(1)}, u32[]{:S(2)}, u32[]{:S(2)}) %collective-permute-start.1) | collective-permute-done | bytes 73760 | tf_op jit(solution)/shard_map/ppermute | solution.py:339
  27.5 2.2 %collective-permute-done.m1.x1 = bf16[2,144,128]{2,1,0:T(8,128)(2,1)S(1)} collective-permute-done((bf16[2,144,128]{2,1,0:T(8,128)(2,1)S(1)}, bf16[2,144,128]{2,1,0:T(8,128)(2,1)S(1)}, u32[]{:S(2)}, u32[]{:S(2)}) %collective-permute-start) | collective-permute-done | bytes 73760 | tf_op jit(solution)/shard_map/ppermute | solution.py:339
  29.7 0.5 row_map.1
  30.2 5.1 %collective-permute-start.5 = (bf16[2,144,128]{2,1,0:T(8,128)(2,1)S(1)}, bf16[2,144,128]{2,1,0:T(8,128)(2,1)S(1)}, u32[]{:S(2)}, u32[]{:S(2)}) collective-permute-start(bf16[2,144,128]{2,1,0:T(8,128)(2,1)S(1)} %row_map.1), channel_id=1, source_target_pairs={{0,64},{8,72},{16,80},{24,88},{32,96},{40,104},{48,112},{56,120},{... | collective-permute-start | bytes 221192 | tf_op jit(solution)/shard_map/ppermute | solution.py:343
  35.3 1.3 %collective-permute-start.4 = (bf16[2,144,128]{2,1,0:T(8,128)(2,1)S(1)}, bf16[2,144,128]{2,1,0:T(8,128)(2,1)S(1)}, u32[]{:S(2)}, u32[]{:S(2)}) collective-permute-start(bf16[2,144,128]{2,1,0:T(8,128)(2,1)S(1)} %row_map.1), channel_id=1, source_target_pairs={{0,96},{8,104},{16,112},{24,120},{1,97},{9,105},{17,113},{25,121},... | collective-permute-start | bytes 221192 | tf_op jit(solution)/shard_map/ppermute | solution.py:343
  36.6 2.0 %collective-permute-start.3 = (bf16[2,144,128]{2,1,0:T(8,128)(2,1)S(1)}, bf16[2,144,128]{2,1,0:T(8,128)(2,1)S(1)}, u32[]{:S(2)}, u32[]{:S(2)}) collective-permute-start(bf16[2,144,128]{2,1,0:T(8,128)(2,1)S(1)} %row_map.1), channel_id=1, source_target_pairs={{0,32},{8,40},{16,48},{24,56},{32,64},{40,72},{48,80},{56,88},{64,... | collective-permute-start | bytes 221192 | tf_op jit(solution)/shard_map/ppermute | solution.py:343
  38.6 1.9 %collective-permute-done.3.y1 = bf16[2,144,128]{2,1,0:T(8,128)(2,1)S(1)} collective-permute-done((bf16[2,144,128]{2,1,0:T(8,128)(2,1)S(1)}, bf16[2,144,128]{2,1,0:T(8,128)(2,1)S(1)}, u32[]{:S(2)}, u32[]{:S(2)}) %collective-permute-start.3) | collective-permute-done | bytes 73760 | tf_op jit(solution)/shard_map/ppermute | solution.py:343
  40.5 3.7 %replay.1 = (f32[256,256]{1,0:T(8,128)S(1)}, bf16[256,256]{1,0:T(8,128)(2,1)S(1)}) custom-call(f32[32,128]{1,0:T(8,128)S(1)} %get-tuple-element.14.kept_ref, f32[2,128]{1,0:T(2,128)S(1)} %bitcast.31, bf16[2,144,128]{2,1,0:T(8,128)(2,1)S(1)} %collective-permute-done.3.y1, bf16[2,144,128]{2,1,0:T(8,128)(2,1)S(1)} %collective-permute-done.4.y3, ...), custom_call_target="tpu_custom_call" | custom-call | tf_op jit(solution)/shard_map/replay/pallas_call | solution.py:284
  44.2 3.9 %collective-permute-start.8 = (bf16[256,256]{1,0:T(8,128)(2,1)S(1)}, bf16[256,256]{1,0:T(8,128)(2,1)S(1)}, u32[]{:S(2)}, u32[]{:S(2)}) collective-permute-start(bf16[256,256]{1,0:T(8,128)(2,1)S(1)} %get-tuple-element.20.m0), channel_id=1, source_target_pairs={{0,4},{1,5},{2,6},{3,7},{4,0},{5,1},{6,2},{7,3},{8,12},{9,13},{10,... | collective-permute-start | bytes 393224 | tf_op jit(solution)/shard_map/ppermute | solution.py:347
  48.2 0.7 collective-permute-start.7
  48.9 1.3 %collective-permute-start.6 = (bf16[256,256]{1,0:T(8,128)(2,1)S(1)}, bf16[256,256]{1,0:T(8,128)(2,1)S(1)}, u32[]{:S(2)}, u32[]{:S(2)}) collective-permute-start(bf16[256,256]{1,0:T(8,128)(2,1)S(1)} %get-tuple-element.20.m0), channel_id=1, source_target_pairs={{0,2},{1,3},{2,4},{3,5},{4,6},{5,7},{6,0},{7,1},{8,10},{9,11},{10,... | collective-permute-start | bytes 393224 | tf_op jit(solution)/shard_map/ppermute | solution.py:347
  50.2 1.8 %collective-permute-done.8.m2 = bf16[256,256]{1,0:T(8,128)(2,1)S(1)} collective-permute-done((bf16[256,256]{1,0:T(8,128)(2,1)S(1)}, bf16[256,256]{1,0:T(8,128)(2,1)S(1)}, u32[]{:S(2)}, u32[]{:S(2)}) %collective-permute-start.8) | collective-permute-done | bytes 131104 | tf_op jit(solution)/shard_map/ppermute | solution.py:347
  52.0 1.5 %collective-permute-done.7.m3 = bf16[256,256]{1,0:T(8,128)(2,1)S(1)} collective-permute-done((bf16[256,256]{1,0:T(8,128)(2,1)S(1)}, bf16[256,256]{1,0:T(8,128)(2,1)S(1)}, u32[]{:S(2)}, u32[]{:S(2)}) %collective-permute-start.7) | collective-permute-done | bytes 131104 | tf_op jit(solution)/shard_map/ppermute | solution.py:347
  53.5 1.5 %collective-permute-done.6.m1 = bf16[256,256]{1,0:T(8,128)(2,1)S(1)} collective-permute-done((bf16[256,256]{1,0:T(8,128)(2,1)S(1)}, bf16[256,256]{1,0:T(8,128)(2,1)S(1)}, u32[]{:S(2)}, u32[]{:S(2)}) %collective-permute-start.6) | collective-permute-done | bytes 131104 | tf_op jit(solution)/shard_map/ppermute | solution.py:347
  55.1 0.1 collective-permute-start.9
  55.2 1.9 %collective-permute-done.9.theirs_ref = bf16[4,256,256]{2,1,0:T(8,128)(2,1)S(1)} collective-permute-done((bf16[4,256,256]{2,1,0:T(8,128)(2,1)S(1)}, bf16[4,256,256]{2,1,0:T(8,128)(2,1)S(1)}, u32[]{:S(2)}, u32[]{:S(2)}) %collective-permute-start.9) | collective-permute-done | bytes 524320 | tf_op jit(solution)/shard_map/ppermute | solution.py:355
  57.1 3.5 %forward.1 = (bf16[4,256,256]{2,1,0:T(8,128)(2,1)S(1)}, bf16[4,256,256]{2,1,0:T(8,128)(2,1)S(1)}) custom-call(bf16[256,256]{1,0:T(8,128)(2,1)S(1)} %get-tuple-element.20.m0, bf16[256,256]{1,0:T(8,128)(2,1)S(1)} %collective-permute-done.6.m1, bf16[256,256]{1,0:T(8,128)(2,1)S(1)} %collective-permute-done.7.m3, bf16[256,256]{1,0:T(8,128)(2,1)S(1)} %collective-permute-done.8.m2, ...), custom_call_target="tpu_custom_call" | custom-call | tf_op jit(solution)/shard_map/forward/pallas_call | solution.py:327
  60.6 0.2 collective-permute-start.10
  60.8 1.8 %collective-permute-done.10 = bf16[4,256,256]{2,1,0:T(8,128)(2,1)S(1)} collective-permute-done((bf16[4,256,256]{2,1,0:T(8,128)(2,1)S(1)}, bf16[4,256,256]{2,1,0:T(8,128)(2,1)S(1)}, u32[]{:S(2)}, u32[]{:S(2)}) %collective-permute-start.10) | collective-permute-done | bytes 524320 | tf_op jit(solution)/shard_map/ppermute | solution.py:355
  62.6 0.1 fusion.5
  62.8 1.2 %collective-permute-start.11 = (bf16[256,256]{1,0:T(8,128)(2,1)S(1)}, bf16[256,256]{1,0:T(8,128)(2,1)S(1)}, u32[]{:S(2)}, u32[]{:S(2)}) collective-permute-start(bf16[256,256]{1,0:T(8,128)(2,1)S(1)} %get-tuple-element.25), channel_id=1, source_target_pairs={{0,4},{1,5},{2,6},{3,7},{4,0},{5,1},{6,2},{7,3},{8,12},{9,13},{10,... | collective-permute-start | bytes 393224 | tf_op jit(solution)/shard_map/ppermute | solution.py:347
  64.0 1.6 %collective-permute-start.13 = (bf16[256,256]{1,0:T(8,128)(2,1)S(1)}, bf16[256,256]{1,0:T(8,128)(2,1)S(1)}, u32[]{:S(2)}, u32[]{:S(2)}) collective-permute-start(bf16[256,256]{1,0:T(8,128)(2,1)S(1)} %get-tuple-element.26), channel_id=1, source_target_pairs={{0,6},{1,7},{2,0},{3,1},{4,2},{5,3},{6,4},{7,5},{8,14},{9,15},{10,... | collective-permute-start | bytes 393224 | tf_op jit(solution)/shard_map/ppermute | solution.py:347
  65.6 0.4 collective-permute-start.12
  66.1 4.7 %collective-permute-done.11 = bf16[256,256]{1,0:T(8,128)(2,1)S(1)} collective-permute-done((bf16[256,256]{1,0:T(8,128)(2,1)S(1)}, bf16[256,256]{1,0:T(8,128)(2,1)S(1)}, u32[]{:S(2)}, u32[]{:S(2)}) %collective-permute-start.11) | collective-permute-done | bytes 131104 | tf_op jit(solution)/shard_map/ppermute | solution.py:347
  70.7 0.5 collective-permute-done.13
  71.2 1.5 %collective-permute-done.12 = bf16[256,256]{1,0:T(8,128)(2,1)S(1)} collective-permute-done((bf16[256,256]{1,0:T(8,128)(2,1)S(1)}, bf16[256,256]{1,0:T(8,128)(2,1)S(1)}, u32[]{:S(2)}, u32[]{:S(2)}) %collective-permute-start.12) | collective-permute-done | bytes 131104 | tf_op jit(solution)/shard_map/ppermute | solution.py:347
  72.7 0.7 %fusion.4 = bf16[256,256]{1,0:T(8,128)(2,1)} fusion(f32[256,256]{1,0:T(8,128)S(1)} %get-tuple-element.19, f32[4,256,256]{2,1,0:T(8,128)S(1)} %get-tuple-element.24, bf16[256,256]{1,0:T(8,128)(2,1)S(1)} %collective-permute-done.13, bf16[256,256]{1,0:T(8,128)(2,1)S(1)} %collective-permute-done.12, bf16[256,256]{1,0:T(8,128)(2,1)S(1)} %collective-permute-done.11), kind=kLoop, calls=%fused_computation.7 | loop fusion | flops 524288 | bytes 1048576 | tf_op jit(solution)/shard_map/convert_element_type | solution.py:384
  (14 shorter events, 0.1 us)
Async XLA Ops:
  0.0 40.5 %copy-start.4 = (f32[256]{0:T(256)S(1)}, f32[256]{0:T(256)}, u32[]{:S(2)}) copy-start(f32[256]{0:T(256)} %param.14) | copy-start | bytes 3076
  0.0 40.5 %copy-start.3 = (f32[256]{0:T(256)S(1)}, f32[256]{0:T(256)}, u32[]{:S(2)}) copy-start(f32[256]{0:T(256)} %param.13) | copy-start | bytes 3076
  19.8 5.9 %collective-permute-start.2 = (bf16[2,144,128]{2,1,0:T(8,128)(2,1)S(1)}, bf16[2,144,128]{2,1,0:T(8,128)(2,1)S(1)}, u32[]{:S(2)}, u32[]{:S(2)}) collective-permute-start(bf16[2,144,128]{2,1,0:T(8,128)(2,1)S(1)} %get-tuple-element.15.m0), channel_id=1, source_target_pairs={{0,16},{8,24},{16,0},{24,8},{32,48},{40,56},{48,32},{56,40},{64,80... | collective-permute-start | bytes 221192 | tf_op jit(solution)/shard_map/ppermute | solution.py:339
  23.0 4.5 %collective-permute-start.1 = (bf16[2,144,128]{2,1,0:T(8,128)(2,1)S(1)}, bf16[2,144,128]{2,1,0:T(8,128)(2,1)S(1)}, u32[]{:S(2)}, u32[]{:S(2)}) collective-permute-start(bf16[2,144,128]{2,1,0:T(8,128)(2,1)S(1)} %get-tuple-element.15.m0), channel_id=1, source_target_pairs={{0,24},{8,0},{16,8},{24,16},{32,56},{40,32},{48,40},{56,48},{64,88... | collective-permute-start | bytes 221192 | tf_op jit(solution)/shard_map/ppermute | solution.py:339
  24.1 5.6 %collective-permute-start = (bf16[2,144,128]{2,1,0:T(8,128)(2,1)S(1)}, bf16[2,144,128]{2,1,0:T(8,128)(2,1)S(1)}, u32[]{:S(2)}, u32[]{:S(2)}) collective-permute-start(bf16[2,144,128]{2,1,0:T(8,128)(2,1)S(1)} %get-tuple-element.15.m0), channel_id=1, source_target_pairs={{0,8},{8,16},{16,24},{24,0},{32,40},{40,48},{48,56},{56,32},{64,72... | collective-permute-start | bytes 221192 | tf_op jit(solution)/shard_map/ppermute | solution.py:339
  30.2 8.4 %collective-permute-start.5 = (bf16[2,144,128]{2,1,0:T(8,128)(2,1)S(1)}, bf16[2,144,128]{2,1,0:T(8,128)(2,1)S(1)}, u32[]{:S(2)}, u32[]{:S(2)}) collective-permute-start(bf16[2,144,128]{2,1,0:T(8,128)(2,1)S(1)} %row_map.1), channel_id=1, source_target_pairs={{0,64},{8,72},{16,80},{24,88},{32,96},{40,104},{48,112},{56,120},{... | collective-permute-start | bytes 221192 | tf_op jit(solution)/shard_map/ppermute | solution.py:343
  35.3 3.3 %collective-permute-start.4 = (bf16[2,144,128]{2,1,0:T(8,128)(2,1)S(1)}, bf16[2,144,128]{2,1,0:T(8,128)(2,1)S(1)}, u32[]{:S(2)}, u32[]{:S(2)}) collective-permute-start(bf16[2,144,128]{2,1,0:T(8,128)(2,1)S(1)} %row_map.1), channel_id=1, source_target_pairs={{0,96},{8,104},{16,112},{24,120},{1,97},{9,105},{17,113},{25,121},... | collective-permute-start | bytes 221192 | tf_op jit(solution)/shard_map/ppermute | solution.py:343
  36.6 3.9 %collective-permute-start.3 = (bf16[2,144,128]{2,1,0:T(8,128)(2,1)S(1)}, bf16[2,144,128]{2,1,0:T(8,128)(2,1)S(1)}, u32[]{:S(2)}, u32[]{:S(2)}) collective-permute-start(bf16[2,144,128]{2,1,0:T(8,128)(2,1)S(1)} %row_map.1), channel_id=1, source_target_pairs={{0,32},{8,40},{16,48},{24,56},{32,64},{40,72},{48,80},{56,88},{64,... | collective-permute-start | bytes 221192 | tf_op jit(solution)/shard_map/ppermute | solution.py:343
  40.5 16.6 %copy-start = (bf16[2048,1024]{1,0:T(8,128)(2,1)S(1)}, bf16[2048,1024]{1,0:T(8,128)(2,1)}, u32[]{:S(2)}) copy-start(bf16[2048,1024]{1,0:T(8,128)(2,1)} %gate_ref.1) | copy-start | bytes 12582916
  40.5 16.6 %copy-start.1 = (bf16[2048,1024]{1,0:T(8,128)(2,1)S(1)}, bf16[2048,1024]{1,0:T(8,128)(2,1)}, u32[]{:S(2)}) copy-start(bf16[2048,1024]{1,0:T(8,128)(2,1)} %up_ref.1) | copy-start | bytes 12582916
  40.5 16.6 %copy-start.2 = (bf16[1024,2048]{1,0:T(8,128)(2,1)S(1)}, bf16[1024,2048]{1,0:T(8,128)(2,1)}, u32[]{:S(2)}) copy-start(bf16[1024,2048]{1,0:T(8,128)(2,1)} %down_ref.1) | copy-start | bytes 12582916
  44.2 7.8 %collective-permute-start.8 = (bf16[256,256]{1,0:T(8,128)(2,1)S(1)}, bf16[256,256]{1,0:T(8,128)(2,1)S(1)}, u32[]{:S(2)}, u32[]{:S(2)}) collective-permute-start(bf16[256,256]{1,0:T(8,128)(2,1)S(1)} %get-tuple-element.20.m0), channel_id=1, source_target_pairs={{0,4},{1,5},{2,6},{3,7},{4,0},{5,1},{6,2},{7,3},{8,12},{9,13},{10,... | collective-permute-start | bytes 393224 | tf_op jit(solution)/shard_map/ppermute | solution.py:347
  48.2 5.4 %collective-permute-start.7 = (bf16[256,256]{1,0:T(8,128)(2,1)S(1)}, bf16[256,256]{1,0:T(8,128)(2,1)S(1)}, u32[]{:S(2)}, u32[]{:S(2)}) collective-permute-start(bf16[256,256]{1,0:T(8,128)(2,1)S(1)} %get-tuple-element.20.m0), channel_id=1, source_target_pairs={{0,6},{1,7},{2,0},{3,1},{4,2},{5,3},{6,4},{7,5},{8,14},{9,15},{10,... | collective-permute-start | bytes 393224 | tf_op jit(solution)/shard_map/ppermute | solution.py:347
  48.9 6.2 %collective-permute-start.6 = (bf16[256,256]{1,0:T(8,128)(2,1)S(1)}, bf16[256,256]{1,0:T(8,128)(2,1)S(1)}, u32[]{:S(2)}, u32[]{:S(2)}) collective-permute-start(bf16[256,256]{1,0:T(8,128)(2,1)S(1)} %get-tuple-element.20.m0), channel_id=1, source_target_pairs={{0,2},{1,3},{2,4},{3,5},{4,6},{5,7},{6,0},{7,1},{8,10},{9,11},{10,... | collective-permute-start | bytes 393224 | tf_op jit(solution)/shard_map/ppermute | solution.py:347
  55.1 2.0 %collective-permute-start.9 = (bf16[4,256,256]{2,1,0:T(8,128)(2,1)S(1)}, bf16[4,256,256]{2,1,0:T(8,128)(2,1)S(1)}, u32[]{:S(2)}, u32[]{:S(2)}) collective-permute-start(bf16[4,256,256]{2,1,0:T(8,128)(2,1)S(1)} %pad_maximum_fusion), channel_id=1, source_target_pairs={{0,1},{1,0},{2,3},{3,2},{4,5},{5,4},{6,7},{7,6},{8,9},{9,8},{10,11... | collective-permute-start | bytes 1572872 | tf_op jit(solution)/shard_map/ppermute | solution.py:355
  60.6 2.0 %collective-permute-start.10 = (bf16[4,256,256]{2,1,0:T(8,128)(2,1)S(1)}, bf16[4,256,256]{2,1,0:T(8,128)(2,1)S(1)}, u32[]{:S(2)}, u32[]{:S(2)}) collective-permute-start(bf16[4,256,256]{2,1,0:T(8,128)(2,1)S(1)} %get-tuple-element.22), channel_id=1, source_target_pairs={{0,1},{1,0},{2,3},{3,2},{4,5},{5,4},{6,7},{7,6},{8,9},{9,8},{10,11... | collective-permute-start | bytes 1572872 | tf_op jit(solution)/shard_map/ppermute | solution.py:355
  62.8 7.9 %collective-permute-start.11 = (bf16[256,256]{1,0:T(8,128)(2,1)S(1)}, bf16[256,256]{1,0:T(8,128)(2,1)S(1)}, u32[]{:S(2)}, u32[]{:S(2)}) collective-permute-start(bf16[256,256]{1,0:T(8,128)(2,1)S(1)} %get-tuple-element.25), channel_id=1, source_target_pairs={{0,4},{1,5},{2,6},{3,7},{4,0},{5,1},{6,2},{7,3},{8,12},{9,13},{10,... | collective-permute-start | bytes 393224 | tf_op jit(solution)/shard_map/ppermute | solution.py:347
  64.0 7.2 %collective-permute-start.13 = (bf16[256,256]{1,0:T(8,128)(2,1)S(1)}, bf16[256,256]{1,0:T(8,128)(2,1)S(1)}, u32[]{:S(2)}, u32[]{:S(2)}) collective-permute-start(bf16[256,256]{1,0:T(8,128)(2,1)S(1)} %get-tuple-element.26), channel_id=1, source_target_pairs={{0,6},{1,7},{2,0},{3,1},{4,2},{5,3},{6,4},{7,5},{8,14},{9,15},{10,... | collective-permute-start | bytes 393224 | tf_op jit(solution)/shard_map/ppermute | solution.py:347
  65.6 7.1 %collective-permute-start.12 = (bf16[256,256]{1,0:T(8,128)(2,1)S(1)}, bf16[256,256]{1,0:T(8,128)(2,1)S(1)}, u32[]{:S(2)}, u32[]{:S(2)}) collective-permute-start(bf16[256,256]{1,0:T(8,128)(2,1)S(1)} %get-tuple-element.27), channel_id=1, source_target_pairs={{0,2},{1,3},{2,4},{3,5},{4,6},{5,7},{6,0},{7,1},{8,10},{9,11},{10,... | collective-permute-start | bytes 393224 | tf_op jit(solution)/shard_map/ppermute | solution.py:347

commit v6 on v5

--- a/solution.py
+++ b/solution.py
@@ -294,45 +294,77 @@
     )(kept, init, *y_maps, *x_maps, off, grp, gain, pltpu.with_memory_space_constraint(q, pltpu.VMEM))
 
 
-def forward_kernel(m0, m1, m3, m2, theirs_ref, gate_ref, up_ref, down_ref, keep_ref, send_ref, hidden):
-    z, core = places()[2:]
+def weight_rows(k, c):
+    z = places()[2]
+    return pl.multiple_of((lax.rem(z + k, 4) * 2 + c) * 2 * WIDTH, 2 * WIDTH)
+
+
+def products(parts, gate_ref, up_ref, n):
     wide = 2 * WIDTH
-
-    def at(k, c):
-        return pl.multiple_of((lax.rem(z + k, 4) * 2 + c) * wide, wide)
-
-    parts = [(m0, 0, 0), (m1, 3, 0), (m2, 2, 0), (m3, 1, 0)]
-    parts += [(theirs_ref.at[i], (4 - k) % 4, 1) for i, k in enumerate((0, 1, 3, 2))]
+    gate = up = None
+    for ref, row in parts:
+        chunk = ref[...]
+        g = jnp.dot(chunk, gate_ref[pl.ds(row, wide), n : n + wide], preferred_element_type=F32)
+        u = jnp.dot(chunk, up_ref[pl.ds(row, wide), n : n + wide], preferred_element_type=F32)
+        gate = g if gate is None else gate + g
+        up = u if up is None else up + u
+    return gate, up
+
+
+def early_kernel(m0, m1, m3, theirs_ref, gate_ref, up_ref, gate_out, up_out):
+    core = places()[3]
+    way = 1 - 2 * core
+    parts = [(ref, weight_rows(4 + k * way, core)) for ref, k in zip((m0, m1, m3), (0, -1, 1))]
+    parts += [(theirs_ref.at[i], weight_rows(4 + k * way, 1 - core)) for i, k in enumerate((0, 1, -1))]
+    wide = 2 * WIDTH
     for n in range(0, gate_ref.shape[1], wide):
-        gate = up = None
-        for ref, k, other in parts:
-            chunk = ref[...]
-            row = at(k, 1 - core if other else core)
-            g = jnp.dot(chunk, gate_ref[pl.ds(row, wide), n : n + wide], preferred_element_type=F32)
-            u = jnp.dot(chunk, up_ref[pl.ds(row, wide), n : n + wide], preferred_element_type=F32)
-            gate = g if gate is None else gate + g
-            up = u if up is None else up + u
+        gate_out[:, n : n + wide], up_out[:, n : n + wide] = products(parts, gate_ref, up_ref, n)
+
+
+def late_kernel(m2, theirs_ref, gate_in, up_in, gate_ref, up_ref, down_ref, keep_ref, send_ref, hidden):
+    core = places()[3]
+    parts = [(m2, weight_rows(2, core)), (theirs_ref, weight_rows(2, 1 - core))]
+    wide = 2 * WIDTH
+    for n in range(0, gate_ref.shape[1], wide):
+        gate, up = products(parts, gate_ref, up_ref, n)
+        gate = gate + gate_in[:, n : n + wide]
+        up = up + up_in[:, n : n + wide]
         hidden[:, n : n + wide] = (gate / (1.0 + jnp.exp(-gate)) * up).astype(BF16)
     low = hidden[...]
     for ref, c in ((send_ref, 1 - core), (keep_ref, core)):
         for k in range(4):
-            out = jnp.dot(low, down_ref[:, pl.ds(at(k, c), wide)], preferred_element_type=F32)
+            out = jnp.dot(low, down_ref[:, pl.ds(weight_rows(k, c), wide)], preferred_element_type=F32)
             ref[k] = out.astype(BF16)
 
 
-def forward(mine, theirs, gate_weight, up_weight, down_weight):
-    steps = mine[0].shape[0]
-    weights = [pltpu.with_memory_space_constraint(w, pltpu.VMEM) for w in (gate_weight, up_weight, down_weight)]
+def forward(normed, gate_weight, up_weight, down_weight):
+    steps, units = normed.shape[0], gate_weight.shape[1]
+    gate_weight, up_weight, down_weight = [
+        pltpu.with_memory_space_constraint(w, pltpu.VMEM) for w in (gate_weight, up_weight, down_weight)
+    ]
+    one, last = z_round(normed, 1), z_round(normed, -1)
+    two = z_round(one, 1)
+    near = other_core(jnp.stack([normed, one, last]))
+    wide = pltpu.VMEM((steps, units), F32)
+    gate, up = pl.pallas_call(
+        early_kernel,
+        out_shape=(wide, wide),
+        in_specs=[VMEM] * 6,
+        out_specs=(VMEM, VMEM),
+        compiler_params=pltpu.CompilerParams(vmem_limit_bytes=16_000_000),
+        name="early",
+    )(normed, one, last, near, gate_weight, up_weight)
+    two, gate = lax.optimization_barrier((two, gate))
     half = jax.ShapeDtypeStruct((4, steps, 2 * WIDTH), BF16)
     return pl.pallas_call(
-        forward_kernel,
+        late_kernel,
         out_shape=(half, half),
-        in_specs=[VMEM] * 8,
+        in_specs=[VMEM] * 7,
         out_specs=(VMEM, VMEM),
-        scratch_shapes=[pltpu.VMEM((steps, gate_weight.shape[1]), BF16)],
+        scratch_shapes=[pltpu.VMEM((steps, units), BF16)],
         compiler_params=pltpu.CompilerParams(vmem_limit_bytes=16_000_000),
-        name="forward",
-    )(*mine, theirs, *weights)
+        name="late",
+    )(two, other_core(two), gate, up, gate_weight, up_weight, down_weight)
 
 
 def x_back(v, k):
@@ -340,7 +372,7 @@
 
 
 def y_back(v, k):
-    return lax.ppermute(v, "tm", [(y * 4 + x, (y + k) * 4 + x) for y in range(4 - k) for x in range(4)])
+    return lax.ppermute(v, "tm", [(y * 4 + x, (y + k) % 4 * 4 + x) for y in range(4) for x in range(4)])
 
 
 def z_back(v, k):
@@ -349,6 +381,12 @@
 
 def three(back, v):
     return [back(v, k) for k in (1, 3, 2)]
+
+
+def z_round(v, way):
+    return lax.ppermute(
+        v, "block", [(z * 2 + c, (z + way * (1 - 2 * c)) % 4 * 2 + c) for z in range(4) for c in range(2)]
+    )
 
 
 def other_core(v):
@@ -373,9 +411,7 @@
     states, normed = replay(
         kept, initial_state.reshape(2, WIDTH), y_maps, x_maps, off, grp, norm_gain.reshape(2, WIDTH), q
     )
-    mine = [normed] + three(z_back, normed)
-    theirs = other_core(jnp.stack(mine))
-    keep, sent = forward(mine, theirs, gate_weight, up_weight, down_weight)
+    keep, sent = forward(normed, gate_weight, up_weight, down_weight)
     chip = keep.astype(F32) + other_core(sent).astype(F32)
     low = chip.astype(BF16)
     mixed = chip[0]

time: 74.4 us -> 77.6 us (1.043)
  waiting for transfers between devices: 21.8 us -> 30.6 us
  starting transfers between devices: 23.1 us -> 17.2 us
    ppermute x3 -> x6, waiting for transfers between devices: 1.95 us -> 13.4 us  [the longest x3 8.8 us: z_round(): lax.ppermute(v, 'block', [(z * 2 + c, (z + way * (1 - 2 * c)) % 4 * 2 + c...]
    ppermute x6 -> x3, starting transfers between devices: 9.24 us -> 2.18 us  [z_back(): lax.ppermute(v, 'block', [(z * 2 + c, (z + k) % 4 * 2 + c) for z in range...]
    ppermute x6 -> x3, waiting for transfers between devices: 11.5 us -> 7.74 us  [z_back(): lax.ppermute(v, 'block', [(z * 2 + c, (z + k) % 4 * 2 + c) for z in range...]
    ppermute x3 -> x6, starting transfers between devices: 8.35 us -> 9.46 us  [the longest x3 5.29 us: y_back(): lax.ppermute(v, 'tm', [(y * 4 + x, (y + k) % 4 * 4 + x) for y in range(4)...]
    ppermute x2 -> x3, waiting for transfers between devices: 3.68 us -> 4.74 us  [other_core(): return lax.ppermute(v, 'block', [(s, s ^ 1) for s in range(8)])]
    pallas_call x1 -> x2, Pallas kernels: 3.49 us -> 3.82 us  [the longest x1 1.92 us: forward(): pl.pallas_call(late_kernel, out_shape=(half, half), in_specs=[VMEM] * 7,...]
  transfers between devices with their start and end apart: 14 -> 15, of which waited for: 12 -> 14; matrix products, arithmetic and copies ran while one was open for 0% -> 0% of each run, Pallas kernels for 0% -> 2%
where the time goes in v6:
time: 77.6 us; the launch traced here: 76.6 us
  waiting for transfers between devices  30.6 us (39%)
  Pallas kernels  27.8 us (36%)
  starting transfers between devices  17.2 us (22%)
  other arithmetic  0.93 us (1%)
    pallas_call x1, Pallas kernels, compose(): pl.pallas_call(compose_kernel, out_shape=(pltpu.VMEM((SPAN, 2 * GROUPS, W...  19.8 us
    ppermute x3, waiting for transfers between devices, z_round(): lax.ppermute(v, 'block', [(z * 2 + c, (z + way * (1 - 2 * c)) % 4 * 2 + c...  8.8 us
    ppermute x3, waiting for transfers between devices, z_back(): lax.ppermute(v, 'block', [(z * 2 + c, (z + k) % 4 * 2 + c) for z in range...  7.74 us
    ppermute x3, starting transfers between devices, y_back(): lax.ppermute(v, 'tm', [(y * 4 + x, (y + k) % 4 * 4 + x) for y in range(4)...  5.29 us
    ppermute x3, starting transfers between devices, x_back(): lax.ppermute(v, 'tm', [(y * 4 + x, y * 4 + (x + k) % 4) for y in range(4)...  5.21 us
    ppermute x3, waiting for transfers between devices, other_core(): return lax.ppermute(v, 'block', [(s, s ^ 1) for s in range(8)])  4.74 us
    ppermute x3, waiting for transfers between devices, x_back(): lax.ppermute(v, 'tm', [(y * 4 + x, y * 4 + (x + k) % 4) for y in range(4)...  4.68 us
    ppermute x3, waiting for transfers between devices, y_back(): lax.ppermute(v, 'tm', [(y * 4 + x, (y + k) % 4 * 4 + x) for y in range(4)...  4.59 us
  transfers between devices with their start and end apart: 15, of which 14 were waited for; matrix products, arithmetic and copies ran while one was open for 0% of the time, Pallas kernels for 2%

profile of v6, /device:TPU:0, one launch (start us, length us, event | category | flops | bytes accessed | tf_op | source)
XLA Modules:
  0.0 76.6 jit_solution(6175465150925352306)
XLA Ops:
  0.0 19.8 %compose.1 = (bf16[16,32,128,128]{3,2,1,0:T(8,128)(2,1)S(1)}, f32[512,128]{1,0:T(8,128)S(1)}, bf16[2,144,128]{2,1,0:T(8,128)(2,1)S(1)}, bf16[32,128,128]{2,1,0:T(8,128)(2,1)S(1)}, f32[32,128]{1,0:T(8,128)S(1)}) custom-call(f32[64,256]{1,0:T(8,128)} %bitcast.32, f32[2,256]{1,0:T(2,128)} %bitcast.33, f32[2,256]{1,0:T(2,128)} %bitcast.34, ...), custom_call_target="tpu_custom_call" | custom-call | tf_op jit(solution)/shard_map/compose/pallas_call | solution.py:192
  19.8 3.2 %collective-permute-start.2 = (bf16[2,144,128]{2,1,0:T(8,128)(2,1)S(1)}, bf16[2,144,128]{2,1,0:T(8,128)(2,1)S(1)}, u32[]{:S(2)}, u32[]{:S(2)}) collective-permute-start(bf16[2,144,128]{2,1,0:T(8,128)(2,1)S(1)} %get-tuple-element.19.m0), channel_id=1, source_target_pairs={{0,16},{8,24},{16,0},{24,8},{32,48},{40,56},{48,32},{56,40},{64,80... | collective-permute-start | bytes 221192 | tf_op jit(solution)/shard_map/ppermute | solution.py:371
  23.0 1.1 %collective-permute-start.1 = (bf16[2,144,128]{2,1,0:T(8,128)(2,1)S(1)}, bf16[2,144,128]{2,1,0:T(8,128)(2,1)S(1)}, u32[]{:S(2)}, u32[]{:S(2)}) collective-permute-start(bf16[2,144,128]{2,1,0:T(8,128)(2,1)S(1)} %get-tuple-element.19.m0), channel_id=1, source_target_pairs={{0,24},{8,0},{16,8},{24,16},{32,56},{40,32},{48,40},{56,48},{64,88... | collective-permute-start | bytes 221192 | tf_op jit(solution)/shard_map/ppermute | solution.py:371
  24.1 0.9 %collective-permute-start = (bf16[2,144,128]{2,1,0:T(8,128)(2,1)S(1)}, bf16[2,144,128]{2,1,0:T(8,128)(2,1)S(1)}, u32[]{:S(2)}, u32[]{:S(2)}) collective-permute-start(bf16[2,144,128]{2,1,0:T(8,128)(2,1)S(1)} %get-tuple-element.19.m0), channel_id=1, source_target_pairs={{0,8},{8,16},{16,24},{24,0},{32,40},{40,48},{48,56},{56,32},{64,72... | collective-permute-start | bytes 221192 | tf_op jit(solution)/shard_map/ppermute | solution.py:371
  25.0 0.7 collective-permute-done.2.m2.x2
  25.7 1.7 %collective-permute-done.1.m3.x3 = bf16[2,144,128]{2,1,0:T(8,128)(2,1)S(1)} collective-permute-done((bf16[2,144,128]{2,1,0:T(8,128)(2,1)S(1)}, bf16[2,144,128]{2,1,0:T(8,128)(2,1)S(1)}, u32[]{:S(2)}, u32[]{:S(2)}) %collective-permute-start.1) | collective-permute-done | bytes 73760 | tf_op jit(solution)/shard_map/ppermute | solution.py:371
  27.5 2.2 %collective-permute-done.m1.x1 = bf16[2,144,128]{2,1,0:T(8,128)(2,1)S(1)} collective-permute-done((bf16[2,144,128]{2,1,0:T(8,128)(2,1)S(1)}, bf16[2,144,128]{2,1,0:T(8,128)(2,1)S(1)}, u32[]{:S(2)}, u32[]{:S(2)}) %collective-permute-start) | collective-permute-done | bytes 73760 | tf_op jit(solution)/shard_map/ppermute | solution.py:371
  29.7 0.5 row_map.1
  30.2 3.3 %collective-permute-start.5 = (bf16[2,144,128]{2,1,0:T(8,128)(2,1)S(1)}, bf16[2,144,128]{2,1,0:T(8,128)(2,1)S(1)}, u32[]{:S(2)}, u32[]{:S(2)}) collective-permute-start(bf16[2,144,128]{2,1,0:T(8,128)(2,1)S(1)} %row_map.1), channel_id=1, source_target_pairs={{0,64},{8,72},{16,80},{24,88},{32,96},{40,104},{48,112},{56,120},{... | collective-permute-start | bytes 221192 | tf_op jit(solution)/shard_map/ppermute | solution.py:375
  33.5 1.1 %collective-permute-start.4 = (bf16[2,144,128]{2,1,0:T(8,128)(2,1)S(1)}, bf16[2,144,128]{2,1,0:T(8,128)(2,1)S(1)}, u32[]{:S(2)}, u32[]{:S(2)}) collective-permute-start(bf16[2,144,128]{2,1,0:T(8,128)(2,1)S(1)} %row_map.1), channel_id=1, source_target_pairs={{0,96},{8,104},{16,112},{24,120},{32,0},{40,8},{48,16},{56,24},{64... | collective-permute-start | bytes 221192 | tf_op jit(solution)/shard_map/ppermute | solution.py:375
  34.5 1.0 %collective-permute-start.3 = (bf16[2,144,128]{2,1,0:T(8,128)(2,1)S(1)}, bf16[2,144,128]{2,1,0:T(8,128)(2,1)S(1)}, u32[]{:S(2)}, u32[]{:S(2)}) collective-permute-start(bf16[2,144,128]{2,1,0:T(8,128)(2,1)S(1)} %row_map.1), channel_id=1, source_target_pairs={{0,32},{8,40},{16,48},{24,56},{32,64},{40,72},{48,80},{56,88},{64,... | collective-permute-start | bytes 221192 | tf_op jit(solution)/shard_map/ppermute | solution.py:375
  35.5 0.7 collective-permute-done.5.y2
  36.2 1.6 %collective-permute-done.4.y3 = bf16[2,144,128]{2,1,0:T(8,128)(2,1)S(1)} collective-permute-done((bf16[2,144,128]{2,1,0:T(8,128)(2,1)S(1)}, bf16[2,144,128]{2,1,0:T(8,128)(2,1)S(1)}, u32[]{:S(2)}, u32[]{:S(2)}) %collective-permute-start.4) | collective-permute-done | bytes 73760 | tf_op jit(solution)/shard_map/ppermute | solution.py:375
  37.8 2.3 %collective-permute-done.3.y1 = bf16[2,144,128]{2,1,0:T(8,128)(2,1)S(1)} collective-permute-done((bf16[2,144,128]{2,1,0:T(8,128)(2,1)S(1)}, bf16[2,144,128]{2,1,0:T(8,128)(2,1)S(1)}, u32[]{:S(2)}, u32[]{:S(2)}) %collective-permute-start.3) | collective-permute-done | bytes 73760 | tf_op jit(solution)/shard_map/ppermute | solution.py:375
  40.1 3.7 %replay.1 = (f32[256,256]{1,0:T(8,128)S(1)}, bf16[256,256]{1,0:T(8,128)(2,1)S(1)}) custom-call(f32[32,128]{1,0:T(8,128)S(1)} %get-tuple-element.18.kept_ref, f32[2,128]{1,0:T(2,128)S(1)} %bitcast.29, bf16[2,144,128]{2,1,0:T(8,128)(2,1)S(1)} %collective-permute-done.3.y1, bf16[2,144,128]{2,1,0:T(8,128)(2,1)S(1)} %collective-permute-done.4.y3, ...), custom_call_target="tpu_custom_call" | custom-call | tf_op jit(solution)/shard_map/replay/pallas_call | solution.py:284
  43.8 4.1 %collective-permute-start.8 = (bf16[256,256]{1,0:T(8,128)(2,1)S(1)}, bf16[256,256]{1,0:T(8,128)(2,1)S(1)}, u32[]{:S(2)}, u32[]{:S(2)}) collective-permute-start(bf16[256,256]{1,0:T(8,128)(2,1)S(1)} %get-tuple-element.24.m0), channel_id=1, source_target_pairs={{0,6},{1,3},{2,0},{3,5},{4,2},{5,7},{6,4},{7,1},{8,14},{9,11},{10,... | collective-permute-start | bytes 393224 | tf_op jit(solution)/shard_map/ppermute | solution.py:387
  47.9 2.5 %collective-permute-done.8.m3 = bf16[256,256]{1,0:T(8,128)(2,1)S(1)} collective-permute-done((bf16[256,256]{1,0:T(8,128)(2,1)S(1)}, bf16[256,256]{1,0:T(8,128)(2,1)S(1)}, u32[]{:S(2)}, u32[]{:S(2)}) %collective-permute-start.8) | collective-permute-done | bytes 131104 | tf_op jit(solution)/shard_map/ppermute | solution.py:387
  50.4 3.7 %collective-permute-done.6.m1 = bf16[256,256]{1,0:T(8,128)(2,1)S(1)} collective-permute-done((bf16[256,256]{1,0:T(8,128)(2,1)S(1)}, bf16[256,256]{1,0:T(8,128)(2,1)S(1)}, u32[]{:S(2)}, u32[]{:S(2)}) %collective-permute-start.6) | collective-permute-done | bytes 131104 | tf_op jit(solution)/shard_map/ppermute | solution.py:387
  54.3 1.6 %collective-permute-done.9.theirs_ref = bf16[3,256,256]{2,1,0:T(8,128)(2,1)S(1)} collective-permute-done((bf16[3,256,256]{2,1,0:T(8,128)(2,1)S(1)}, bf16[3,256,256]{2,1,0:T(8,128)(2,1)S(1)}, u32[]{:S(2)}, u32[]{:S(2)}) %collective-permute-start.9) | collective-permute-done | bytes 393248 | tf_op jit(solution)/shard_map/ppermute | solution.py:393
  55.9 1.9 %early.1 = (f32[256,1024]{1,0:T(8,128)S(1)}, f32[256,1024]{1,0:T(8,128)S(1)}) custom-call(bf16[256,256]{1,0:T(8,128)(2,1)S(1)} %get-tuple-element.24.m0, bf16[256,256]{1,0:T(8,128)(2,1)S(1)} %collective-permute-done.6.m1, bf16[256,256]{1,0:T(8,128)(2,1)S(1)} %collective-permute-done.8.m3, bf16[3,256,256]{2,1,0:T(8,128)(2,1)S(1)} %collective-permute-done.9.theirs_ref, ...), custom_call_target="tpu_custom_call" | custom-call | tf_op jit(solution)/shard_map/early/pallas_call | solution.py:349
  57.8 2.6 %collective-permute-done.7.m2 = bf16[256,256]{1,0:T(8,128)(2,1)S(1)} collective-permute-done((bf16[256,256]{1,0:T(8,128)(2,1)S(1)}, bf16[256,256]{1,0:T(8,128)(2,1)S(1)}, u32[]{:S(2)}, u32[]{:S(2)}) %collective-permute-start.7) | collective-permute-done | bytes 131104 | tf_op jit(solution)/shard_map/ppermute | solution.py:387
  60.4 1.3 %collective-permute-done.10.theirs_ref = bf16[256,256]{1,0:T(8,128)(2,1)S(1)} collective-permute-done((bf16[256,256]{1,0:T(8,128)(2,1)S(1)}, bf16[256,256]{1,0:T(8,128)(2,1)S(1)}, u32[]{:S(2)}, u32[]{:S(2)}) %collective-permute-start.10) | collective-permute-done | bytes 131104 | tf_op jit(solution)/shard_map/ppermute | solution.py:393
  61.8 1.9 %late.1 = (bf16[4,256,256]{2,1,0:T(8,128)(2,1)S(1)}, bf16[4,256,256]{2,1,0:T(8,128)(2,1)S(1)}) custom-call(bf16[256,256]{1,0:T(8,128)(2,1)S(1)} %collective-permute-done.7.m2, bf16[256,256]{1,0:T(8,128)(2,1)S(1)} %collective-permute-done.10.theirs_ref, f32[256,1024]{1,0:T(8,128)S(1)} %get-tuple-element.27.gate_in, f32[256,1024]{1,0:T(8,128)S(1)} %get-tuple-element.28.up_in, ...), custom_call_target="tpu_custom_call" | custom-call | tf_op jit(solution)/shard_map/late/pallas_call | solution.py:359
  63.7 0.2 collective-permute-start.11
  63.9 1.8 %collective-permute-done.11 = bf16[4,256,256]{2,1,0:T(8,128)(2,1)S(1)} collective-permute-done((bf16[4,256,256]{2,1,0:T(8,128)(2,1)S(1)}, bf16[4,256,256]{2,1,0:T(8,128)(2,1)S(1)}, u32[]{:S(2)}, u32[]{:S(2)}) %collective-permute-start.11) | collective-permute-done | bytes 524320 | tf_op jit(solution)/shard_map/ppermute | solution.py:393
  65.7 0.1 fusion.5
  65.9 0.1 collective-permute-start.12
  66.0 1.4 %collective-permute-start.14 = (bf16[256,256]{1,0:T(8,128)(2,1)S(1)}, bf16[256,256]{1,0:T(8,128)(2,1)S(1)}, u32[]{:S(2)}, u32[]{:S(2)}) collective-permute-start(bf16[256,256]{1,0:T(8,128)(2,1)S(1)} %get-tuple-element.34), channel_id=1, source_target_pairs={{0,6},{1,7},{2,0},{3,1},{4,2},{5,3},{6,4},{7,5},{8,14},{9,15},{10,... | collective-permute-start | bytes 393224 | tf_op jit(solution)/shard_map/ppermute | solution.py:379
  67.4 0.7 collective-permute-start.13
  68.1 5.7 %collective-permute-done.12 = bf16[256,256]{1,0:T(8,128)(2,1)S(1)} collective-permute-done((bf16[256,256]{1,0:T(8,128)(2,1)S(1)}, bf16[256,256]{1,0:T(8,128)(2,1)S(1)}, u32[]{:S(2)}, u32[]{:S(2)}) %collective-permute-start.12) | collective-permute-done | bytes 131104 | tf_op jit(solution)/shard_map/ppermute | solution.py:379
  73.8 2.0 %collective-permute-done.13 = bf16[256,256]{1,0:T(8,128)(2,1)S(1)} collective-permute-done((bf16[256,256]{1,0:T(8,128)(2,1)S(1)}, bf16[256,256]{1,0:T(8,128)(2,1)S(1)}, u32[]{:S(2)}, u32[]{:S(2)}) %collective-permute-start.13) | collective-permute-done | bytes 131104 | tf_op jit(solution)/shard_map/ppermute | solution.py:379
  75.8 0.7 fusion.4
  (17 shorter events, 0.3 us)
Async XLA Ops:
  0.0 40.1 %copy-start.4 = (f32[256]{0:T(256)S(1)}, f32[256]{0:T(256)}, u32[]{:S(2)}) copy-start(f32[256]{0:T(256)} %param.14) | copy-start | bytes 3076
  0.0 40.1 %copy-start.3 = (f32[256]{0:T(256)S(1)}, f32[256]{0:T(256)}, u32[]{:S(2)}) copy-start(f32[256]{0:T(256)} %param.13) | copy-start | bytes 3076
  19.8 5.9 %collective-permute-start.2 = (bf16[2,144,128]{2,1,0:T(8,128)(2,1)S(1)}, bf16[2,144,128]{2,1,0:T(8,128)(2,1)S(1)}, u32[]{:S(2)}, u32[]{:S(2)}) collective-permute-start(bf16[2,144,128]{2,1,0:T(8,128)(2,1)S(1)} %get-tuple-element.19.m0), channel_id=1, source_target_pairs={{0,16},{8,24},{16,0},{24,8},{32,48},{40,56},{48,32},{56,40},{64,80... | collective-permute-start | bytes 221192 | tf_op jit(solution)/shard_map/ppermute | solution.py:371
  23.0 4.5 %collective-permute-start.1 = (bf16[2,144,128]{2,1,0:T(8,128)(2,1)S(1)}, bf16[2,144,128]{2,1,0:T(8,128)(2,1)S(1)}, u32[]{:S(2)}, u32[]{:S(2)}) collective-permute-start(bf16[2,144,128]{2,1,0:T(8,128)(2,1)S(1)} %get-tuple-element.19.m0), channel_id=1, source_target_pairs={{0,24},{8,0},{16,8},{24,16},{32,56},{40,32},{48,40},{56,48},{64,88... | collective-permute-start | bytes 221192 | tf_op jit(solution)/shard_map/ppermute | solution.py:371
  24.1 5.6 %collective-permute-start = (bf16[2,144,128]{2,1,0:T(8,128)(2,1)S(1)}, bf16[2,144,128]{2,1,0:T(8,128)(2,1)S(1)}, u32[]{:S(2)}, u32[]{:S(2)}) collective-permute-start(bf16[2,144,128]{2,1,0:T(8,128)(2,1)S(1)} %get-tuple-element.19.m0), channel_id=1, source_target_pairs={{0,8},{8,16},{16,24},{24,0},{32,40},{40,48},{48,56},{56,32},{64,72... | collective-permute-start | bytes 221192 | tf_op jit(solution)/shard_map/ppermute | solution.py:371
  30.2 6.0 %collective-permute-start.5 = (bf16[2,144,128]{2,1,0:T(8,128)(2,1)S(1)}, bf16[2,144,128]{2,1,0:T(8,128)(2,1)S(1)}, u32[]{:S(2)}, u32[]{:S(2)}) collective-permute-start(bf16[2,144,128]{2,1,0:T(8,128)(2,1)S(1)} %row_map.1), channel_id=1, source_target_pairs={{0,64},{8,72},{16,80},{24,88},{32,96},{40,104},{48,112},{56,120},{... | collective-permute-start | bytes 221192 | tf_op jit(solution)/shard_map/ppermute | solution.py:375
  33.5 4.4 %collective-permute-start.4 = (bf16[2,144,128]{2,1,0:T(8,128)(2,1)S(1)}, bf16[2,144,128]{2,1,0:T(8,128)(2,1)S(1)}, u32[]{:S(2)}, u32[]{:S(2)}) collective-permute-start(bf16[2,144,128]{2,1,0:T(8,128)(2,1)S(1)} %row_map.1), channel_id=1, source_target_pairs={{0,96},{8,104},{16,112},{24,120},{32,0},{40,8},{48,16},{56,24},{64... | collective-permute-start | bytes 221192 | tf_op jit(solution)/shard_map/ppermute | solution.py:375
  34.5 5.6 %collective-permute-start.3 = (bf16[2,144,128]{2,1,0:T(8,128)(2,1)S(1)}, bf16[2,144,128]{2,1,0:T(8,128)(2,1)S(1)}, u32[]{:S(2)}, u32[]{:S(2)}) collective-permute-start(bf16[2,144,128]{2,1,0:T(8,128)(2,1)S(1)} %row_map.1), channel_id=1, source_target_pairs={{0,32},{8,40},{16,48},{24,56},{32,64},{40,72},{48,80},{56,88},{64,... | collective-permute-start | bytes 221192 | tf_op jit(solution)/shard_map/ppermute | solution.py:375
  40.1 15.8 %copy-start = (bf16[2048,1024]{1,0:T(8,128)(2,1)S(1)}, bf16[2048,1024]{1,0:T(8,128)(2,1)}, u32[]{:S(2)}) copy-start(bf16[2048,1024]{1,0:T(8,128)(2,1)} %gate_ref.3) | copy-start | bytes 12582916
  40.1 15.8 %copy-start.1 = (bf16[2048,1024]{1,0:T(8,128)(2,1)S(1)}, bf16[2048,1024]{1,0:T(8,128)(2,1)}, u32[]{:S(2)}) copy-start(bf16[2048,1024]{1,0:T(8,128)(2,1)} %up_ref.3) | copy-start | bytes 12582916
  43.8 6.6 %collective-permute-start.8 = (bf16[256,256]{1,0:T(8,128)(2,1)S(1)}, bf16[256,256]{1,0:T(8,128)(2,1)S(1)}, u32[]{:S(2)}, u32[]{:S(2)}) collective-permute-start(bf16[256,256]{1,0:T(8,128)(2,1)S(1)} %get-tuple-element.24.m0), channel_id=1, source_target_pairs={{0,6},{1,3},{2,0},{3,5},{4,2},{5,7},{6,4},{7,1},{8,14},{9,11},{10,... | collective-permute-start | bytes 393224 | tf_op jit(solution)/shard_map/ppermute | solution.py:387
  47.9 6.2 %collective-permute-start.6 = (bf16[256,256]{1,0:T(8,128)(2,1)S(1)}, bf16[256,256]{1,0:T(8,128)(2,1)S(1)}, u32[]{:S(2)}, u32[]{:S(2)}) collective-permute-start(bf16[256,256]{1,0:T(8,128)(2,1)S(1)} %get-tuple-element.24.m0), channel_id=1, source_target_pairs={{0,2},{1,7},{2,4},{3,1},{4,6},{5,3},{6,0},{7,5},{8,10},{9,15},{10,... | collective-permute-start | bytes 393224 | tf_op jit(solution)/shard_map/ppermute | solution.py:387
  54.1 7.7 %copy-start.2 = (bf16[1024,2048]{1,0:T(8,128)(2,1)S(1)}, bf16[1024,2048]{1,0:T(8,128)(2,1)}, u32[]{:S(2)}) copy-start(bf16[1024,2048]{1,0:T(8,128)(2,1)} %down_ref.1) | copy-start | bytes 12582916
  54.1 1.8 %collective-permute-start.9 = (bf16[3,256,256]{2,1,0:T(8,128)(2,1)S(1)}, bf16[3,256,256]{2,1,0:T(8,128)(2,1)S(1)}, u32[]{:S(2)}, u32[]{:S(2)}) collective-permute-start(bf16[3,256,256]{2,1,0:T(8,128)(2,1)S(1)} %pad_maximum_fusion), channel_id=1, source_target_pairs={{0,1},{1,0},{2,3},{3,2},{4,5},{5,4},{6,7},{7,6},{8,9},{9,8},{10,11... | collective-permute-start | bytes 1179656 | tf_op jit(solution)/shard_map/ppermute | solution.py:393
  54.2 6.2 %collective-permute-start.7 = (bf16[256,256]{1,0:T(8,128)(2,1)S(1)}, bf16[256,256]{1,0:T(8,128)(2,1)S(1)}, u32[]{:S(2)}, u32[]{:S(2)}) collective-permute-start(bf16[256,256]{1,0:T(8,128)(2,1)S(1)} %collective-permute-done.6.m1), channel_id=1, source_target_pairs={{0,2},{1,7},{2,4},{3,1},{4,6},{5,3},{6,0},{7,5},{8,10},{9,15},{10,... | collective-permute-start | bytes 393224 | tf_op jit(solution)/shard_map/ppermute | solution.py:387
  60.4 1.3 %collective-permute-start.10 = (bf16[256,256]{1,0:T(8,128)(2,1)S(1)}, bf16[256,256]{1,0:T(8,128)(2,1)S(1)}, u32[]{:S(2)}, u32[]{:S(2)}) collective-permute-start(bf16[256,256]{1,0:T(8,128)(2,1)S(1)} %collective-permute-done.7.m2), channel_id=1, source_target_pairs={{0,1},{1,0},{2,3},{3,2},{4,5},{5,4},{6,7},{7,6},{8,9},{9,8},{10,11... | collective-permute-start | bytes 393224 | tf_op jit(solution)/shard_map/ppermute | solution.py:393
  63.7 2.0 %collective-permute-start.11 = (bf16[4,256,256]{2,1,0:T(8,128)(2,1)S(1)}, bf16[4,256,256]{2,1,0:T(8,128)(2,1)S(1)}, u32[]{:S(2)}, u32[]{:S(2)}) collective-permute-start(bf16[4,256,256]{2,1,0:T(8,128)(2,1)S(1)} %get-tuple-element.30), channel_id=1, source_target_pairs={{0,1},{1,0},{2,3},{3,2},{4,5},{5,4},{6,7},{7,6},{8,9},{9,8},{10,11... | collective-permute-start | bytes 1572872 | tf_op jit(solution)/shard_map/ppermute | solution.py:393
  65.9 7.9 %collective-permute-start.12 = (bf16[256,256]{1,0:T(8,128)(2,1)S(1)}, bf16[256,256]{1,0:T(8,128)(2,1)S(1)}, u32[]{:S(2)}, u32[]{:S(2)}) collective-permute-start(bf16[256,256]{1,0:T(8,128)(2,1)S(1)} %get-tuple-element.33), channel_id=1, source_target_pairs={{0,4},{1,5},{2,6},{3,7},{4,0},{5,1},{6,2},{7,3},{8,12},{9,13},{10,... | collective-permute-start | bytes 393224 | tf_op jit(solution)/shard_map/ppermute | solution.py:379
  66.0 7.8 %collective-permute-start.14 = (bf16[256,256]{1,0:T(8,128)(2,1)S(1)}, bf16[256,256]{1,0:T(8,128)(2,1)S(1)}, u32[]{:S(2)}, u32[]{:S(2)}) collective-permute-start(bf16[256,256]{1,0:T(8,128)(2,1)S(1)} %get-tuple-element.34), channel_id=1, source_target_pairs={{0,6},{1,7},{2,0},{3,1},{4,2},{5,3},{6,4},{7,5},{8,14},{9,15},{10,... | collective-permute-start | bytes 393224 | tf_op jit(solution)/shard_map/ppermute | solution.py:379
  67.4 8.4 %collective-permute-start.13 = (bf16[256,256]{1,0:T(8,128)(2,1)S(1)}, bf16[256,256]{1,0:T(8,128)(2,1)S(1)}, u32[]{:S(2)}, u32[]{:S(2)}) collective-permute-start(bf16[256,256]{1,0:T(8,128)(2,1)S(1)} %get-tuple-element.35), channel_id=1, source_target_pairs={{0,2},{1,3},{2,4},{3,5},{4,6},{5,7},{6,0},{7,1},{8,10},{9,11},{10,... | collective-permute-start | bytes 393224 | tf_op jit(solution)/shard_map/ppermute | solution.py:379

commit v7 on v4

--- a/solution.py
+++ b/solution.py
@@ -14,6 +14,7 @@
 SPAN = 16
 WIDTH = 128
 ROWS = 144
+VECTOR_STEPS = 5
 PITCH = 129
 MAP_ROWS = 144
 VMEM = pl.BlockSpec(memory_space=pltpu.VMEM)
@@ -263,11 +264,13 @@
             spread = jnp.broadcast_to(h, (WIDTH, WIDTH)).T
             last = off_ref[pl.ds(b * steps + g * SPAN + SPAN - 1, 1), :]
             parts = two_parts(h)
-            after.append(h * kept_ref[pl.ds(c, 1), :] + parts_times(parts, grp_ref[c]) + last)
-            rows = [jnp.sum(q_ref[s, c].astype(F32) * spread, axis=0, keepdims=True) for s in range(4)]
-            for s in range(4, SPAN, 2):
+            moved = h * kept_ref[pl.ds(c, 1), :] + parts_times(parts, grp_ref[c])
+            after.append(moved + last)
+            rows = [jnp.sum(q_ref[s, c].astype(F32) * spread, axis=0, keepdims=True) for s in range(VECTOR_STEPS)]
+            for s in range(VECTOR_STEPS, SPAN - 1, 2):
                 pair = parts_times(parts, jnp.concatenate([q_ref[s, c], q_ref[s + 1, c]], axis=1))
                 rows += [pair[:, :WIDTH], pair[:, WIDTH:]]
+            rows.append(moved)
             base = pl.multiple_of(g * SPAN, SPAN)
             states = jnp.concatenate(rows, axis=0) + off_ref[pl.ds(b * steps + base, SPAN), :]
             states_ref[pl.ds(base, SPAN), b * WIDTH : (b + 1) * WIDTH] = states
@@ -294,7 +297,7 @@
     )(kept, init, *y_maps, *x_maps, off, grp, gain, pltpu.with_memory_space_constraint(q, pltpu.VMEM))
 
 
-def forward_kernel(m0, m1, m2, m3, theirs_ref, gate_ref, up_ref, down_ref, keep_ref, send_ref, hidden):
+def forward_kernel(m0, m1, m3, m2, theirs_ref, gate_ref, up_ref, down_ref, send_ref, hidden):
     z, core = places()[2:]
     wide = 2 * WIDTH
 
@@ -302,7 +305,7 @@
         return pl.multiple_of((lax.rem(z + k, 4) * 2 + c) * wide, wide)
 
     parts = [(m0, 0, 0), (m1, 3, 0), (m2, 2, 0), (m3, 1, 0)]
-    parts += [(theirs_ref.at[k], (4 - k) % 4, 1) for k in range(4)]
+    parts += [(theirs_ref.at[i], (4 - k) % 4, 1) for i, k in enumerate((0, 1, 3, 2))]
     for n in range(0, gate_ref.shape[1], wide):
         gate = up = None
         for ref, k, other in parts:
@@ -313,26 +316,40 @@
             gate = g if gate is None else gate + g
             up = u if up is None else up + u
         hidden[:, n : n + wide] = (gate / (1.0 + jnp.exp(-gate)) * up).astype(BF16)
-    low = hidden[...]
-    for ref, c in ((send_ref, 1 - core), (keep_ref, core)):
-        for k in range(4):
-            out = jnp.dot(low, down_ref[:, pl.ds(at(k, c), wide)], preferred_element_type=F32)
-            ref[k] = out.astype(BF16)
+    for k in range(4):
+        columns = down_ref[:, pl.ds(at(k, 1 - core), wide)]
+        send_ref[k] = jnp.dot(hidden[...], columns, preferred_element_type=F32).astype(BF16)
+
+
+def keep_kernel(hidden, down_ref, keep_ref):
+    z, core = places()[2:]
+    wide = 2 * WIDTH
+    for k in range(4):
+        columns = down_ref[:, pl.ds(pl.multiple_of((lax.rem(z + k, 4) * 2 + core) * wide, wide), wide)]
+        keep_ref[k] = jnp.dot(hidden[...], columns, preferred_element_type=F32)
 
 
 def forward(mine, theirs, gate_weight, up_weight, down_weight):
-    steps = mine[0].shape[0]
+    steps, units = mine[0].shape[0], gate_weight.shape[1]
     weights = [pltpu.with_memory_space_constraint(w, pltpu.VMEM) for w in (gate_weight, up_weight, down_weight)]
-    half = jax.ShapeDtypeStruct((4, steps, 2 * WIDTH), BF16)
-    return pl.pallas_call(
+    params = pltpu.CompilerParams(vmem_limit_bytes=16_000_000)
+    sent, hidden = pl.pallas_call(
         forward_kernel,
-        out_shape=(half, half),
+        out_shape=(pltpu.VMEM((4, steps, 2 * WIDTH), BF16), pltpu.VMEM((steps, units), BF16)),
         in_specs=[VMEM] * 8,
         out_specs=(VMEM, VMEM),
-        scratch_shapes=[pltpu.VMEM((steps, gate_weight.shape[1]), BF16)],
-        compiler_params=pltpu.CompilerParams(vmem_limit_bytes=16_000_000),
+        compiler_params=params,
         name="forward",
     )(*mine, theirs, *weights)
+    kept = pl.pallas_call(
+        keep_kernel,
+        out_shape=pltpu.VMEM((4, steps, 2 * WIDTH), F32),
+        in_specs=[VMEM] * 2,
+        out_specs=VMEM,
+        compiler_params=params,
+        name="keep",
+    )(hidden, weights[2])
+    return kept, sent
 
 
 def x_back(v, k):
@@ -369,13 +386,13 @@
     states, normed = replay(
         kept, initial_state.reshape(2, WIDTH), y_maps, x_maps, off, grp, norm_gain.reshape(2, WIDTH), q
     )
-    mine = [normed] + [z_back(normed, k) for k in (1, 2, 3)]
+    mine = [normed] + [z_back(normed, k) for k in (1, 3, 2)]
     theirs = other_core(jnp.stack(mine))
     keep, sent = forward(mine, theirs, gate_weight, up_weight, down_weight)
-    chip = keep.astype(F32) + other_core(sent).astype(F32)
+    chip = keep + other_core(sent).astype(F32)
     low = chip.astype(BF16)
     mixed = chip[0]
-    for k in (1, 2, 3):
+    for k in (2, 1, 3):
         mixed = mixed + z_back(low[k], k).astype(F32)
     return (states + mixed).astype(BF16)
 

time: 73.5 us -> 72.6 us (0.988)
  waiting for transfers between devices: 26.6 us -> 24.6 us
    ppermute x6, waiting for transfers between devices: 12.8 us -> 11.5 us  [z_back(): lax.ppermute(v, 'block', [(z * 2 + c, (z + k) % 4 * 2 + c) for z in range...]
    ppermute x2, waiting for transfers between devices: 3.69 us -> 2.93 us  [other_core(): return lax.ppermute(v, 'block', [(s, s ^ 1) for s in range(8)])]
    pallas_call x1 -> x2, Pallas kernels: 3.49 us -> 3.69 us  [the longest x1 2.95 us: forward(): pl.pallas_call(forward_kernel, out_shape=(pltpu.VMEM((4, steps, 2 * WIDTH...]
  transfers between devices with their start and end apart: 14 -> 14, of which waited for: 14 -> 14; matrix products, arithmetic and copies ran while one was open for 0% -> 0% of each run, Pallas kernels for 0% -> 1%
where the time goes in v7:
time: 72.6 us; the launch traced here: 72.1 us
  Pallas kernels  27.6 us (38%)
  waiting for transfers between devices  24.6 us (34%)
  starting transfers between devices  18.8 us (26%)
  other arithmetic  0.96 us (1%)
    pallas_call x1, Pallas kernels, compose(): pl.pallas_call(compose_kernel, out_shape=(pltpu.VMEM((SPAN, 2 * GROUPS, W...  19.8 us
    ppermute x6, waiting for transfers between devices, z_back(): lax.ppermute(v, 'block', [(z * 2 + c, (z + k) % 4 * 2 + c) for z in range...  11.5 us
    ppermute x6, starting transfers between devices, z_back(): lax.ppermute(v, 'block', [(z * 2 + c, (z + k) % 4 * 2 + c) for z in range...  9.25 us
    ppermute x3, waiting for transfers between devices, x_back(): lax.ppermute(v, 'tm', [(y * 4 + x, y * 4 + (x + k) % 4) for y in range(4)...  5.12 us
    ppermute x3, waiting for transfers between devices, y_back(): lax.ppermute(v, 'tm', [(y * 4 + x, (y + k) % 4 * 4 + x) for y in range(4)...  5.04 us
    ppermute x3, starting transfers between devices, y_back(): lax.ppermute(v, 'tm', [(y * 4 + x, (y + k) % 4 * 4 + x) for y in range(4)...  4.69 us
    ppermute x3, starting transfers between devices, x_back(): lax.ppermute(v, 'tm', [(y * 4 + x, y * 4 + (x + k) % 4) for y in range(4)...  4.6 us
    pallas_call x1, Pallas kernels, replay(): pl.pallas_call(replay_kernel, out_shape=(jax.ShapeDtypeStruct((steps, 2 *...  3.61 us
  transfers between devices with their start and end apart: 14, of which 14 were waited for; matrix products, arithmetic and copies ran while one was open for 0% of the time, Pallas kernels for 1%

profile of v7, /device:TPU:0, one launch (start us, length us, event | category | flops | bytes accessed | tf_op | source)
XLA Modules:
  0.0 72.1 jit_solution(4832070051384503929)
XLA Ops:
  0.0 19.8 %compose.1 = (bf16[16,32,128,128]{3,2,1,0:T(8,128)(2,1)S(1)}, f32[512,128]{1,0:T(8,128)S(1)}, bf16[2,144,128]{2,1,0:T(8,128)(2,1)S(1)}, bf16[32,128,128]{2,1,0:T(8,128)(2,1)S(1)}, f32[32,128]{1,0:T(8,128)S(1)}) custom-call(f32[64,256]{1,0:T(8,128)} %bitcast.34, f32[2,256]{1,0:T(2,128)} %bitcast.35, f32[2,256]{1,0:T(2,128)} %bitcast.36, ...), custom_call_target="tpu_custom_call" | custom-call | tf_op jit(solution)/shard_map/compose/pallas_call | solution.py:193
  19.8 2.9 %collective-permute-start.2 = (bf16[2,144,128]{2,1,0:T(8,128)(2,1)S(1)}, bf16[2,144,128]{2,1,0:T(8,128)(2,1)S(1)}, u32[]{:S(2)}, u32[]{:S(2)}) collective-permute-start(bf16[2,144,128]{2,1,0:T(8,128)(2,1)S(1)} %get-tuple-element.15.m0), channel_id=1, source_target_pairs={{0,24},{8,0},{16,8},{24,16},{32,56},{40,32},{48,40},{56,48},{64,88... | collective-permute-start | bytes 221192 | tf_op jit(solution)/shard_map/ppermute | solution.py:356
  22.7 0.8 %collective-permute-start.1 = (bf16[2,144,128]{2,1,0:T(8,128)(2,1)S(1)}, bf16[2,144,128]{2,1,0:T(8,128)(2,1)S(1)}, u32[]{:S(2)}, u32[]{:S(2)}) collective-permute-start(bf16[2,144,128]{2,1,0:T(8,128)(2,1)S(1)} %get-tuple-element.15.m0), channel_id=1, source_target_pairs={{0,16},{8,24},{16,0},{24,8},{32,48},{40,56},{48,32},{56,40},{64,80... | collective-permute-start | bytes 221192 | tf_op jit(solution)/shard_map/ppermute | solution.py:356
  23.5 0.9 %collective-permute-start = (bf16[2,144,128]{2,1,0:T(8,128)(2,1)S(1)}, bf16[2,144,128]{2,1,0:T(8,128)(2,1)S(1)}, u32[]{:S(2)}, u32[]{:S(2)}) collective-permute-start(bf16[2,144,128]{2,1,0:T(8,128)(2,1)S(1)} %get-tuple-element.15.m0), channel_id=1, source_target_pairs={{0,8},{8,16},{16,24},{24,0},{32,40},{40,48},{48,56},{56,32},{64,72... | collective-permute-start | bytes 221192 | tf_op jit(solution)/shard_map/ppermute | solution.py:356
  24.4 0.7 collective-permute-done.2.m3.x3
  25.1 3.7 %collective-permute-done.1.m2.x2 = bf16[2,144,128]{2,1,0:T(8,128)(2,1)S(1)} collective-permute-done((bf16[2,144,128]{2,1,0:T(8,128)(2,1)S(1)}, bf16[2,144,128]{2,1,0:T(8,128)(2,1)S(1)}, u32[]{:S(2)}, u32[]{:S(2)}) %collective-permute-start.1) | collective-permute-done | bytes 73760 | tf_op jit(solution)/shard_map/ppermute | solution.py:356
  28.8 0.7 %collective-permute-done.m1.x1 = bf16[2,144,128]{2,1,0:T(8,128)(2,1)S(1)} collective-permute-done((bf16[2,144,128]{2,1,0:T(8,128)(2,1)S(1)}, bf16[2,144,128]{2,1,0:T(8,128)(2,1)S(1)}, u32[]{:S(2)}, u32[]{:S(2)}) %collective-permute-start) | collective-permute-done | bytes 73760 | tf_op jit(solution)/shard_map/ppermute | solution.py:356
  29.5 0.5 row_map.1
  30.0 3.1 %collective-permute-start.5 = (bf16[2,144,128]{2,1,0:T(8,128)(2,1)S(1)}, bf16[2,144,128]{2,1,0:T(8,128)(2,1)S(1)}, u32[]{:S(2)}, u32[]{:S(2)}) collective-permute-start(bf16[2,144,128]{2,1,0:T(8,128)(2,1)S(1)} %row_map.1), channel_id=1, source_target_pairs={{0,96},{8,104},{16,112},{24,120},{32,0},{40,8},{48,16},{56,24},{64... | collective-permute-start | bytes 221192 | tf_op jit(solution)/shard_map/ppermute | solution.py:360
  33.1 0.6 collective-permute-start.4
  33.7 1.0 %collective-permute-start.3 = (bf16[2,144,128]{2,1,0:T(8,128)(2,1)S(1)}, bf16[2,144,128]{2,1,0:T(8,128)(2,1)S(1)}, u32[]{:S(2)}, u32[]{:S(2)}) collective-permute-start(bf16[2,144,128]{2,1,0:T(8,128)(2,1)S(1)} %row_map.1), channel_id=1, source_target_pairs={{0,32},{8,40},{16,48},{24,56},{32,64},{40,72},{48,80},{56,88},{64,... | collective-permute-start | bytes 221192 | tf_op jit(solution)/shard_map/ppermute | solution.py:360
  34.7 0.5 collective-permute-done.5.y3
  35.2 3.8 %collective-permute-done.4.y2 = bf16[2,144,128]{2,1,0:T(8,128)(2,1)S(1)} collective-permute-done((bf16[2,144,128]{2,1,0:T(8,128)(2,1)S(1)}, bf16[2,144,128]{2,1,0:T(8,128)(2,1)S(1)}, u32[]{:S(2)}, u32[]{:S(2)}) %collective-permute-start.4) | collective-permute-done | bytes 73760 | tf_op jit(solution)/shard_map/ppermute | solution.py:360
  39.0 0.7 %collective-permute-done.3.y1 = bf16[2,144,128]{2,1,0:T(8,128)(2,1)S(1)} collective-permute-done((bf16[2,144,128]{2,1,0:T(8,128)(2,1)S(1)}, bf16[2,144,128]{2,1,0:T(8,128)(2,1)S(1)}, u32[]{:S(2)}, u32[]{:S(2)}) %collective-permute-start.3) | collective-permute-done | bytes 73760 | tf_op jit(solution)/shard_map/ppermute | solution.py:360
  39.8 3.6 %replay.1 = (f32[256,256]{1,0:T(8,128)S(1)}, bf16[256,256]{1,0:T(8,128)(2,1)S(1)}) custom-call(f32[32,128]{1,0:T(8,128)S(1)} %get-tuple-element.14.kept_ref, f32[2,128]{1,0:T(2,128)S(1)} %bitcast.31, bf16[2,144,128]{2,1,0:T(8,128)(2,1)S(1)} %collective-permute-done.3.y1, bf16[2,144,128]{2,1,0:T(8,128)(2,1)S(1)} %collective-permute-done.4.y2, ...), custom_call_target="tpu_custom_call" | custom-call | tf_op jit(solution)/shard_map/replay/pallas_call | solution.py:287
  43.4 4.0 %collective-permute-start.8 = (bf16[256,256]{1,0:T(8,128)(2,1)S(1)}, bf16[256,256]{1,0:T(8,128)(2,1)S(1)}, u32[]{:S(2)}, u32[]{:S(2)}) collective-permute-start(bf16[256,256]{1,0:T(8,128)(2,1)S(1)} %get-tuple-element.20.m0), channel_id=1, source_target_pairs={{0,4},{1,5},{2,6},{3,7},{4,0},{5,1},{6,2},{7,3},{8,12},{9,13},{10,... | collective-permute-start | bytes 393224 | tf_op jit(solution)/shard_map/ppermute | solution.py:364
  47.3 0.7 collective-permute-start.7
  48.1 1.3 %collective-permute-start.6 = (bf16[256,256]{1,0:T(8,128)(2,1)S(1)}, bf16[256,256]{1,0:T(8,128)(2,1)S(1)}, u32[]{:S(2)}, u32[]{:S(2)}) collective-permute-start(bf16[256,256]{1,0:T(8,128)(2,1)S(1)} %get-tuple-element.20.m0), channel_id=1, source_target_pairs={{0,2},{1,3},{2,4},{3,5},{4,6},{5,7},{6,0},{7,1},{8,10},{9,11},{10,... | collective-permute-start | bytes 393224 | tf_op jit(solution)/shard_map/ppermute | solution.py:364
  49.4 1.4 %collective-permute-done.8.m2 = bf16[256,256]{1,0:T(8,128)(2,1)S(1)} collective-permute-done((bf16[256,256]{1,0:T(8,128)(2,1)S(1)}, bf16[256,256]{1,0:T(8,128)(2,1)S(1)}, u32[]{:S(2)}, u32[]{:S(2)}) %collective-permute-start.8) | collective-permute-done | bytes 131104 | tf_op jit(solution)/shard_map/ppermute | solution.py:364
  50.8 1.9 %collective-permute-done.7.m3 = bf16[256,256]{1,0:T(8,128)(2,1)S(1)} collective-permute-done((bf16[256,256]{1,0:T(8,128)(2,1)S(1)}, bf16[256,256]{1,0:T(8,128)(2,1)S(1)}, u32[]{:S(2)}, u32[]{:S(2)}) %collective-permute-start.7) | collective-permute-done | bytes 131104 | tf_op jit(solution)/shard_map/ppermute | solution.py:364
  52.7 1.5 %collective-permute-done.6.m1 = bf16[256,256]{1,0:T(8,128)(2,1)S(1)} collective-permute-done((bf16[256,256]{1,0:T(8,128)(2,1)S(1)}, bf16[256,256]{1,0:T(8,128)(2,1)S(1)}, u32[]{:S(2)}, u32[]{:S(2)}) %collective-permute-start.6) | collective-permute-done | bytes 131104 | tf_op jit(solution)/shard_map/ppermute | solution.py:364
  54.4 1.9 %collective-permute-done.9.theirs_ref = bf16[4,256,256]{2,1,0:T(8,128)(2,1)S(1)} collective-permute-done((bf16[4,256,256]{2,1,0:T(8,128)(2,1)S(1)}, bf16[4,256,256]{2,1,0:T(8,128)(2,1)S(1)}, u32[]{:S(2)}, u32[]{:S(2)}) %collective-permute-start.9) | collective-permute-done | bytes 524320 | tf_op jit(solution)/shard_map/ppermute | solution.py:368
  56.3 2.9 %forward.1 = (bf16[4,256,256]{2,1,0:T(8,128)(2,1)S(1)}, bf16[256,1024]{1,0:T(8,128)(2,1)S(1)}) custom-call(bf16[256,256]{1,0:T(8,128)(2,1)S(1)} %get-tuple-element.20.m0, bf16[256,256]{1,0:T(8,128)(2,1)S(1)} %collective-permute-done.6.m1, bf16[256,256]{1,0:T(8,128)(2,1)S(1)} %collective-permute-done.7.m3, bf16[256,256]{1,0:T(8,128)(2,1)S(1)} %collective-permute-done.8.m2, ...), custom_call_target="tpu_custom_call" | custom-call | tf_op jit(solution)/shard_map/forward/pallas_call | solution.py:336
  59.5 0.7 %keep.1 = f32[4,256,256]{2,1,0:T(8,128)S(1)} custom-call(bf16[256,1024]{1,0:T(8,128)(2,1)S(1)} %get-tuple-element.21.hidden, bf16[1024,2048]{1,0:T(8,128)(2,1)S(1)} %copy-done), custom_call_target="tpu_custom_call" | custom-call | tf_op jit(solution)/shard_map/keep/pallas_call | solution.py:344
  60.2 1.0 %collective-permute-done.10 = bf16[4,256,256]{2,1,0:T(8,128)(2,1)S(1)} collective-permute-done((bf16[4,256,256]{2,1,0:T(8,128)(2,1)S(1)}, bf16[4,256,256]{2,1,0:T(8,128)(2,1)S(1)}, u32[]{:S(2)}, u32[]{:S(2)}) %collective-permute-start.10) | collective-permute-done | bytes 524320 | tf_op jit(solution)/shard_map/ppermute | solution.py:368
  61.4 1.2 %collective-permute-start.11 = (bf16[256,256]{1,0:T(8,128)(2,1)S(1)}, bf16[256,256]{1,0:T(8,128)(2,1)S(1)}, u32[]{:S(2)}, u32[]{:S(2)}) collective-permute-start(bf16[256,256]{1,0:T(8,128)(2,1)S(1)} %get-tuple-element.25), channel_id=1, source_target_pairs={{0,4},{1,5},{2,6},{3,7},{4,0},{5,1},{6,2},{7,3},{8,12},{9,13},{10,... | collective-permute-start | bytes 393224 | tf_op jit(solution)/shard_map/ppermute | solution.py:364
  62.7 1.6 %collective-permute-start.13 = (bf16[256,256]{1,0:T(8,128)(2,1)S(1)}, bf16[256,256]{1,0:T(8,128)(2,1)S(1)}, u32[]{:S(2)}, u32[]{:S(2)}) collective-permute-start(bf16[256,256]{1,0:T(8,128)(2,1)S(1)} %get-tuple-element.26), channel_id=1, source_target_pairs={{0,6},{1,7},{2,0},{3,1},{4,2},{5,3},{6,4},{7,5},{8,14},{9,15},{10,... | collective-permute-start | bytes 393224 | tf_op jit(solution)/shard_map/ppermute | solution.py:364
  64.3 0.4 collective-permute-start.12
  64.7 4.6 %collective-permute-done.11 = bf16[256,256]{1,0:T(8,128)(2,1)S(1)} collective-permute-done((bf16[256,256]{1,0:T(8,128)(2,1)S(1)}, bf16[256,256]{1,0:T(8,128)(2,1)S(1)}, u32[]{:S(2)}, u32[]{:S(2)}) %collective-permute-start.11) | collective-permute-done | bytes 131104 | tf_op jit(solution)/shard_map/ppermute | solution.py:364
  69.4 0.5 collective-permute-done.13
  69.9 1.5 %collective-permute-done.12 = bf16[256,256]{1,0:T(8,128)(2,1)S(1)} collective-permute-done((bf16[256,256]{1,0:T(8,128)(2,1)S(1)}, bf16[256,256]{1,0:T(8,128)(2,1)S(1)}, u32[]{:S(2)}, u32[]{:S(2)}) %collective-permute-start.12) | collective-permute-done | bytes 131104 | tf_op jit(solution)/shard_map/ppermute | solution.py:364
  71.4 0.7 %fusion.4 = bf16[256,256]{1,0:T(8,128)(2,1)} fusion(f32[256,256]{1,0:T(8,128)S(1)} %get-tuple-element.19, f32[4,256,256]{2,1,0:T(8,128)S(1)} %get-tuple-element.24, bf16[256,256]{1,0:T(8,128)(2,1)S(1)} %collective-permute-done.13, bf16[256,256]{1,0:T(8,128)(2,1)S(1)} %collective-permute-done.12, bf16[256,256]{1,0:T(8,128)(2,1)S(1)} %collective-permute-done.11), kind=kLoop, calls=%fused_computation.7 | loop fusion | flops 524288 | bytes 1048576 | tf_op jit(solution)/shard_map/convert_element_type | solution.py:397
  (15 shorter events, 0.6 us)
Async XLA Ops:
  0.0 39.8 %copy-start.4 = (f32[256]{0:T(256)S(1)}, f32[256]{0:T(256)}, u32[]{:S(2)}) copy-start(f32[256]{0:T(256)} %param.14) | copy-start | bytes 3076
  0.0 39.8 %copy-start.3 = (f32[256]{0:T(256)S(1)}, f32[256]{0:T(256)}, u32[]{:S(2)}) copy-start(f32[256]{0:T(256)} %param.13) | copy-start | bytes 3076
  19.8 5.3 %collective-permute-start.2 = (bf16[2,144,128]{2,1,0:T(8,128)(2,1)S(1)}, bf16[2,144,128]{2,1,0:T(8,128)(2,1)S(1)}, u32[]{:S(2)}, u32[]{:S(2)}) collective-permute-start(bf16[2,144,128]{2,1,0:T(8,128)(2,1)S(1)} %get-tuple-element.15.m0), channel_id=1, source_target_pairs={{0,24},{8,0},{16,8},{24,16},{32,56},{40,32},{48,40},{56,48},{64,88... | collective-permute-start | bytes 221192 | tf_op jit(solution)/shard_map/ppermute | solution.py:356
  22.7 6.1 %collective-permute-start.1 = (bf16[2,144,128]{2,1,0:T(8,128)(2,1)S(1)}, bf16[2,144,128]{2,1,0:T(8,128)(2,1)S(1)}, u32[]{:S(2)}, u32[]{:S(2)}) collective-permute-start(bf16[2,144,128]{2,1,0:T(8,128)(2,1)S(1)} %get-tuple-element.15.m0), channel_id=1, source_target_pairs={{0,16},{8,24},{16,0},{24,8},{32,48},{40,56},{48,32},{56,40},{64,80... | collective-permute-start | bytes 221192 | tf_op jit(solution)/shard_map/ppermute | solution.py:356
  23.5 6.0 %collective-permute-start = (bf16[2,144,128]{2,1,0:T(8,128)(2,1)S(1)}, bf16[2,144,128]{2,1,0:T(8,128)(2,1)S(1)}, u32[]{:S(2)}, u32[]{:S(2)}) collective-permute-start(bf16[2,144,128]{2,1,0:T(8,128)(2,1)S(1)} %get-tuple-element.15.m0), channel_id=1, source_target_pairs={{0,8},{8,16},{16,24},{24,0},{32,40},{40,48},{48,56},{56,32},{64,72... | collective-permute-start | bytes 221192 | tf_op jit(solution)/shard_map/ppermute | solution.py:356
  30.0 5.2 %collective-permute-start.5 = (bf16[2,144,128]{2,1,0:T(8,128)(2,1)S(1)}, bf16[2,144,128]{2,1,0:T(8,128)(2,1)S(1)}, u32[]{:S(2)}, u32[]{:S(2)}) collective-permute-start(bf16[2,144,128]{2,1,0:T(8,128)(2,1)S(1)} %row_map.1), channel_id=1, source_target_pairs={{0,96},{8,104},{16,112},{24,120},{32,0},{40,8},{48,16},{56,24},{64... | collective-permute-start | bytes 221192 | tf_op jit(solution)/shard_map/ppermute | solution.py:360
  33.1 5.9 %collective-permute-start.4 = (bf16[2,144,128]{2,1,0:T(8,128)(2,1)S(1)}, bf16[2,144,128]{2,1,0:T(8,128)(2,1)S(1)}, u32[]{:S(2)}, u32[]{:S(2)}) collective-permute-start(bf16[2,144,128]{2,1,0:T(8,128)(2,1)S(1)} %row_map.1), channel_id=1, source_target_pairs={{0,64},{8,72},{16,80},{24,88},{32,96},{40,104},{48,112},{56,120},{... | collective-permute-start | bytes 221192 | tf_op jit(solution)/shard_map/ppermute | solution.py:360
  33.7 6.0 %collective-permute-start.3 = (bf16[2,144,128]{2,1,0:T(8,128)(2,1)S(1)}, bf16[2,144,128]{2,1,0:T(8,128)(2,1)S(1)}, u32[]{:S(2)}, u32[]{:S(2)}) collective-permute-start(bf16[2,144,128]{2,1,0:T(8,128)(2,1)S(1)} %row_map.1), channel_id=1, source_target_pairs={{0,32},{8,40},{16,48},{24,56},{32,64},{40,72},{48,80},{56,88},{64,... | collective-permute-start | bytes 221192 | tf_op jit(solution)/shard_map/ppermute | solution.py:360
  39.8 16.5 %copy-start = (bf16[1024,2048]{1,0:T(8,128)(2,1)S(1)}, bf16[1024,2048]{1,0:T(8,128)(2,1)}, u32[]{:S(2)}) copy-start(bf16[1024,2048]{1,0:T(8,128)(2,1)} %down_ref.3) | copy-start | bytes 12582916
  39.8 16.5 %copy-start.1 = (bf16[2048,1024]{1,0:T(8,128)(2,1)S(1)}, bf16[2048,1024]{1,0:T(8,128)(2,1)}, u32[]{:S(2)}) copy-start(bf16[2048,1024]{1,0:T(8,128)(2,1)} %gate_ref.1) | copy-start | bytes 12582916
  39.8 16.5 %copy-start.2 = (bf16[2048,1024]{1,0:T(8,128)(2,1)S(1)}, bf16[2048,1024]{1,0:T(8,128)(2,1)}, u32[]{:S(2)}) copy-start(bf16[2048,1024]{1,0:T(8,128)(2,1)} %up_ref.1) | copy-start | bytes 12582916
  43.4 7.4 %collective-permute-start.8 = (bf16[256,256]{1,0:T(8,128)(2,1)S(1)}, bf16[256,256]{1,0:T(8,128)(2,1)S(1)}, u32[]{:S(2)}, u32[]{:S(2)}) collective-permute-start(bf16[256,256]{1,0:T(8,128)(2,1)S(1)} %get-tuple-element.20.m0), channel_id=1, source_target_pairs={{0,4},{1,5},{2,6},{3,7},{4,0},{5,1},{6,2},{7,3},{8,12},{9,13},{10,... | collective-permute-start | bytes 393224 | tf_op jit(solution)/shard_map/ppermute | solution.py:364
  47.3 5.4 %collective-permute-start.7 = (bf16[256,256]{1,0:T(8,128)(2,1)S(1)}, bf16[256,256]{1,0:T(8,128)(2,1)S(1)}, u32[]{:S(2)}, u32[]{:S(2)}) collective-permute-start(bf16[256,256]{1,0:T(8,128)(2,1)S(1)} %get-tuple-element.20.m0), channel_id=1, source_target_pairs={{0,6},{1,7},{2,0},{3,1},{4,2},{5,3},{6,4},{7,5},{8,14},{9,15},{10,... | collective-permute-start | bytes 393224 | tf_op jit(solution)/shard_map/ppermute | solution.py:364
  48.1 6.2 %collective-permute-start.6 = (bf16[256,256]{1,0:T(8,128)(2,1)S(1)}, bf16[256,256]{1,0:T(8,128)(2,1)S(1)}, u32[]{:S(2)}, u32[]{:S(2)}) collective-permute-start(bf16[256,256]{1,0:T(8,128)(2,1)S(1)} %get-tuple-element.20.m0), channel_id=1, source_target_pairs={{0,2},{1,3},{2,4},{3,5},{4,6},{5,7},{6,0},{7,1},{8,10},{9,11},{10,... | collective-permute-start | bytes 393224 | tf_op jit(solution)/shard_map/ppermute | solution.py:364
  54.3 2.0 %collective-permute-start.9 = (bf16[4,256,256]{2,1,0:T(8,128)(2,1)S(1)}, bf16[4,256,256]{2,1,0:T(8,128)(2,1)S(1)}, u32[]{:S(2)}, u32[]{:S(2)}) collective-permute-start(bf16[4,256,256]{2,1,0:T(8,128)(2,1)S(1)} %pad_maximum_fusion), channel_id=1, source_target_pairs={{0,1},{1,0},{2,3},{3,2},{4,5},{5,4},{6,7},{7,6},{8,9},{9,8},{10,11... | collective-permute-start | bytes 1572872 | tf_op jit(solution)/shard_map/ppermute | solution.py:368
  59.3 2.0 %collective-permute-start.10 = (bf16[4,256,256]{2,1,0:T(8,128)(2,1)S(1)}, bf16[4,256,256]{2,1,0:T(8,128)(2,1)S(1)}, u32[]{:S(2)}, u32[]{:S(2)}) collective-permute-start(bf16[4,256,256]{2,1,0:T(8,128)(2,1)S(1)} %get-tuple-element.22), channel_id=1, source_target_pairs={{0,1},{1,0},{2,3},{3,2},{4,5},{5,4},{6,7},{7,6},{8,9},{9,8},{10,11... | collective-permute-start | bytes 1572872 | tf_op jit(solution)/shard_map/ppermute | solution.py:368
  61.4 7.9 %collective-permute-start.11 = (bf16[256,256]{1,0:T(8,128)(2,1)S(1)}, bf16[256,256]{1,0:T(8,128)(2,1)S(1)}, u32[]{:S(2)}, u32[]{:S(2)}) collective-permute-start(bf16[256,256]{1,0:T(8,128)(2,1)S(1)} %get-tuple-element.25), channel_id=1, source_target_pairs={{0,4},{1,5},{2,6},{3,7},{4,0},{5,1},{6,2},{7,3},{8,12},{9,13},{10,... | collective-permute-start | bytes 393224 | tf_op jit(solution)/shard_map/ppermute | solution.py:364
  62.7 7.2 %collective-permute-start.13 = (bf16[256,256]{1,0:T(8,128)(2,1)S(1)}, bf16[256,256]{1,0:T(8,128)(2,1)S(1)}, u32[]{:S(2)}, u32[]{:S(2)}) collective-permute-start(bf16[256,256]{1,0:T(8,128)(2,1)S(1)} %get-tuple-element.26), channel_id=1, source_target_pairs={{0,6},{1,7},{2,0},{3,1},{4,2},{5,3},{6,4},{7,5},{8,14},{9,15},{10,... | collective-permute-start | bytes 393224 | tf_op jit(solution)/shard_map/ppermute | solution.py:364
  64.3 7.1 %collective-permute-start.12 = (bf16[256,256]{1,0:T(8,128)(2,1)S(1)}, bf16[256,256]{1,0:T(8,128)(2,1)S(1)}, u32[]{:S(2)}, u32[]{:S(2)}) collective-permute-start(bf16[256,256]{1,0:T(8,128)(2,1)S(1)} %get-tuple-element.27), channel_id=1, source_target_pairs={{0,2},{1,3},{2,4},{3,5},{4,6},{5,7},{6,0},{7,1},{8,10},{9,11},{10,... | collective-permute-start | bytes 393224 | tf_op jit(solution)/shard_map/ppermute | solution.py:364

commit v8 on v7

--- a/solution.py
+++ b/solution.py
@@ -15,6 +15,7 @@
 WIDTH = 128
 ROWS = 144
 VECTOR_STEPS = 5
+CHIPS = (0, 2, 3, 1)
 PITCH = 129
 MAP_ROWS = 144
 VMEM = pl.BlockSpec(memory_space=pltpu.VMEM)
@@ -297,15 +298,15 @@
     )(kept, init, *y_maps, *x_maps, off, grp, gain, pltpu.with_memory_space_constraint(q, pltpu.VMEM))
 
 
-def forward_kernel(m0, m1, m3, m2, theirs_ref, gate_ref, up_ref, down_ref, send_ref, hidden):
+def forward_kernel(m0, m2, m3, m1, theirs_ref, gate_ref, up_ref, down_ref, send_ref, hidden):
     z, core = places()[2:]
     wide = 2 * WIDTH
 
     def at(k, c):
-        return pl.multiple_of((lax.rem(z + k, 4) * 2 + c) * wide, wide)
-
-    parts = [(m0, 0, 0), (m1, 3, 0), (m2, 2, 0), (m3, 1, 0)]
-    parts += [(theirs_ref.at[i], (4 - k) % 4, 1) for i, k in enumerate((0, 1, 3, 2))]
+        return pl.multiple_of((lax.bitwise_xor(z, k) * 2 + c) * wide, wide)
+
+    parts = [(ref, k, 0) for k, ref in zip(CHIPS, (m0, m2, m3, m1))]
+    parts += [(theirs_ref.at[i], k, 1) for i, k in enumerate(CHIPS)]
     for n in range(0, gate_ref.shape[1], wide):
         gate = up = None
         for ref, k, other in parts:
@@ -325,7 +326,7 @@
     z, core = places()[2:]
     wide = 2 * WIDTH
     for k in range(4):
-        columns = down_ref[:, pl.ds(pl.multiple_of((lax.rem(z + k, 4) * 2 + core) * wide, wide), wide)]
+        columns = down_ref[:, pl.ds(pl.multiple_of((lax.bitwise_xor(z, k) * 2 + core) * wide, wide), wide)]
         keep_ref[k] = jnp.dot(hidden[...], columns, preferred_element_type=F32)
 
 
@@ -360,8 +361,8 @@
     return lax.ppermute(v, "tm", [(y * 4 + x, (y + k) % 4 * 4 + x) for y in range(4) for x in range(4)])
 
 
-def z_back(v, k):
-    return lax.ppermute(v, "block", [(z * 2 + c, (z + k) % 4 * 2 + c) for z in range(4) for c in range(2)])
+def z_exchange(v, k):
+    return lax.ppermute(v, "block", [(z * 2 + c, (z ^ k) * 2 + c) for z in range(4) for c in range(2)])
 
 
 def other_core(v):
@@ -386,14 +387,14 @@
     states, normed = replay(
         kept, initial_state.reshape(2, WIDTH), y_maps, x_maps, off, grp, norm_gain.reshape(2, WIDTH), q
     )
-    mine = [normed] + [z_back(normed, k) for k in (1, 3, 2)]
+    mine = [normed if k == 0 else z_exchange(normed, k) for k in CHIPS]
     theirs = other_core(jnp.stack(mine))
     keep, sent = forward(mine, theirs, gate_weight, up_weight, down_weight)
     chip = keep + other_core(sent).astype(F32)
     low = chip.astype(BF16)
     mixed = chip[0]
-    for k in (2, 1, 3):
-        mixed = mixed + z_back(low[k], k).astype(F32)
+    for k in (1, 2, 3):
+        mixed = mixed + z_exchange(low[k], k).astype(F32)
     return (states + mixed).astype(BF16)
 
 

time: 72.6 us -> 73 us (level)
  transfers between devices with their start and end apart: 14 -> 14, of which waited for: 14 -> 13; matrix products, arithmetic and copies ran while one was open for 0% -> 0% of each run, Pallas kernels for 1% -> 1%
where the time goes in v8:
time: 73 us; the launch traced here: 72.7 us
  Pallas kernels  27.6 us (38%)
  waiting for transfers between devices  24.7 us (34%)
  starting transfers between devices  19.3 us (26%)
  other arithmetic  0.96 us (1%)
    pallas_call x1, Pallas kernels, compose(): pl.pallas_call(compose_kernel, out_shape=(pltpu.VMEM((SPAN, 2 * GROUPS, W...  19.8 us
    ppermute x6, waiting for transfers between devices, z_exchange(): lax.ppermute(v, 'block', [(z * 2 + c, (z ^ k) * 2 + c) for z in range(4)...  11.6 us
    ppermute x6, starting transfers between devices, z_exchange(): lax.ppermute(v, 'block', [(z * 2 + c, (z ^ k) * 2 + c) for z in range(4)...  9.75 us
    ppermute x3, waiting for transfers between devices, x_back(): lax.ppermute(v, 'tm', [(y * 4 + x, y * 4 + (x + k) % 4) for y in range(4)...  5.12 us
    ppermute x3, waiting for transfers between devices, y_back(): lax.ppermute(v, 'tm', [(y * 4 + x, (y + k) % 4 * 4 + x) for y in range(4)...  5.04 us
    ppermute x3, starting transfers between devices, y_back(): lax.ppermute(v, 'tm', [(y * 4 + x, (y + k) % 4 * 4 + x) for y in range(4)...  4.69 us
    ppermute x3, starting transfers between devices, x_back(): lax.ppermute(v, 'tm', [(y * 4 + x, y * 4 + (x + k) % 4) for y in range(4)...  4.6 us
    pallas_call x1, Pallas kernels, replay(): pl.pallas_call(replay_kernel, out_shape=(jax.ShapeDtypeStruct((steps, 2 *...  3.61 us
  transfers between devices with their start and end apart: 14, of which 13 were waited for; matrix products, arithmetic and copies ran while one was open for 0% of the time, Pallas kernels for 1%

profile of v8, /device:TPU:0, one launch (start us, length us, event | category | flops | bytes accessed | tf_op | source)
XLA Modules:
  0.0 72.7 jit_solution(17702442127135262535)
XLA Ops:
  0.0 19.8 %compose.1 = (bf16[16,32,128,128]{3,2,1,0:T(8,128)(2,1)S(1)}, f32[512,128]{1,0:T(8,128)S(1)}, bf16[2,144,128]{2,1,0:T(8,128)(2,1)S(1)}, bf16[32,128,128]{2,1,0:T(8,128)(2,1)S(1)}, f32[32,128]{1,0:T(8,128)S(1)}) custom-call(f32[64,256]{1,0:T(8,128)} %bitcast.34, f32[2,256]{1,0:T(2,128)} %bitcast.35, f32[2,256]{1,0:T(2,128)} %bitcast.36, ...), custom_call_target="tpu_custom_call" | custom-call | tf_op jit(solution)/shard_map/compose/pallas_call | solution.py:194
  19.8 2.9 %collective-permute-start.2 = (bf16[2,144,128]{2,1,0:T(8,128)(2,1)S(1)}, bf16[2,144,128]{2,1,0:T(8,128)(2,1)S(1)}, u32[]{:S(2)}, u32[]{:S(2)}) collective-permute-start(bf16[2,144,128]{2,1,0:T(8,128)(2,1)S(1)} %get-tuple-element.15.m0), channel_id=1, source_target_pairs={{0,24},{8,0},{16,8},{24,16},{32,56},{40,32},{48,40},{56,48},{64,88... | collective-permute-start | bytes 221192 | tf_op jit(solution)/shard_map/ppermute | solution.py:357
  22.7 0.8 %collective-permute-start.1 = (bf16[2,144,128]{2,1,0:T(8,128)(2,1)S(1)}, bf16[2,144,128]{2,1,0:T(8,128)(2,1)S(1)}, u32[]{:S(2)}, u32[]{:S(2)}) collective-permute-start(bf16[2,144,128]{2,1,0:T(8,128)(2,1)S(1)} %get-tuple-element.15.m0), channel_id=1, source_target_pairs={{0,16},{8,24},{16,0},{24,8},{32,48},{40,56},{48,32},{56,40},{64,80... | collective-permute-start | bytes 221192 | tf_op jit(solution)/shard_map/ppermute | solution.py:357
  23.5 0.9 %collective-permute-start = (bf16[2,144,128]{2,1,0:T(8,128)(2,1)S(1)}, bf16[2,144,128]{2,1,0:T(8,128)(2,1)S(1)}, u32[]{:S(2)}, u32[]{:S(2)}) collective-permute-start(bf16[2,144,128]{2,1,0:T(8,128)(2,1)S(1)} %get-tuple-element.15.m0), channel_id=1, source_target_pairs={{0,8},{8,16},{16,24},{24,0},{32,40},{40,48},{48,56},{56,32},{64,72... | collective-permute-start | bytes 221192 | tf_op jit(solution)/shard_map/ppermute | solution.py:357
  24.4 0.7 collective-permute-done.2.m3.x3
  25.1 3.7 %collective-permute-done.1.m2.x2 = bf16[2,144,128]{2,1,0:T(8,128)(2,1)S(1)} collective-permute-done((bf16[2,144,128]{2,1,0:T(8,128)(2,1)S(1)}, bf16[2,144,128]{2,1,0:T(8,128)(2,1)S(1)}, u32[]{:S(2)}, u32[]{:S(2)}) %collective-permute-start.1) | collective-permute-done | bytes 73760 | tf_op jit(solution)/shard_map/ppermute | solution.py:357
  28.8 0.7 %collective-permute-done.m1.x1 = bf16[2,144,128]{2,1,0:T(8,128)(2,1)S(1)} collective-permute-done((bf16[2,144,128]{2,1,0:T(8,128)(2,1)S(1)}, bf16[2,144,128]{2,1,0:T(8,128)(2,1)S(1)}, u32[]{:S(2)}, u32[]{:S(2)}) %collective-permute-start) | collective-permute-done | bytes 73760 | tf_op jit(solution)/shard_map/ppermute | solution.py:357
  29.5 0.5 row_map.1
  30.0 3.1 %collective-permute-start.5 = (bf16[2,144,128]{2,1,0:T(8,128)(2,1)S(1)}, bf16[2,144,128]{2,1,0:T(8,128)(2,1)S(1)}, u32[]{:S(2)}, u32[]{:S(2)}) collective-permute-start(bf16[2,144,128]{2,1,0:T(8,128)(2,1)S(1)} %row_map.1), channel_id=1, source_target_pairs={{0,96},{8,104},{16,112},{24,120},{32,0},{40,8},{48,16},{56,24},{64... | collective-permute-start | bytes 221192 | tf_op jit(solution)/shard_map/ppermute | solution.py:361
  33.1 0.6 collective-permute-start.4
  33.7 1.0 %collective-permute-start.3 = (bf16[2,144,128]{2,1,0:T(8,128)(2,1)S(1)}, bf16[2,144,128]{2,1,0:T(8,128)(2,1)S(1)}, u32[]{:S(2)}, u32[]{:S(2)}) collective-permute-start(bf16[2,144,128]{2,1,0:T(8,128)(2,1)S(1)} %row_map.1), channel_id=1, source_target_pairs={{0,32},{8,40},{16,48},{24,56},{32,64},{40,72},{48,80},{56,88},{64,... | collective-permute-start | bytes 221192 | tf_op jit(solution)/shard_map/ppermute | solution.py:361
  34.7 0.5 collective-permute-done.5.y3
  35.2 3.8 %collective-permute-done.4.y2 = bf16[2,144,128]{2,1,0:T(8,128)(2,1)S(1)} collective-permute-done((bf16[2,144,128]{2,1,0:T(8,128)(2,1)S(1)}, bf16[2,144,128]{2,1,0:T(8,128)(2,1)S(1)}, u32[]{:S(2)}, u32[]{:S(2)}) %collective-permute-start.4) | collective-permute-done | bytes 73760 | tf_op jit(solution)/shard_map/ppermute | solution.py:361
  39.0 0.7 %collective-permute-done.3.y1 = bf16[2,144,128]{2,1,0:T(8,128)(2,1)S(1)} collective-permute-done((bf16[2,144,128]{2,1,0:T(8,128)(2,1)S(1)}, bf16[2,144,128]{2,1,0:T(8,128)(2,1)S(1)}, u32[]{:S(2)}, u32[]{:S(2)}) %collective-permute-start.3) | collective-permute-done | bytes 73760 | tf_op jit(solution)/shard_map/ppermute | solution.py:361
  39.8 3.6 %replay.1 = (f32[256,256]{1,0:T(8,128)S(1)}, bf16[256,256]{1,0:T(8,128)(2,1)S(1)}) custom-call(f32[32,128]{1,0:T(8,128)S(1)} %get-tuple-element.14.kept_ref, f32[2,128]{1,0:T(2,128)S(1)} %bitcast.31, bf16[2,144,128]{2,1,0:T(8,128)(2,1)S(1)} %collective-permute-done.3.y1, bf16[2,144,128]{2,1,0:T(8,128)(2,1)S(1)} %collective-permute-done.4.y2, ...), custom_call_target="tpu_custom_call" | custom-call | tf_op jit(solution)/shard_map/replay/pallas_call | solution.py:288
  43.4 2.0 %collective-permute-start.8 = (bf16[256,256]{1,0:T(8,128)(2,1)S(1)}, bf16[256,256]{1,0:T(8,128)(2,1)S(1)}, u32[]{:S(2)}, u32[]{:S(2)}) collective-permute-start(bf16[256,256]{1,0:T(8,128)(2,1)S(1)} %get-tuple-element.20.m0), channel_id=1, source_target_pairs={{0,2},{1,3},{2,0},{3,1},{4,6},{5,7},{6,4},{7,5},{8,10},{9,11},{10,... | collective-permute-start | bytes 393224 | tf_op jit(solution)/shard_map/ppermute | solution.py:365
  45.4 2.5 %collective-permute-start.7 = (bf16[256,256]{1,0:T(8,128)(2,1)S(1)}, bf16[256,256]{1,0:T(8,128)(2,1)S(1)}, u32[]{:S(2)}, u32[]{:S(2)}) collective-permute-start(bf16[256,256]{1,0:T(8,128)(2,1)S(1)} %get-tuple-element.20.m0), channel_id=1, source_target_pairs={{0,6},{1,7},{2,4},{3,5},{4,2},{5,3},{6,0},{7,1},{8,14},{9,15},{10,... | collective-permute-start | bytes 393224 | tf_op jit(solution)/shard_map/ppermute | solution.py:365
  47.9 1.1 %collective-permute-start.6 = (bf16[256,256]{1,0:T(8,128)(2,1)S(1)}, bf16[256,256]{1,0:T(8,128)(2,1)S(1)}, u32[]{:S(2)}, u32[]{:S(2)}) collective-permute-start(bf16[256,256]{1,0:T(8,128)(2,1)S(1)} %get-tuple-element.20.m0), channel_id=1, source_target_pairs={{0,4},{1,5},{2,6},{3,7},{4,0},{5,1},{6,2},{7,3},{8,12},{9,13},{10,... | collective-permute-start | bytes 393224 | tf_op jit(solution)/shard_map/ppermute | solution.py:365
  49.0 0.5 collective-permute-done.8.m1
  49.5 2.3 %collective-permute-done.7.m3 = bf16[256,256]{1,0:T(8,128)(2,1)S(1)} collective-permute-done((bf16[256,256]{1,0:T(8,128)(2,1)S(1)}, bf16[256,256]{1,0:T(8,128)(2,1)S(1)}, u32[]{:S(2)}, u32[]{:S(2)}) %collective-permute-start.7) | collective-permute-done | bytes 131104 | tf_op jit(solution)/shard_map/ppermute | solution.py:365
  51.8 2.5 %collective-permute-done.6.m2 = bf16[256,256]{1,0:T(8,128)(2,1)S(1)} collective-permute-done((bf16[256,256]{1,0:T(8,128)(2,1)S(1)}, bf16[256,256]{1,0:T(8,128)(2,1)S(1)}, u32[]{:S(2)}, u32[]{:S(2)}) %collective-permute-start.6) | collective-permute-done | bytes 131104 | tf_op jit(solution)/shard_map/ppermute | solution.py:365
  54.5 1.9 %collective-permute-done.9.theirs_ref = bf16[4,256,256]{2,1,0:T(8,128)(2,1)S(1)} collective-permute-done((bf16[4,256,256]{2,1,0:T(8,128)(2,1)S(1)}, bf16[4,256,256]{2,1,0:T(8,128)(2,1)S(1)}, u32[]{:S(2)}, u32[]{:S(2)}) %collective-permute-start.9) | collective-permute-done | bytes 524320 | tf_op jit(solution)/shard_map/ppermute | solution.py:369
  56.5 2.9 %forward.1 = (bf16[4,256,256]{2,1,0:T(8,128)(2,1)S(1)}, bf16[256,1024]{1,0:T(8,128)(2,1)S(1)}) custom-call(bf16[256,256]{1,0:T(8,128)(2,1)S(1)} %get-tuple-element.20.m0, bf16[256,256]{1,0:T(8,128)(2,1)S(1)} %collective-permute-done.6.m2, bf16[256,256]{1,0:T(8,128)(2,1)S(1)} %collective-permute-done.7.m3, bf16[256,256]{1,0:T(8,128)(2,1)S(1)} %collective-permute-done.8.m1, ...), custom_call_target="tpu_custom_call" | custom-call | tf_op jit(solution)/shard_map/forward/pallas_call | solution.py:337
  59.4 0.2 collective-permute-start.10
  59.6 0.7 %keep.1 = f32[4,256,256]{2,1,0:T(8,128)S(1)} custom-call(bf16[256,1024]{1,0:T(8,128)(2,1)S(1)} %get-tuple-element.21.hidden, bf16[1024,2048]{1,0:T(8,128)(2,1)S(1)} %copy-done), custom_call_target="tpu_custom_call" | custom-call | tf_op jit(solution)/shard_map/keep/pallas_call | solution.py:345
  60.4 1.0 %collective-permute-done.10 = bf16[4,256,256]{2,1,0:T(8,128)(2,1)S(1)} collective-permute-done((bf16[4,256,256]{2,1,0:T(8,128)(2,1)S(1)}, bf16[4,256,256]{2,1,0:T(8,128)(2,1)S(1)}, u32[]{:S(2)}, u32[]{:S(2)}) %collective-permute-start.10) | collective-permute-done | bytes 524320 | tf_op jit(solution)/shard_map/ppermute | solution.py:369
  61.6 1.1 %collective-permute-start.11 = (bf16[256,256]{1,0:T(8,128)(2,1)S(1)}, bf16[256,256]{1,0:T(8,128)(2,1)S(1)}, u32[]{:S(2)}, u32[]{:S(2)}) collective-permute-start(bf16[256,256]{1,0:T(8,128)(2,1)S(1)} %get-tuple-element.25), channel_id=1, source_target_pairs={{0,2},{1,3},{2,0},{3,1},{4,6},{5,7},{6,4},{7,5},{8,10},{9,11},{10,... | collective-permute-start | bytes 393224 | tf_op jit(solution)/shard_map/ppermute | solution.py:365
  62.7 0.6 collective-permute-start.13
  63.3 2.5 %collective-permute-start.12 = (bf16[256,256]{1,0:T(8,128)(2,1)S(1)}, bf16[256,256]{1,0:T(8,128)(2,1)S(1)}, u32[]{:S(2)}, u32[]{:S(2)}) collective-permute-start(bf16[256,256]{1,0:T(8,128)(2,1)S(1)} %get-tuple-element.27), channel_id=1, source_target_pairs={{0,4},{1,5},{2,6},{3,7},{4,0},{5,1},{6,2},{7,3},{8,12},{9,13},{10,... | collective-permute-start | bytes 393224 | tf_op jit(solution)/shard_map/ppermute | solution.py:365
  65.8 1.7 %collective-permute-done.11 = bf16[256,256]{1,0:T(8,128)(2,1)S(1)} collective-permute-done((bf16[256,256]{1,0:T(8,128)(2,1)S(1)}, bf16[256,256]{1,0:T(8,128)(2,1)S(1)}, u32[]{:S(2)}, u32[]{:S(2)}) %collective-permute-start.11) | collective-permute-done | bytes 131104 | tf_op jit(solution)/shard_map/ppermute | solution.py:365
  67.4 4.5 %collective-permute-done.13 = bf16[256,256]{1,0:T(8,128)(2,1)S(1)} collective-permute-done((bf16[256,256]{1,0:T(8,128)(2,1)S(1)}, bf16[256,256]{1,0:T(8,128)(2,1)S(1)}, u32[]{:S(2)}, u32[]{:S(2)}) %collective-permute-start.13) | collective-permute-done | bytes 131104 | tf_op jit(solution)/shard_map/ppermute | solution.py:365
  72.0 0.7 %fusion.4 = bf16[256,256]{1,0:T(8,128)(2,1)} fusion(f32[256,256]{1,0:T(8,128)S(1)} %get-tuple-element.19, f32[4,256,256]{2,1,0:T(8,128)S(1)} %get-tuple-element.24, bf16[256,256]{1,0:T(8,128)(2,1)S(1)} %collective-permute-done.13, bf16[256,256]{1,0:T(8,128)(2,1)S(1)} %collective-permute-done.12, bf16[256,256]{1,0:T(8,128)(2,1)S(1)} %collective-permute-done.11), kind=kLoop, calls=%fused_computation.7 | loop fusion | flops 524288 | bytes 1048576 | tf_op jit(solution)/shard_map/convert_element_type | solution.py:398
  (15 shorter events, 0.4 us)
Async XLA Ops:
  0.0 39.8 %copy-start.4 = (f32[256]{0:T(256)S(1)}, f32[256]{0:T(256)}, u32[]{:S(2)}) copy-start(f32[256]{0:T(256)} %param.14) | copy-start | bytes 3076
  0.0 39.8 %copy-start.3 = (f32[256]{0:T(256)S(1)}, f32[256]{0:T(256)}, u32[]{:S(2)}) copy-start(f32[256]{0:T(256)} %param.13) | copy-start | bytes 3076
  19.8 5.3 %collective-permute-start.2 = (bf16[2,144,128]{2,1,0:T(8,128)(2,1)S(1)}, bf16[2,144,128]{2,1,0:T(8,128)(2,1)S(1)}, u32[]{:S(2)}, u32[]{:S(2)}) collective-permute-start(bf16[2,144,128]{2,1,0:T(8,128)(2,1)S(1)} %get-tuple-element.15.m0), channel_id=1, source_target_pairs={{0,24},{8,0},{16,8},{24,16},{32,56},{40,32},{48,40},{56,48},{64,88... | collective-permute-start | bytes 221192 | tf_op jit(solution)/shard_map/ppermute | solution.py:357
  22.7 6.1 %collective-permute-start.1 = (bf16[2,144,128]{2,1,0:T(8,128)(2,1)S(1)}, bf16[2,144,128]{2,1,0:T(8,128)(2,1)S(1)}, u32[]{:S(2)}, u32[]{:S(2)}) collective-permute-start(bf16[2,144,128]{2,1,0:T(8,128)(2,1)S(1)} %get-tuple-element.15.m0), channel_id=1, source_target_pairs={{0,16},{8,24},{16,0},{24,8},{32,48},{40,56},{48,32},{56,40},{64,80... | collective-permute-start | bytes 221192 | tf_op jit(solution)/shard_map/ppermute | solution.py:357
  23.5 6.0 %collective-permute-start = (bf16[2,144,128]{2,1,0:T(8,128)(2,1)S(1)}, bf16[2,144,128]{2,1,0:T(8,128)(2,1)S(1)}, u32[]{:S(2)}, u32[]{:S(2)}) collective-permute-start(bf16[2,144,128]{2,1,0:T(8,128)(2,1)S(1)} %get-tuple-element.15.m0), channel_id=1, source_target_pairs={{0,8},{8,16},{16,24},{24,0},{32,40},{40,48},{48,56},{56,32},{64,72... | collective-permute-start | bytes 221192 | tf_op jit(solution)/shard_map/ppermute | solution.py:357
  30.0 5.2 %collective-permute-start.5 = (bf16[2,144,128]{2,1,0:T(8,128)(2,1)S(1)}, bf16[2,144,128]{2,1,0:T(8,128)(2,1)S(1)}, u32[]{:S(2)}, u32[]{:S(2)}) collective-permute-start(bf16[2,144,128]{2,1,0:T(8,128)(2,1)S(1)} %row_map.1), channel_id=1, source_target_pairs={{0,96},{8,104},{16,112},{24,120},{32,0},{40,8},{48,16},{56,24},{64... | collective-permute-start | bytes 221192 | tf_op jit(solution)/shard_map/ppermute | solution.py:361
  33.1 5.9 %collective-permute-start.4 = (bf16[2,144,128]{2,1,0:T(8,128)(2,1)S(1)}, bf16[2,144,128]{2,1,0:T(8,128)(2,1)S(1)}, u32[]{:S(2)}, u32[]{:S(2)}) collective-permute-start(bf16[2,144,128]{2,1,0:T(8,128)(2,1)S(1)} %row_map.1), channel_id=1, source_target_pairs={{0,64},{8,72},{16,80},{24,88},{32,96},{40,104},{48,112},{56,120},{... | collective-permute-start | bytes 221192 | tf_op jit(solution)/shard_map/ppermute | solution.py:361
  33.7 6.0 %collective-permute-start.3 = (bf16[2,144,128]{2,1,0:T(8,128)(2,1)S(1)}, bf16[2,144,128]{2,1,0:T(8,128)(2,1)S(1)}, u32[]{:S(2)}, u32[]{:S(2)}) collective-permute-start(bf16[2,144,128]{2,1,0:T(8,128)(2,1)S(1)} %row_map.1), channel_id=1, source_target_pairs={{0,32},{8,40},{16,48},{24,56},{32,64},{40,72},{48,80},{56,88},{64,... | collective-permute-start | bytes 221192 | tf_op jit(solution)/shard_map/ppermute | solution.py:361
  39.8 16.7 %copy-start = (bf16[1024,2048]{1,0:T(8,128)(2,1)S(1)}, bf16[1024,2048]{1,0:T(8,128)(2,1)}, u32[]{:S(2)}) copy-start(bf16[1024,2048]{1,0:T(8,128)(2,1)} %down_ref.3) | copy-start | bytes 12582916
  39.8 16.7 %copy-start.1 = (bf16[2048,1024]{1,0:T(8,128)(2,1)S(1)}, bf16[2048,1024]{1,0:T(8,128)(2,1)}, u32[]{:S(2)}) copy-start(bf16[2048,1024]{1,0:T(8,128)(2,1)} %gate_ref.1) | copy-start | bytes 12582916
  39.8 16.7 %copy-start.2 = (bf16[2048,1024]{1,0:T(8,128)(2,1)S(1)}, bf16[2048,1024]{1,0:T(8,128)(2,1)}, u32[]{:S(2)}) copy-start(bf16[2048,1024]{1,0:T(8,128)(2,1)} %up_ref.1) | copy-start | bytes 12582916
  43.4 6.1 %collective-permute-start.8 = (bf16[256,256]{1,0:T(8,128)(2,1)S(1)}, bf16[256,256]{1,0:T(8,128)(2,1)S(1)}, u32[]{:S(2)}, u32[]{:S(2)}) collective-permute-start(bf16[256,256]{1,0:T(8,128)(2,1)S(1)} %get-tuple-element.20.m0), channel_id=1, source_target_pairs={{0,2},{1,3},{2,0},{3,1},{4,6},{5,7},{6,4},{7,5},{8,10},{9,11},{10,... | collective-permute-start | bytes 393224 | tf_op jit(solution)/shard_map/ppermute | solution.py:365
  45.4 6.5 %collective-permute-start.7 = (bf16[256,256]{1,0:T(8,128)(2,1)S(1)}, bf16[256,256]{1,0:T(8,128)(2,1)S(1)}, u32[]{:S(2)}, u32[]{:S(2)}) collective-permute-start(bf16[256,256]{1,0:T(8,128)(2,1)S(1)} %get-tuple-element.20.m0), channel_id=1, source_target_pairs={{0,6},{1,7},{2,4},{3,5},{4,2},{5,3},{6,0},{7,1},{8,14},{9,15},{10,... | collective-permute-start | bytes 393224 | tf_op jit(solution)/shard_map/ppermute | solution.py:365
  47.9 6.5 %collective-permute-start.6 = (bf16[256,256]{1,0:T(8,128)(2,1)S(1)}, bf16[256,256]{1,0:T(8,128)(2,1)S(1)}, u32[]{:S(2)}, u32[]{:S(2)}) collective-permute-start(bf16[256,256]{1,0:T(8,128)(2,1)S(1)} %get-tuple-element.20.m0), channel_id=1, source_target_pairs={{0,4},{1,5},{2,6},{3,7},{4,0},{5,1},{6,2},{7,3},{8,12},{9,13},{10,... | collective-permute-start | bytes 393224 | tf_op jit(solution)/shard_map/ppermute | solution.py:365
  54.5 2.0 %collective-permute-start.9 = (bf16[4,256,256]{2,1,0:T(8,128)(2,1)S(1)}, bf16[4,256,256]{2,1,0:T(8,128)(2,1)S(1)}, u32[]{:S(2)}, u32[]{:S(2)}) collective-permute-start(bf16[4,256,256]{2,1,0:T(8,128)(2,1)S(1)} %pad_maximum_fusion), channel_id=1, source_target_pairs={{0,1},{1,0},{2,3},{3,2},{4,5},{5,4},{6,7},{7,6},{8,9},{9,8},{10,11... | collective-permute-start | bytes 1572872 | tf_op jit(solution)/shard_map/ppermute | solution.py:369
  59.4 2.0 %collective-permute-start.10 = (bf16[4,256,256]{2,1,0:T(8,128)(2,1)S(1)}, bf16[4,256,256]{2,1,0:T(8,128)(2,1)S(1)}, u32[]{:S(2)}, u32[]{:S(2)}) collective-permute-start(bf16[4,256,256]{2,1,0:T(8,128)(2,1)S(1)} %get-tuple-element.22), channel_id=1, source_target_pairs={{0,1},{1,0},{2,3},{3,2},{4,5},{5,4},{6,7},{7,6},{8,9},{9,8},{10,11... | collective-permute-start | bytes 1572872 | tf_op jit(solution)/shard_map/ppermute | solution.py:369
  61.6 5.8 %collective-permute-start.11 = (bf16[256,256]{1,0:T(8,128)(2,1)S(1)}, bf16[256,256]{1,0:T(8,128)(2,1)S(1)}, u32[]{:S(2)}, u32[]{:S(2)}) collective-permute-start(bf16[256,256]{1,0:T(8,128)(2,1)S(1)} %get-tuple-element.25), channel_id=1, source_target_pairs={{0,2},{1,3},{2,0},{3,1},{4,6},{5,7},{6,4},{7,5},{8,10},{9,11},{10,... | collective-permute-start | bytes 393224 | tf_op jit(solution)/shard_map/ppermute | solution.py:365
  62.7 9.3 %collective-permute-start.13 = (bf16[256,256]{1,0:T(8,128)(2,1)S(1)}, bf16[256,256]{1,0:T(8,128)(2,1)S(1)}, u32[]{:S(2)}, u32[]{:S(2)}) collective-permute-start(bf16[256,256]{1,0:T(8,128)(2,1)S(1)} %get-tuple-element.26), channel_id=1, source_target_pairs={{0,6},{1,7},{2,4},{3,5},{4,2},{5,3},{6,0},{7,1},{8,14},{9,15},{10,... | collective-permute-start | bytes 393224 | tf_op jit(solution)/shard_map/ppermute | solution.py:365
  63.3 8.7 %collective-permute-start.12 = (bf16[256,256]{1,0:T(8,128)(2,1)S(1)}, bf16[256,256]{1,0:T(8,128)(2,1)S(1)}, u32[]{:S(2)}, u32[]{:S(2)}) collective-permute-start(bf16[256,256]{1,0:T(8,128)(2,1)S(1)} %get-tuple-element.27), channel_id=1, source_target_pairs={{0,4},{1,5},{2,6},{3,7},{4,0},{5,1},{6,2},{7,3},{8,12},{9,13},{10,... | collective-permute-start | bytes 393224 | tf_op jit(solution)/shard_map/ppermute | solution.py:365

commit v9 on v7

--- a/solution.py
+++ b/solution.py
@@ -297,50 +297,79 @@
     )(kept, init, *y_maps, *x_maps, off, grp, gain, pltpu.with_memory_space_constraint(q, pltpu.VMEM))
 
 
-def forward_kernel(m0, m1, m3, m2, theirs_ref, gate_ref, up_ref, down_ref, send_ref, hidden):
-    z, core = places()[2:]
+def weight_rows(k, c):
+    z = places()[2]
+    return pl.multiple_of((lax.rem(z + k, 4) * 2 + c) * 2 * WIDTH, 2 * WIDTH)
+
+
+def products(parts, gate_ref, up_ref, n):
     wide = 2 * WIDTH
-
-    def at(k, c):
-        return pl.multiple_of((lax.rem(z + k, 4) * 2 + c) * wide, wide)
-
-    parts = [(m0, 0, 0), (m1, 3, 0), (m2, 2, 0), (m3, 1, 0)]
-    parts += [(theirs_ref.at[i], (4 - k) % 4, 1) for i, k in enumerate((0, 1, 3, 2))]
+    gate = up = None
+    for ref, row in parts:
+        chunk = ref[...]
+        g = jnp.dot(chunk, gate_ref[pl.ds(row, wide), n : n + wide], preferred_element_type=F32)
+        u = jnp.dot(chunk, up_ref[pl.ds(row, wide), n : n + wide], preferred_element_type=F32)
+        gate = g if gate is None else gate + g
+        up = u if up is None else up + u
+    return gate, up
+
+
+AHEAD = (0, 3, 1, 2)
+
+
+def mine_kernel(m0, m1, m3, m2, gate_ref, up_ref, gate_out, up_out):
+    core = places()[3]
+    parts = [(ref, weight_rows(k, core)) for ref, k in zip((m0, m1, m3, m2), AHEAD)]
+    wide = 2 * WIDTH
     for n in range(0, gate_ref.shape[1], wide):
-        gate = up = None
-        for ref, k, other in parts:
-            chunk = ref[...]
-            row = at(k, 1 - core if other else core)
-            g = jnp.dot(chunk, gate_ref[pl.ds(row, wide), n : n + wide], preferred_element_type=F32)
-            u = jnp.dot(chunk, up_ref[pl.ds(row, wide), n : n + wide], preferred_element_type=F32)
-            gate = g if gate is None else gate + g
-            up = u if up is None else up + u
+        gate_out[:, n : n + wide], up_out[:, n : n + wide] = products(parts, gate_ref, up_ref, n)
+
+
+def forward_kernel(theirs_ref, gate_in, up_in, gate_ref, up_ref, down_ref, send_ref, hidden):
+    core = places()[3]
+    parts = [(theirs_ref.at[i], weight_rows(k, 1 - core)) for i, k in enumerate(AHEAD)]
+    wide = 2 * WIDTH
+    for n in range(0, gate_ref.shape[1], wide):
+        gate, up = products(parts, gate_ref, up_ref, n)
+        gate = gate + gate_in[:, n : n + wide]
+        up = up + up_in[:, n : n + wide]
         hidden[:, n : n + wide] = (gate / (1.0 + jnp.exp(-gate)) * up).astype(BF16)
     for k in range(4):
-        columns = down_ref[:, pl.ds(at(k, 1 - core), wide)]
+        columns = down_ref[:, pl.ds(weight_rows(k, 1 - core), wide)]
         send_ref[k] = jnp.dot(hidden[...], columns, preferred_element_type=F32).astype(BF16)
 
 
 def keep_kernel(hidden, down_ref, keep_ref):
-    z, core = places()[2:]
-    wide = 2 * WIDTH
+    core = places()[3]
     for k in range(4):
-        columns = down_ref[:, pl.ds(pl.multiple_of((lax.rem(z + k, 4) * 2 + core) * wide, wide), wide)]
+        columns = down_ref[:, pl.ds(weight_rows(k, core), 2 * WIDTH)]
         keep_ref[k] = jnp.dot(hidden[...], columns, preferred_element_type=F32)
 
 
-def forward(mine, theirs, gate_weight, up_weight, down_weight):
+def forward(mine, gate_weight, up_weight, down_weight):
     steps, units = mine[0].shape[0], gate_weight.shape[1]
-    weights = [pltpu.with_memory_space_constraint(w, pltpu.VMEM) for w in (gate_weight, up_weight, down_weight)]
+    gate_weight, up_weight, down_weight = [
+        pltpu.with_memory_space_constraint(w, pltpu.VMEM) for w in (gate_weight, up_weight, down_weight)
+    ]
     params = pltpu.CompilerParams(vmem_limit_bytes=16_000_000)
+    theirs = other_core(jnp.stack(mine))
+    part = pltpu.VMEM((steps, units), F32)
+    gate, up = pl.pallas_call(
+        mine_kernel,
+        out_shape=(part, part),
+        in_specs=[VMEM] * 6,
+        out_specs=(VMEM, VMEM),
+        compiler_params=params,
+        name="mine",
+    )(*mine, gate_weight, up_weight)
     sent, hidden = pl.pallas_call(
         forward_kernel,
         out_shape=(pltpu.VMEM((4, steps, 2 * WIDTH), BF16), pltpu.VMEM((steps, units), BF16)),
-        in_specs=[VMEM] * 8,
+        in_specs=[VMEM] * 6,
         out_specs=(VMEM, VMEM),
         compiler_params=params,
         name="forward",
-    )(*mine, theirs, *weights)
+    )(theirs, gate, up, gate_weight, up_weight, down_weight)
     kept = pl.pallas_call(
         keep_kernel,
         out_shape=pltpu.VMEM((4, steps, 2 * WIDTH), F32),
@@ -348,7 +377,7 @@
         out_specs=VMEM,
         compiler_params=params,
         name="keep",
-    )(hidden, weights[2])
+    )(hidden, down_weight)
     return kept, sent
 
 
@@ -387,8 +416,7 @@
         kept, initial_state.reshape(2, WIDTH), y_maps, x_maps, off, grp, norm_gain.reshape(2, WIDTH), q
     )
     mine = [normed] + [z_back(normed, k) for k in (1, 3, 2)]
-    theirs = other_core(jnp.stack(mine))
-    keep, sent = forward(mine, theirs, gate_weight, up_weight, down_weight)
+    keep, sent = forward(mine, gate_weight, up_weight, down_weight)
     chip = keep + other_core(sent).astype(F32)
     low = chip.astype(BF16)
     mixed = chip[0]

time: 72.6 us -> 71.8 us (0.989)
  waiting for transfers between devices: 24.6 us -> 23.4 us
    pallas_call x0 -> x1, Pallas kernels: none -> 1.32 us  [forward(): pl.pallas_call(mine_kernel, out_shape=(part, part), in_specs=[VMEM] * 6,...]
    ppermute x2, waiting for transfers between devices: 2.93 us -> 1.69 us  [other_core(): return lax.ppermute(v, 'block', [(s, s ^ 1) for s in range(8)])]
    pallas_call x1, Pallas kernels: 2.95 us -> 1.95 us  [forward(): pl.pallas_call(forward_kernel, out_shape=(pltpu.VMEM((4, steps, 2 * WIDTH...]
  transfers between devices with their start and end apart: 14 -> 14, of which waited for: 14 -> 14; matrix products, arithmetic and copies ran while one was open for 0% -> 0% of each run, Pallas kernels for 1% -> 3%
where the time goes in v9:
time: 71.8 us; the launch traced here: 71.3 us
  Pallas kernels  27.9 us (39%)
  waiting for transfers between devices  23.4 us (33%)
  starting transfers between devices  18.7 us (26%)
  other arithmetic  0.96 us (1%)
    pallas_call x1, Pallas kernels, compose(): pl.pallas_call(compose_kernel, out_shape=(pltpu.VMEM((SPAN, 2 * GROUPS, W...  19.8 us
    ppermute x6, waiting for transfers between devices, z_back(): lax.ppermute(v, 'block', [(z * 2 + c, (z + k) % 4 * 2 + c) for z in range...  11.5 us
    ppermute x6, starting transfers between devices, z_back(): lax.ppermute(v, 'block', [(z * 2 + c, (z + k) % 4 * 2 + c) for z in range...  9.25 us
    ppermute x3, waiting for transfers between devices, x_back(): lax.ppermute(v, 'tm', [(y * 4 + x, y * 4 + (x + k) % 4) for y in range(4)...  5.12 us
    ppermute x3, waiting for transfers between devices, y_back(): lax.ppermute(v, 'tm', [(y * 4 + x, (y + k) % 4 * 4 + x) for y in range(4)...  5.04 us
    ppermute x3, starting transfers between devices, y_back(): lax.ppermute(v, 'tm', [(y * 4 + x, (y + k) % 4 * 4 + x) for y in range(4)...  4.69 us
    ppermute x3, starting transfers between devices, x_back(): lax.ppermute(v, 'tm', [(y * 4 + x, y * 4 + (x + k) % 4) for y in range(4)...  4.6 us
    pallas_call x1, Pallas kernels, replay(): pl.pallas_call(replay_kernel, out_shape=(jax.ShapeDtypeStruct((steps, 2 *...  3.61 us
  transfers between devices with their start and end apart: 14, of which 14 were waited for; matrix products, arithmetic and copies ran while one was open for 0% of the time, Pallas kernels for 3%

profile of v9, /device:TPU:0, one launch (start us, length us, event | category | flops | bytes accessed | tf_op | source)
XLA Modules:
  0.0 71.3 jit_solution(15478819095085693032)
XLA Ops:
  0.0 19.8 %compose.1 = (bf16[16,32,128,128]{3,2,1,0:T(8,128)(2,1)S(1)}, f32[512,128]{1,0:T(8,128)S(1)}, bf16[2,144,128]{2,1,0:T(8,128)(2,1)S(1)}, bf16[32,128,128]{2,1,0:T(8,128)(2,1)S(1)}, f32[32,128]{1,0:T(8,128)S(1)}) custom-call(f32[64,256]{1,0:T(8,128)} %bitcast.34, f32[2,256]{1,0:T(2,128)} %bitcast.35, f32[2,256]{1,0:T(2,128)} %bitcast.36, ...), custom_call_target="tpu_custom_call" | custom-call | tf_op jit(solution)/shard_map/compose/pallas_call | solution.py:193
  19.8 2.9 %collective-permute-start.2 = (bf16[2,144,128]{2,1,0:T(8,128)(2,1)S(1)}, bf16[2,144,128]{2,1,0:T(8,128)(2,1)S(1)}, u32[]{:S(2)}, u32[]{:S(2)}) collective-permute-start(bf16[2,144,128]{2,1,0:T(8,128)(2,1)S(1)} %get-tuple-element.17.m0), channel_id=1, source_target_pairs={{0,24},{8,0},{16,8},{24,16},{32,56},{40,32},{48,40},{56,48},{64,88... | collective-permute-start | bytes 221192 | tf_op jit(solution)/shard_map/ppermute | solution.py:385
  22.7 0.8 %collective-permute-start.1 = (bf16[2,144,128]{2,1,0:T(8,128)(2,1)S(1)}, bf16[2,144,128]{2,1,0:T(8,128)(2,1)S(1)}, u32[]{:S(2)}, u32[]{:S(2)}) collective-permute-start(bf16[2,144,128]{2,1,0:T(8,128)(2,1)S(1)} %get-tuple-element.17.m0), channel_id=1, source_target_pairs={{0,16},{8,24},{16,0},{24,8},{32,48},{40,56},{48,32},{56,40},{64,80... | collective-permute-start | bytes 221192 | tf_op jit(solution)/shard_map/ppermute | solution.py:385
  23.5 0.9 %collective-permute-start = (bf16[2,144,128]{2,1,0:T(8,128)(2,1)S(1)}, bf16[2,144,128]{2,1,0:T(8,128)(2,1)S(1)}, u32[]{:S(2)}, u32[]{:S(2)}) collective-permute-start(bf16[2,144,128]{2,1,0:T(8,128)(2,1)S(1)} %get-tuple-element.17.m0), channel_id=1, source_target_pairs={{0,8},{8,16},{16,24},{24,0},{32,40},{40,48},{48,56},{56,32},{64,72... | collective-permute-start | bytes 221192 | tf_op jit(solution)/shard_map/ppermute | solution.py:385
  24.4 0.7 %collective-permute-done.2.m3.x3 = bf16[2,144,128]{2,1,0:T(8,128)(2,1)S(1)} collective-permute-done((bf16[2,144,128]{2,1,0:T(8,128)(2,1)S(1)}, bf16[2,144,128]{2,1,0:T(8,128)(2,1)S(1)}, u32[]{:S(2)}, u32[]{:S(2)}) %collective-permute-start.2) | collective-permute-done | bytes 73760 | tf_op jit(solution)/shard_map/ppermute | solution.py:385
  25.1 3.7 %collective-permute-done.1.m2.x2 = bf16[2,144,128]{2,1,0:T(8,128)(2,1)S(1)} collective-permute-done((bf16[2,144,128]{2,1,0:T(8,128)(2,1)S(1)}, bf16[2,144,128]{2,1,0:T(8,128)(2,1)S(1)}, u32[]{:S(2)}, u32[]{:S(2)}) %collective-permute-start.1) | collective-permute-done | bytes 73760 | tf_op jit(solution)/shard_map/ppermute | solution.py:385
  28.8 0.7 %collective-permute-done.m1.x1 = bf16[2,144,128]{2,1,0:T(8,128)(2,1)S(1)} collective-permute-done((bf16[2,144,128]{2,1,0:T(8,128)(2,1)S(1)}, bf16[2,144,128]{2,1,0:T(8,128)(2,1)S(1)}, u32[]{:S(2)}, u32[]{:S(2)}) %collective-permute-start) | collective-permute-done | bytes 73760 | tf_op jit(solution)/shard_map/ppermute | solution.py:385
  29.5 0.5 row_map.1
  30.0 3.1 %collective-permute-start.5 = (bf16[2,144,128]{2,1,0:T(8,128)(2,1)S(1)}, bf16[2,144,128]{2,1,0:T(8,128)(2,1)S(1)}, u32[]{:S(2)}, u32[]{:S(2)}) collective-permute-start(bf16[2,144,128]{2,1,0:T(8,128)(2,1)S(1)} %row_map.1), channel_id=1, source_target_pairs={{0,96},{8,104},{16,112},{24,120},{32,0},{40,8},{48,16},{56,24},{64... | collective-permute-start | bytes 221192 | tf_op jit(solution)/shard_map/ppermute | solution.py:389
  33.1 0.6 collective-permute-start.4
  33.7 1.0 %collective-permute-start.3 = (bf16[2,144,128]{2,1,0:T(8,128)(2,1)S(1)}, bf16[2,144,128]{2,1,0:T(8,128)(2,1)S(1)}, u32[]{:S(2)}, u32[]{:S(2)}) collective-permute-start(bf16[2,144,128]{2,1,0:T(8,128)(2,1)S(1)} %row_map.1), channel_id=1, source_target_pairs={{0,32},{8,40},{16,48},{24,56},{32,64},{40,72},{48,80},{56,88},{64,... | collective-permute-start | bytes 221192 | tf_op jit(solution)/shard_map/ppermute | solution.py:389
  34.7 0.5 collective-permute-done.5.y3
  35.2 3.8 %collective-permute-done.4.y2 = bf16[2,144,128]{2,1,0:T(8,128)(2,1)S(1)} collective-permute-done((bf16[2,144,128]{2,1,0:T(8,128)(2,1)S(1)}, bf16[2,144,128]{2,1,0:T(8,128)(2,1)S(1)}, u32[]{:S(2)}, u32[]{:S(2)}) %collective-permute-start.4) | collective-permute-done | bytes 73760 | tf_op jit(solution)/shard_map/ppermute | solution.py:389
  39.0 0.7 %collective-permute-done.3.y1 = bf16[2,144,128]{2,1,0:T(8,128)(2,1)S(1)} collective-permute-done((bf16[2,144,128]{2,1,0:T(8,128)(2,1)S(1)}, bf16[2,144,128]{2,1,0:T(8,128)(2,1)S(1)}, u32[]{:S(2)}, u32[]{:S(2)}) %collective-permute-start.3) | collective-permute-done | bytes 73760 | tf_op jit(solution)/shard_map/ppermute | solution.py:389
  39.8 3.6 %replay.1 = (f32[256,256]{1,0:T(8,128)S(1)}, bf16[256,256]{1,0:T(8,128)(2,1)S(1)}) custom-call(f32[32,128]{1,0:T(8,128)S(1)} %get-tuple-element.16.kept_ref, f32[2,128]{1,0:T(2,128)S(1)} %bitcast.31, bf16[2,144,128]{2,1,0:T(8,128)(2,1)S(1)} %collective-permute-done.3.y1, bf16[2,144,128]{2,1,0:T(8,128)(2,1)S(1)} %collective-permute-done.4.y2, ...), custom_call_target="tpu_custom_call" | custom-call | tf_op jit(solution)/shard_map/replay/pallas_call | solution.py:287
  43.4 4.0 %collective-permute-start.8 = (bf16[256,256]{1,0:T(8,128)(2,1)S(1)}, bf16[256,256]{1,0:T(8,128)(2,1)S(1)}, u32[]{:S(2)}, u32[]{:S(2)}) collective-permute-start(bf16[256,256]{1,0:T(8,128)(2,1)S(1)} %get-tuple-element.22.m0), channel_id=1, source_target_pairs={{0,4},{1,5},{2,6},{3,7},{4,0},{5,1},{6,2},{7,3},{8,12},{9,13},{10,... | collective-permute-start | bytes 393224 | tf_op jit(solution)/shard_map/ppermute | solution.py:393
  47.3 0.7 collective-permute-start.7
  48.0 1.3 %collective-permute-start.6 = (bf16[256,256]{1,0:T(8,128)(2,1)S(1)}, bf16[256,256]{1,0:T(8,128)(2,1)S(1)}, u32[]{:S(2)}, u32[]{:S(2)}) collective-permute-start(bf16[256,256]{1,0:T(8,128)(2,1)S(1)} %get-tuple-element.22.m0), channel_id=1, source_target_pairs={{0,2},{1,3},{2,4},{3,5},{4,6},{5,7},{6,0},{7,1},{8,10},{9,11},{10,... | collective-permute-start | bytes 393224 | tf_op jit(solution)/shard_map/ppermute | solution.py:393
  49.4 1.4 %collective-permute-done.8.m2 = bf16[256,256]{1,0:T(8,128)(2,1)S(1)} collective-permute-done((bf16[256,256]{1,0:T(8,128)(2,1)S(1)}, bf16[256,256]{1,0:T(8,128)(2,1)S(1)}, u32[]{:S(2)}, u32[]{:S(2)}) %collective-permute-start.8) | collective-permute-done | bytes 131104 | tf_op jit(solution)/shard_map/ppermute | solution.py:393
  50.8 1.9 %collective-permute-done.7.m3 = bf16[256,256]{1,0:T(8,128)(2,1)S(1)} collective-permute-done((bf16[256,256]{1,0:T(8,128)(2,1)S(1)}, bf16[256,256]{1,0:T(8,128)(2,1)S(1)}, u32[]{:S(2)}, u32[]{:S(2)}) %collective-permute-start.7) | collective-permute-done | bytes 131104 | tf_op jit(solution)/shard_map/ppermute | solution.py:393
  52.7 1.5 %collective-permute-done.6.m1 = bf16[256,256]{1,0:T(8,128)(2,1)S(1)} collective-permute-done((bf16[256,256]{1,0:T(8,128)(2,1)S(1)}, bf16[256,256]{1,0:T(8,128)(2,1)S(1)}, u32[]{:S(2)}, u32[]{:S(2)}) %collective-permute-start.6) | collective-permute-done | bytes 131104 | tf_op jit(solution)/shard_map/ppermute | solution.py:393
  54.4 1.3 %mine.1 = (f32[256,1024]{1,0:T(8,128)S(1)}, f32[256,1024]{1,0:T(8,128)S(1)}) custom-call(bf16[256,256]{1,0:T(8,128)(2,1)S(1)} %get-tuple-element.22.m0, bf16[256,256]{1,0:T(8,128)(2,1)S(1)} %collective-permute-done.6.m1, bf16[256,256]{1,0:T(8,128)(2,1)S(1)} %collective-permute-done.7.m3, bf16[256,256]{1,0:T(8,128)(2,1)S(1)} %collective-permute-done.8.m2, ...), custom_call_target="tpu_custom_call" | custom-call | tf_op jit(solution)/shard_map/mine/pallas_call | solution.py:357
  55.7 0.5 collective-permute-done.9.theirs_ref
  56.5 1.9 %forward.1 = (bf16[4,256,256]{2,1,0:T(8,128)(2,1)S(1)}, bf16[256,1024]{1,0:T(8,128)(2,1)S(1)}) custom-call(bf16[4,256,256]{2,1,0:T(8,128)(2,1)S(1)} %collective-permute-done.9.theirs_ref, f32[256,1024]{1,0:T(8,128)S(1)} %get-tuple-element.23.gate_in, f32[256,1024]{1,0:T(8,128)S(1)} %get-tuple-element.24.up_in, bf16[2048,1024]{1,0:T(8,128)(2,1)S(1)} %copy-done, ...), custom_call_target="tpu_custom_call" | custom-call | tf_op jit(solution)/shard_map/forward/pallas_call | solution.py:365
  58.5 0.7 %keep.1 = f32[4,256,256]{2,1,0:T(8,128)S(1)} custom-call(bf16[256,1024]{1,0:T(8,128)(2,1)S(1)} %get-tuple-element.25.hidden, bf16[1024,2048]{1,0:T(8,128)(2,1)S(1)} %copy-done.2), custom_call_target="tpu_custom_call" | custom-call | tf_op jit(solution)/shard_map/keep/pallas_call | solution.py:373
  59.3 1.1 %collective-permute-done.10 = bf16[4,256,256]{2,1,0:T(8,128)(2,1)S(1)} collective-permute-done((bf16[4,256,256]{2,1,0:T(8,128)(2,1)S(1)}, bf16[4,256,256]{2,1,0:T(8,128)(2,1)S(1)}, u32[]{:S(2)}, u32[]{:S(2)}) %collective-permute-start.10) | collective-permute-done | bytes 524320 | tf_op jit(solution)/shard_map/ppermute | solution.py:397
  60.6 1.2 %collective-permute-start.11 = (bf16[256,256]{1,0:T(8,128)(2,1)S(1)}, bf16[256,256]{1,0:T(8,128)(2,1)S(1)}, u32[]{:S(2)}, u32[]{:S(2)}) collective-permute-start(bf16[256,256]{1,0:T(8,128)(2,1)S(1)} %get-tuple-element.29), channel_id=1, source_target_pairs={{0,4},{1,5},{2,6},{3,7},{4,0},{5,1},{6,2},{7,3},{8,12},{9,13},{10,... | collective-permute-start | bytes 393224 | tf_op jit(solution)/shard_map/ppermute | solution.py:393
  61.9 1.6 %collective-permute-start.13 = (bf16[256,256]{1,0:T(8,128)(2,1)S(1)}, bf16[256,256]{1,0:T(8,128)(2,1)S(1)}, u32[]{:S(2)}, u32[]{:S(2)}) collective-permute-start(bf16[256,256]{1,0:T(8,128)(2,1)S(1)} %get-tuple-element.30), channel_id=1, source_target_pairs={{0,6},{1,7},{2,0},{3,1},{4,2},{5,3},{6,4},{7,5},{8,14},{9,15},{10,... | collective-permute-start | bytes 393224 | tf_op jit(solution)/shard_map/ppermute | solution.py:393
  63.9 4.6 %collective-permute-done.11 = bf16[256,256]{1,0:T(8,128)(2,1)S(1)} collective-permute-done((bf16[256,256]{1,0:T(8,128)(2,1)S(1)}, bf16[256,256]{1,0:T(8,128)(2,1)S(1)}, u32[]{:S(2)}, u32[]{:S(2)}) %collective-permute-start.11) | collective-permute-done | bytes 131104 | tf_op jit(solution)/shard_map/ppermute | solution.py:393
  68.5 0.5 collective-permute-done.13
  69.0 1.5 %collective-permute-done.12 = bf16[256,256]{1,0:T(8,128)(2,1)S(1)} collective-permute-done((bf16[256,256]{1,0:T(8,128)(2,1)S(1)}, bf16[256,256]{1,0:T(8,128)(2,1)S(1)}, u32[]{:S(2)}, u32[]{:S(2)}) %collective-permute-start.12) | collective-permute-done | bytes 131104 | tf_op jit(solution)/shard_map/ppermute | solution.py:393
  70.6 0.7 %fusion.4 = bf16[256,256]{1,0:T(8,128)(2,1)} fusion(f32[256,256]{1,0:T(8,128)S(1)} %get-tuple-element.21, f32[4,256,256]{2,1,0:T(8,128)S(1)} %get-tuple-element.28, bf16[256,256]{1,0:T(8,128)(2,1)S(1)} %collective-permute-done.13, bf16[256,256]{1,0:T(8,128)(2,1)S(1)} %collective-permute-done.12, bf16[256,256]{1,0:T(8,128)(2,1)S(1)} %collective-permute-done.11), kind=kLoop, calls=%fused_computation.7 | loop fusion | flops 524288 | bytes 1048576 | tf_op jit(solution)/shard_map/convert_element_type | solution.py:425
  (16 shorter events, 1.0 us)
Async XLA Ops:
  0.0 39.8 %copy-start.4 = (f32[256]{0:T(256)S(1)}, f32[256]{0:T(256)}, u32[]{:S(2)}) copy-start(f32[256]{0:T(256)} %param.14) | copy-start | bytes 3076
  0.0 39.8 %copy-start.3 = (f32[256]{0:T(256)S(1)}, f32[256]{0:T(256)}, u32[]{:S(2)}) copy-start(f32[256]{0:T(256)} %param.13) | copy-start | bytes 3076
  19.8 5.3 %collective-permute-start.2 = (bf16[2,144,128]{2,1,0:T(8,128)(2,1)S(1)}, bf16[2,144,128]{2,1,0:T(8,128)(2,1)S(1)}, u32[]{:S(2)}, u32[]{:S(2)}) collective-permute-start(bf16[2,144,128]{2,1,0:T(8,128)(2,1)S(1)} %get-tuple-element.17.m0), channel_id=1, source_target_pairs={{0,24},{8,0},{16,8},{24,16},{32,56},{40,32},{48,40},{56,48},{64,88... | collective-permute-start | bytes 221192 | tf_op jit(solution)/shard_map/ppermute | solution.py:385
  22.7 6.1 %collective-permute-start.1 = (bf16[2,144,128]{2,1,0:T(8,128)(2,1)S(1)}, bf16[2,144,128]{2,1,0:T(8,128)(2,1)S(1)}, u32[]{:S(2)}, u32[]{:S(2)}) collective-permute-start(bf16[2,144,128]{2,1,0:T(8,128)(2,1)S(1)} %get-tuple-element.17.m0), channel_id=1, source_target_pairs={{0,16},{8,24},{16,0},{24,8},{32,48},{40,56},{48,32},{56,40},{64,80... | collective-permute-start | bytes 221192 | tf_op jit(solution)/shard_map/ppermute | solution.py:385
  23.5 6.0 %collective-permute-start = (bf16[2,144,128]{2,1,0:T(8,128)(2,1)S(1)}, bf16[2,144,128]{2,1,0:T(8,128)(2,1)S(1)}, u32[]{:S(2)}, u32[]{:S(2)}) collective-permute-start(bf16[2,144,128]{2,1,0:T(8,128)(2,1)S(1)} %get-tuple-element.17.m0), channel_id=1, source_target_pairs={{0,8},{8,16},{16,24},{24,0},{32,40},{40,48},{48,56},{56,32},{64,72... | collective-permute-start | bytes 221192 | tf_op jit(solution)/shard_map/ppermute | solution.py:385
  30.0 5.2 %collective-permute-start.5 = (bf16[2,144,128]{2,1,0:T(8,128)(2,1)S(1)}, bf16[2,144,128]{2,1,0:T(8,128)(2,1)S(1)}, u32[]{:S(2)}, u32[]{:S(2)}) collective-permute-start(bf16[2,144,128]{2,1,0:T(8,128)(2,1)S(1)} %row_map.1), channel_id=1, source_target_pairs={{0,96},{8,104},{16,112},{24,120},{32,0},{40,8},{48,16},{56,24},{64... | collective-permute-start | bytes 221192 | tf_op jit(solution)/shard_map/ppermute | solution.py:389
  33.1 5.9 %collective-permute-start.4 = (bf16[2,144,128]{2,1,0:T(8,128)(2,1)S(1)}, bf16[2,144,128]{2,1,0:T(8,128)(2,1)S(1)}, u32[]{:S(2)}, u32[]{:S(2)}) collective-permute-start(bf16[2,144,128]{2,1,0:T(8,128)(2,1)S(1)} %row_map.1), channel_id=1, source_target_pairs={{0,64},{8,72},{16,80},{24,88},{32,96},{40,104},{48,112},{56,120},{... | collective-permute-start | bytes 221192 | tf_op jit(solution)/shard_map/ppermute | solution.py:389
  33.7 6.0 %collective-permute-start.3 = (bf16[2,144,128]{2,1,0:T(8,128)(2,1)S(1)}, bf16[2,144,128]{2,1,0:T(8,128)(2,1)S(1)}, u32[]{:S(2)}, u32[]{:S(2)}) collective-permute-start(bf16[2,144,128]{2,1,0:T(8,128)(2,1)S(1)} %row_map.1), channel_id=1, source_target_pairs={{0,32},{8,40},{16,48},{24,56},{32,64},{40,72},{48,80},{56,88},{64,... | collective-permute-start | bytes 221192 | tf_op jit(solution)/shard_map/ppermute | solution.py:389
  39.8 14.6 %copy-start = (bf16[2048,1024]{1,0:T(8,128)(2,1)S(1)}, bf16[2048,1024]{1,0:T(8,128)(2,1)}, u32[]{:S(2)}) copy-start(bf16[2048,1024]{1,0:T(8,128)(2,1)} %gate_ref.3) | copy-start | bytes 12582916
  39.8 14.6 %copy-start.1 = (bf16[2048,1024]{1,0:T(8,128)(2,1)S(1)}, bf16[2048,1024]{1,0:T(8,128)(2,1)}, u32[]{:S(2)}) copy-start(bf16[2048,1024]{1,0:T(8,128)(2,1)} %up_ref.3) | copy-start | bytes 12582916
  43.4 7.4 %collective-permute-start.8 = (bf16[256,256]{1,0:T(8,128)(2,1)S(1)}, bf16[256,256]{1,0:T(8,128)(2,1)S(1)}, u32[]{:S(2)}, u32[]{:S(2)}) collective-permute-start(bf16[256,256]{1,0:T(8,128)(2,1)S(1)} %get-tuple-element.22.m0), channel_id=1, source_target_pairs={{0,4},{1,5},{2,6},{3,7},{4,0},{5,1},{6,2},{7,3},{8,12},{9,13},{10,... | collective-permute-start | bytes 393224 | tf_op jit(solution)/shard_map/ppermute | solution.py:393
  47.3 5.4 %collective-permute-start.7 = (bf16[256,256]{1,0:T(8,128)(2,1)S(1)}, bf16[256,256]{1,0:T(8,128)(2,1)S(1)}, u32[]{:S(2)}, u32[]{:S(2)}) collective-permute-start(bf16[256,256]{1,0:T(8,128)(2,1)S(1)} %get-tuple-element.22.m0), channel_id=1, source_target_pairs={{0,6},{1,7},{2,0},{3,1},{4,2},{5,3},{6,4},{7,5},{8,14},{9,15},{10,... | collective-permute-start | bytes 393224 | tf_op jit(solution)/shard_map/ppermute | solution.py:393
  48.0 6.2 %collective-permute-start.6 = (bf16[256,256]{1,0:T(8,128)(2,1)S(1)}, bf16[256,256]{1,0:T(8,128)(2,1)S(1)}, u32[]{:S(2)}, u32[]{:S(2)}) collective-permute-start(bf16[256,256]{1,0:T(8,128)(2,1)S(1)} %get-tuple-element.22.m0), channel_id=1, source_target_pairs={{0,2},{1,3},{2,4},{3,5},{4,6},{5,7},{6,0},{7,1},{8,10},{9,11},{10,... | collective-permute-start | bytes 393224 | tf_op jit(solution)/shard_map/ppermute | solution.py:393
  54.3 2.2 %copy-start.2 = (bf16[1024,2048]{1,0:T(8,128)(2,1)S(1)}, bf16[1024,2048]{1,0:T(8,128)(2,1)}, u32[]{:S(2)}) copy-start(bf16[1024,2048]{1,0:T(8,128)(2,1)} %down_ref.3) | copy-start | bytes 12582916
  54.3 2.0 %collective-permute-start.9 = (bf16[4,256,256]{2,1,0:T(8,128)(2,1)S(1)}, bf16[4,256,256]{2,1,0:T(8,128)(2,1)S(1)}, u32[]{:S(2)}, u32[]{:S(2)}) collective-permute-start(bf16[4,256,256]{2,1,0:T(8,128)(2,1)S(1)} %pad_maximum_fusion), channel_id=1, source_target_pairs={{0,1},{1,0},{2,3},{3,2},{4,5},{5,4},{6,7},{7,6},{8,9},{9,8},{10,11... | collective-permute-start | bytes 1572872 | tf_op jit(solution)/shard_map/ppermute | solution.py:397
  58.4 2.0 %collective-permute-start.10 = (bf16[4,256,256]{2,1,0:T(8,128)(2,1)S(1)}, bf16[4,256,256]{2,1,0:T(8,128)(2,1)S(1)}, u32[]{:S(2)}, u32[]{:S(2)}) collective-permute-start(bf16[4,256,256]{2,1,0:T(8,128)(2,1)S(1)} %get-tuple-element.26), channel_id=1, source_target_pairs={{0,1},{1,0},{2,3},{3,2},{4,5},{5,4},{6,7},{7,6},{8,9},{9,8},{10,11... | collective-permute-start | bytes 1572872 | tf_op jit(solution)/shard_map/ppermute | solution.py:397
  60.6 7.9 %collective-permute-start.11 = (bf16[256,256]{1,0:T(8,128)(2,1)S(1)}, bf16[256,256]{1,0:T(8,128)(2,1)S(1)}, u32[]{:S(2)}, u32[]{:S(2)}) collective-permute-start(bf16[256,256]{1,0:T(8,128)(2,1)S(1)} %get-tuple-element.29), channel_id=1, source_target_pairs={{0,4},{1,5},{2,6},{3,7},{4,0},{5,1},{6,2},{7,3},{8,12},{9,13},{10,... | collective-permute-start | bytes 393224 | tf_op jit(solution)/shard_map/ppermute | solution.py:393
  61.9 7.2 %collective-permute-start.13 = (bf16[256,256]{1,0:T(8,128)(2,1)S(1)}, bf16[256,256]{1,0:T(8,128)(2,1)S(1)}, u32[]{:S(2)}, u32[]{:S(2)}) collective-permute-start(bf16[256,256]{1,0:T(8,128)(2,1)S(1)} %get-tuple-element.30), channel_id=1, source_target_pairs={{0,6},{1,7},{2,0},{3,1},{4,2},{5,3},{6,4},{7,5},{8,14},{9,15},{10,... | collective-permute-start | bytes 393224 | tf_op jit(solution)/shard_map/ppermute | solution.py:393
  63.5 7.1 %collective-permute-start.12 = (bf16[256,256]{1,0:T(8,128)(2,1)S(1)}, bf16[256,256]{1,0:T(8,128)(2,1)S(1)}, u32[]{:S(2)}, u32[]{:S(2)}) collective-permute-start(bf16[256,256]{1,0:T(8,128)(2,1)S(1)} %get-tuple-element.31), channel_id=1, source_target_pairs={{0,2},{1,3},{2,4},{3,5},{4,6},{5,7},{6,0},{7,1},{8,10},{9,11},{10,... | collective-permute-start | bytes 393224 | tf_op jit(solution)/shard_map/ppermute | solution.py:393

commit v10 on v9

--- a/solution.py
+++ b/solution.py
@@ -83,12 +83,13 @@
     cols = lax.broadcasted_iota(jnp.int32, (WIDTH, WIDTH), 1)
     eye = (rows == cols).astype(F32)
     noise = noise_ref[...].T
-    drive = jnp.dot(noise, iw_ref[...], precision=lax.Precision.HIGHEST, preferred_element_type=F32)
-    kept = retain_ref[...]
-    scale = jnp.sqrt(1.0 - kept * kept)
-    for b in range(2):
-        spread = jnp.broadcast_to(scale[b : b + 1, :], (WIDTH, steps)).T
-        off_ref[b * steps : (b + 1) * steps, :] = drive[:, b * WIDTH : (b + 1) * WIDTH] * spread
+    def drive_rows():
+        drive = jnp.dot(noise, iw_ref[...], precision=lax.Precision.HIGHEST, preferred_element_type=F32)
+        kept = retain_ref[...]
+        scale = jnp.sqrt(1.0 - kept * kept)
+        for b in range(2):
+            spread = jnp.broadcast_to(scale[b : b + 1, :], (WIDTH, steps)).T
+            off_ref[b * steps : (b + 1) * steps, :] = drive[:, b * WIDTH : (b + 1) * WIDTH] * spread
 
     def skew_body(base, i, carry):
         for b in range(2):
@@ -99,7 +100,9 @@
 
     for k in range(4):
         loads[k].wait()
-        lax.fori_loop(0, 16, functools.partial(skew_body, 16 * k), 0, unroll=8)
+        if k == 1:
+            drive_rows()
+        lax.fori_loop(0, 16, functools.partial(skew_body, 16 * k), 0, unroll=16)
     low = (noise.astype(BF16).astype(F32) * (1.0 / 64.0)).astype(BF16)
 
     def build_body(j, carry):
@@ -111,7 +114,7 @@
             am[pl.ds(b * steps * PITCH + j, steps, stride=PITCH), :] = out[:, b * WIDTH : (b + 1) * WIDTH]
         return carry
 
-    lax.fori_loop(0, WIDTH, build_body, 0, unroll=16)
+    lax.fori_loop(0, WIDTH, build_body, 0, unroll=32)
     tail_rows = ROWS - WIDTH
     tail_row = lax.broadcasted_iota(jnp.int32, (tail_rows, WIDTH), 0)
     zero = jnp.zeros((WIDTH, WIDTH), BF16)

time: 71.8 us -> 71.3 us (level)
  no operation moved by 1% of the time
where the time goes in v10:
time: 71.3 us; the launch traced here: 70.8 us
  Pallas kernels  27.4 us (38%)
  waiting for transfers between devices  23.4 us (33%)
  starting transfers between devices  18.7 us (26%)
  other arithmetic  0.96 us (1%)
    pallas_call x1, Pallas kernels, compose(): pl.pallas_call(compose_kernel, out_shape=(pltpu.VMEM((SPAN, 2 * GROUPS, W...  19.2 us
    ppermute x6, waiting for transfers between devices, z_back(): lax.ppermute(v, 'block', [(z * 2 + c, (z + k) % 4 * 2 + c) for z in range...  11.5 us
    ppermute x6, starting transfers between devices, z_back(): lax.ppermute(v, 'block', [(z * 2 + c, (z + k) % 4 * 2 + c) for z in range...  9.23 us
    ppermute x3, waiting for transfers between devices, x_back(): lax.ppermute(v, 'tm', [(y * 4 + x, y * 4 + (x + k) % 4) for y in range(4)...  5.12 us
    ppermute x3, waiting for transfers between devices, y_back(): lax.ppermute(v, 'tm', [(y * 4 + x, (y + k) % 4 * 4 + x) for y in range(4)...  5.04 us
    ppermute x3, starting transfers between devices, y_back(): lax.ppermute(v, 'tm', [(y * 4 + x, (y + k) % 4 * 4 + x) for y in range(4)...  4.69 us
    ppermute x3, starting transfers between devices, x_back(): lax.ppermute(v, 'tm', [(y * 4 + x, y * 4 + (x + k) % 4) for y in range(4)...  4.6 us
    pallas_call x1, Pallas kernels, replay(): pl.pallas_call(replay_kernel, out_shape=(jax.ShapeDtypeStruct((steps, 2 *...  3.61 us
  transfers between devices with their start and end apart: 14, of which 14 were waited for; matrix products, arithmetic and copies ran while one was open for 0% of the time, Pallas kernels for 3%

profile of v10, /device:TPU:0, one launch (start us, length us, event | category | flops | bytes accessed | tf_op | source)
XLA Modules:
  0.0 70.8 jit_solution(770150740822221827)
XLA Ops:
  0.0 19.2 %compose.1 = (bf16[16,32,128,128]{3,2,1,0:T(8,128)(2,1)S(1)}, f32[512,128]{1,0:T(8,128)S(1)}, bf16[2,144,128]{2,1,0:T(8,128)(2,1)S(1)}, bf16[32,128,128]{2,1,0:T(8,128)(2,1)S(1)}, f32[32,128]{1,0:T(8,128)S(1)}) custom-call(f32[64,256]{1,0:T(8,128)} %bitcast.34, f32[2,256]{1,0:T(2,128)} %bitcast.35, f32[2,256]{1,0:T(2,128)} %bitcast.36, ...), custom_call_target="tpu_custom_call" | custom-call | tf_op jit(solution)/shard_map/compose/pallas_call | solution.py:196
  19.2 2.9 %collective-permute-start.2 = (bf16[2,144,128]{2,1,0:T(8,128)(2,1)S(1)}, bf16[2,144,128]{2,1,0:T(8,128)(2,1)S(1)}, u32[]{:S(2)}, u32[]{:S(2)}) collective-permute-start(bf16[2,144,128]{2,1,0:T(8,128)(2,1)S(1)} %get-tuple-element.17.m0), channel_id=1, source_target_pairs={{0,24},{8,0},{16,8},{24,16},{32,56},{40,32},{48,40},{56,48},{64,88... | collective-permute-start | bytes 221192 | tf_op jit(solution)/shard_map/ppermute | solution.py:388
  22.2 0.8 %collective-permute-start.1 = (bf16[2,144,128]{2,1,0:T(8,128)(2,1)S(1)}, bf16[2,144,128]{2,1,0:T(8,128)(2,1)S(1)}, u32[]{:S(2)}, u32[]{:S(2)}) collective-permute-start(bf16[2,144,128]{2,1,0:T(8,128)(2,1)S(1)} %get-tuple-element.17.m0), channel_id=1, source_target_pairs={{0,16},{8,24},{16,0},{24,8},{32,48},{40,56},{48,32},{56,40},{64,80... | collective-permute-start | bytes 221192 | tf_op jit(solution)/shard_map/ppermute | solution.py:388
  23.0 0.9 %collective-permute-start = (bf16[2,144,128]{2,1,0:T(8,128)(2,1)S(1)}, bf16[2,144,128]{2,1,0:T(8,128)(2,1)S(1)}, u32[]{:S(2)}, u32[]{:S(2)}) collective-permute-start(bf16[2,144,128]{2,1,0:T(8,128)(2,1)S(1)} %get-tuple-element.17.m0), channel_id=1, source_target_pairs={{0,8},{8,16},{16,24},{24,0},{32,40},{40,48},{48,56},{56,32},{64,72... | collective-permute-start | bytes 221192 | tf_op jit(solution)/shard_map/ppermute | solution.py:388
  23.9 0.7 %collective-permute-done.2.m3.x3 = bf16[2,144,128]{2,1,0:T(8,128)(2,1)S(1)} collective-permute-done((bf16[2,144,128]{2,1,0:T(8,128)(2,1)S(1)}, bf16[2,144,128]{2,1,0:T(8,128)(2,1)S(1)}, u32[]{:S(2)}, u32[]{:S(2)}) %collective-permute-start.2) | collective-permute-done | bytes 73760 | tf_op jit(solution)/shard_map/ppermute | solution.py:388
  24.6 3.7 %collective-permute-done.1.m2.x2 = bf16[2,144,128]{2,1,0:T(8,128)(2,1)S(1)} collective-permute-done((bf16[2,144,128]{2,1,0:T(8,128)(2,1)S(1)}, bf16[2,144,128]{2,1,0:T(8,128)(2,1)S(1)}, u32[]{:S(2)}, u32[]{:S(2)}) %collective-permute-start.1) | collective-permute-done | bytes 73760 | tf_op jit(solution)/shard_map/ppermute | solution.py:388
  28.2 0.7 %collective-permute-done.m1.x1 = bf16[2,144,128]{2,1,0:T(8,128)(2,1)S(1)} collective-permute-done((bf16[2,144,128]{2,1,0:T(8,128)(2,1)S(1)}, bf16[2,144,128]{2,1,0:T(8,128)(2,1)S(1)}, u32[]{:S(2)}, u32[]{:S(2)}) %collective-permute-start) | collective-permute-done | bytes 73760 | tf_op jit(solution)/shard_map/ppermute | solution.py:388
  29.0 0.5 row_map.1
  29.5 3.1 %collective-permute-start.5 = (bf16[2,144,128]{2,1,0:T(8,128)(2,1)S(1)}, bf16[2,144,128]{2,1,0:T(8,128)(2,1)S(1)}, u32[]{:S(2)}, u32[]{:S(2)}) collective-permute-start(bf16[2,144,128]{2,1,0:T(8,128)(2,1)S(1)} %row_map.1), channel_id=1, source_target_pairs={{0,96},{8,104},{16,112},{24,120},{32,0},{40,8},{48,16},{56,24},{64... | collective-permute-start | bytes 221192 | tf_op jit(solution)/shard_map/ppermute | solution.py:392
  32.6 0.6 collective-permute-start.4
  33.2 1.0 %collective-permute-start.3 = (bf16[2,144,128]{2,1,0:T(8,128)(2,1)S(1)}, bf16[2,144,128]{2,1,0:T(8,128)(2,1)S(1)}, u32[]{:S(2)}, u32[]{:S(2)}) collective-permute-start(bf16[2,144,128]{2,1,0:T(8,128)(2,1)S(1)} %row_map.1), channel_id=1, source_target_pairs={{0,32},{8,40},{16,48},{24,56},{32,64},{40,72},{48,80},{56,88},{64,... | collective-permute-start | bytes 221192 | tf_op jit(solution)/shard_map/ppermute | solution.py:392
  34.2 0.5 collective-permute-done.5.y3
  34.7 3.8 %collective-permute-done.4.y2 = bf16[2,144,128]{2,1,0:T(8,128)(2,1)S(1)} collective-permute-done((bf16[2,144,128]{2,1,0:T(8,128)(2,1)S(1)}, bf16[2,144,128]{2,1,0:T(8,128)(2,1)S(1)}, u32[]{:S(2)}, u32[]{:S(2)}) %collective-permute-start.4) | collective-permute-done | bytes 73760 | tf_op jit(solution)/shard_map/ppermute | solution.py:392
  38.5 0.7 %collective-permute-done.3.y1 = bf16[2,144,128]{2,1,0:T(8,128)(2,1)S(1)} collective-permute-done((bf16[2,144,128]{2,1,0:T(8,128)(2,1)S(1)}, bf16[2,144,128]{2,1,0:T(8,128)(2,1)S(1)}, u32[]{:S(2)}, u32[]{:S(2)}) %collective-permute-start.3) | collective-permute-done | bytes 73760 | tf_op jit(solution)/shard_map/ppermute | solution.py:392
  39.2 3.6 %replay.1 = (f32[256,256]{1,0:T(8,128)S(1)}, bf16[256,256]{1,0:T(8,128)(2,1)S(1)}) custom-call(f32[32,128]{1,0:T(8,128)S(1)} %get-tuple-element.16.kept_ref, f32[2,128]{1,0:T(2,128)S(1)} %bitcast.31, bf16[2,144,128]{2,1,0:T(8,128)(2,1)S(1)} %collective-permute-done.3.y1, bf16[2,144,128]{2,1,0:T(8,128)(2,1)S(1)} %collective-permute-done.4.y2, ...), custom_call_target="tpu_custom_call" | custom-call | tf_op jit(solution)/shard_map/replay/pallas_call | solution.py:290
  42.9 3.9 %collective-permute-start.8 = (bf16[256,256]{1,0:T(8,128)(2,1)S(1)}, bf16[256,256]{1,0:T(8,128)(2,1)S(1)}, u32[]{:S(2)}, u32[]{:S(2)}) collective-permute-start(bf16[256,256]{1,0:T(8,128)(2,1)S(1)} %get-tuple-element.22.m0), channel_id=1, source_target_pairs={{0,4},{1,5},{2,6},{3,7},{4,0},{5,1},{6,2},{7,3},{8,12},{9,13},{10,... | collective-permute-start | bytes 393224 | tf_op jit(solution)/shard_map/ppermute | solution.py:396
  46.8 0.7 %collective-permute-start.7 = (bf16[256,256]{1,0:T(8,128)(2,1)S(1)}, bf16[256,256]{1,0:T(8,128)(2,1)S(1)}, u32[]{:S(2)}, u32[]{:S(2)}) collective-permute-start(bf16[256,256]{1,0:T(8,128)(2,1)S(1)} %get-tuple-element.22.m0), channel_id=1, source_target_pairs={{0,6},{1,7},{2,0},{3,1},{4,2},{5,3},{6,4},{7,5},{8,14},{9,15},{10,... | collective-permute-start | bytes 393224 | tf_op jit(solution)/shard_map/ppermute | solution.py:396
  47.5 1.3 %collective-permute-start.6 = (bf16[256,256]{1,0:T(8,128)(2,1)S(1)}, bf16[256,256]{1,0:T(8,128)(2,1)S(1)}, u32[]{:S(2)}, u32[]{:S(2)}) collective-permute-start(bf16[256,256]{1,0:T(8,128)(2,1)S(1)} %get-tuple-element.22.m0), channel_id=1, source_target_pairs={{0,2},{1,3},{2,4},{3,5},{4,6},{5,7},{6,0},{7,1},{8,10},{9,11},{10,... | collective-permute-start | bytes 393224 | tf_op jit(solution)/shard_map/ppermute | solution.py:396
  48.8 1.4 %collective-permute-done.8.m2 = bf16[256,256]{1,0:T(8,128)(2,1)S(1)} collective-permute-done((bf16[256,256]{1,0:T(8,128)(2,1)S(1)}, bf16[256,256]{1,0:T(8,128)(2,1)S(1)}, u32[]{:S(2)}, u32[]{:S(2)}) %collective-permute-start.8) | collective-permute-done | bytes 131104 | tf_op jit(solution)/shard_map/ppermute | solution.py:396
  50.3 1.9 %collective-permute-done.7.m3 = bf16[256,256]{1,0:T(8,128)(2,1)S(1)} collective-permute-done((bf16[256,256]{1,0:T(8,128)(2,1)S(1)}, bf16[256,256]{1,0:T(8,128)(2,1)S(1)}, u32[]{:S(2)}, u32[]{:S(2)}) %collective-permute-start.7) | collective-permute-done | bytes 131104 | tf_op jit(solution)/shard_map/ppermute | solution.py:396
  52.2 1.5 %collective-permute-done.6.m1 = bf16[256,256]{1,0:T(8,128)(2,1)S(1)} collective-permute-done((bf16[256,256]{1,0:T(8,128)(2,1)S(1)}, bf16[256,256]{1,0:T(8,128)(2,1)S(1)}, u32[]{:S(2)}, u32[]{:S(2)}) %collective-permute-start.6) | collective-permute-done | bytes 131104 | tf_op jit(solution)/shard_map/ppermute | solution.py:396
  53.9 1.3 %mine.1 = (f32[256,1024]{1,0:T(8,128)S(1)}, f32[256,1024]{1,0:T(8,128)S(1)}) custom-call(bf16[256,256]{1,0:T(8,128)(2,1)S(1)} %get-tuple-element.22.m0, bf16[256,256]{1,0:T(8,128)(2,1)S(1)} %collective-permute-done.6.m1, bf16[256,256]{1,0:T(8,128)(2,1)S(1)} %collective-permute-done.7.m3, bf16[256,256]{1,0:T(8,128)(2,1)S(1)} %collective-permute-done.8.m2, ...), custom_call_target="tpu_custom_call" | custom-call | tf_op jit(solution)/shard_map/mine/pallas_call | solution.py:360
  55.2 0.5 collective-permute-done.9.theirs_ref
  56.0 2.0 %forward.1 = (bf16[4,256,256]{2,1,0:T(8,128)(2,1)S(1)}, bf16[256,1024]{1,0:T(8,128)(2,1)S(1)}) custom-call(bf16[4,256,256]{2,1,0:T(8,128)(2,1)S(1)} %collective-permute-done.9.theirs_ref, f32[256,1024]{1,0:T(8,128)S(1)} %get-tuple-element.23.gate_in, f32[256,1024]{1,0:T(8,128)S(1)} %get-tuple-element.24.up_in, bf16[2048,1024]{1,0:T(8,128)(2,1)S(1)} %copy-done, ...), custom_call_target="tpu_custom_call" | custom-call | tf_op jit(solution)/shard_map/forward/pallas_call | solution.py:368
  58.0 0.7 %keep.1 = f32[4,256,256]{2,1,0:T(8,128)S(1)} custom-call(bf16[256,1024]{1,0:T(8,128)(2,1)S(1)} %get-tuple-element.25.hidden, bf16[1024,2048]{1,0:T(8,128)(2,1)S(1)} %copy-done.2), custom_call_target="tpu_custom_call" | custom-call | tf_op jit(solution)/shard_map/keep/pallas_call | solution.py:376
  58.8 1.1 %collective-permute-done.10 = bf16[4,256,256]{2,1,0:T(8,128)(2,1)S(1)} collective-permute-done((bf16[4,256,256]{2,1,0:T(8,128)(2,1)S(1)}, bf16[4,256,256]{2,1,0:T(8,128)(2,1)S(1)}, u32[]{:S(2)}, u32[]{:S(2)}) %collective-permute-start.10) | collective-permute-done | bytes 524320 | tf_op jit(solution)/shard_map/ppermute | solution.py:400
  60.1 1.2 %collective-permute-start.11 = (bf16[256,256]{1,0:T(8,128)(2,1)S(1)}, bf16[256,256]{1,0:T(8,128)(2,1)S(1)}, u32[]{:S(2)}, u32[]{:S(2)}) collective-permute-start(bf16[256,256]{1,0:T(8,128)(2,1)S(1)} %get-tuple-element.29), channel_id=1, source_target_pairs={{0,4},{1,5},{2,6},{3,7},{4,0},{5,1},{6,2},{7,3},{8,12},{9,13},{10,... | collective-permute-start | bytes 393224 | tf_op jit(solution)/shard_map/ppermute | solution.py:396
  61.3 1.6 %collective-permute-start.13 = (bf16[256,256]{1,0:T(8,128)(2,1)S(1)}, bf16[256,256]{1,0:T(8,128)(2,1)S(1)}, u32[]{:S(2)}, u32[]{:S(2)}) collective-permute-start(bf16[256,256]{1,0:T(8,128)(2,1)S(1)} %get-tuple-element.30), channel_id=1, source_target_pairs={{0,6},{1,7},{2,0},{3,1},{4,2},{5,3},{6,4},{7,5},{8,14},{9,15},{10,... | collective-permute-start | bytes 393224 | tf_op jit(solution)/shard_map/ppermute | solution.py:396
  63.4 4.7 %collective-permute-done.11 = bf16[256,256]{1,0:T(8,128)(2,1)S(1)} collective-permute-done((bf16[256,256]{1,0:T(8,128)(2,1)S(1)}, bf16[256,256]{1,0:T(8,128)(2,1)S(1)}, u32[]{:S(2)}, u32[]{:S(2)}) %collective-permute-start.11) | collective-permute-done | bytes 131104 | tf_op jit(solution)/shard_map/ppermute | solution.py:396
  68.0 0.5 collective-permute-done.13
  68.5 1.5 %collective-permute-done.12 = bf16[256,256]{1,0:T(8,128)(2,1)S(1)} collective-permute-done((bf16[256,256]{1,0:T(8,128)(2,1)S(1)}, bf16[256,256]{1,0:T(8,128)(2,1)S(1)}, u32[]{:S(2)}, u32[]{:S(2)}) %collective-permute-start.12) | collective-permute-done | bytes 131104 | tf_op jit(solution)/shard_map/ppermute | solution.py:396
  70.0 0.7 %fusion.4 = bf16[256,256]{1,0:T(8,128)(2,1)} fusion(f32[256,256]{1,0:T(8,128)S(1)} %get-tuple-element.21, f32[4,256,256]{2,1,0:T(8,128)S(1)} %get-tuple-element.28, bf16[256,256]{1,0:T(8,128)(2,1)S(1)} %collective-permute-done.13, bf16[256,256]{1,0:T(8,128)(2,1)S(1)} %collective-permute-done.12, bf16[256,256]{1,0:T(8,128)(2,1)S(1)} %collective-permute-done.11), kind=kLoop, calls=%fused_computation.7 | loop fusion | flops 524288 | bytes 1048576 | tf_op jit(solution)/shard_map/convert_element_type | solution.py:428
  (16 shorter events, 1.0 us)
Async XLA Ops:
  0.0 39.2 %copy-start.4 = (f32[256]{0:T(256)S(1)}, f32[256]{0:T(256)}, u32[]{:S(2)}) copy-start(f32[256]{0:T(256)} %param.14) | copy-start | bytes 3076
  0.0 39.2 %copy-start.3 = (f32[256]{0:T(256)S(1)}, f32[256]{0:T(256)}, u32[]{:S(2)}) copy-start(f32[256]{0:T(256)} %param.13) | copy-start | bytes 3076
  19.2 5.3 %collective-permute-start.2 = (bf16[2,144,128]{2,1,0:T(8,128)(2,1)S(1)}, bf16[2,144,128]{2,1,0:T(8,128)(2,1)S(1)}, u32[]{:S(2)}, u32[]{:S(2)}) collective-permute-start(bf16[2,144,128]{2,1,0:T(8,128)(2,1)S(1)} %get-tuple-element.17.m0), channel_id=1, source_target_pairs={{0,24},{8,0},{16,8},{24,16},{32,56},{40,32},{48,40},{56,48},{64,88... | collective-permute-start | bytes 221192 | tf_op jit(solution)/shard_map/ppermute | solution.py:388
  22.2 6.1 %collective-permute-start.1 = (bf16[2,144,128]{2,1,0:T(8,128)(2,1)S(1)}, bf16[2,144,128]{2,1,0:T(8,128)(2,1)S(1)}, u32[]{:S(2)}, u32[]{:S(2)}) collective-permute-start(bf16[2,144,128]{2,1,0:T(8,128)(2,1)S(1)} %get-tuple-element.17.m0), channel_id=1, source_target_pairs={{0,16},{8,24},{16,0},{24,8},{32,48},{40,56},{48,32},{56,40},{64,80... | collective-permute-start | bytes 221192 | tf_op jit(solution)/shard_map/ppermute | solution.py:388
  23.0 6.0 %collective-permute-start = (bf16[2,144,128]{2,1,0:T(8,128)(2,1)S(1)}, bf16[2,144,128]{2,1,0:T(8,128)(2,1)S(1)}, u32[]{:S(2)}, u32[]{:S(2)}) collective-permute-start(bf16[2,144,128]{2,1,0:T(8,128)(2,1)S(1)} %get-tuple-element.17.m0), channel_id=1, source_target_pairs={{0,8},{8,16},{16,24},{24,0},{32,40},{40,48},{48,56},{56,32},{64,72... | collective-permute-start | bytes 221192 | tf_op jit(solution)/shard_map/ppermute | solution.py:388
  29.5 5.2 %collective-permute-start.5 = (bf16[2,144,128]{2,1,0:T(8,128)(2,1)S(1)}, bf16[2,144,128]{2,1,0:T(8,128)(2,1)S(1)}, u32[]{:S(2)}, u32[]{:S(2)}) collective-permute-start(bf16[2,144,128]{2,1,0:T(8,128)(2,1)S(1)} %row_map.1), channel_id=1, source_target_pairs={{0,96},{8,104},{16,112},{24,120},{32,0},{40,8},{48,16},{56,24},{64... | collective-permute-start | bytes 221192 | tf_op jit(solution)/shard_map/ppermute | solution.py:392
  32.6 5.9 %collective-permute-start.4 = (bf16[2,144,128]{2,1,0:T(8,128)(2,1)S(1)}, bf16[2,144,128]{2,1,0:T(8,128)(2,1)S(1)}, u32[]{:S(2)}, u32[]{:S(2)}) collective-permute-start(bf16[2,144,128]{2,1,0:T(8,128)(2,1)S(1)} %row_map.1), channel_id=1, source_target_pairs={{0,64},{8,72},{16,80},{24,88},{32,96},{40,104},{48,112},{56,120},{... | collective-permute-start | bytes 221192 | tf_op jit(solution)/shard_map/ppermute | solution.py:392
  33.2 6.0 %collective-permute-start.3 = (bf16[2,144,128]{2,1,0:T(8,128)(2,1)S(1)}, bf16[2,144,128]{2,1,0:T(8,128)(2,1)S(1)}, u32[]{:S(2)}, u32[]{:S(2)}) collective-permute-start(bf16[2,144,128]{2,1,0:T(8,128)(2,1)S(1)} %row_map.1), channel_id=1, source_target_pairs={{0,32},{8,40},{16,48},{24,56},{32,64},{40,72},{48,80},{56,88},{64,... | collective-permute-start | bytes 221192 | tf_op jit(solution)/shard_map/ppermute | solution.py:392
  39.2 14.6 %copy-start = (bf16[2048,1024]{1,0:T(8,128)(2,1)S(1)}, bf16[2048,1024]{1,0:T(8,128)(2,1)}, u32[]{:S(2)}) copy-start(bf16[2048,1024]{1,0:T(8,128)(2,1)} %gate_ref.3) | copy-start | bytes 12582916
  39.2 14.6 %copy-start.1 = (bf16[2048,1024]{1,0:T(8,128)(2,1)S(1)}, bf16[2048,1024]{1,0:T(8,128)(2,1)}, u32[]{:S(2)}) copy-start(bf16[2048,1024]{1,0:T(8,128)(2,1)} %up_ref.3) | copy-start | bytes 12582916
  42.9 7.4 %collective-permute-start.8 = (bf16[256,256]{1,0:T(8,128)(2,1)S(1)}, bf16[256,256]{1,0:T(8,128)(2,1)S(1)}, u32[]{:S(2)}, u32[]{:S(2)}) collective-permute-start(bf16[256,256]{1,0:T(8,128)(2,1)S(1)} %get-tuple-element.22.m0), channel_id=1, source_target_pairs={{0,4},{1,5},{2,6},{3,7},{4,0},{5,1},{6,2},{7,3},{8,12},{9,13},{10,... | collective-permute-start | bytes 393224 | tf_op jit(solution)/shard_map/ppermute | solution.py:396
  46.8 5.4 %collective-permute-start.7 = (bf16[256,256]{1,0:T(8,128)(2,1)S(1)}, bf16[256,256]{1,0:T(8,128)(2,1)S(1)}, u32[]{:S(2)}, u32[]{:S(2)}) collective-permute-start(bf16[256,256]{1,0:T(8,128)(2,1)S(1)} %get-tuple-element.22.m0), channel_id=1, source_target_pairs={{0,6},{1,7},{2,0},{3,1},{4,2},{5,3},{6,4},{7,5},{8,14},{9,15},{10,... | collective-permute-start | bytes 393224 | tf_op jit(solution)/shard_map/ppermute | solution.py:396
  47.5 6.2 %collective-permute-start.6 = (bf16[256,256]{1,0:T(8,128)(2,1)S(1)}, bf16[256,256]{1,0:T(8,128)(2,1)S(1)}, u32[]{:S(2)}, u32[]{:S(2)}) collective-permute-start(bf16[256,256]{1,0:T(8,128)(2,1)S(1)} %get-tuple-element.22.m0), channel_id=1, source_target_pairs={{0,2},{1,3},{2,4},{3,5},{4,6},{5,7},{6,0},{7,1},{8,10},{9,11},{10,... | collective-permute-start | bytes 393224 | tf_op jit(solution)/shard_map/ppermute | solution.py:396
  53.8 2.2 %copy-start.2 = (bf16[1024,2048]{1,0:T(8,128)(2,1)S(1)}, bf16[1024,2048]{1,0:T(8,128)(2,1)}, u32[]{:S(2)}) copy-start(bf16[1024,2048]{1,0:T(8,128)(2,1)} %down_ref.3) | copy-start | bytes 12582916
  53.8 2.0 %collective-permute-start.9 = (bf16[4,256,256]{2,1,0:T(8,128)(2,1)S(1)}, bf16[4,256,256]{2,1,0:T(8,128)(2,1)S(1)}, u32[]{:S(2)}, u32[]{:S(2)}) collective-permute-start(bf16[4,256,256]{2,1,0:T(8,128)(2,1)S(1)} %pad_maximum_fusion), channel_id=1, source_target_pairs={{0,1},{1,0},{2,3},{3,2},{4,5},{5,4},{6,7},{7,6},{8,9},{9,8},{10,11... | collective-permute-start | bytes 1572872 | tf_op jit(solution)/shard_map/ppermute | solution.py:400
  57.9 2.0 %collective-permute-start.10 = (bf16[4,256,256]{2,1,0:T(8,128)(2,1)S(1)}, bf16[4,256,256]{2,1,0:T(8,128)(2,1)S(1)}, u32[]{:S(2)}, u32[]{:S(2)}) collective-permute-start(bf16[4,256,256]{2,1,0:T(8,128)(2,1)S(1)} %get-tuple-element.26), channel_id=1, source_target_pairs={{0,1},{1,0},{2,3},{3,2},{4,5},{5,4},{6,7},{7,6},{8,9},{9,8},{10,11... | collective-permute-start | bytes 1572872 | tf_op jit(solution)/shard_map/ppermute | solution.py:400
  60.1 7.9 %collective-permute-start.11 = (bf16[256,256]{1,0:T(8,128)(2,1)S(1)}, bf16[256,256]{1,0:T(8,128)(2,1)S(1)}, u32[]{:S(2)}, u32[]{:S(2)}) collective-permute-start(bf16[256,256]{1,0:T(8,128)(2,1)S(1)} %get-tuple-element.29), channel_id=1, source_target_pairs={{0,4},{1,5},{2,6},{3,7},{4,0},{5,1},{6,2},{7,3},{8,12},{9,13},{10,... | collective-permute-start | bytes 393224 | tf_op jit(solution)/shard_map/ppermute | solution.py:396
  61.3 7.2 %collective-permute-start.13 = (bf16[256,256]{1,0:T(8,128)(2,1)S(1)}, bf16[256,256]{1,0:T(8,128)(2,1)S(1)}, u32[]{:S(2)}, u32[]{:S(2)}) collective-permute-start(bf16[256,256]{1,0:T(8,128)(2,1)S(1)} %get-tuple-element.30), channel_id=1, source_target_pairs={{0,6},{1,7},{2,0},{3,1},{4,2},{5,3},{6,4},{7,5},{8,14},{9,15},{10,... | collective-permute-start | bytes 393224 | tf_op jit(solution)/shard_map/ppermute | solution.py:396
  62.9 7.1 %collective-permute-start.12 = (bf16[256,256]{1,0:T(8,128)(2,1)S(1)}, bf16[256,256]{1,0:T(8,128)(2,1)S(1)}, u32[]{:S(2)}, u32[]{:S(2)}) collective-permute-start(bf16[256,256]{1,0:T(8,128)(2,1)S(1)} %get-tuple-element.31), channel_id=1, source_target_pairs={{0,2},{1,3},{2,4},{3,5},{4,6},{5,7},{6,0},{7,1},{8,10},{9,11},{10,... | collective-permute-start | bytes 393224 | tf_op jit(solution)/shard_map/ppermute | solution.py:396

commit v11 on v10

--- a/solution.py
+++ b/solution.py
@@ -114,7 +114,7 @@
             am[pl.ds(b * steps * PITCH + j, steps, stride=PITCH), :] = out[:, b * WIDTH : (b + 1) * WIDTH]
         return carry
 
-    lax.fori_loop(0, WIDTH, build_body, 0, unroll=32)
+    lax.fori_loop(0, WIDTH, build_body, 0, unroll=64)
     tail_rows = ROWS - WIDTH
     tail_row = lax.broadcasted_iota(jnp.int32, (tail_rows, WIDTH), 0)
     zero = jnp.zeros((WIDTH, WIDTH), BF16)
@@ -282,7 +282,7 @@
             normed_ref[pl.ds(base, SPAN), b * WIDTH : (b + 1) * WIDTH] = normed.astype(BF16)
         return tuple(after)
 
-    lax.fori_loop(0, GROUPS, group, tuple(entry), unroll=8)
+    lax.fori_loop(0, GROUPS, group, tuple(entry), unroll=16)
 
 
 def replay(kept, init, y_maps, x_maps, off, grp, gain, q):
@@ -422,10 +422,10 @@
     keep, sent = forward(mine, gate_weight, up_weight, down_weight)
     chip = keep + other_core(sent).astype(F32)
     low = chip.astype(BF16)
-    mixed = chip[0]
+    mixed = lax.optimization_barrier(states + chip[0])
     for k in (2, 1, 3):
         mixed = mixed + z_back(low[k], k).astype(F32)
-    return (states + mixed).astype(BF16)
+    return mixed.astype(BF16)
 
 
 def solution(mesh):

time: 71.3 us -> 70.8 us (level)
  no operation moved by 1% of the time
where the time goes in v11:
time: 70.8 us; the launch traced here: 70.3 us
  Pallas kernels  26.9 us (38%)
  waiting for transfers between devices  23.2 us (33%)
  starting transfers between devices  19 us (27%)
  other arithmetic  0.96 us (1%)
    pallas_call x1, Pallas kernels, compose(): pl.pallas_call(compose_kernel, out_shape=(pltpu.VMEM((SPAN, 2 * GROUPS, W...  19 us
    ppermute x6, waiting for transfers between devices, z_back(): lax.ppermute(v, 'block', [(z * 2 + c, (z + k) % 4 * 2 + c) for z in range...  11.5 us
    ppermute x6, starting transfers between devices, z_back(): lax.ppermute(v, 'block', [(z * 2 + c, (z + k) % 4 * 2 + c) for z in range...  9.25 us
    ppermute x3, waiting for transfers between devices, x_back(): lax.ppermute(v, 'tm', [(y * 4 + x, y * 4 + (x + k) % 4) for y in range(4)...  5.13 us
    ppermute x3, waiting for transfers between devices, y_back(): lax.ppermute(v, 'tm', [(y * 4 + x, (y + k) % 4 * 4 + x) for y in range(4)...  5.04 us
    ppermute x3, starting transfers between devices, y_back(): lax.ppermute(v, 'tm', [(y * 4 + x, (y + k) % 4 * 4 + x) for y in range(4)...  4.68 us
    ppermute x3, starting transfers between devices, x_back(): lax.ppermute(v, 'tm', [(y * 4 + x, y * 4 + (x + k) % 4) for y in range(4)...  4.59 us
    pallas_call x1, Pallas kernels, replay(): pl.pallas_call(replay_kernel, out_shape=(jax.ShapeDtypeStruct((steps, 2 *...  3.4 us
  transfers between devices with their start and end apart: 14, of which 14 were waited for; matrix products, arithmetic and copies ran while one was open for 0% of the time, Pallas kernels for 3%

profile of v11, /device:TPU:0, one launch (start us, length us, event | category | flops | bytes accessed | tf_op | source)
XLA Modules:
  0.0 70.3 jit_solution(14603939182051132918)
XLA Ops:
  0.0 19.0 %compose.1 = (bf16[16,32,128,128]{3,2,1,0:T(8,128)(2,1)S(1)}, f32[512,128]{1,0:T(8,128)S(1)}, bf16[2,144,128]{2,1,0:T(8,128)(2,1)S(1)}, bf16[32,128,128]{2,1,0:T(8,128)(2,1)S(1)}, f32[32,128]{1,0:T(8,128)S(1)}) custom-call(f32[64,256]{1,0:T(8,128)} %bitcast.26, f32[2,256]{1,0:T(2,128)} %bitcast.27, f32[2,256]{1,0:T(2,128)} %bitcast.28, ...), custom_call_target="tpu_custom_call" | custom-call | tf_op jit(solution)/shard_map/compose/pallas_call | solution.py:196
  19.0 2.9 %collective-permute-start.2 = (bf16[2,144,128]{2,1,0:T(8,128)(2,1)S(1)}, bf16[2,144,128]{2,1,0:T(8,128)(2,1)S(1)}, u32[]{:S(2)}, u32[]{:S(2)}) collective-permute-start(bf16[2,144,128]{2,1,0:T(8,128)(2,1)S(1)} %get-tuple-element.17.m0), channel_id=1, source_target_pairs={{0,24},{8,0},{16,8},{24,16},{32,56},{40,32},{48,40},{56,48},{64,88... | collective-permute-start | bytes 221192 | tf_op jit(solution)/shard_map/ppermute | solution.py:388
  21.9 0.8 %collective-permute-start.1 = (bf16[2,144,128]{2,1,0:T(8,128)(2,1)S(1)}, bf16[2,144,128]{2,1,0:T(8,128)(2,1)S(1)}, u32[]{:S(2)}, u32[]{:S(2)}) collective-permute-start(bf16[2,144,128]{2,1,0:T(8,128)(2,1)S(1)} %get-tuple-element.17.m0), channel_id=1, source_target_pairs={{0,16},{8,24},{16,0},{24,8},{32,48},{40,56},{48,32},{56,40},{64,80... | collective-permute-start | bytes 221192 | tf_op jit(solution)/shard_map/ppermute | solution.py:388
  22.7 0.9 %collective-permute-start = (bf16[2,144,128]{2,1,0:T(8,128)(2,1)S(1)}, bf16[2,144,128]{2,1,0:T(8,128)(2,1)S(1)}, u32[]{:S(2)}, u32[]{:S(2)}) collective-permute-start(bf16[2,144,128]{2,1,0:T(8,128)(2,1)S(1)} %get-tuple-element.17.m0), channel_id=1, source_target_pairs={{0,8},{8,16},{16,24},{24,0},{32,40},{40,48},{48,56},{56,32},{64,72... | collective-permute-start | bytes 221192 | tf_op jit(solution)/shard_map/ppermute | solution.py:388
  23.6 0.7 %collective-permute-done.2.m3.x3 = bf16[2,144,128]{2,1,0:T(8,128)(2,1)S(1)} collective-permute-done((bf16[2,144,128]{2,1,0:T(8,128)(2,1)S(1)}, bf16[2,144,128]{2,1,0:T(8,128)(2,1)S(1)}, u32[]{:S(2)}, u32[]{:S(2)}) %collective-permute-start.2) | collective-permute-done | bytes 73760 | tf_op jit(solution)/shard_map/ppermute | solution.py:388
  24.3 3.7 %collective-permute-done.1.m2.x2 = bf16[2,144,128]{2,1,0:T(8,128)(2,1)S(1)} collective-permute-done((bf16[2,144,128]{2,1,0:T(8,128)(2,1)S(1)}, bf16[2,144,128]{2,1,0:T(8,128)(2,1)S(1)}, u32[]{:S(2)}, u32[]{:S(2)}) %collective-permute-start.1) | collective-permute-done | bytes 73760 | tf_op jit(solution)/shard_map/ppermute | solution.py:388
  28.0 0.7 %collective-permute-done.m1.x1 = bf16[2,144,128]{2,1,0:T(8,128)(2,1)S(1)} collective-permute-done((bf16[2,144,128]{2,1,0:T(8,128)(2,1)S(1)}, bf16[2,144,128]{2,1,0:T(8,128)(2,1)S(1)}, u32[]{:S(2)}, u32[]{:S(2)}) %collective-permute-start) | collective-permute-done | bytes 73760 | tf_op jit(solution)/shard_map/ppermute | solution.py:388
  28.7 0.5 row_map.1
  29.2 3.1 %collective-permute-start.5 = (bf16[2,144,128]{2,1,0:T(8,128)(2,1)S(1)}, bf16[2,144,128]{2,1,0:T(8,128)(2,1)S(1)}, u32[]{:S(2)}, u32[]{:S(2)}) collective-permute-start(bf16[2,144,128]{2,1,0:T(8,128)(2,1)S(1)} %row_map.1), channel_id=1, source_target_pairs={{0,96},{8,104},{16,112},{24,120},{32,0},{40,8},{48,16},{56,24},{64... | collective-permute-start | bytes 221192 | tf_op jit(solution)/shard_map/ppermute | solution.py:392
  32.3 0.6 collective-permute-start.4
  32.9 1.0 %collective-permute-start.3 = (bf16[2,144,128]{2,1,0:T(8,128)(2,1)S(1)}, bf16[2,144,128]{2,1,0:T(8,128)(2,1)S(1)}, u32[]{:S(2)}, u32[]{:S(2)}) collective-permute-start(bf16[2,144,128]{2,1,0:T(8,128)(2,1)S(1)} %row_map.1), channel_id=1, source_target_pairs={{0,32},{8,40},{16,48},{24,56},{32,64},{40,72},{48,80},{56,88},{64,... | collective-permute-start | bytes 221192 | tf_op jit(solution)/shard_map/ppermute | solution.py:392
  33.9 0.5 collective-permute-done.5.y3
  34.4 3.8 %collective-permute-done.4.y2 = bf16[2,144,128]{2,1,0:T(8,128)(2,1)S(1)} collective-permute-done((bf16[2,144,128]{2,1,0:T(8,128)(2,1)S(1)}, bf16[2,144,128]{2,1,0:T(8,128)(2,1)S(1)}, u32[]{:S(2)}, u32[]{:S(2)}) %collective-permute-start.4) | collective-permute-done | bytes 73760 | tf_op jit(solution)/shard_map/ppermute | solution.py:392
  38.2 0.7 %collective-permute-done.3.y1 = bf16[2,144,128]{2,1,0:T(8,128)(2,1)S(1)} collective-permute-done((bf16[2,144,128]{2,1,0:T(8,128)(2,1)S(1)}, bf16[2,144,128]{2,1,0:T(8,128)(2,1)S(1)}, u32[]{:S(2)}, u32[]{:S(2)}) %collective-permute-start.3) | collective-permute-done | bytes 73760 | tf_op jit(solution)/shard_map/ppermute | solution.py:392
  39.0 3.4 %replay.1 = (f32[256,256]{1,0:T(8,128)S(1)}, bf16[256,256]{1,0:T(8,128)(2,1)S(1)}) custom-call(f32[32,128]{1,0:T(8,128)S(1)} %get-tuple-element.16.kept_ref, f32[2,128]{1,0:T(2,128)S(1)} %bitcast.23, bf16[2,144,128]{2,1,0:T(8,128)(2,1)S(1)} %collective-permute-done.3.y1, bf16[2,144,128]{2,1,0:T(8,128)(2,1)S(1)} %collective-permute-done.4.y2, ...), custom_call_target="tpu_custom_call" | custom-call | tf_op jit(solution)/shard_map/replay/pallas_call | solution.py:290
  42.4 4.0 %collective-permute-start.8 = (bf16[256,256]{1,0:T(8,128)(2,1)S(1)}, bf16[256,256]{1,0:T(8,128)(2,1)S(1)}, u32[]{:S(2)}, u32[]{:S(2)}) collective-permute-start(bf16[256,256]{1,0:T(8,128)(2,1)S(1)} %get-tuple-element.22.m0), channel_id=1, source_target_pairs={{0,4},{1,5},{2,6},{3,7},{4,0},{5,1},{6,2},{7,3},{8,12},{9,13},{10,... | collective-permute-start | bytes 393224 | tf_op jit(solution)/shard_map/ppermute | solution.py:396
  46.3 0.7 collective-permute-start.7
  47.0 1.3 %collective-permute-start.6 = (bf16[256,256]{1,0:T(8,128)(2,1)S(1)}, bf16[256,256]{1,0:T(8,128)(2,1)S(1)}, u32[]{:S(2)}, u32[]{:S(2)}) collective-permute-start(bf16[256,256]{1,0:T(8,128)(2,1)S(1)} %get-tuple-element.22.m0), channel_id=1, source_target_pairs={{0,2},{1,3},{2,4},{3,5},{4,6},{5,7},{6,0},{7,1},{8,10},{9,11},{10,... | collective-permute-start | bytes 393224 | tf_op jit(solution)/shard_map/ppermute | solution.py:396
  48.3 1.4 %collective-permute-done.8.m2 = bf16[256,256]{1,0:T(8,128)(2,1)S(1)} collective-permute-done((bf16[256,256]{1,0:T(8,128)(2,1)S(1)}, bf16[256,256]{1,0:T(8,128)(2,1)S(1)}, u32[]{:S(2)}, u32[]{:S(2)}) %collective-permute-start.8) | collective-permute-done | bytes 131104 | tf_op jit(solution)/shard_map/ppermute | solution.py:396
  49.8 1.9 %collective-permute-done.7.m3 = bf16[256,256]{1,0:T(8,128)(2,1)S(1)} collective-permute-done((bf16[256,256]{1,0:T(8,128)(2,1)S(1)}, bf16[256,256]{1,0:T(8,128)(2,1)S(1)}, u32[]{:S(2)}, u32[]{:S(2)}) %collective-permute-start.7) | collective-permute-done | bytes 131104 | tf_op jit(solution)/shard_map/ppermute | solution.py:396
  51.7 1.5 %collective-permute-done.6.m1 = bf16[256,256]{1,0:T(8,128)(2,1)S(1)} collective-permute-done((bf16[256,256]{1,0:T(8,128)(2,1)S(1)}, bf16[256,256]{1,0:T(8,128)(2,1)S(1)}, u32[]{:S(2)}, u32[]{:S(2)}) %collective-permute-start.6) | collective-permute-done | bytes 131104 | tf_op jit(solution)/shard_map/ppermute | solution.py:396
  53.6 1.3 %mine.1 = (f32[256,1024]{1,0:T(8,128)S(1)}, f32[256,1024]{1,0:T(8,128)S(1)}) custom-call(bf16[256,256]{1,0:T(8,128)(2,1)S(1)} %get-tuple-element.22.m0, bf16[256,256]{1,0:T(8,128)(2,1)S(1)} %collective-permute-done.6.m1, bf16[256,256]{1,0:T(8,128)(2,1)S(1)} %collective-permute-done.7.m3, bf16[256,256]{1,0:T(8,128)(2,1)S(1)} %collective-permute-done.8.m2, ...), custom_call_target="tpu_custom_call" | custom-call | tf_op jit(solution)/shard_map/mine/pallas_call | solution.py:360
  54.9 0.5 collective-permute-done.9.theirs_ref
  55.5 2.0 %forward.1 = (bf16[4,256,256]{2,1,0:T(8,128)(2,1)S(1)}, bf16[256,1024]{1,0:T(8,128)(2,1)S(1)}) custom-call(bf16[4,256,256]{2,1,0:T(8,128)(2,1)S(1)} %collective-permute-done.9.theirs_ref, f32[256,1024]{1,0:T(8,128)S(1)} %get-tuple-element.23.gate_in, f32[256,1024]{1,0:T(8,128)S(1)} %get-tuple-element.24.up_in, bf16[2048,1024]{1,0:T(8,128)(2,1)S(1)} %copy-done, ...), custom_call_target="tpu_custom_call" | custom-call | tf_op jit(solution)/shard_map/forward/pallas_call | solution.py:368
  57.6 0.7 %keep.1 = f32[4,256,256]{2,1,0:T(8,128)S(1)} custom-call(bf16[256,1024]{1,0:T(8,128)(2,1)S(1)} %get-tuple-element.25.hidden, bf16[1024,2048]{1,0:T(8,128)(2,1)S(1)} %copy-done.2), custom_call_target="tpu_custom_call" | custom-call | tf_op jit(solution)/shard_map/keep/pallas_call | solution.py:376
  58.4 1.1 %collective-permute-done.10 = bf16[4,256,256]{2,1,0:T(8,128)(2,1)S(1)} collective-permute-done((bf16[4,256,256]{2,1,0:T(8,128)(2,1)S(1)}, bf16[4,256,256]{2,1,0:T(8,128)(2,1)S(1)}, u32[]{:S(2)}, u32[]{:S(2)}) %collective-permute-start.10) | collective-permute-done | bytes 524320 | tf_op jit(solution)/shard_map/ppermute | solution.py:400
  59.6 1.2 %collective-permute-start.11 = (bf16[256,256]{1,0:T(8,128)(2,1)S(1)}, bf16[256,256]{1,0:T(8,128)(2,1)S(1)}, u32[]{:S(2)}, u32[]{:S(2)}) collective-permute-start(bf16[256,256]{1,0:T(8,128)(2,1)S(1)} %get-tuple-element.29), channel_id=1, source_target_pairs={{0,4},{1,5},{2,6},{3,7},{4,0},{5,1},{6,2},{7,3},{8,12},{9,13},{10,... | collective-permute-start | bytes 393224 | tf_op jit(solution)/shard_map/ppermute | solution.py:396
  60.9 1.6 %collective-permute-start.13 = (bf16[256,256]{1,0:T(8,128)(2,1)S(1)}, bf16[256,256]{1,0:T(8,128)(2,1)S(1)}, u32[]{:S(2)}, u32[]{:S(2)}) collective-permute-start(bf16[256,256]{1,0:T(8,128)(2,1)S(1)} %get-tuple-element.30), channel_id=1, source_target_pairs={{0,6},{1,7},{2,0},{3,1},{4,2},{5,3},{6,4},{7,5},{8,14},{9,15},{10,... | collective-permute-start | bytes 393224 | tf_op jit(solution)/shard_map/ppermute | solution.py:396
  62.9 4.6 %collective-permute-done.11 = bf16[256,256]{1,0:T(8,128)(2,1)S(1)} collective-permute-done((bf16[256,256]{1,0:T(8,128)(2,1)S(1)}, bf16[256,256]{1,0:T(8,128)(2,1)S(1)}, u32[]{:S(2)}, u32[]{:S(2)}) %collective-permute-start.11) | collective-permute-done | bytes 131104 | tf_op jit(solution)/shard_map/ppermute | solution.py:396
  67.5 0.5 collective-permute-done.13
  68.0 1.5 %collective-permute-done.12 = bf16[256,256]{1,0:T(8,128)(2,1)S(1)} collective-permute-done((bf16[256,256]{1,0:T(8,128)(2,1)S(1)}, bf16[256,256]{1,0:T(8,128)(2,1)S(1)}, u32[]{:S(2)}, u32[]{:S(2)}) %collective-permute-start.12) | collective-permute-done | bytes 131104 | tf_op jit(solution)/shard_map/ppermute | solution.py:396
  69.5 0.7 %add_convert_fusion = bf16[256,256]{1,0:T(8,128)(2,1)} fusion(bf16[256,256]{1,0:T(8,128)(2,1)S(1)} %collective-permute-done.13, bf16[256,256]{1,0:T(8,128)(2,1)S(1)} %collective-permute-done.12, f32[256,256]{1,0:T(8,128)S(1)} %fusion, bf16[256,256]{1,0:T(8,128)(2,1)S(1)} %collective-permute-done.11), kind=kLoop, calls=%fused_computation.4 | loop fusion | flops 458752 | bytes 786432 | tf_op jit(solution)/shard_map/convert_element_type | solution.py:428
  (17 shorter events, 1.2 us)
Async XLA Ops:
  0.0 38.9 %copy-start.4 = (f32[256]{0:T(256)S(1)}, f32[256]{0:T(256)}, u32[]{:S(2)}) copy-start(f32[256]{0:T(256)} %param.14) | copy-start | bytes 3076
  0.0 38.9 %copy-start.3 = (f32[256]{0:T(256)S(1)}, f32[256]{0:T(256)}, u32[]{:S(2)}) copy-start(f32[256]{0:T(256)} %param.13) | copy-start | bytes 3076
  19.0 5.3 %collective-permute-start.2 = (bf16[2,144,128]{2,1,0:T(8,128)(2,1)S(1)}, bf16[2,144,128]{2,1,0:T(8,128)(2,1)S(1)}, u32[]{:S(2)}, u32[]{:S(2)}) collective-permute-start(bf16[2,144,128]{2,1,0:T(8,128)(2,1)S(1)} %get-tuple-element.17.m0), channel_id=1, source_target_pairs={{0,24},{8,0},{16,8},{24,16},{32,56},{40,32},{48,40},{56,48},{64,88... | collective-permute-start | bytes 221192 | tf_op jit(solution)/shard_map/ppermute | solution.py:388
  21.9 6.1 %collective-permute-start.1 = (bf16[2,144,128]{2,1,0:T(8,128)(2,1)S(1)}, bf16[2,144,128]{2,1,0:T(8,128)(2,1)S(1)}, u32[]{:S(2)}, u32[]{:S(2)}) collective-permute-start(bf16[2,144,128]{2,1,0:T(8,128)(2,1)S(1)} %get-tuple-element.17.m0), channel_id=1, source_target_pairs={{0,16},{8,24},{16,0},{24,8},{32,48},{40,56},{48,32},{56,40},{64,80... | collective-permute-start | bytes 221192 | tf_op jit(solution)/shard_map/ppermute | solution.py:388
  22.7 6.0 %collective-permute-start = (bf16[2,144,128]{2,1,0:T(8,128)(2,1)S(1)}, bf16[2,144,128]{2,1,0:T(8,128)(2,1)S(1)}, u32[]{:S(2)}, u32[]{:S(2)}) collective-permute-start(bf16[2,144,128]{2,1,0:T(8,128)(2,1)S(1)} %get-tuple-element.17.m0), channel_id=1, source_target_pairs={{0,8},{8,16},{16,24},{24,0},{32,40},{40,48},{48,56},{56,32},{64,72... | collective-permute-start | bytes 221192 | tf_op jit(solution)/shard_map/ppermute | solution.py:388
  29.2 5.2 %collective-permute-start.5 = (bf16[2,144,128]{2,1,0:T(8,128)(2,1)S(1)}, bf16[2,144,128]{2,1,0:T(8,128)(2,1)S(1)}, u32[]{:S(2)}, u32[]{:S(2)}) collective-permute-start(bf16[2,144,128]{2,1,0:T(8,128)(2,1)S(1)} %row_map.1), channel_id=1, source_target_pairs={{0,96},{8,104},{16,112},{24,120},{32,0},{40,8},{48,16},{56,24},{64... | collective-permute-start | bytes 221192 | tf_op jit(solution)/shard_map/ppermute | solution.py:392
  32.3 5.9 %collective-permute-start.4 = (bf16[2,144,128]{2,1,0:T(8,128)(2,1)S(1)}, bf16[2,144,128]{2,1,0:T(8,128)(2,1)S(1)}, u32[]{:S(2)}, u32[]{:S(2)}) collective-permute-start(bf16[2,144,128]{2,1,0:T(8,128)(2,1)S(1)} %row_map.1), channel_id=1, source_target_pairs={{0,64},{8,72},{16,80},{24,88},{32,96},{40,104},{48,112},{56,120},{... | collective-permute-start | bytes 221192 | tf_op jit(solution)/shard_map/ppermute | solution.py:392
  32.9 6.0 %collective-permute-start.3 = (bf16[2,144,128]{2,1,0:T(8,128)(2,1)S(1)}, bf16[2,144,128]{2,1,0:T(8,128)(2,1)S(1)}, u32[]{:S(2)}, u32[]{:S(2)}) collective-permute-start(bf16[2,144,128]{2,1,0:T(8,128)(2,1)S(1)} %row_map.1), channel_id=1, source_target_pairs={{0,32},{8,40},{16,48},{24,56},{32,64},{40,72},{48,80},{56,88},{64,... | collective-permute-start | bytes 221192 | tf_op jit(solution)/shard_map/ppermute | solution.py:392
  38.9 14.6 %copy-start = (bf16[2048,1024]{1,0:T(8,128)(2,1)S(1)}, bf16[2048,1024]{1,0:T(8,128)(2,1)}, u32[]{:S(2)}) copy-start(bf16[2048,1024]{1,0:T(8,128)(2,1)} %gate_ref.3) | copy-start | bytes 12582916
  39.0 14.6 %copy-start.1 = (bf16[2048,1024]{1,0:T(8,128)(2,1)S(1)}, bf16[2048,1024]{1,0:T(8,128)(2,1)}, u32[]{:S(2)}) copy-start(bf16[2048,1024]{1,0:T(8,128)(2,1)} %up_ref.3) | copy-start | bytes 12582916
  42.4 7.4 %collective-permute-start.8 = (bf16[256,256]{1,0:T(8,128)(2,1)S(1)}, bf16[256,256]{1,0:T(8,128)(2,1)S(1)}, u32[]{:S(2)}, u32[]{:S(2)}) collective-permute-start(bf16[256,256]{1,0:T(8,128)(2,1)S(1)} %get-tuple-element.22.m0), channel_id=1, source_target_pairs={{0,4},{1,5},{2,6},{3,7},{4,0},{5,1},{6,2},{7,3},{8,12},{9,13},{10,... | collective-permute-start | bytes 393224 | tf_op jit(solution)/shard_map/ppermute | solution.py:396
  46.3 5.4 %collective-permute-start.7 = (bf16[256,256]{1,0:T(8,128)(2,1)S(1)}, bf16[256,256]{1,0:T(8,128)(2,1)S(1)}, u32[]{:S(2)}, u32[]{:S(2)}) collective-permute-start(bf16[256,256]{1,0:T(8,128)(2,1)S(1)} %get-tuple-element.22.m0), channel_id=1, source_target_pairs={{0,6},{1,7},{2,0},{3,1},{4,2},{5,3},{6,4},{7,5},{8,14},{9,15},{10,... | collective-permute-start | bytes 393224 | tf_op jit(solution)/shard_map/ppermute | solution.py:396
  47.0 6.2 %collective-permute-start.6 = (bf16[256,256]{1,0:T(8,128)(2,1)S(1)}, bf16[256,256]{1,0:T(8,128)(2,1)S(1)}, u32[]{:S(2)}, u32[]{:S(2)}) collective-permute-start(bf16[256,256]{1,0:T(8,128)(2,1)S(1)} %get-tuple-element.22.m0), channel_id=1, source_target_pairs={{0,2},{1,3},{2,4},{3,5},{4,6},{5,7},{6,0},{7,1},{8,10},{9,11},{10,... | collective-permute-start | bytes 393224 | tf_op jit(solution)/shard_map/ppermute | solution.py:396
  53.3 2.2 %copy-start.2 = (bf16[1024,2048]{1,0:T(8,128)(2,1)S(1)}, bf16[1024,2048]{1,0:T(8,128)(2,1)}, u32[]{:S(2)}) copy-start(bf16[1024,2048]{1,0:T(8,128)(2,1)} %down_ref.3) | copy-start | bytes 12582916
  53.3 2.2 %collective-permute-start.9 = (bf16[4,256,256]{2,1,0:T(8,128)(2,1)S(1)}, bf16[4,256,256]{2,1,0:T(8,128)(2,1)S(1)}, u32[]{:S(2)}, u32[]{:S(2)}) collective-permute-start(bf16[4,256,256]{2,1,0:T(8,128)(2,1)S(1)} %pad_maximum_fusion), channel_id=1, source_target_pairs={{0,1},{1,0},{2,3},{3,2},{4,5},{5,4},{6,7},{7,6},{8,9},{9,8},{10,11... | collective-permute-start | bytes 1572872 | tf_op jit(solution)/shard_map/ppermute | solution.py:400
  57.4 2.0 %collective-permute-start.10 = (bf16[4,256,256]{2,1,0:T(8,128)(2,1)S(1)}, bf16[4,256,256]{2,1,0:T(8,128)(2,1)S(1)}, u32[]{:S(2)}, u32[]{:S(2)}) collective-permute-start(bf16[4,256,256]{2,1,0:T(8,128)(2,1)S(1)} %get-tuple-element.26), channel_id=1, source_target_pairs={{0,1},{1,0},{2,3},{3,2},{4,5},{5,4},{6,7},{7,6},{8,9},{9,8},{10,11... | collective-permute-start | bytes 1572872 | tf_op jit(solution)/shard_map/ppermute | solution.py:400
  59.6 7.9 %collective-permute-start.11 = (bf16[256,256]{1,0:T(8,128)(2,1)S(1)}, bf16[256,256]{1,0:T(8,128)(2,1)S(1)}, u32[]{:S(2)}, u32[]{:S(2)}) collective-permute-start(bf16[256,256]{1,0:T(8,128)(2,1)S(1)} %get-tuple-element.29), channel_id=1, source_target_pairs={{0,4},{1,5},{2,6},{3,7},{4,0},{5,1},{6,2},{7,3},{8,12},{9,13},{10,... | collective-permute-start | bytes 393224 | tf_op jit(solution)/shard_map/ppermute | solution.py:396
  60.9 7.2 %collective-permute-start.13 = (bf16[256,256]{1,0:T(8,128)(2,1)S(1)}, bf16[256,256]{1,0:T(8,128)(2,1)S(1)}, u32[]{:S(2)}, u32[]{:S(2)}) collective-permute-start(bf16[256,256]{1,0:T(8,128)(2,1)S(1)} %get-tuple-element.30), channel_id=1, source_target_pairs={{0,6},{1,7},{2,0},{3,1},{4,2},{5,3},{6,4},{7,5},{8,14},{9,15},{10,... | collective-permute-start | bytes 393224 | tf_op jit(solution)/shard_map/ppermute | solution.py:396
  62.5 7.1 %collective-permute-start.12 = (bf16[256,256]{1,0:T(8,128)(2,1)S(1)}, bf16[256,256]{1,0:T(8,128)(2,1)S(1)}, u32[]{:S(2)}, u32[]{:S(2)}) collective-permute-start(bf16[256,256]{1,0:T(8,128)(2,1)S(1)} %get-tuple-element.31), channel_id=1, source_target_pairs={{0,2},{1,3},{2,4},{3,5},{4,6},{5,7},{6,0},{7,1},{8,10},{9,11},{10,... | collective-permute-start | bytes 393224 | tf_op jit(solution)/shard_map/ppermute | solution.py:396
